TPU v7x, 32 devices: a whole 2x2x4 slice. The times are simulated.
32 devices in a mesh: groups: 2 (over y), ctx: 4 (over z), exp: 2 (over x), tp: 2 (over core).
Axes of the slice: x: 2, y: 2, z: 4, core: 2. Of those that a mesh axis runs over, the one named last changes fastest.
Arguments:
- queries: bfloat16 [1024, 4096], P(('groups', 'ctx'), ('exp', 'tp')), parts along dimension 0, may hold values from -6 to 6
- keys: bfloat16 [1024, 512], P(('groups', 'ctx')), parts along dimension 0, may hold values from -6 to 6
- values: bfloat16 [1024, 512], P(('groups', 'ctx')), parts along dimension 0, may hold values from -6 to 6
- out_weight: bfloat16 [4096, 2048], P(('exp', 'tp')), may hold values from -0.25 to 0.25
- resid: bfloat16 [1024, 2048], P(('groups', 'ctx', 'exp', 'tp')), parts along dimension 0, may hold values from -6 to 6
- expert_ids: int32 [1024, 8], P(('groups', 'ctx', 'exp')), parts along dimension 0, may hold values from 0 to 63, all different within a row; in each aligned block of 64 rows (0 to 63, 64 to 127, ...) at most 8 rows name the same one
- router_probs: float32 [1024, 8], P(('groups', 'ctx', 'exp')), parts along dimension 0, may hold values from 0.05 to 1
- w_gate: bfloat16 [128, 2048, 384], P(('ctx', 'exp'), None, 'tp'), may hold values from -0.125 to 0.125
- w_up: bfloat16 [128, 2048, 384], P(('ctx', 'exp'), None, 'tp'), may hold values from -0.125 to 0.125
- w_down: bfloat16 [128, 384, 2048], P(('ctx', 'exp'), 'tp'), may hold values from -0.4375 to 0.4375
Outputs:
- layer_out: bfloat16 [1024, 2048], P(('groups', 'ctx', 'exp', 'tp')), parts along dimension 0
There are 2 independent parts, one for each index of `groups`. A program takes and returns all parts, laid end to end along the dimension named above; an argument that names none is the same for every part. Nothing has to cross between parts.
Inputs may be any that keep to these rules, and one draw needn't show every extreme that they name: `expert_ids`: each row names 8 different experts. Within the rows held by one index of ctx and exp (aligned blocks of 128 / 2 rows), no expert is named more than 8 times; in some such blocks some expert is named exactly 8 times.
All inputs are finite; a program needn't handle non-finite values.
Results may differ from a plain program's by a relative error of at most 0.01.
Values may be sent and summed in bfloat16 or wider, within the bound.
No kernel may reach another device: no remote copies, remote signals or barrier semaphores. Data moves between devices by JAX's collectives and lax.ppermute only.
A program may use at most 128 MiB of HBM per device.

v0:
```python
import math

import jax
import jax.numpy as jnp
from jax import lax
from jax.sharding import PartitionSpec as P

HEAD_DIMENSION = 128
QUERY_HEADS = 32
KEY_VALUE_HEADS = 4
EXPERTS = 64
TOPK = 8


def attend_blocks(blocks, key_head, value_head, heads_here):
    score_scale = 1.0 / math.sqrt(HEAD_DIMENSION)

    def make_state(query_rows):
        row_total = query_rows.shape[0]
        return (
            jnp.full((row_total, heads_here), -1e30, jnp.float32),
            jnp.zeros((row_total, heads_here), jnp.float32),
            jnp.zeros((row_total, heads_here, HEAD_DIMENSION), jnp.float32),
        )

    initial = tuple((make_state(query_rows) for query_rows, query_places in blocks))

    def fold_keys(carry, piece, first):
        key_piece, value_piece = piece
        key_places = jnp.arange(key_piece.shape[0], dtype=jnp.int32)
        updated = []
        for (query_rows, query_places), state in zip(blocks, carry):

            def refresh(state, query_rows=query_rows, query_places=query_places):
                running_max, running_sum, accum = state
                shaped = query_rows.reshape(query_rows.shape[0], heads_here, HEAD_DIMENSION)
                scores = (
                    jnp.einsum("qhd,kd->qhk", shaped, key_piece, preferred_element_type=jnp.float32)
                    * score_scale
                )
                allowed = key_places[None, None, :] <= query_places[:, None, None]
                scores = jnp.where(allowed, scores, -1e30)
                new_max = jnp.maximum(running_max, jnp.max(scores, axis=2))
                weights = jnp.where(allowed, jnp.exp(scores - new_max[:, :, None]), 0.0)
                running_sum = jnp.sum(weights, axis=2)
                accum = jnp.einsum(
                    "qhk,kd->qhd",
                    weights,
                    value_piece.astype(jnp.float32),
                    precision=lax.Precision.HIGHEST,
                )
                return (new_max, running_sum, accum)

            needed = first <= query_places[-1]
            updated.append(lax.cond(needed, refresh, lambda state: state, state))
        return tuple(updated)

    final = fold_keys(
        initial,
        (
            lax.all_gather(key_head, "ctx", axis=0, tiled=True),
            lax.all_gather(value_head, "ctx", axis=0, tiled=True),
        ),
        jnp.int32(0),
    )
    results = []
    for (query_rows, query_places), state in zip(blocks, final):
        running_max, running_sum, accum = state
        results.append(
            (accum / running_sum[:, :, None])
            .reshape(query_rows.shape[0], heads_here * HEAD_DIMENSION)
            .astype(jnp.bfloat16)
        )
    return results


def run_experts(inputs, w_gate, w_up, w_down):
    gate_out = jnp.einsum("rnd,rdf->rnf", inputs, w_gate, preferred_element_type=jnp.float32)
    up_out = jnp.einsum("rnd,rdf->rnf", inputs, w_up, preferred_element_type=jnp.float32)
    activated = (jax.nn.silu(gate_out) * up_out).astype(jnp.bfloat16)
    return jnp.einsum("rnf,rfd->rnd", activated, w_down, preferred_element_type=jnp.float32).astype(
        jnp.bfloat16
    )


def on_device(
    queries, keys, values, out_weight, resid, expert_ids, router_probs, w_gate, w_up, w_down
):
    rows_ctx = queries.shape[0]
    heads_here = queries.shape[1] // HEAD_DIMENSION
    group_width = QUERY_HEADS // KEY_VALUE_HEADS
    head_rank = lax.axis_index(("exp", "tp"))
    shared = head_rank * heads_here // group_width
    key_head = lax.dynamic_slice_in_dim(keys, shared * HEAD_DIMENSION, HEAD_DIMENSION, 1)
    value_head = lax.dynamic_slice_in_dim(values, shared * HEAD_DIMENSION, HEAD_DIMENSION, 1)
    cycle_rank = lax.axis_index("ctx")
    own_places = cycle_rank * rows_ctx + jnp.arange(rows_ctx, dtype=jnp.int32)
    attended = attend_blocks([(queries, own_places)], key_head, value_head, heads_here)[0]
    projected = lax.psum_scatter(
        jnp.dot(attended, out_weight, preferred_element_type=jnp.float32).astype(jnp.bfloat16),
        ("exp", "tp"),
        scatter_dimension=0,
        tiled=True,
    ).astype(jnp.float32)
    hidden = resid.astype(jnp.float32) + projected
    mean_square = jnp.mean(hidden * hidden, axis=1, keepdims=True)
    normed = (hidden * lax.rsqrt(mean_square + 1e-06)).astype(jnp.bfloat16)
    pair_rows = lax.all_gather(normed, "tp", axis=0, tiled=True)
    slot_count = min(8, expert_ids.shape[0])
    gate_weights = router_probs / jnp.sum(router_probs, axis=1, keepdims=True)
    flat_ids = expert_ids.reshape(-1)
    assigned = flat_ids.shape[0]
    onehot = (flat_ids[:, None] == jnp.arange(EXPERTS, dtype=jnp.int32)[None, :]).astype(jnp.int32)
    slots = jnp.sum(onehot * (jnp.cumsum(onehot, axis=0) - 1), axis=1)
    token_of = jnp.arange(assigned, dtype=jnp.int32) // TOPK
    peer_count = lax.axis_size(("ctx", "exp"))
    rows_here = w_gate.shape[0]
    cell_parts = []
    for half_index in range(2):
        half_rows_id = 2 * flat_ids + half_index
        target = half_rows_id // rows_here
        local_row = half_rows_id % rows_here
        cell_parts.append((local_row * slot_count + slots) * peer_count + target)
    cells = jnp.concatenate(cell_parts)
    table = (
        jnp.full((rows_here * slot_count * peer_count,), -1, jnp.int32)
        .at[cells]
        .set(jnp.concatenate([token_of, token_of]))
    )
    send_buffer = jnp.where(
        table[:, None] >= 0, pair_rows[jnp.maximum(table, 0)], jnp.zeros((), jnp.bfloat16)
    )
    model_width = pair_rows.shape[1]
    received = lax.all_to_all(
        send_buffer.reshape(rows_here * slot_count, peer_count, model_width),
        ("ctx", "exp"),
        split_axis=1,
        concat_axis=1,
        tiled=True,
    )
    expert_out = run_experts(
        received.reshape(rows_here, slot_count * peer_count, model_width), w_gate, w_up, w_down
    )
    returned = lax.all_to_all(
        expert_out.reshape(rows_here * slot_count, peer_count, model_width),
        ("ctx", "exp"),
        split_axis=1,
        concat_axis=1,
        tiled=True,
    )
    returned_flat = returned.reshape(rows_here * slot_count * peer_count, model_width)
    gathered = returned_flat[cells].reshape(2, expert_ids.shape[0], TOPK, model_width)
    routed_part = jnp.einsum(
        "hakd,ak->ad", gathered.astype(jnp.float32), gate_weights, precision=lax.Precision.HIGHEST
    )
    routed = lax.psum_scatter(
        routed_part.astype(jnp.bfloat16), "tp", scatter_dimension=0, tiled=True
    ).astype(jnp.float32)
    return (hidden + routed).astype(jnp.bfloat16)


def solution(mesh):
    in_specs = (
        P(("groups", "ctx"), ("exp", "tp")),
        P(("groups", "ctx"), None),
        P(("groups", "ctx"), None),
        P(("exp", "tp"), None),
        P(("groups", "ctx", "exp", "tp"), None),
        P(("groups", "ctx", "exp"), None),
        P(("groups", "ctx", "exp"), None),
        P(("ctx", "exp"), None, "tp"),
        P(("ctx", "exp"), None, "tp"),
        P(("ctx", "exp"), "tp", None),
    )
    out_specs = P(("groups", "ctx", "exp", "tp"), None)
    return jax.shard_map(
        on_device, mesh=mesh, in_specs=in_specs, out_specs=out_specs, check_vma=False
    )
```

profile of v0, /device:TPU:0, one launch (start us, length us, event | category | flops | bytes accessed | tf_op | source)
XLA Modules:
  0.0 357.5 jit_solution(8199557762816016982)
XLA Ops:
  6.5 0.9 copy-done
  7.4 15.0 %all_gather.10 = bf16[512,128]{1,0:T(8,128)(2,1)S(1)} all-gather(bf16[128,128]{1,0:T(8,128)(2,1)S(1)} %constant_dynamic-slice_fusion), channel_id=1, replica_groups=mesh['groups'=2,'ctx'=4,'exp'=2,'tp'=2] {'ctx'}, dimensions={0}, use_global_device_ids=true | all-gather | bytes 163840 | tf_op jit(solution)/shard_map/all_gather | solution.py:62
  22.5 0.8 constant_dynamic-slice_fusion.1
  23.3 13.5 %all_gather.9 = bf16[512,128]{1,0:T(8,128)(2,1)S(1)} all-gather(bf16[128,128]{1,0:T(8,128)(2,1)S(1)} %constant_dynamic-slice_fusion.1), channel_id=1, replica_groups=mesh['groups'=2,'ctx'=4,'exp'=2,'tp'=2] {'ctx'}, dimensions={0}, use_global_device_ids=true | all-gather | bytes 163840 | tf_op jit(solution)/shard_map/all_gather | solution.py:61
  36.8 0.6 slice.9
  38.0 4.1 %conditional.1 = (f32[128,8]{0,1:T(8,128)S(1)}, f32[128,8,128]{0,2,1:T(8,128)S(1)}) conditional(s32[]{:T(128)} %bitcast.2, () %tuple.13, (s32[512]{0:T(512)S(1)}, s32[128]{0:T(128)S(1)}, bf16[128,1024]{1,0:T(8,128)(2,1)}, bf16[512,128]{1,0:T(8,128)(2,1)S(1)}, bf16[512,128]{1,0:T(8,128)(2,1)S(1)}) %tuple.14), branch_computations={%region_0.1_spmd, %region_1.4_spmd} | conditional | flops 945880064 | bytes 7629328 | solution.py:55
  38.0 0.1 broadcast_compare_fusion
  38.1 1.5 fusion
  39.7 1.7 fusion.1
  41.4 0.7 fusion.2
  42.1 0.0 copy-start.6
  42.1 0.0 copy-start.3
  42.1 0.1 divide_convert_fusion
  42.2 3.7 %convolution_convert_fusion.1 = bf16[128,2048]{1,0:T(8,128)(2,1)} fusion(bf16[128,1024]{0,1:T(8,128)(2,1)S(1)} %bitcast.65, bf16[1024,2048]{1,0:T(8,128)(2,1)} %param.15), kind=kOutput, calls=%fused_computation.27 | convolution fusion | flops 537133056 | bytes 4980736 | tf_op jit(solution)/shard_map/dot_general | solution.py:100
  45.9 0.0 reduce-scatter.3.cloned.1.call-update
  45.9 0.1 copy.22
  46.0 0.1 eq.29
  46.1 1.2 reduce-window.6
  47.3 0.2 slice_reduce_fusion
  47.6 0.1 reshape.170
  47.7 0.1 fusion.24
  47.9 4.3 %scatter_custom_fusion = s32[1024]{0:T(1024)S(1)} fusion(s32[1024]{0:T(1024)S(1)} %bitcast.67, s32[1024]{0:T(1024)S(1)} %pad_add_fusion, s32[]{:T(128)} %constant.112.clone.1), kind=kCustom, calls=%fused_computation.82 | custom fusion | bytes 4100 | tf_op jit(solution)/shard_map/scatter | solution.py:128
  52.2 0.1 broadcast_in_dim.58
  52.3 0.1 copy.25
  52.4 16.6 %reduce-scatter.3.cloned.1.call-done = bf16[32,2048]{1,0:T(8,128)(2,1)} async-done(((bf16[128,2048]{1,0:T(8,128)(2,1)}), bf16[32,2048]{1,0:T(8,128)(2,1)}) %reduce-scatter.3.cloned.1.call-update) | async-done | bytes 131088 | tf_op jit(solution)/shard_map/reduce_scatter | solution.py:99
  69.0 1.1 multiply_reduce_fusion
  70.1 1.0 multiply_convert_fusion
  71.1 2.0 all_gather.11
  73.0 6.0 %gather_fusion = bf16[1024,2048]{1,0:T(8,128)(2,1)} fusion(bf16[64,2048]{1,0:T(8,128)(2,1)S(1)} %all_gather.11, s32[1024]{0:T(1024)S(1)} %maximum_clamp_fusion), kind=kCustom, calls=%fused_computation | custom fusion | bytes 8392704 | tf_op jit(solution)/shard_map/gather | solution.py:131
  79.1 8.5 %copy_select_fusion = bf16[128,8,2048]{2,0,1:T(8,128)(2,1)S(1)} fusion(bf16[128,8,2048]{2,1,0:T(8,128)(2,1)} %bitcast.62, pred[128,8]{0,1:T(8,128)(4,1)S(1)} %copy.25), kind=kLoop, calls=%fused_computation.25 | loop fusion | flops 2097152 | bytes 8389632 | tf_op jit(solution)/shard_map/jit(_where)/select_n | solution.py:130
  87.6 97.8 %all_to_all.10 = bf16[128,8,2048]{2,0,1:T(8,128)(2,1)S(1)} all-to-all(bf16[128,8,2048]{2,0,1:T(8,128)(2,1)S(1)} %copy_select_fusion), channel_id=1, replica_groups=mesh['groups'=2,'ctx'=4,'exp'=2,'tp'=2] {'ctx','exp'}, dimensions={1} | all-to-all | bytes 8388608 | tf_op jit(solution)/shard_map/all_to_all | solution.py:134
  185.4 2.3 copy.27
  187.7 2.0 copy-done.2
  189.7 8.7 %fusion.44 = f32[16,64,192]{2,1,0:T(8,128)S(1)} fusion(bf16[16,64,2048]{2,1,0:T(8,128)(2,1)S(1)} %bitcast.60, bf16[16,2048,192]{1,2,0:T(8,128)(2,1)} %param.19), kind=kOutput, calls=%fused_computation.94 | convolution fusion | flops 805306368 | bytes 17563648 | tf_op jit(solution)/shard_map/rnd,rdf->rnf/dot_general | solution.py:78
  198.4 14.0 %convolution_convert_fusion = bf16[16,64,2048]{2,1,0:T(8,128)(2,1)} fusion(bf16[16,192,2048]{2,1,0:T(8,128)(2,1)} %param.21, bf16[16,64,2048]{2,1,0:T(8,128)(2,1)} %bitcast.61, bf16[16,2048,192]{1,2,0:T(8,128)(2,1)} %param.20, f32[16,64,192]{2,1,0:T(8,128)S(1)} %fusion.44), kind=kOutput, calls=%fused_computation.26 | convolution fusion | flops 1613889536 | bytes 34340864 | tf_op jit(solution)/shard_map/rnf,rfd->rnd/dot_general | solution.py:81
  212.3 6.5 %copy.28 = bf16[128,8,2048]{2,0,1:T(8,128)(2,1)} copy(bf16[128,8,2048]{2,1,0:T(8,128)(2,1)} %bitcast.63) | data formatting | bytes 8388608 | tf_op jit(solution)/shard_map/reshape | solution.py:145
  218.8 4.7 %all-to-all-start.1 = ((bf16[128,8,2048]{2,0,1:T(8,128)(2,1)}), bf16[128,8,2048]{2,0,1:T(8,128)(2,1)}, u32[]{:S(2)}, u32[]{:S(2)}) async-start(bf16[128,8,2048]{2,0,1:T(8,128)(2,1)} %copy.28), calls=%async_computation.2 | async-start | bytes 8388608 | tf_op jit(solution)/shard_map/all_to_all | solution.py:144
  223.5 0.3 reduce-scatter.5.cloned.1.call-start
  223.8 0.1 copy.30
  223.9 91.9 %all-to-all-done.1 = bf16[128,8,2048]{2,0,1:T(8,128)(2,1)} async-done(((bf16[128,8,2048]{2,0,1:T(8,128)(2,1)}), bf16[128,8,2048]{2,0,1:T(8,128)(2,1)}, u32[]{:S(2)}, u32[]{:S(2)}) %all-to-all-start.1) | async-done | bytes 4194336 | tf_op jit(solution)/shard_map/all_to_all | solution.py:144
  315.8 6.5 %copy.46 = bf16[128,8,2048]{2,1,0:T(8,128)(2,1)} copy(bf16[128,8,2048]{2,0,1:T(8,128)(2,1)} %all-to-all-done.1) | data formatting | bytes 8388608 | tf_op jit(solution)/shard_map/all_to_all | solution.py:144
  322.3 11.6 %gather_fusion.1 = bf16[1024,2048]{1,0:T(8,128)(2,1)} fusion(bf16[1024,2048]{1,0:T(8,128)(2,1)} %bitcast.59, s32[1024]{0:T(1024)S(1)} %broadcast_clamp_fusion), kind=kCustom, calls=%fused_computation.1 | custom fusion | bytes 8392704 | tf_op jit(solution)/shard_map/gather | solution.py:152
  333.8 3.7 %convert_reduce_fusion = f32[64,8,2048]{2,1,0:T(8,128)S(1)} fusion(bf16[2,64,8,2048]{3,2,1,0:T(8,128)(2,1)} %bitcast.64), kind=kLoop, calls=%fused_computation.23 | loop fusion | flops 3145728 | bytes 8388608 | tf_op jit(solution)/shard_map/hakd,ak->ad/reduce_sum | solution.py:153
  337.5 3.8 %fusion.45 = bf16[64,1,2048]{2,1,0:T(2,128)(2,1)S(1)} fusion(f32[64,8,2048]{2,1,0:T(8,128)S(1)} %convert_reduce_fusion, f32[64,8,1]{1,2,0:T(1,128)S(1)} %copy.30), kind=kOutput, calls=%fused_computation.95 | convolution fusion | flops 12582912 | bytes 4458496 | tf_op jit(solution)/shard_map/hakd,ak->ad/dot_general | solution.py:153
  341.4 0.8 copy.47
  342.2 0.0 reduce-scatter.5.cloned.1.call-update
  342.2 6.8 %reduce-scatter.5.cloned.1.call-done = bf16[32,2048]{1,0:T(8,128)(2,1)} async-done(((bf16[64,2048]{1,0:T(8,128)(2,1)}), bf16[32,2048]{1,0:T(8,128)(2,1)}) %reduce-scatter.5.cloned.1.call-update) | async-done | bytes 131088 | tf_op jit(solution)/shard_map/reduce_scatter | solution.py:156
  349.1 1.6 add_convert_fusion
  (28 shorter events, 0.2 us)
Async XLA Ops:
  6.5 0.9 copy-start
  6.5 62.4 %reduce-scatter.3.cloned.1.call-start = ((), (), s32[]{:S(2)}) async-start(), calls=%async_computation.4 | async-start | bytes 655360 | tf_op jit(solution)/shard_map/reduce_scatter | solution.py:99
  42.1 3.8 %copy-start.6 = (s32[64,8]{0,1:T(8,128)S(1)}, s32[64,8]{0,1:T(8,128)}, u32[]{:S(2)}) copy-start(s32[64,8]{0,1:T(8,128)} %param.17) | copy-start | bytes 6148
  42.1 26.9 %copy-start.3 = (bf16[32,2048]{1,0:T(8,128)(2,1)S(1)}, bf16[32,2048]{1,0:T(8,128)(2,1)}, u32[]{:S(2)}) copy-start(bf16[32,2048]{1,0:T(8,128)(2,1)} %param.16) | copy-start | bytes 393220
  187.7 2.0 copy-start.2
  218.8 5.0 %copy-start.5 = (f32[64,8]{0,1:T(8,128)S(1)}, f32[64,8]{0,1:T(8,128)}, u32[]{:S(2)}) copy-start(f32[64,8]{0,1:T(8,128)} %param.18) | copy-start | bytes 6148
  218.8 97.0 %all-to-all-start.1 = ((bf16[128,8,2048]{2,0,1:T(8,128)(2,1)}), bf16[128,8,2048]{2,0,1:T(8,128)(2,1)}, u32[]{:S(2)}, u32[]{:S(2)}) async-start(bf16[128,8,2048]{2,0,1:T(8,128)(2,1)} %copy.28), calls=%async_computation.2 | async-start | bytes 8388608 | tf_op jit(solution)/shard_map/all_to_all | solution.py:144
  223.5 125.6 %reduce-scatter.5.cloned.1.call-start = ((), (), s32[]{:S(2)}) async-start(), calls=%async_computation.5 | async-start | bytes 393216 | tf_op jit(solution)/shard_map/reduce_scatter | solution.py:156
  333.8 16.9 %copy-start.1 = (bf16[128,512]{1,0:T(8,128)(2,1)S(1)}, bf16[128,512]{1,0:T(8,128)(2,1)}, u32[]{:S(2)}) copy-start(bf16[128,512]{1,0:T(8,128)(2,1)} %param.14) | copy-start | bytes 393220
  337.5 11.5 %copy-start.4 = (bf16[32,2048]{1,0:T(8,128)(2,1)S(1)}, bf16[32,2048]{1,0:T(8,128)(2,1)}, u32[]{:S(2)}) copy-start(bf16[32,2048]{1,0:T(8,128)(2,1)} %reduce-scatter.3.cloned.1.call-done) | copy-start | bytes 393220
Sparse Core Ops, SparseCore 0:
  46.0 22.8 reduce-scatter.2
  342.3 6.6 reduce-scatter.4
where the time goes:
time: 358 us
  blocking collectives  128 us (36%)
  waiting for transfers between devices  115 us (32%)
  local copies, waits for them, and re-layouts  42.9 us (12%)
  matrix products  33.4 us (9%)
  other arithmetic  18.2 us (5%)
  between operations  14.2 us (4%)
  starting transfers between devices  4.94 us (1%)
    all_to_all x1, blocking collectives, on_device(): lax.all_to_all(send_buffer.reshape(rows_here * slot_count, peer_count, mo...  97.8 us
    all_to_all x1, waiting for transfers between devices, on_device(): lax.all_to_all(expert_out.reshape(rows_here * slot_count, peer_count, mod...  91.9 us
    reduce_scatter x1, waiting for transfers between devices, on_device(): lax.psum_scatter(jnp.dot(attended, out_weight, preferred_element_type=jnp...  16.6 us
    all_gather x1, blocking collectives, attend_blocks(): lax.all_gather(value_head, 'ctx', axis=0, tiled=True)  15 us
    dot_general x1, matrix products, run_experts(): jnp.einsum('rnf,rfd->rnd', activated, w_down, preferred_element_type=jnp....  14 us
    all_gather x1, blocking collectives, attend_blocks(): lax.all_gather(key_head, 'ctx', axis=0, tiled=True)  13.5 us
    gather x1, local copies, waits for them, and re-layouts, on_device(): returned_flat[cells].reshape(2, expert_ids.shape[0], TOPK, model_width)  11.6 us
    dot_general x1, matrix products, run_experts(): jnp.einsum('rnd,rdf->rnf', inputs, w_gate, preferred_element_type=jnp.flo...  8.69 us
  transfers between devices with their start and end apart: 3, of which 3 were waited for; matrix products, arithmetic and copies ran while one was open for 2% of the time, Pallas kernels for 0%

commit v1 on v0

v1 whole, which is shorter than its diff:
```python
import functools
import math

import jax
import jax.numpy as jnp
from jax import lax
from jax.experimental import pallas as pl
from jax.experimental.pallas import tpu as pltpu
from jax.sharding import PartitionSpec as P

HEAD_DIMENSION = 128
QUERY_HEADS = 32
KEY_VALUE_HEADS = 4
EXPERTS = 64
TOPK = 8
MIB = 1 << 20
BF = jnp.bfloat16
F32 = jnp.float32


def shift(x, axis, steps):
    size = lax.axis_size(axis)
    steps = steps % size
    if steps == 0:
        return x
    return lax.ppermute(x, axis, [(i, (i + steps) % size) for i in range(size)])


def attention_kernel(n_ctx, n_exp, n_tp, rows, heads, relative, place, q_ref, *refs):
    kv_refs, w_ref, o_ref = refs[:n_ctx], refs[n_ctx], refs[n_ctx + 1]
    k_all, v_all, att, att_rel = refs[n_ctx + 2 :]
    ctx, exp, tp = place[0], place[1], place[2]
    for z in range(n_ctx):
        k_all[z * rows : (z + 1) * rows, :] = kv_refs[z][:rows, :HEAD_DIMENSION]
        v_all[z * rows : (z + 1) * rows, :] = kv_refs[z][:rows, HEAD_DIMENSION:]
    column = lax.broadcasted_iota(jnp.int32, (rows, n_ctx * rows), 1)
    row = lax.broadcasted_iota(jnp.int32, (rows, n_ctx * rows), 0)
    allowed = (column <= row) | ((column >= rows) & (column < (ctx + 1) * rows))
    scale = 1.0 / math.sqrt(HEAD_DIMENSION)
    for h in range(heads):
        q = q_ref[:, h * HEAD_DIMENSION : (h + 1) * HEAD_DIMENSION]
        s = lax.dot_general(q, k_all[...], (((1,), (1,)), ((), ())), preferred_element_type=F32)
        s = jnp.where(allowed, s * scale, -1e30)
        weights = jnp.exp(s - jnp.max(s, axis=1, keepdims=True))
        total = jnp.sum(weights, axis=1, keepdims=True)
        out = jnp.dot(weights.astype(BF), v_all[...], preferred_element_type=F32)
        att[:, h * HEAD_DIMENSION : (h + 1) * HEAD_DIMENSION] = (out / total).astype(BF)
    part = rows // (n_exp * n_tp)
    if not relative:
        o_ref[...] = jnp.dot(att[...], w_ref[...], preferred_element_type=F32).astype(BF)
        return
    for t in range(n_tp):
        for x in range(n_exp):
            owner = lax.rem(exp - x + n_exp, n_exp) * n_tp + lax.rem(tp - t + n_tp, n_tp)
            source = pl.ds(pl.multiple_of(owner * part, part), part)
            at = (t * n_exp + x) * part
            att_rel[at : at + part, :] = att[source, :]
    o_ref[...] = jnp.dot(att_rel[...], w_ref[...], preferred_element_type=F32).astype(BF)


def attend_project(queries, pieces, out_weight, place, n_exp, n_tp, relative):
    rows, width = queries.shape
    n_ctx = len(pieces)
    model = out_weight.shape[1]
    vmem = pl.BlockSpec(memory_space=pltpu.VMEM)
    return pl.pallas_call(
        functools.partial(
            attention_kernel, n_ctx, n_exp, n_tp, rows, width // HEAD_DIMENSION, relative
        ),
        out_shape=jax.ShapeDtypeStruct((rows, model), BF),
        in_specs=[pl.BlockSpec(memory_space=pltpu.SMEM)] + [vmem] * (n_ctx + 2),
        out_specs=vmem,
        scratch_shapes=[
            pltpu.VMEM((n_ctx * rows, HEAD_DIMENSION), BF),
            pltpu.VMEM((n_ctx * rows, HEAD_DIMENSION), BF),
            pltpu.VMEM((rows, width), BF),
            pltpu.VMEM((rows, width), BF),
        ],
        compiler_params=pltpu.CompilerParams(vmem_limit_bytes=32 * MIB),
        cost_estimate=pl.CostEstimate(
            flops=2 * rows * width * (2 * n_ctx * rows + model),
            bytes_accessed=2 * (rows * width + width * model + rows * model),
            transcendentals=rows * n_ctx * rows * (width // HEAD_DIMENSION),
        ),
        name="attend_project",
    )(place, queries, *pieces, out_weight)


def expert_kernel(n_pieces, tokens, slots, halves, key_ref, weight_ref, *refs):
    pieces = refs[:n_pieces]
    wg_ref, wu_ref, wd_ref, mine_ref, other_ref = refs[n_pieces : n_pieces + 5]
    x_all, pick_all, out_all = refs[n_pieces + 5 :]
    step = pl.program_id(0)
    last = pl.num_programs(0) - 1
    part = tokens // n_pieces

    @pl.when(step == 0)
    def _():
        for i, piece in enumerate(pieces):
            x_all[i * part : (i + 1) * part, :] = piece[...]

    slot = lax.broadcasted_iota(jnp.int32, (slots, tokens), 0)
    chosen = slot == key_ref[pl.ds(step, 1), :]
    pick = jnp.where(chosen, 1.0, 0.0).astype(BF)
    scale = jnp.sum(jnp.where(chosen, weight_ref[pl.ds(step, 1), :], 0.0), axis=1, keepdims=True)
    x = jnp.dot(pick, x_all[...], preferred_element_type=F32).astype(BF)
    out = None
    for h in range(halves):
        gate = jnp.dot(x, wg_ref[h], preferred_element_type=F32)
        up = jnp.dot(x, wu_ref[h], preferred_element_type=F32)
        act = (gate * jax.nn.sigmoid(gate) * up).astype(BF)
        term = jnp.dot(act, wd_ref[h], preferred_element_type=F32)
        out = term if out is None else out + term
    here = pl.ds(pl.multiple_of(step * slots, slots), slots)
    pick_all[here, :] = pick
    out_all[here, :] = (out * scale).astype(BF)

    @pl.when(step == last)
    def _():
        routed = lax.dot_general(
            pick_all[...], out_all[...], (((0,), (0,)), ((), ())), preferred_element_type=F32
        ).astype(BF)
        half = tokens // 2
        mine_ref[...] = routed[:half]
        other_ref[...] = routed[half:]


def run_experts(keys, weights, pieces, w_gate, w_up, w_down, slots):
    n_exp, tokens = keys.shape
    rows, model, hidden = w_gate.shape
    halves = rows // n_exp
    part = tokens // len(pieces)

    def whole(shape):
        return pl.BlockSpec(shape, lambda e: (0,) * len(shape), pipeline_mode=pl.Buffered(1))

    out = jax.ShapeDtypeStruct((tokens // 2, model), BF)
    return pl.pallas_call(
        functools.partial(expert_kernel, len(pieces), tokens, slots, halves),
        grid=(n_exp,),
        out_shape=(out, out),
        in_specs=[whole((n_exp, tokens))] * 2
        + [whole((part, model))] * len(pieces)
        + [
            pl.BlockSpec((halves, model, hidden), lambda e: (e, 0, 0)),
            pl.BlockSpec((halves, model, hidden), lambda e: (e, 0, 0)),
            pl.BlockSpec((halves, hidden, model), lambda e: (e, 0, 0)),
        ],
        out_specs=[whole((tokens // 2, model))] * 2,
        scratch_shapes=[
            pltpu.VMEM((tokens, model), BF),
            pltpu.VMEM((n_exp * slots, tokens), BF),
            pltpu.VMEM((n_exp * slots, model), BF),
        ],
        compiler_params=pltpu.CompilerParams(vmem_limit_bytes=48 * MIB),
        cost_estimate=pl.CostEstimate(
            flops=2 * n_exp * slots * model * (3 * halves * hidden + 2 * tokens),
            bytes_accessed=6 * rows * model * hidden + 4 * tokens * model,
            transcendentals=n_exp * slots * halves * hidden,
        ),
        name="experts",
    )(keys, weights, *pieces, w_gate, w_up, w_down)


def experts_plain(keys, weights, x, w_gate, w_up, w_down, slots):
    n_exp = keys.shape[0]
    rows, model, hidden = w_gate.shape
    pick = (keys[:, None, :] == jnp.arange(slots, dtype=jnp.int32)[None, :, None]).astype(BF)
    scale = jnp.sum(pick.astype(F32) * weights[:, None, :], axis=2)
    chosen = jnp.einsum("est,td->esd", pick, x, preferred_element_type=F32).astype(BF)
    chosen = jnp.repeat(chosen, rows // n_exp, axis=0)
    gate = jnp.einsum("rsd,rdf->rsf", chosen, w_gate, preferred_element_type=F32)
    up = jnp.einsum("rsd,rdf->rsf", chosen, w_up, preferred_element_type=F32)
    act = (jax.nn.silu(gate) * up).astype(BF)
    out = jnp.einsum("rsf,rfd->rsd", act, w_down, preferred_element_type=F32)
    out = jnp.sum(out.reshape(n_exp, rows // n_exp, slots, model), axis=1)
    out = (out * scale[:, :, None]).astype(BF)
    return jnp.einsum("est,esd->td", pick, out, preferred_element_type=F32).astype(BF)


def on_device(
    queries, keys, values, out_weight, resid, expert_ids, router_probs, w_gate, w_up, w_down
):
    n_ctx, n_exp, n_tp = (lax.axis_size(a) for a in ("ctx", "exp", "tp"))
    ctx, exp, tp = (lax.axis_index(a) for a in ("ctx", "exp", "tp"))
    place = jnp.stack([ctx, exp, tp]).astype(jnp.int32)
    rows = queries.shape[0]
    part, model = resid.shape
    block = expert_ids.shape[0]
    heads_here = queries.shape[1] // HEAD_DIMENSION
    small = n_ctx * n_exp <= 8 and part % 16 == 0

    shared = (exp * n_tp + tp) * heads_here // (QUERY_HEADS // KEY_VALUE_HEADS)
    key_head = lax.dynamic_slice_in_dim(keys, shared * HEAD_DIMENSION, HEAD_DIMENSION, 1)
    value_head = lax.dynamic_slice_in_dim(values, shared * HEAD_DIMENSION, HEAD_DIMENSION, 1)
    gate_weights = router_probs / jnp.sum(router_probs, axis=1, keepdims=True)
    high = lax.reduce_precision(gate_weights, 8, 7)
    low = gate_weights - high
    routing = jnp.concatenate(
        [expert_ids.astype(F32).T, high.T, low.T], axis=1
    ).astype(BF)
    routing = jnp.pad(routing, ((0, 16 - TOPK), (0, 2 * HEAD_DIMENSION - 3 * block)))
    kv = jnp.concatenate([jnp.concatenate([key_head, value_head], axis=1), routing], axis=0)
    kv_pieces = [shift(kv, "ctx", z) for z in range(n_ctx)]
    routing = jnp.stack([piece[rows : rows + TOPK, : 3 * block] for piece in kv_pieces])
    routing = jnp.stack([shift(routing, "exp", x) for x in range(n_exp)], axis=1)

    routing = routing.reshape(n_ctx, n_exp, TOPK, 3, n_tp, part)
    routing = jnp.stack(
        [
            lax.dynamic_index_in_dim(routing, (tp - t) % n_tp, 4, keepdims=False)
            for t in range(n_tp)
        ],
        axis=4,
    )
    routing = routing.transpose(3, 2, 4, 0, 1, 5).astype(F32)
    ids = routing[0].astype(jnp.int32)
    probs = routing[1] + routing[2]
    rows_here = w_gate.shape[0]
    experts_here = max(1, rows_here // 2)
    device = ctx * n_exp + exp
    first = device * rows_here // 2
    local = first + jnp.arange(experts_here, dtype=jnp.int32)
    hit = ids[None] == local.reshape(-1, 1, 1, 1, 1, 1)
    named = jnp.any(hit, axis=1)
    weight = jnp.sum(jnp.where(hit, probs[None], 0.0), axis=1)
    cap = min(8, block)
    flat = named.transpose(0, 2, 3, 1, 4).reshape(-1, block)
    before = jnp.arange(block)[:, None] < jnp.arange(block)[None, :]
    rank = jnp.dot(flat.astype(BF), before.astype(BF), preferred_element_type=F32)
    rank = rank.astype(jnp.int32).reshape(experts_here, n_ctx, n_exp, n_tp, part)
    rank = rank.transpose(0, 3, 1, 2, 4)
    blocks = jnp.arange(n_ctx * n_exp, dtype=jnp.int32).reshape(1, 1, n_ctx, n_exp, 1)
    cells = jnp.where(named, blocks * cap + rank, -1).reshape(experts_here, -1)
    weight = weight.reshape(experts_here, -1)
    slots = n_ctx * n_exp * cap

    projected = attend_project(
        queries, kv_pieces, out_weight, place, n_exp, n_tp, small
    )
    hidden = resid.astype(F32)
    if small:
        projected = projected.reshape(n_tp, n_exp * part, model)
        summed = projected[0].astype(F32)
        for t in range(1, n_tp):
            summed = summed + shift(projected[t], "tp", -t).astype(F32)
        summed = summed.astype(BF).reshape(n_exp, part, model)
        hidden = hidden + summed[0].astype(F32)
        for x in range(1, n_exp):
            hidden = hidden + shift(summed[x], "exp", -x).astype(F32)
    else:
        hidden = hidden + lax.psum_scatter(
            projected, ("exp", "tp"), scatter_dimension=0, tiled=True
        ).astype(F32)
    mean_square = jnp.mean(hidden * hidden, axis=1, keepdims=True)
    normed = (hidden * lax.rsqrt(mean_square + 1e-06)).astype(BF)

    if small:
        along_z = [shift(normed, "ctx", z) for z in range(n_ctx)]
        chip = [shift(piece, "exp", x) for piece in along_z for x in range(n_exp)]
        pieces = [shift(piece, "tp", t) for t in range(n_tp) for piece in chip]
        mine, other = run_experts(cells, weight, pieces, w_gate, w_up, w_down, slots)
        both = mine.astype(F32) + shift(other, "tp", -1).astype(F32)
        both = both.astype(BF).reshape(n_ctx, n_exp, part, model)
        routed = None
        for z in range(n_ctx):
            line = both[z, 0].astype(F32)
            for x in range(1, n_exp):
                line = line + shift(both[z, x], "exp", -x).astype(F32)
            if z:
                line = shift(line.astype(BF), "ctx", -z).astype(F32)
            routed = line if routed is None else routed + line
    else:
        tokens = n_ctx * n_exp * n_tp * part
        x = lax.all_gather(normed, ("ctx", "exp", "tp"), axis=0, tiled=True)

        def absolute(table):
            table = table.reshape(experts_here, n_tp, n_ctx, n_exp, part)
            for axis, size, me in ((1, n_tp, tp), (2, n_ctx, ctx), (3, n_exp, exp)):
                order = (me - jnp.arange(size, dtype=jnp.int32)) % size
                table = jnp.take(table, order, axis=axis)
            return table.transpose(0, 2, 3, 1, 4).reshape(experts_here, tokens)

        partial = experts_plain(
            absolute(cells), absolute(weight), x, w_gate, w_up, w_down, slots
        )
        routed = lax.psum_scatter(
            partial, ("ctx", "exp", "tp"), scatter_dimension=0, tiled=True
        ).astype(F32)
    return (hidden + routed).astype(BF)


def solution(mesh):
    in_specs = (
        P(("groups", "ctx"), ("exp", "tp")),
        P(("groups", "ctx"), None),
        P(("groups", "ctx"), None),
        P(("exp", "tp"), None),
        P(("groups", "ctx", "exp", "tp"), None),
        P(("groups", "ctx", "exp"), None),
        P(("groups", "ctx", "exp"), None),
        P(("ctx", "exp"), None, "tp"),
        P(("ctx", "exp"), None, "tp"),
        P(("ctx", "exp"), "tp", None),
    )
    out_specs = P(("groups", "ctx", "exp", "tp"), None)
    return jax.shard_map(
        on_device, mesh=mesh, in_specs=in_specs, out_specs=out_specs, check_vma=False
    )
```

time: 358 us -> 148 us (0.41)
  blocking collectives: 128 us -> 0 us
  waiting for transfers between devices: 115 us -> 44.5 us
  matrix products: 33.4 us -> 0.13 us
  Pallas kernels: 0 us -> 24.2 us
  starting transfers between devices: 4.94 us -> 24.9 us
  between operations: 14.2 us -> 0.28 us
  other arithmetic: 18.2 us -> 5.89 us
    all_to_all x1 -> x0, blocking collectives: 97.8 us -> none  [on_device(): lax.all_to_all(send_buffer.reshape(rows_here * slot_count, peer_count, mo...]
    all_to_all x1 -> x0, waiting for transfers between devices: 91.9 us -> none  [on_device(): lax.all_to_all(expert_out.reshape(rows_here * slot_count, peer_count, mod...]
    ppermute x0 -> x29, waiting for transfers between devices: none -> 44.5 us  [shift(): return lax.ppermute(x, axis, [(i, (i + steps) % size) for i in range(size)])]
    unnamed x15 -> x8, local copies, waits for them, and re-layouts: 2.97 us -> 44.4 us
    dot_general x5 -> x1, matrix products: 31.7 us -> 0.13 us  [on_device(): jnp.dot(flat.astype(BF), before.astype(BF), preferred_element_type=F32)]
    all_gather x3 -> x0, blocking collectives: 30.5 us -> none  [the longest x1 15 us: attend_blocks(): lax.all_gather(value_head, 'ctx', axis=0, tiled=True)]
    ppermute x0 -> x29, starting transfers between devices: none -> 24.9 us  [shift(): return lax.ppermute(x, axis, [(i, (i + steps) % size) for i in range(size)])]
    pallas_call x0 -> x2, Pallas kernels: none -> 24.2 us  [the longest x1 20.8 us: run_experts(): pl.pallas_call(functools.partial(expert_kernel, len(pieces), tokens, slot...]
  transfers between devices with their start and end apart: 3 -> 29, of which waited for: 3 -> 15; matrix products, arithmetic and copies ran while one was open for 2% -> 31% of each run, Pallas kernels for 0% -> 0%
where the time goes in v1:
time: 148 us; the launch traced here: 146 us
  local copies, waits for them, and re-layouts  46.4 us (31%)
  waiting for transfers between devices  44.5 us (30%)
  starting transfers between devices  24.9 us (17%)
  Pallas kernels  24.2 us (16%)
  other arithmetic  5.89 us (4%)
    ppermute x29, waiting for transfers between devices, shift(): return lax.ppermute(x, axis, [(i, (i + steps) % size) for i in range(size)])  44.5 us
    unnamed x8, local copies, waits for them, and re-layouts  44.4 us
    ppermute x29, starting transfers between devices, shift(): return lax.ppermute(x, axis, [(i, (i + steps) % size) for i in range(size)])  24.9 us
    pallas_call x1, Pallas kernels, run_experts(): pl.pallas_call(functools.partial(expert_kernel, len(pieces), tokens, slot...  20.8 us
    pallas_call x1, Pallas kernels, attend_project(): pl.pallas_call(functools.partial(attention_kernel, n_ctx, n_exp, n_tp, ro...  3.46 us
  transfers between devices with their start and end apart: 29, of which 15 were waited for; matrix products, arithmetic and copies ran while one was open for 31% of the time, Pallas kernels for 0%

profile of v1, /device:TPU:0, one launch (start us, length us, event | category | flops | bytes accessed | tf_op | source)
XLA Modules:
  0.0 146.3 jit_solution(16815864066361850712)
XLA Ops:
  0.0 0.7 reduce_sum.27
  0.7 0.7 fusion.20
  1.4 0.8 convert_bitcast_fusion.1
  2.2 0.8 constant_dynamic-slice_fusion.2
  3.0 5.1 %collective-permute-start.2 = (bf16[144,256]{1,0:T(8,128)(2,1)S(1)}, bf16[144,256]{1,0:T(8,128)(2,1)S(1)}, u32[]{:S(2)}, u32[]{:S(2)}) collective-permute-start(bf16[144,256]{1,0:T(8,128)(2,1)S(1)} %pad_maximum_fusion.1.refs_0_), channel_id=1, source_target_pairs={{0,12},{4,0},{8,4},{12,8},{1,13},{5,1},{9,5},{13,9},{2,14},{6,2},{... | collective-permute-start | bytes 221192 | tf_op jit(solution)/shard_map/ppermute | solution.py:26
  8.1 1.0 collective-permute-start
  9.2 0.7 reduce-precision_bitcast_fusion
  10.0 0.8 collective-permute-done.2.refs_3_
  10.9 4.3 %collective-permute-done.1.refs_2_ = bf16[144,256]{1,0:T(8,128)(2,1)S(1)} collective-permute-done((bf16[144,256]{1,0:T(8,128)(2,1)S(1)}, bf16[144,256]{1,0:T(8,128)(2,1)S(1)}, u32[]{:S(2)}, u32[]{:S(2)}) %collective-permute-start.1) | collective-permute-done | bytes 73760 | tf_op jit(solution)/shard_map/ppermute | solution.py:26
  15.1 2.2 %copy-done = bf16[1024,2048]{1,0:T(8,128)(2,1)S(1)} copy-done((bf16[1024,2048]{1,0:T(8,128)(2,1)S(1)}, bf16[1024,2048]{1,0:T(8,128)(2,1)}, u32[]{:S(2)}) %copy-start) | copy-done | bytes 4194328
  17.3 0.9 copy-done.1
  18.3 3.5 %attend_project.1 = bf16[128,2048]{1,0:T(8,128)(2,1)S(1)} custom-call(s32[3]{0:T(128)S(1)} %pad_add_fusion.place, bf16[128,1024]{1,0:T(8,128)(2,1)S(1)} %copy-done.1, bf16[144,256]{1,0:T(8,128)(2,1)S(1)} %pad_maximum_fusion.1.refs_0_, bf16[144,256]{1,0:T(8,128)(2,1)S(1)} %collective-permute-done.refs_1_, ...), custom_call_target="tpu_custom_call" | custom-call | flops 805306368 | bytes 4980736 | tf_op jit(solution)/shard_map/attend_project/pallas_call | solution.py:66
  21.9 1.6 %collective-permute-start.5 = (bf16[4,8,192]{2,1,0:T(8,128)(2,1)S(1)}, bf16[4,8,192]{2,1,0:T(8,128)(2,1)S(1)}, u32[]{:S(2)}, u32[]{:S(2)}) collective-permute-start(bf16[4,8,192]{2,1,0:T(8,128)(2,1)S(1)} %pad_maximum_fusion.2), channel_id=1, source_target_pairs={{0,2},{2,0},{1,3},{3,1},{4,6},{6,4},{5,7},{7,5},{8,10},{10,8},{9,1... | collective-permute-start | bytes 36872 | tf_op jit(solution)/shard_map/ppermute | solution.py:26
  23.6 20.6 %copy.37.refs_16_ = bf16[16,2048,192]{2,1,0:T(8,128)(2,1)} copy(bf16[16,2048,192]{1,2,0:T(8,128)(2,1)} %param.17) | data formatting | bytes 25165824 | tf_op args[7]
  44.2 20.6 %copy.38.refs_17_ = bf16[16,2048,192]{2,1,0:T(8,128)(2,1)} copy(bf16[16,2048,192]{1,2,0:T(8,128)(2,1)} %param.18) | data formatting | bytes 25165824 | tf_op args[8]
  65.5 0.6 collective-permute-start.4
  66.6 4.6 %collective-permute-done.4 = bf16[32,2048]{1,0:T(8,128)(2,1)S(1)} collective-permute-done((bf16[32,2048]{1,0:T(8,128)(2,1)S(1)}, bf16[32,2048]{1,0:T(8,128)(2,1)S(1)}, u32[]{:S(2)}, u32[]{:S(2)}) %collective-permute-start.4) | collective-permute-done | bytes 131104 | tf_op jit(solution)/shard_map/ppermute | solution.py:26
  71.5 2.1 %collective-permute-start.11 = (bf16[32,2048]{1,0:T(8,128)(2,1)S(1)}, bf16[32,2048]{1,0:T(8,128)(2,1)S(1)}, u32[]{:S(2)}, u32[]{:S(2)}) collective-permute-start(bf16[32,2048]{1,0:T(8,128)(2,1)S(1)} %multiply_convert_fusion.refs_0_), channel_id=1, source_target_pairs={{0,12},{4,0},{8,4},{12,8},{1,13},{5,1},{9,5},{13,9},{2,14},{6,2},{... | collective-permute-start | bytes 393224 | tf_op jit(solution)/shard_map/ppermute | solution.py:26
  73.6 1.9 %collective-permute-start.7 = (bf16[32,2048]{1,0:T(8,128)(2,1)S(1)}, bf16[32,2048]{1,0:T(8,128)(2,1)S(1)}, u32[]{:S(2)}, u32[]{:S(2)}) collective-permute-start(bf16[32,2048]{1,0:T(8,128)(2,1)S(1)} %multiply_convert_fusion.refs_0_), channel_id=1, source_target_pairs={{0,4},{4,8},{8,12},{12,0},{1,5},{5,9},{9,13},{13,1},{2,6},{6,10},{... | collective-permute-start | bytes 393224 | tf_op jit(solution)/shard_map/ppermute | solution.py:26
  75.5 0.5 collective-permute-start.6
  76.1 0.3 fusion
  76.4 1.1 collective-permute-done.11.refs_6_
  77.5 0.6 collective-permute-start.12
  78.1 7.9 %collective-permute-done.9.refs_4_ = bf16[32,2048]{1,0:T(8,128)(2,1)S(1)} collective-permute-done((bf16[32,2048]{1,0:T(8,128)(2,1)S(1)}, bf16[32,2048]{1,0:T(8,128)(2,1)S(1)}, u32[]{:S(2)}, u32[]{:S(2)}) %collective-permute-start.9) | collective-permute-done | bytes 131104 | tf_op jit(solution)/shard_map/ppermute | solution.py:26
  86.0 0.5 collective-permute-start.10
  86.6 1.5 %collective-permute-start.8 = (bf16[32,2048]{1,0:T(8,128)(2,1)S(1)}, bf16[32,2048]{1,0:T(8,128)(2,1)S(1)}, u32[]{:S(2)}, u32[]{:S(2)}) collective-permute-start(bf16[32,2048]{1,0:T(8,128)(2,1)S(1)} %collective-permute-done.7.refs_2_), channel_id=1, source_target_pairs={{0,2},{2,0},{1,3},{3,1},{4,6},{6,4},{5,7},{7,5},{8,10},{10,8},{9,1... | collective-permute-start | bytes 393224 | tf_op jit(solution)/shard_map/ppermute | solution.py:26
  88.1 0.3 compare_reduce_fusion
  88.9 0.5 collective-permute-start.14
  89.5 2.8 %collective-permute-done.10.refs_5_ = bf16[32,2048]{1,0:T(8,128)(2,1)S(1)} collective-permute-done((bf16[32,2048]{1,0:T(8,128)(2,1)S(1)}, bf16[32,2048]{1,0:T(8,128)(2,1)S(1)}, u32[]{:S(2)}, u32[]{:S(2)}) %collective-permute-start.10) | collective-permute-done | bytes 131104 | tf_op jit(solution)/shard_map/ppermute | solution.py:26
  92.3 2.4 %collective-permute-done.8.refs_3_ = bf16[32,2048]{1,0:T(8,128)(2,1)S(1)} collective-permute-done((bf16[32,2048]{1,0:T(8,128)(2,1)S(1)}, bf16[32,2048]{1,0:T(8,128)(2,1)S(1)}, u32[]{:S(2)}, u32[]{:S(2)}) %collective-permute-start.8) | collective-permute-done | bytes 131104 | tf_op jit(solution)/shard_map/ppermute | solution.py:26
  95.0 1.1 collective-permute-done.16.refs_11_
  96.1 20.8 %experts.1 = (bf16[256,2048]{1,0:T(8,128)(2,1)S(1)}, bf16[256,2048]{1,0:T(8,128)(2,1)S(1)}) custom-call(s32[8,512]{1,0:T(8,128)S(1)} %reshape.133.key_ref, f32[8,512]{1,0:T(8,128)S(1)} %reshape.134.weight_ref, bf16[32,2048]{1,0:T(8,128)(2,1)S(1)} %multiply_convert_fusion.refs_0_, bf16[32,2048]{1,0:T(8,128)(2,1)S(1)} %collective-permute-done.6.refs_1_, ...), custom_call_target="tpu_custom_call" | custom-call | flops 4563402752 | bytes 41943040 | tf_op jit(solution)/shard_map/experts/pallas_call | solution.py:138
  117.1 2.5 %collective-permute-done.21 = bf16[256,2048]{1,0:T(8,128)(2,1)S(1)} collective-permute-done((bf16[256,2048]{1,0:T(8,128)(2,1)S(1)}, bf16[256,2048]{1,0:T(8,128)(2,1)S(1)}, u32[]{:S(2)}, u32[]{:S(2)}) %collective-permute-start.21) | collective-permute-done | bytes 1048608 | tf_op jit(solution)/shard_map/ppermute | solution.py:26
  119.6 0.4 add_convert_fusion
  120.0 0.6 collective-permute-start.27
  120.6 1.5 %collective-permute-start.25 = (bf16[32,2048]{1,0:T(8,128)(2,1)S(1)}, bf16[32,2048]{1,0:T(8,128)(2,1)S(1)}, u32[]{:S(2)}, u32[]{:S(2)}) collective-permute-start(bf16[32,2048]{1,0:T(8,128)(2,1)S(1)} %get-tuple-element.11), channel_id=1, source_target_pairs={{0,2},{2,0},{1,3},{3,1},{4,6},{6,4},{5,7},{7,5},{8,10},{10,8},{9,1... | collective-permute-start | bytes 393224 | tf_op jit(solution)/shard_map/ppermute | solution.py:26
  122.1 0.5 collective-permute-start.23
  122.7 1.5 %collective-permute-start.22 = (bf16[32,2048]{1,0:T(8,128)(2,1)S(1)}, bf16[32,2048]{1,0:T(8,128)(2,1)S(1)}, u32[]{:S(2)}, u32[]{:S(2)}) collective-permute-start(bf16[32,2048]{1,0:T(8,128)(2,1)S(1)} %get-tuple-element.9), channel_id=1, source_target_pairs={{0,2},{2,0},{1,3},{3,1},{4,6},{6,4},{5,7},{7,5},{8,10},{10,8},{9,1... | collective-permute-start | bytes 393224 | tf_op jit(solution)/shard_map/ppermute | solution.py:26
  124.2 2.3 %collective-permute-done.27 = bf16[32,2048]{1,0:T(8,128)(2,1)S(1)} collective-permute-done((bf16[32,2048]{1,0:T(8,128)(2,1)S(1)}, bf16[32,2048]{1,0:T(8,128)(2,1)S(1)}, u32[]{:S(2)}, u32[]{:S(2)}) %collective-permute-start.27) | collective-permute-done | bytes 131104 | tf_op jit(solution)/shard_map/ppermute | solution.py:26
  126.5 2.8 %collective-permute-done.25 = bf16[32,2048]{1,0:T(8,128)(2,1)S(1)} collective-permute-done((bf16[32,2048]{1,0:T(8,128)(2,1)S(1)}, bf16[32,2048]{1,0:T(8,128)(2,1)S(1)}, u32[]{:S(2)}, u32[]{:S(2)}) %collective-permute-start.25) | collective-permute-done | bytes 131104 | tf_op jit(solution)/shard_map/ppermute | solution.py:26
  129.3 2.8 %collective-permute-done.23 = bf16[32,2048]{1,0:T(8,128)(2,1)S(1)} collective-permute-done((bf16[32,2048]{1,0:T(8,128)(2,1)S(1)}, bf16[32,2048]{1,0:T(8,128)(2,1)S(1)}, u32[]{:S(2)}, u32[]{:S(2)}) %collective-permute-start.23) | collective-permute-done | bytes 131104 | tf_op jit(solution)/shard_map/ppermute | solution.py:26
  132.2 1.0 collective-permute-start.24
  133.2 1.1 collective-permute-start.28
  134.3 2.3 %collective-permute-start.26 = (bf16[32,2048]{1,0:T(8,128)(2,1)S(1)}, bf16[32,2048]{1,0:T(8,128)(2,1)S(1)}, u32[]{:S(2)}, u32[]{:S(2)}) collective-permute-start(bf16[32,2048]{1,0:T(8,128)(2,1)S(1)} %get-tuple-element.15), channel_id=1, source_target_pairs={{0,8},{4,12},{8,0},{12,4},{1,9},{5,13},{9,1},{13,5},{2,10},{6,14},... | collective-permute-start | bytes 393224 | tf_op jit(solution)/shard_map/ppermute | solution.py:26
  136.6 3.0 %collective-permute-done.24 = bf16[32,2048]{1,0:T(8,128)(2,1)S(1)} collective-permute-done((bf16[32,2048]{1,0:T(8,128)(2,1)S(1)}, bf16[32,2048]{1,0:T(8,128)(2,1)S(1)}, u32[]{:S(2)}, u32[]{:S(2)}) %collective-permute-start.24) | collective-permute-done | bytes 131104 | tf_op jit(solution)/shard_map/ppermute | solution.py:26
  139.5 2.6 %collective-permute-done.28 = bf16[32,2048]{1,0:T(8,128)(2,1)S(1)} collective-permute-done((bf16[32,2048]{1,0:T(8,128)(2,1)S(1)}, bf16[32,2048]{1,0:T(8,128)(2,1)S(1)}, u32[]{:S(2)}, u32[]{:S(2)}) %collective-permute-start.28) | collective-permute-done | bytes 131104 | tf_op jit(solution)/shard_map/ppermute | solution.py:26
  142.2 3.4 %collective-permute-done.26 = bf16[32,2048]{1,0:T(8,128)(2,1)S(1)} collective-permute-done((bf16[32,2048]{1,0:T(8,128)(2,1)S(1)}, bf16[32,2048]{1,0:T(8,128)(2,1)S(1)}, u32[]{:S(2)}, u32[]{:S(2)}) %collective-permute-start.26) | collective-permute-done | bytes 131104 | tf_op jit(solution)/shard_map/ppermute | solution.py:26
  145.5 0.8 fusion.8
  (65 shorter events, 3.3 us)
Async XLA Ops:
  3.0 7.8 %collective-permute-start.2 = (bf16[144,256]{1,0:T(8,128)(2,1)S(1)}, bf16[144,256]{1,0:T(8,128)(2,1)S(1)}, u32[]{:S(2)}, u32[]{:S(2)}) collective-permute-start(bf16[144,256]{1,0:T(8,128)(2,1)S(1)} %pad_maximum_fusion.1.refs_0_), channel_id=1, source_target_pairs={{0,12},{4,0},{8,4},{12,8},{1,13},{5,1},{9,5},{13,9},{2,14},{6,2},{... | collective-permute-start | bytes 221192 | tf_op jit(solution)/shard_map/ppermute | solution.py:26
  8.1 7.0 %collective-permute-start.1 = (bf16[144,256]{1,0:T(8,128)(2,1)S(1)}, bf16[144,256]{1,0:T(8,128)(2,1)S(1)}, u32[]{:S(2)}, u32[]{:S(2)}) collective-permute-start(bf16[144,256]{1,0:T(8,128)(2,1)S(1)} %pad_maximum_fusion.1.refs_0_), channel_id=1, source_target_pairs={{0,8},{4,12},{8,0},{12,4},{1,9},{5,13},{9,1},{13,5},{2,10},{6,14},... | collective-permute-start | bytes 221192 | tf_op jit(solution)/shard_map/ppermute | solution.py:26
  8.1 7.0 %collective-permute-start = (bf16[144,256]{1,0:T(8,128)(2,1)S(1)}, bf16[144,256]{1,0:T(8,128)(2,1)S(1)}, u32[]{:S(2)}, u32[]{:S(2)}) collective-permute-start(bf16[144,256]{1,0:T(8,128)(2,1)S(1)} %pad_maximum_fusion.1.refs_0_), channel_id=1, source_target_pairs={{0,4},{4,8},{8,12},{12,0},{1,5},{5,9},{9,13},{13,1},{2,6},{6,10},{... | collective-permute-start | bytes 221192 | tf_op jit(solution)/shard_map/ppermute | solution.py:26
  15.1 2.2 %copy-start = (bf16[1024,2048]{1,0:T(8,128)(2,1)S(1)}, bf16[1024,2048]{1,0:T(8,128)(2,1)}, u32[]{:S(2)}) copy-start(bf16[1024,2048]{1,0:T(8,128)(2,1)} %refs_4_.1) | copy-start | bytes 12582916
  17.3 0.9 copy-start.1
  21.8 43.6 %collective-permute-start.3 = (bf16[64,2048]{1,0:T(8,128)(2,1)S(1)}, bf16[64,2048]{1,0:T(8,128)(2,1)S(1)}, u32[]{:S(2)}, u32[]{:S(2)}) collective-permute-start(bf16[64,2048]{1,0:T(8,128)(2,1)S(1)} %slice.78), channel_id=1, source_target_pairs={{0,1},{1,0},{2,3},{3,2},{4,5},{5,4},{6,7},{7,6},{8,9},{9,8},{10,11... | collective-permute-start | bytes 786440 | tf_op jit(solution)/shard_map/ppermute | solution.py:26
  21.9 43.2 %collective-permute-start.5 = (bf16[4,8,192]{2,1,0:T(8,128)(2,1)S(1)}, bf16[4,8,192]{2,1,0:T(8,128)(2,1)S(1)}, u32[]{:S(2)}, u32[]{:S(2)}) collective-permute-start(bf16[4,8,192]{2,1,0:T(8,128)(2,1)S(1)} %pad_maximum_fusion.2), channel_id=1, source_target_pairs={{0,2},{2,0},{1,3},{3,1},{4,6},{6,4},{5,7},{7,5},{8,10},{10,8},{9,1... | collective-permute-start | bytes 36872 | tf_op jit(solution)/shard_map/ppermute | solution.py:26
  44.2 27.0 %copy-start.2 = (bf16[32,2048]{1,0:T(8,128)(2,1)S(1)}, bf16[32,2048]{1,0:T(8,128)(2,1)}, u32[]{:S(2)}) copy-start(bf16[32,2048]{1,0:T(8,128)(2,1)} %param.14) | copy-start | bytes 393220
  65.5 5.7 %collective-permute-start.4 = (bf16[32,2048]{1,0:T(8,128)(2,1)S(1)}, bf16[32,2048]{1,0:T(8,128)(2,1)S(1)}, u32[]{:S(2)}, u32[]{:S(2)}) collective-permute-start(bf16[32,2048]{1,0:T(8,128)(2,1)S(1)} %slice.80), channel_id=1, source_target_pairs={{0,2},{2,0},{1,3},{3,1},{4,6},{6,4},{5,7},{7,5},{8,10},{10,8},{9,1... | collective-permute-start | bytes 393224 | tf_op jit(solution)/shard_map/ppermute | solution.py:26
  71.4 6.1 %collective-permute-start.13 = (bf16[32,2048]{1,0:T(8,128)(2,1)S(1)}, bf16[32,2048]{1,0:T(8,128)(2,1)S(1)}, u32[]{:S(2)}, u32[]{:S(2)}) collective-permute-start(bf16[32,2048]{1,0:T(8,128)(2,1)S(1)} %multiply_convert_fusion.refs_0_), channel_id=1, source_target_pairs={{0,1},{1,0},{2,3},{3,2},{4,5},{5,4},{6,7},{7,6},{8,9},{9,8},{10,11... | collective-permute-start | bytes 393224 | tf_op jit(solution)/shard_map/ppermute | solution.py:26
  71.5 6.0 %collective-permute-start.11 = (bf16[32,2048]{1,0:T(8,128)(2,1)S(1)}, bf16[32,2048]{1,0:T(8,128)(2,1)S(1)}, u32[]{:S(2)}, u32[]{:S(2)}) collective-permute-start(bf16[32,2048]{1,0:T(8,128)(2,1)S(1)} %multiply_convert_fusion.refs_0_), channel_id=1, source_target_pairs={{0,12},{4,0},{8,4},{12,8},{1,13},{5,1},{9,5},{13,9},{2,14},{6,2},{... | collective-permute-start | bytes 393224 | tf_op jit(solution)/shard_map/ppermute | solution.py:26
  73.6 12.4 %collective-permute-start.9 = (bf16[32,2048]{1,0:T(8,128)(2,1)S(1)}, bf16[32,2048]{1,0:T(8,128)(2,1)S(1)}, u32[]{:S(2)}, u32[]{:S(2)}) collective-permute-start(bf16[32,2048]{1,0:T(8,128)(2,1)S(1)} %multiply_convert_fusion.refs_0_), channel_id=1, source_target_pairs={{0,8},{4,12},{8,0},{12,4},{1,9},{5,13},{9,1},{13,5},{2,10},{6,14},... | collective-permute-start | bytes 393224 | tf_op jit(solution)/shard_map/ppermute | solution.py:26
  73.6 12.4 %collective-permute-start.7 = (bf16[32,2048]{1,0:T(8,128)(2,1)S(1)}, bf16[32,2048]{1,0:T(8,128)(2,1)S(1)}, u32[]{:S(2)}, u32[]{:S(2)}) collective-permute-start(bf16[32,2048]{1,0:T(8,128)(2,1)S(1)} %multiply_convert_fusion.refs_0_), channel_id=1, source_target_pairs={{0,4},{4,8},{8,12},{12,0},{1,5},{5,9},{9,13},{13,1},{2,6},{6,10},{... | collective-permute-start | bytes 393224 | tf_op jit(solution)/shard_map/ppermute | solution.py:26
  75.5 11.0 %collective-permute-start.6 = (bf16[32,2048]{1,0:T(8,128)(2,1)S(1)}, bf16[32,2048]{1,0:T(8,128)(2,1)S(1)}, u32[]{:S(2)}, u32[]{:S(2)}) collective-permute-start(bf16[32,2048]{1,0:T(8,128)(2,1)S(1)} %multiply_convert_fusion.refs_0_), channel_id=1, source_target_pairs={{0,2},{2,0},{1,3},{3,1},{4,6},{6,4},{5,7},{7,5},{8,10},{10,8},{9,1... | collective-permute-start | bytes 393224 | tf_op jit(solution)/shard_map/ppermute | solution.py:26
  77.5 11.3 %collective-permute-start.19 = (bf16[32,2048]{1,0:T(8,128)(2,1)S(1)}, bf16[32,2048]{1,0:T(8,128)(2,1)S(1)}, u32[]{:S(2)}, u32[]{:S(2)}) collective-permute-start(bf16[32,2048]{1,0:T(8,128)(2,1)S(1)} %collective-permute-done.11.refs_6_), channel_id=1, source_target_pairs={{0,1},{1,0},{2,3},{3,2},{4,5},{5,4},{6,7},{7,6},{8,9},{9,8},{10,11... | collective-permute-start | bytes 393224 | tf_op jit(solution)/shard_map/ppermute | solution.py:26
  77.5 11.4 %collective-permute-start.12 = (bf16[32,2048]{1,0:T(8,128)(2,1)S(1)}, bf16[32,2048]{1,0:T(8,128)(2,1)S(1)}, u32[]{:S(2)}, u32[]{:S(2)}) collective-permute-start(bf16[32,2048]{1,0:T(8,128)(2,1)S(1)} %collective-permute-done.11.refs_6_), channel_id=1, source_target_pairs={{0,2},{2,0},{1,3},{3,1},{4,6},{6,4},{5,7},{7,5},{8,10},{10,8},{9,1... | collective-permute-start | bytes 393224 | tf_op jit(solution)/shard_map/ppermute | solution.py:26
  86.0 3.4 %collective-permute-start.17 = (bf16[32,2048]{1,0:T(8,128)(2,1)S(1)}, bf16[32,2048]{1,0:T(8,128)(2,1)S(1)}, u32[]{:S(2)}, u32[]{:S(2)}) collective-permute-start(bf16[32,2048]{1,0:T(8,128)(2,1)S(1)} %collective-permute-done.9.refs_4_), channel_id=1, source_target_pairs={{0,1},{1,0},{2,3},{3,2},{4,5},{5,4},{6,7},{7,6},{8,9},{9,8},{10,11... | collective-permute-start | bytes 393224 | tf_op jit(solution)/shard_map/ppermute | solution.py:26
  86.0 6.3 %collective-permute-start.10 = (bf16[32,2048]{1,0:T(8,128)(2,1)S(1)}, bf16[32,2048]{1,0:T(8,128)(2,1)S(1)}, u32[]{:S(2)}, u32[]{:S(2)}) collective-permute-start(bf16[32,2048]{1,0:T(8,128)(2,1)S(1)} %collective-permute-done.9.refs_4_), channel_id=1, source_target_pairs={{0,2},{2,0},{1,3},{3,1},{4,6},{6,4},{5,7},{7,5},{8,10},{10,8},{9,1... | collective-permute-start | bytes 393224 | tf_op jit(solution)/shard_map/ppermute | solution.py:26
  86.6 8.2 %collective-permute-start.8 = (bf16[32,2048]{1,0:T(8,128)(2,1)S(1)}, bf16[32,2048]{1,0:T(8,128)(2,1)S(1)}, u32[]{:S(2)}, u32[]{:S(2)}) collective-permute-start(bf16[32,2048]{1,0:T(8,128)(2,1)S(1)} %collective-permute-done.7.refs_2_), channel_id=1, source_target_pairs={{0,2},{2,0},{1,3},{3,1},{4,6},{6,4},{5,7},{7,5},{8,10},{10,8},{9,1... | collective-permute-start | bytes 393224 | tf_op jit(solution)/shard_map/ppermute | solution.py:26
  88.8 6.1 %collective-permute-start.15 = (bf16[32,2048]{1,0:T(8,128)(2,1)S(1)}, bf16[32,2048]{1,0:T(8,128)(2,1)S(1)}, u32[]{:S(2)}, u32[]{:S(2)}) collective-permute-start(bf16[32,2048]{1,0:T(8,128)(2,1)S(1)} %collective-permute-done.7.refs_2_), channel_id=1, source_target_pairs={{0,1},{1,0},{2,3},{3,2},{4,5},{5,4},{6,7},{7,6},{8,9},{9,8},{10,11... | collective-permute-start | bytes 393224 | tf_op jit(solution)/shard_map/ppermute | solution.py:26
  88.9 6.1 %collective-permute-start.14 = (bf16[32,2048]{1,0:T(8,128)(2,1)S(1)}, bf16[32,2048]{1,0:T(8,128)(2,1)S(1)}, u32[]{:S(2)}, u32[]{:S(2)}) collective-permute-start(bf16[32,2048]{1,0:T(8,128)(2,1)S(1)} %collective-permute-done.6.refs_1_), channel_id=1, source_target_pairs={{0,1},{1,0},{2,3},{3,2},{4,5},{5,4},{6,7},{7,6},{8,9},{9,8},{10,11... | collective-permute-start | bytes 393224 | tf_op jit(solution)/shard_map/ppermute | solution.py:26
  89.4 5.6 %collective-permute-start.20 = (bf16[32,2048]{1,0:T(8,128)(2,1)S(1)}, bf16[32,2048]{1,0:T(8,128)(2,1)S(1)}, u32[]{:S(2)}, u32[]{:S(2)}) collective-permute-start(bf16[32,2048]{1,0:T(8,128)(2,1)S(1)} %collective-permute-done.12.refs_7_), channel_id=1, source_target_pairs={{0,1},{1,0},{2,3},{3,2},{4,5},{5,4},{6,7},{7,6},{8,9},{9,8},{10,11... | collective-permute-start | bytes 393224 | tf_op jit(solution)/shard_map/ppermute | solution.py:26
  92.3 2.7 %collective-permute-start.18 = (bf16[32,2048]{1,0:T(8,128)(2,1)S(1)}, bf16[32,2048]{1,0:T(8,128)(2,1)S(1)}, u32[]{:S(2)}, u32[]{:S(2)}) collective-permute-start(bf16[32,2048]{1,0:T(8,128)(2,1)S(1)} %collective-permute-done.10.refs_5_), channel_id=1, source_target_pairs={{0,1},{1,0},{2,3},{3,2},{4,5},{5,4},{6,7},{7,6},{8,9},{9,8},{10,11... | collective-permute-start | bytes 393224 | tf_op jit(solution)/shard_map/ppermute | solution.py:26
  94.8 1.3 collective-permute-start.16
  116.9 2.7 %collective-permute-start.21 = (bf16[256,2048]{1,0:T(8,128)(2,1)S(1)}, bf16[256,2048]{1,0:T(8,128)(2,1)S(1)}, u32[]{:S(2)}, u32[]{:S(2)}) collective-permute-start(bf16[256,2048]{1,0:T(8,128)(2,1)S(1)} %get-tuple-element.8), channel_id=1, source_target_pairs={{0,1},{1,0},{2,3},{3,2},{4,5},{5,4},{6,7},{7,6},{8,9},{9,8},{10,11... | collective-permute-start | bytes 3145736 | tf_op jit(solution)/shard_map/ppermute | solution.py:26
  120.0 6.4 %collective-permute-start.27 = (bf16[32,2048]{1,0:T(8,128)(2,1)S(1)}, bf16[32,2048]{1,0:T(8,128)(2,1)S(1)}, u32[]{:S(2)}, u32[]{:S(2)}) collective-permute-start(bf16[32,2048]{1,0:T(8,128)(2,1)S(1)} %get-tuple-element.10), channel_id=1, source_target_pairs={{0,2},{2,0},{1,3},{3,1},{4,6},{6,4},{5,7},{7,5},{8,10},{10,8},{9,1... | collective-permute-start | bytes 393224 | tf_op jit(solution)/shard_map/ppermute | solution.py:26
  120.6 8.6 %collective-permute-start.25 = (bf16[32,2048]{1,0:T(8,128)(2,1)S(1)}, bf16[32,2048]{1,0:T(8,128)(2,1)S(1)}, u32[]{:S(2)}, u32[]{:S(2)}) collective-permute-start(bf16[32,2048]{1,0:T(8,128)(2,1)S(1)} %get-tuple-element.11), channel_id=1, source_target_pairs={{0,2},{2,0},{1,3},{3,1},{4,6},{6,4},{5,7},{7,5},{8,10},{10,8},{9,1... | collective-permute-start | bytes 393224 | tf_op jit(solution)/shard_map/ppermute | solution.py:26
  122.1 9.9 %collective-permute-start.23 = (bf16[32,2048]{1,0:T(8,128)(2,1)S(1)}, bf16[32,2048]{1,0:T(8,128)(2,1)S(1)}, u32[]{:S(2)}, u32[]{:S(2)}) collective-permute-start(bf16[32,2048]{1,0:T(8,128)(2,1)S(1)} %get-tuple-element.12), channel_id=1, source_target_pairs={{0,2},{2,0},{1,3},{3,1},{4,6},{6,4},{5,7},{7,5},{8,10},{10,8},{9,1... | collective-permute-start | bytes 393224 | tf_op jit(solution)/shard_map/ppermute | solution.py:26
  122.7 13.9 %collective-permute-start.22 = (bf16[32,2048]{1,0:T(8,128)(2,1)S(1)}, bf16[32,2048]{1,0:T(8,128)(2,1)S(1)}, u32[]{:S(2)}, u32[]{:S(2)}) collective-permute-start(bf16[32,2048]{1,0:T(8,128)(2,1)S(1)} %get-tuple-element.9), channel_id=1, source_target_pairs={{0,2},{2,0},{1,3},{3,1},{4,6},{6,4},{5,7},{7,5},{8,10},{10,8},{9,1... | collective-permute-start | bytes 393224 | tf_op jit(solution)/shard_map/ppermute | solution.py:26
  132.2 7.4 %collective-permute-start.24 = (bf16[32,2048]{1,0:T(8,128)(2,1)S(1)}, bf16[32,2048]{1,0:T(8,128)(2,1)S(1)}, u32[]{:S(2)}, u32[]{:S(2)}) collective-permute-start(bf16[32,2048]{1,0:T(8,128)(2,1)S(1)} %get-tuple-element.13), channel_id=1, source_target_pairs={{0,12},{4,0},{8,4},{12,8},{1,13},{5,1},{9,5},{13,9},{2,14},{6,2},{... | collective-permute-start | bytes 393224 | tf_op jit(solution)/shard_map/ppermute | solution.py:26
  133.2 9.0 %collective-permute-start.28 = (bf16[32,2048]{1,0:T(8,128)(2,1)S(1)}, bf16[32,2048]{1,0:T(8,128)(2,1)S(1)}, u32[]{:S(2)}, u32[]{:S(2)}) collective-permute-start(bf16[32,2048]{1,0:T(8,128)(2,1)S(1)} %get-tuple-element.14), channel_id=1, source_target_pairs={{0,4},{4,8},{8,12},{12,0},{1,5},{5,9},{9,13},{13,1},{2,6},{6,10},{... | collective-permute-start | bytes 393224 | tf_op jit(solution)/shard_map/ppermute | solution.py:26
  134.3 11.3 %collective-permute-start.26 = (bf16[32,2048]{1,0:T(8,128)(2,1)S(1)}, bf16[32,2048]{1,0:T(8,128)(2,1)S(1)}, u32[]{:S(2)}, u32[]{:S(2)}) collective-permute-start(bf16[32,2048]{1,0:T(8,128)(2,1)S(1)} %get-tuple-element.15), channel_id=1, source_target_pairs={{0,8},{4,12},{8,0},{12,4},{1,9},{5,13},{9,1},{13,5},{2,10},{6,14},... | collective-permute-start | bytes 393224 | tf_op jit(solution)/shard_map/ppermute | solution.py:26

commit v2 on v1

--- a/solution.py
+++ b/solution.py
@@ -26,9 +26,15 @@
     return lax.ppermute(x, axis, [(i, (i + steps) % size) for i in range(size)])
 
 
+def dot_rows(a, b):
+    return lax.dot_general(a, b, (((1,), (1,)), ((), ())), preferred_element_type=F32)
+
+
 def attention_kernel(n_ctx, n_exp, n_tp, rows, heads, relative, place, q_ref, *refs):
     kv_refs, w_ref, o_ref = refs[:n_ctx], refs[n_ctx], refs[n_ctx + 1]
-    k_all, v_all, att, att_rel = refs[n_ctx + 2 :]
+    k_all, v_all, att, att_rel, w_all, w_sem = refs[n_ctx + 2 :]
+    fetch = pltpu.make_async_copy(w_ref, w_all, w_sem)
+    fetch.start()
     ctx, exp, tp = place[0], place[1], place[2]
     for z in range(n_ctx):
         k_all[z * rows : (z + 1) * rows, :] = kv_refs[z][:rows, :HEAD_DIMENSION]
@@ -39,7 +45,7 @@
     scale = 1.0 / math.sqrt(HEAD_DIMENSION)
     for h in range(heads):
         q = q_ref[:, h * HEAD_DIMENSION : (h + 1) * HEAD_DIMENSION]
-        s = lax.dot_general(q, k_all[...], (((1,), (1,)), ((), ())), preferred_element_type=F32)
+        s = dot_rows(q, k_all[...])
         s = jnp.where(allowed, s * scale, -1e30)
         weights = jnp.exp(s - jnp.max(s, axis=1, keepdims=True))
         total = jnp.sum(weights, axis=1, keepdims=True)
@@ -47,7 +53,8 @@
         att[:, h * HEAD_DIMENSION : (h + 1) * HEAD_DIMENSION] = (out / total).astype(BF)
     part = rows // (n_exp * n_tp)
     if not relative:
-        o_ref[...] = jnp.dot(att[...], w_ref[...], preferred_element_type=F32).astype(BF)
+        fetch.wait()
+        o_ref[...] = jnp.dot(att[...], w_all[...], preferred_element_type=F32).astype(BF)
         return
     for t in range(n_tp):
         for x in range(n_exp):
@@ -55,7 +62,8 @@
             source = pl.ds(pl.multiple_of(owner * part, part), part)
             at = (t * n_exp + x) * part
             att_rel[at : at + part, :] = att[source, :]
-    o_ref[...] = jnp.dot(att_rel[...], w_ref[...], preferred_element_type=F32).astype(BF)
+    fetch.wait()
+    o_ref[...] = jnp.dot(att_rel[...], w_all[...], preferred_element_type=F32).astype(BF)
 
 
 def attend_project(queries, pieces, out_weight, place, n_exp, n_tp, relative):
@@ -68,13 +76,16 @@
             attention_kernel, n_ctx, n_exp, n_tp, rows, width // HEAD_DIMENSION, relative
         ),
         out_shape=jax.ShapeDtypeStruct((rows, model), BF),
-        in_specs=[pl.BlockSpec(memory_space=pltpu.SMEM)] + [vmem] * (n_ctx + 2),
+        in_specs=[pl.BlockSpec(memory_space=pltpu.SMEM)] + [vmem] * (n_ctx + 1)
+        + [pl.BlockSpec(memory_space=pltpu.HBM)],
         out_specs=vmem,
         scratch_shapes=[
             pltpu.VMEM((n_ctx * rows, HEAD_DIMENSION), BF),
             pltpu.VMEM((n_ctx * rows, HEAD_DIMENSION), BF),
             pltpu.VMEM((rows, width), BF),
             pltpu.VMEM((rows, width), BF),
+            pltpu.VMEM((width, model), BF),
+            pltpu.SemaphoreType.DMA,
         ],
         compiler_params=pltpu.CompilerParams(vmem_limit_bytes=32 * MIB),
         cost_estimate=pl.CostEstimate(
@@ -106,8 +117,8 @@
     x = jnp.dot(pick, x_all[...], preferred_element_type=F32).astype(BF)
     out = None
     for h in range(halves):
-        gate = jnp.dot(x, wg_ref[h], preferred_element_type=F32)
-        up = jnp.dot(x, wu_ref[h], preferred_element_type=F32)
+        gate = dot_rows(x, wg_ref[h])
+        up = dot_rows(x, wu_ref[h])
         act = (gate * jax.nn.sigmoid(gate) * up).astype(BF)
         term = jnp.dot(act, wd_ref[h], preferred_element_type=F32)
         out = term if out is None else out + term
@@ -127,9 +138,11 @@
 
 def run_experts(keys, weights, pieces, w_gate, w_up, w_down, slots):
     n_exp, tokens = keys.shape
-    rows, model, hidden = w_gate.shape
+    rows, hidden, model = w_down.shape
     halves = rows // n_exp
     part = tokens // len(pieces)
+    w_gate = jnp.swapaxes(w_gate, 1, 2)
+    w_up = jnp.swapaxes(w_up, 1, 2)
 
     def whole(shape):
         return pl.BlockSpec(shape, lambda e: (0,) * len(shape), pipeline_mode=pl.Buffered(1))
@@ -142,8 +155,8 @@
         in_specs=[whole((n_exp, tokens))] * 2
         + [whole((part, model))] * len(pieces)
         + [
-            pl.BlockSpec((halves, model, hidden), lambda e: (e, 0, 0)),
-            pl.BlockSpec((halves, model, hidden), lambda e: (e, 0, 0)),
+            pl.BlockSpec((halves, hidden, model), lambda e: (e, 0, 0)),
+            pl.BlockSpec((halves, hidden, model), lambda e: (e, 0, 0)),
             pl.BlockSpec((halves, hidden, model), lambda e: (e, 0, 0)),
         ],
         out_specs=[whole((tokens // 2, model))] * 2,

time: 148 us -> 107 us (0.72)
  local copies, waits for them, and re-layouts: 46.4 us -> 5.15 us
  starting transfers between devices: 24.9 us -> 27.7 us
  waiting for transfers between devices: 44.5 us -> 42.9 us
    unnamed x8 -> x6, local copies, waits for them, and re-layouts: 44.4 us -> 3.14 us
    ppermute x29, starting transfers between devices: 24.9 us -> 27.7 us  [shift(): return lax.ppermute(x, axis, [(i, (i + steps) % size) for i in range(size)])]
    ppermute x29, waiting for transfers between devices: 44.5 us -> 42.9 us  [shift(): return lax.ppermute(x, axis, [(i, (i + steps) % size) for i in range(size)])]
  transfers between devices with their start and end apart: 29 -> 29, of which waited for: 15 -> 16; matrix products, arithmetic and copies ran while one was open for 31% -> 3% of each run, Pallas kernels for 0% -> 0%
where the time goes in v2:
time: 107 us; the launch traced here: 106 us
  waiting for transfers between devices  42.9 us (40%)
  starting transfers between devices  27.7 us (26%)
  Pallas kernels  24.4 us (23%)
  other arithmetic  5.89 us (6%)
  local copies, waits for them, and re-layouts  5.15 us (5%)
    ppermute x29, waiting for transfers between devices, shift(): return lax.ppermute(x, axis, [(i, (i + steps) % size) for i in range(size)])  42.9 us
    ppermute x29, starting transfers between devices, shift(): return lax.ppermute(x, axis, [(i, (i + steps) % size) for i in range(size)])  27.7 us
    pallas_call x1, Pallas kernels, run_experts(): pl.pallas_call(functools.partial(expert_kernel, len(pieces), tokens, slot...  20.5 us
    pallas_call x1, Pallas kernels, attend_project(): pl.pallas_call(functools.partial(attention_kernel, n_ctx, n_exp, n_tp, ro...  3.85 us
    unnamed x6, local copies, waits for them, and re-layouts  3.14 us
  transfers between devices with their start and end apart: 29, of which 16 were waited for; matrix products, arithmetic and copies ran while one was open for 3% of the time, Pallas kernels for 0%

profile of v2, /device:TPU:0, one launch (start us, length us, event | category | flops | bytes accessed | tf_op | source)
XLA Modules:
  0.0 106.5 jit_solution(8393494757949290260)
XLA Ops:
  0.0 0.7 reduce_sum.27
  0.7 0.7 fusion.20
  1.4 0.8 convert_bitcast_fusion.1
  2.2 0.8 constant_dynamic-slice_fusion.2
  3.0 5.1 %collective-permute-start.2 = (bf16[144,256]{1,0:T(8,128)(2,1)S(1)}, bf16[144,256]{1,0:T(8,128)(2,1)S(1)}, u32[]{:S(2)}, u32[]{:S(2)}) collective-permute-start(bf16[144,256]{1,0:T(8,128)(2,1)S(1)} %pad_maximum_fusion.1.refs_0_), channel_id=1, source_target_pairs={{0,12},{4,0},{8,4},{12,8},{1,13},{5,1},{9,5},{13,9},{2,14},{6,2},{... | collective-permute-start | bytes 221192 | tf_op jit(solution)/shard_map/ppermute | solution.py:26
  8.1 1.0 collective-permute-start
  9.2 0.7 reduce-precision_bitcast_fusion
  10.0 0.8 collective-permute-done.2.refs_3_
  10.9 4.3 %collective-permute-done.1.refs_2_ = bf16[144,256]{1,0:T(8,128)(2,1)S(1)} collective-permute-done((bf16[144,256]{1,0:T(8,128)(2,1)S(1)}, bf16[144,256]{1,0:T(8,128)(2,1)S(1)}, u32[]{:S(2)}, u32[]{:S(2)}) %collective-permute-start.1) | collective-permute-done | bytes 73760 | tf_op jit(solution)/shard_map/ppermute | solution.py:26
  15.1 2.2 %copy-done = bf16[1024,2048]{1,0:T(8,128)(2,1)S(1)} copy-done((bf16[1024,2048]{1,0:T(8,128)(2,1)S(1)}, bf16[1024,2048]{1,0:T(8,128)(2,1)}, u32[]{:S(2)}) %copy-start) | copy-done | bytes 4194328
  17.3 0.9 copy-done.1
  18.3 3.8 %attend_project.1 = bf16[128,2048]{1,0:T(8,128)(2,1)S(1)} custom-call(s32[3]{0:T(128)S(1)} %pad_add_fusion.place, bf16[128,1024]{1,0:T(8,128)(2,1)S(1)} %copy-done.1, bf16[144,256]{1,0:T(8,128)(2,1)S(1)} %pad_maximum_fusion.1.refs_0_, bf16[144,256]{1,0:T(8,128)(2,1)S(1)} %collective-permute-done.refs_1_, ...), custom_call_target="tpu_custom_call" | custom-call | flops 805306368 | bytes 4980736 | tf_op jit(solution)/shard_map/attend_project/pallas_call | solution.py:74
  22.3 1.6 %collective-permute-start.5 = (bf16[4,8,192]{2,1,0:T(8,128)(2,1)S(1)}, bf16[4,8,192]{2,1,0:T(8,128)(2,1)S(1)}, u32[]{:S(2)}, u32[]{:S(2)}) collective-permute-start(bf16[4,8,192]{2,1,0:T(8,128)(2,1)S(1)} %pad_maximum_fusion.2), channel_id=1, source_target_pairs={{0,2},{2,0},{1,3},{3,1},{4,6},{6,4},{5,7},{7,5},{8,10},{10,8},{9,1... | collective-permute-start | bytes 36872 | tf_op jit(solution)/shard_map/ppermute | solution.py:26
  24.2 1.9 %collective-permute-done.5 = bf16[4,8,192]{2,1,0:T(8,128)(2,1)S(1)} collective-permute-done((bf16[4,8,192]{2,1,0:T(8,128)(2,1)S(1)}, bf16[4,8,192]{2,1,0:T(8,128)(2,1)S(1)}, u32[]{:S(2)}, u32[]{:S(2)}) %collective-permute-start.5) | collective-permute-done | bytes 12320 | tf_op jit(solution)/shard_map/ppermute | solution.py:26
  26.2 0.2 pad_maximum_fusion
  26.5 1.6 %collective-permute-start.4 = (bf16[32,2048]{1,0:T(8,128)(2,1)S(1)}, bf16[32,2048]{1,0:T(8,128)(2,1)S(1)}, u32[]{:S(2)}, u32[]{:S(2)}) collective-permute-start(bf16[32,2048]{1,0:T(8,128)(2,1)S(1)} %slice.80), channel_id=1, source_target_pairs={{0,2},{2,0},{1,3},{3,1},{4,6},{6,4},{5,7},{7,5},{8,10},{10,8},{9,1... | collective-permute-start | bytes 393224 | tf_op jit(solution)/shard_map/ppermute | solution.py:26
  28.3 0.3 convert_bitcast_fusion
  28.6 3.0 %collective-permute-done.4 = bf16[32,2048]{1,0:T(8,128)(2,1)S(1)} collective-permute-done((bf16[32,2048]{1,0:T(8,128)(2,1)S(1)}, bf16[32,2048]{1,0:T(8,128)(2,1)S(1)}, u32[]{:S(2)}, u32[]{:S(2)}) %collective-permute-start.4) | collective-permute-done | bytes 131104 | tf_op jit(solution)/shard_map/ppermute | solution.py:26
  31.9 2.0 %collective-permute-start.11 = (bf16[32,2048]{1,0:T(8,128)(2,1)S(1)}, bf16[32,2048]{1,0:T(8,128)(2,1)S(1)}, u32[]{:S(2)}, u32[]{:S(2)}) collective-permute-start(bf16[32,2048]{1,0:T(8,128)(2,1)S(1)} %multiply_convert_fusion.refs_0_), channel_id=1, source_target_pairs={{0,12},{4,0},{8,4},{12,8},{1,13},{5,1},{9,5},{13,9},{2,14},{6,2},{... | collective-permute-start | bytes 393224 | tf_op jit(solution)/shard_map/ppermute | solution.py:26
  34.0 1.9 %collective-permute-start.7 = (bf16[32,2048]{1,0:T(8,128)(2,1)S(1)}, bf16[32,2048]{1,0:T(8,128)(2,1)S(1)}, u32[]{:S(2)}, u32[]{:S(2)}) collective-permute-start(bf16[32,2048]{1,0:T(8,128)(2,1)S(1)} %multiply_convert_fusion.refs_0_), channel_id=1, source_target_pairs={{0,4},{4,8},{8,12},{12,0},{1,5},{5,9},{9,13},{13,1},{2,6},{6,10},{... | collective-permute-start | bytes 393224 | tf_op jit(solution)/shard_map/ppermute | solution.py:26
  35.9 1.5 %collective-permute-start.6 = (bf16[32,2048]{1,0:T(8,128)(2,1)S(1)}, bf16[32,2048]{1,0:T(8,128)(2,1)S(1)}, u32[]{:S(2)}, u32[]{:S(2)}) collective-permute-start(bf16[32,2048]{1,0:T(8,128)(2,1)S(1)} %multiply_convert_fusion.refs_0_), channel_id=1, source_target_pairs={{0,2},{2,0},{1,3},{3,1},{4,6},{6,4},{5,7},{7,5},{8,10},{10,8},{9,1... | collective-permute-start | bytes 393224 | tf_op jit(solution)/shard_map/ppermute | solution.py:26
  37.5 0.3 fusion
  37.9 1.5 %collective-permute-start.12 = (bf16[32,2048]{1,0:T(8,128)(2,1)S(1)}, bf16[32,2048]{1,0:T(8,128)(2,1)S(1)}, u32[]{:S(2)}, u32[]{:S(2)}) collective-permute-start(bf16[32,2048]{1,0:T(8,128)(2,1)S(1)} %collective-permute-done.11.refs_6_), channel_id=1, source_target_pairs={{0,2},{2,0},{1,3},{3,1},{4,6},{6,4},{5,7},{7,5},{8,10},{10,8},{9,1... | collective-permute-start | bytes 393224 | tf_op jit(solution)/shard_map/ppermute | solution.py:26
  39.4 7.0 %collective-permute-done.9.refs_4_ = bf16[32,2048]{1,0:T(8,128)(2,1)S(1)} collective-permute-done((bf16[32,2048]{1,0:T(8,128)(2,1)S(1)}, bf16[32,2048]{1,0:T(8,128)(2,1)S(1)}, u32[]{:S(2)}, u32[]{:S(2)}) %collective-permute-start.9) | collective-permute-done | bytes 131104 | tf_op jit(solution)/shard_map/ppermute | solution.py:26
  46.4 1.5 %collective-permute-start.10 = (bf16[32,2048]{1,0:T(8,128)(2,1)S(1)}, bf16[32,2048]{1,0:T(8,128)(2,1)S(1)}, u32[]{:S(2)}, u32[]{:S(2)}) collective-permute-start(bf16[32,2048]{1,0:T(8,128)(2,1)S(1)} %collective-permute-done.9.refs_4_), channel_id=1, source_target_pairs={{0,2},{2,0},{1,3},{3,1},{4,6},{6,4},{5,7},{7,5},{8,10},{10,8},{9,1... | collective-permute-start | bytes 393224 | tf_op jit(solution)/shard_map/ppermute | solution.py:26
  47.9 0.5 collective-permute-start.8
  48.5 0.3 compare_reduce_fusion
  49.3 0.5 collective-permute-start.14
  49.9 2.8 %collective-permute-done.10.refs_5_ = bf16[32,2048]{1,0:T(8,128)(2,1)S(1)} collective-permute-done((bf16[32,2048]{1,0:T(8,128)(2,1)S(1)}, bf16[32,2048]{1,0:T(8,128)(2,1)S(1)}, u32[]{:S(2)}, u32[]{:S(2)}) %collective-permute-start.10) | collective-permute-done | bytes 131104 | tf_op jit(solution)/shard_map/ppermute | solution.py:26
  52.7 2.4 %collective-permute-done.8.refs_3_ = bf16[32,2048]{1,0:T(8,128)(2,1)S(1)} collective-permute-done((bf16[32,2048]{1,0:T(8,128)(2,1)S(1)}, bf16[32,2048]{1,0:T(8,128)(2,1)S(1)}, u32[]{:S(2)}, u32[]{:S(2)}) %collective-permute-start.8) | collective-permute-done | bytes 131104 | tf_op jit(solution)/shard_map/ppermute | solution.py:26
  55.4 1.1 %collective-permute-done.16.refs_11_ = bf16[32,2048]{1,0:T(8,128)(2,1)S(1)} collective-permute-done((bf16[32,2048]{1,0:T(8,128)(2,1)S(1)}, bf16[32,2048]{1,0:T(8,128)(2,1)S(1)}, u32[]{:S(2)}, u32[]{:S(2)}) %collective-permute-start.16) | collective-permute-done | bytes 131104 | tf_op jit(solution)/shard_map/ppermute | solution.py:26
  56.5 20.5 %experts.1 = (bf16[256,2048]{1,0:T(8,128)(2,1)S(1)}, bf16[256,2048]{1,0:T(8,128)(2,1)S(1)}) custom-call(s32[8,512]{1,0:T(8,128)S(1)} %reshape.133.key_ref, f32[8,512]{1,0:T(8,128)S(1)} %reshape.134.weight_ref, bf16[32,2048]{1,0:T(8,128)(2,1)S(1)} %multiply_convert_fusion.refs_0_, bf16[32,2048]{1,0:T(8,128)(2,1)S(1)} %collective-permute-done.6.refs_1_, ...), custom_call_target="tpu_custom_call" | custom-call | flops 4563402752 | bytes 41943040 | tf_op jit(solution)/shard_map/experts/pallas_call | solution.py:151
  77.3 2.5 %collective-permute-done.21 = bf16[256,2048]{1,0:T(8,128)(2,1)S(1)} collective-permute-done((bf16[256,2048]{1,0:T(8,128)(2,1)S(1)}, bf16[256,2048]{1,0:T(8,128)(2,1)S(1)}, u32[]{:S(2)}, u32[]{:S(2)}) %collective-permute-start.21) | collective-permute-done | bytes 1048608 | tf_op jit(solution)/shard_map/ppermute | solution.py:26
  79.8 0.4 add_convert_fusion
  80.2 1.6 %collective-permute-start.27 = (bf16[32,2048]{1,0:T(8,128)(2,1)S(1)}, bf16[32,2048]{1,0:T(8,128)(2,1)S(1)}, u32[]{:S(2)}, u32[]{:S(2)}) collective-permute-start(bf16[32,2048]{1,0:T(8,128)(2,1)S(1)} %get-tuple-element.10), channel_id=1, source_target_pairs={{0,2},{2,0},{1,3},{3,1},{4,6},{6,4},{5,7},{7,5},{8,10},{10,8},{9,1... | collective-permute-start | bytes 393224 | tf_op jit(solution)/shard_map/ppermute | solution.py:26
  81.8 0.5 collective-permute-start.25
  82.3 1.5 %collective-permute-start.23 = (bf16[32,2048]{1,0:T(8,128)(2,1)S(1)}, bf16[32,2048]{1,0:T(8,128)(2,1)S(1)}, u32[]{:S(2)}, u32[]{:S(2)}) collective-permute-start(bf16[32,2048]{1,0:T(8,128)(2,1)S(1)} %get-tuple-element.12), channel_id=1, source_target_pairs={{0,2},{2,0},{1,3},{3,1},{4,6},{6,4},{5,7},{7,5},{8,10},{10,8},{9,1... | collective-permute-start | bytes 393224 | tf_op jit(solution)/shard_map/ppermute | solution.py:26
  83.8 0.5 collective-permute-start.22
  84.3 2.3 %collective-permute-done.27 = bf16[32,2048]{1,0:T(8,128)(2,1)S(1)} collective-permute-done((bf16[32,2048]{1,0:T(8,128)(2,1)S(1)}, bf16[32,2048]{1,0:T(8,128)(2,1)S(1)}, u32[]{:S(2)}, u32[]{:S(2)}) %collective-permute-start.27) | collective-permute-done | bytes 131104 | tf_op jit(solution)/shard_map/ppermute | solution.py:26
  86.6 2.8 %collective-permute-done.25 = bf16[32,2048]{1,0:T(8,128)(2,1)S(1)} collective-permute-done((bf16[32,2048]{1,0:T(8,128)(2,1)S(1)}, bf16[32,2048]{1,0:T(8,128)(2,1)S(1)}, u32[]{:S(2)}, u32[]{:S(2)}) %collective-permute-start.25) | collective-permute-done | bytes 131104 | tf_op jit(solution)/shard_map/ppermute | solution.py:26
  89.4 2.8 %collective-permute-done.23 = bf16[32,2048]{1,0:T(8,128)(2,1)S(1)} collective-permute-done((bf16[32,2048]{1,0:T(8,128)(2,1)S(1)}, bf16[32,2048]{1,0:T(8,128)(2,1)S(1)}, u32[]{:S(2)}, u32[]{:S(2)}) %collective-permute-start.23) | collective-permute-done | bytes 131104 | tf_op jit(solution)/shard_map/ppermute | solution.py:26
  92.3 1.0 collective-permute-start.24
  93.3 1.1 %collective-permute-start.28 = (bf16[32,2048]{1,0:T(8,128)(2,1)S(1)}, bf16[32,2048]{1,0:T(8,128)(2,1)S(1)}, u32[]{:S(2)}, u32[]{:S(2)}) collective-permute-start(bf16[32,2048]{1,0:T(8,128)(2,1)S(1)} %get-tuple-element.14), channel_id=1, source_target_pairs={{0,4},{4,8},{8,12},{12,0},{1,5},{5,9},{9,13},{13,1},{2,6},{6,10},{... | collective-permute-start | bytes 393224 | tf_op jit(solution)/shard_map/ppermute | solution.py:26
  94.4 2.3 %collective-permute-start.26 = (bf16[32,2048]{1,0:T(8,128)(2,1)S(1)}, bf16[32,2048]{1,0:T(8,128)(2,1)S(1)}, u32[]{:S(2)}, u32[]{:S(2)}) collective-permute-start(bf16[32,2048]{1,0:T(8,128)(2,1)S(1)} %get-tuple-element.15), channel_id=1, source_target_pairs={{0,8},{4,12},{8,0},{12,4},{1,9},{5,13},{9,1},{13,5},{2,10},{6,14},... | collective-permute-start | bytes 393224 | tf_op jit(solution)/shard_map/ppermute | solution.py:26
  96.7 3.1 %collective-permute-done.24 = bf16[32,2048]{1,0:T(8,128)(2,1)S(1)} collective-permute-done((bf16[32,2048]{1,0:T(8,128)(2,1)S(1)}, bf16[32,2048]{1,0:T(8,128)(2,1)S(1)}, u32[]{:S(2)}, u32[]{:S(2)}) %collective-permute-start.24) | collective-permute-done | bytes 131104 | tf_op jit(solution)/shard_map/ppermute | solution.py:26
  99.8 2.5 %collective-permute-done.28 = bf16[32,2048]{1,0:T(8,128)(2,1)S(1)} collective-permute-done((bf16[32,2048]{1,0:T(8,128)(2,1)S(1)}, bf16[32,2048]{1,0:T(8,128)(2,1)S(1)}, u32[]{:S(2)}, u32[]{:S(2)}) %collective-permute-start.28) | collective-permute-done | bytes 131104 | tf_op jit(solution)/shard_map/ppermute | solution.py:26
  102.3 3.4 %collective-permute-done.26 = bf16[32,2048]{1,0:T(8,128)(2,1)S(1)} collective-permute-done((bf16[32,2048]{1,0:T(8,128)(2,1)S(1)}, bf16[32,2048]{1,0:T(8,128)(2,1)S(1)}, u32[]{:S(2)}, u32[]{:S(2)}) %collective-permute-start.26) | collective-permute-done | bytes 131104 | tf_op jit(solution)/shard_map/ppermute | solution.py:26
  105.7 0.8 fusion.8
  (63 shorter events, 2.9 us)
Async XLA Ops:
  3.0 28.5 %copy-start.2 = (bf16[32,2048]{1,0:T(8,128)(2,1)S(1)}, bf16[32,2048]{1,0:T(8,128)(2,1)}, u32[]{:S(2)}) copy-start(bf16[32,2048]{1,0:T(8,128)(2,1)} %param.14) | copy-start | bytes 393220
  3.0 7.8 %collective-permute-start.2 = (bf16[144,256]{1,0:T(8,128)(2,1)S(1)}, bf16[144,256]{1,0:T(8,128)(2,1)S(1)}, u32[]{:S(2)}, u32[]{:S(2)}) collective-permute-start(bf16[144,256]{1,0:T(8,128)(2,1)S(1)} %pad_maximum_fusion.1.refs_0_), channel_id=1, source_target_pairs={{0,12},{4,0},{8,4},{12,8},{1,13},{5,1},{9,5},{13,9},{2,14},{6,2},{... | collective-permute-start | bytes 221192 | tf_op jit(solution)/shard_map/ppermute | solution.py:26
  8.1 7.0 %collective-permute-start.1 = (bf16[144,256]{1,0:T(8,128)(2,1)S(1)}, bf16[144,256]{1,0:T(8,128)(2,1)S(1)}, u32[]{:S(2)}, u32[]{:S(2)}) collective-permute-start(bf16[144,256]{1,0:T(8,128)(2,1)S(1)} %pad_maximum_fusion.1.refs_0_), channel_id=1, source_target_pairs={{0,8},{4,12},{8,0},{12,4},{1,9},{5,13},{9,1},{13,5},{2,10},{6,14},... | collective-permute-start | bytes 221192 | tf_op jit(solution)/shard_map/ppermute | solution.py:26
  8.1 7.0 %collective-permute-start = (bf16[144,256]{1,0:T(8,128)(2,1)S(1)}, bf16[144,256]{1,0:T(8,128)(2,1)S(1)}, u32[]{:S(2)}, u32[]{:S(2)}) collective-permute-start(bf16[144,256]{1,0:T(8,128)(2,1)S(1)} %pad_maximum_fusion.1.refs_0_), channel_id=1, source_target_pairs={{0,4},{4,8},{8,12},{12,0},{1,5},{5,9},{9,13},{13,1},{2,6},{6,10},{... | collective-permute-start | bytes 221192 | tf_op jit(solution)/shard_map/ppermute | solution.py:26
  15.1 2.2 %copy-start = (bf16[1024,2048]{1,0:T(8,128)(2,1)S(1)}, bf16[1024,2048]{1,0:T(8,128)(2,1)}, u32[]{:S(2)}) copy-start(bf16[1024,2048]{1,0:T(8,128)(2,1)} %refs_4_.1) | copy-start | bytes 12582916
  17.3 0.9 copy-start.1
  22.2 4.3 %collective-permute-start.3 = (bf16[64,2048]{1,0:T(8,128)(2,1)S(1)}, bf16[64,2048]{1,0:T(8,128)(2,1)S(1)}, u32[]{:S(2)}, u32[]{:S(2)}) collective-permute-start(bf16[64,2048]{1,0:T(8,128)(2,1)S(1)} %slice.78), channel_id=1, source_target_pairs={{0,1},{1,0},{2,3},{3,2},{4,5},{5,4},{6,7},{7,6},{8,9},{9,8},{10,11... | collective-permute-start | bytes 786440 | tf_op jit(solution)/shard_map/ppermute | solution.py:26
  22.3 3.8 %collective-permute-start.5 = (bf16[4,8,192]{2,1,0:T(8,128)(2,1)S(1)}, bf16[4,8,192]{2,1,0:T(8,128)(2,1)S(1)}, u32[]{:S(2)}, u32[]{:S(2)}) collective-permute-start(bf16[4,8,192]{2,1,0:T(8,128)(2,1)S(1)} %pad_maximum_fusion.2), channel_id=1, source_target_pairs={{0,2},{2,0},{1,3},{3,1},{4,6},{6,4},{5,7},{7,5},{8,10},{10,8},{9,1... | collective-permute-start | bytes 36872 | tf_op jit(solution)/shard_map/ppermute | solution.py:26
  26.5 5.0 %collective-permute-start.4 = (bf16[32,2048]{1,0:T(8,128)(2,1)S(1)}, bf16[32,2048]{1,0:T(8,128)(2,1)S(1)}, u32[]{:S(2)}, u32[]{:S(2)}) collective-permute-start(bf16[32,2048]{1,0:T(8,128)(2,1)S(1)} %slice.80), channel_id=1, source_target_pairs={{0,2},{2,0},{1,3},{3,1},{4,6},{6,4},{5,7},{7,5},{8,10},{10,8},{9,1... | collective-permute-start | bytes 393224 | tf_op jit(solution)/shard_map/ppermute | solution.py:26
  31.8 6.1 %collective-permute-start.13 = (bf16[32,2048]{1,0:T(8,128)(2,1)S(1)}, bf16[32,2048]{1,0:T(8,128)(2,1)S(1)}, u32[]{:S(2)}, u32[]{:S(2)}) collective-permute-start(bf16[32,2048]{1,0:T(8,128)(2,1)S(1)} %multiply_convert_fusion.refs_0_), channel_id=1, source_target_pairs={{0,1},{1,0},{2,3},{3,2},{4,5},{5,4},{6,7},{7,6},{8,9},{9,8},{10,11... | collective-permute-start | bytes 393224 | tf_op jit(solution)/shard_map/ppermute | solution.py:26
  31.9 6.0 %collective-permute-start.11 = (bf16[32,2048]{1,0:T(8,128)(2,1)S(1)}, bf16[32,2048]{1,0:T(8,128)(2,1)S(1)}, u32[]{:S(2)}, u32[]{:S(2)}) collective-permute-start(bf16[32,2048]{1,0:T(8,128)(2,1)S(1)} %multiply_convert_fusion.refs_0_), channel_id=1, source_target_pairs={{0,12},{4,0},{8,4},{12,8},{1,13},{5,1},{9,5},{13,9},{2,14},{6,2},{... | collective-permute-start | bytes 393224 | tf_op jit(solution)/shard_map/ppermute | solution.py:26
  34.0 12.5 %collective-permute-start.9 = (bf16[32,2048]{1,0:T(8,128)(2,1)S(1)}, bf16[32,2048]{1,0:T(8,128)(2,1)S(1)}, u32[]{:S(2)}, u32[]{:S(2)}) collective-permute-start(bf16[32,2048]{1,0:T(8,128)(2,1)S(1)} %multiply_convert_fusion.refs_0_), channel_id=1, source_target_pairs={{0,8},{4,12},{8,0},{12,4},{1,9},{5,13},{9,1},{13,5},{2,10},{6,14},... | collective-permute-start | bytes 393224 | tf_op jit(solution)/shard_map/ppermute | solution.py:26
  34.0 12.4 %collective-permute-start.7 = (bf16[32,2048]{1,0:T(8,128)(2,1)S(1)}, bf16[32,2048]{1,0:T(8,128)(2,1)S(1)}, u32[]{:S(2)}, u32[]{:S(2)}) collective-permute-start(bf16[32,2048]{1,0:T(8,128)(2,1)S(1)} %multiply_convert_fusion.refs_0_), channel_id=1, source_target_pairs={{0,4},{4,8},{8,12},{12,0},{1,5},{5,9},{9,13},{13,1},{2,6},{6,10},{... | collective-permute-start | bytes 393224 | tf_op jit(solution)/shard_map/ppermute | solution.py:26
  35.9 12.0 %collective-permute-start.6 = (bf16[32,2048]{1,0:T(8,128)(2,1)S(1)}, bf16[32,2048]{1,0:T(8,128)(2,1)S(1)}, u32[]{:S(2)}, u32[]{:S(2)}) collective-permute-start(bf16[32,2048]{1,0:T(8,128)(2,1)S(1)} %multiply_convert_fusion.refs_0_), channel_id=1, source_target_pairs={{0,2},{2,0},{1,3},{3,1},{4,6},{6,4},{5,7},{7,5},{8,10},{10,8},{9,1... | collective-permute-start | bytes 393224 | tf_op jit(solution)/shard_map/ppermute | solution.py:26
  37.9 11.3 %collective-permute-start.19 = (bf16[32,2048]{1,0:T(8,128)(2,1)S(1)}, bf16[32,2048]{1,0:T(8,128)(2,1)S(1)}, u32[]{:S(2)}, u32[]{:S(2)}) collective-permute-start(bf16[32,2048]{1,0:T(8,128)(2,1)S(1)} %collective-permute-done.11.refs_6_), channel_id=1, source_target_pairs={{0,1},{1,0},{2,3},{3,2},{4,5},{5,4},{6,7},{7,6},{8,9},{9,8},{10,11... | collective-permute-start | bytes 393224 | tf_op jit(solution)/shard_map/ppermute | solution.py:26
  37.9 11.4 %collective-permute-start.12 = (bf16[32,2048]{1,0:T(8,128)(2,1)S(1)}, bf16[32,2048]{1,0:T(8,128)(2,1)S(1)}, u32[]{:S(2)}, u32[]{:S(2)}) collective-permute-start(bf16[32,2048]{1,0:T(8,128)(2,1)S(1)} %collective-permute-done.11.refs_6_), channel_id=1, source_target_pairs={{0,2},{2,0},{1,3},{3,1},{4,6},{6,4},{5,7},{7,5},{8,10},{10,8},{9,1... | collective-permute-start | bytes 393224 | tf_op jit(solution)/shard_map/ppermute | solution.py:26
  46.4 3.4 %collective-permute-start.17 = (bf16[32,2048]{1,0:T(8,128)(2,1)S(1)}, bf16[32,2048]{1,0:T(8,128)(2,1)S(1)}, u32[]{:S(2)}, u32[]{:S(2)}) collective-permute-start(bf16[32,2048]{1,0:T(8,128)(2,1)S(1)} %collective-permute-done.9.refs_4_), channel_id=1, source_target_pairs={{0,1},{1,0},{2,3},{3,2},{4,5},{5,4},{6,7},{7,6},{8,9},{9,8},{10,11... | collective-permute-start | bytes 393224 | tf_op jit(solution)/shard_map/ppermute | solution.py:26
  46.4 6.3 %collective-permute-start.10 = (bf16[32,2048]{1,0:T(8,128)(2,1)S(1)}, bf16[32,2048]{1,0:T(8,128)(2,1)S(1)}, u32[]{:S(2)}, u32[]{:S(2)}) collective-permute-start(bf16[32,2048]{1,0:T(8,128)(2,1)S(1)} %collective-permute-done.9.refs_4_), channel_id=1, source_target_pairs={{0,2},{2,0},{1,3},{3,1},{4,6},{6,4},{5,7},{7,5},{8,10},{10,8},{9,1... | collective-permute-start | bytes 393224 | tf_op jit(solution)/shard_map/ppermute | solution.py:26
  47.9 7.2 %collective-permute-start.8 = (bf16[32,2048]{1,0:T(8,128)(2,1)S(1)}, bf16[32,2048]{1,0:T(8,128)(2,1)S(1)}, u32[]{:S(2)}, u32[]{:S(2)}) collective-permute-start(bf16[32,2048]{1,0:T(8,128)(2,1)S(1)} %collective-permute-done.7.refs_2_), channel_id=1, source_target_pairs={{0,2},{2,0},{1,3},{3,1},{4,6},{6,4},{5,7},{7,5},{8,10},{10,8},{9,1... | collective-permute-start | bytes 393224 | tf_op jit(solution)/shard_map/ppermute | solution.py:26
  49.2 6.1 %collective-permute-start.15 = (bf16[32,2048]{1,0:T(8,128)(2,1)S(1)}, bf16[32,2048]{1,0:T(8,128)(2,1)S(1)}, u32[]{:S(2)}, u32[]{:S(2)}) collective-permute-start(bf16[32,2048]{1,0:T(8,128)(2,1)S(1)} %collective-permute-done.7.refs_2_), channel_id=1, source_target_pairs={{0,1},{1,0},{2,3},{3,2},{4,5},{5,4},{6,7},{7,6},{8,9},{9,8},{10,11... | collective-permute-start | bytes 393224 | tf_op jit(solution)/shard_map/ppermute | solution.py:26
  49.3 6.1 %collective-permute-start.14 = (bf16[32,2048]{1,0:T(8,128)(2,1)S(1)}, bf16[32,2048]{1,0:T(8,128)(2,1)S(1)}, u32[]{:S(2)}, u32[]{:S(2)}) collective-permute-start(bf16[32,2048]{1,0:T(8,128)(2,1)S(1)} %collective-permute-done.6.refs_1_), channel_id=1, source_target_pairs={{0,1},{1,0},{2,3},{3,2},{4,5},{5,4},{6,7},{7,6},{8,9},{9,8},{10,11... | collective-permute-start | bytes 393224 | tf_op jit(solution)/shard_map/ppermute | solution.py:26
  49.8 5.6 %collective-permute-start.20 = (bf16[32,2048]{1,0:T(8,128)(2,1)S(1)}, bf16[32,2048]{1,0:T(8,128)(2,1)S(1)}, u32[]{:S(2)}, u32[]{:S(2)}) collective-permute-start(bf16[32,2048]{1,0:T(8,128)(2,1)S(1)} %collective-permute-done.12.refs_7_), channel_id=1, source_target_pairs={{0,1},{1,0},{2,3},{3,2},{4,5},{5,4},{6,7},{7,6},{8,9},{9,8},{10,11... | collective-permute-start | bytes 393224 | tf_op jit(solution)/shard_map/ppermute | solution.py:26
  52.7 2.7 %collective-permute-start.18 = (bf16[32,2048]{1,0:T(8,128)(2,1)S(1)}, bf16[32,2048]{1,0:T(8,128)(2,1)S(1)}, u32[]{:S(2)}, u32[]{:S(2)}) collective-permute-start(bf16[32,2048]{1,0:T(8,128)(2,1)S(1)} %collective-permute-done.10.refs_5_), channel_id=1, source_target_pairs={{0,1},{1,0},{2,3},{3,2},{4,5},{5,4},{6,7},{7,6},{8,9},{9,8},{10,11... | collective-permute-start | bytes 393224 | tf_op jit(solution)/shard_map/ppermute | solution.py:26
  55.1 1.3 %collective-permute-start.16 = (bf16[32,2048]{1,0:T(8,128)(2,1)S(1)}, bf16[32,2048]{1,0:T(8,128)(2,1)S(1)}, u32[]{:S(2)}, u32[]{:S(2)}) collective-permute-start(bf16[32,2048]{1,0:T(8,128)(2,1)S(1)} %collective-permute-done.8.refs_3_), channel_id=1, source_target_pairs={{0,1},{1,0},{2,3},{3,2},{4,5},{5,4},{6,7},{7,6},{8,9},{9,8},{10,11... | collective-permute-start | bytes 393224 | tf_op jit(solution)/shard_map/ppermute | solution.py:26
  77.0 2.7 %collective-permute-start.21 = (bf16[256,2048]{1,0:T(8,128)(2,1)S(1)}, bf16[256,2048]{1,0:T(8,128)(2,1)S(1)}, u32[]{:S(2)}, u32[]{:S(2)}) collective-permute-start(bf16[256,2048]{1,0:T(8,128)(2,1)S(1)} %get-tuple-element.8), channel_id=1, source_target_pairs={{0,1},{1,0},{2,3},{3,2},{4,5},{5,4},{6,7},{7,6},{8,9},{9,8},{10,11... | collective-permute-start | bytes 3145736 | tf_op jit(solution)/shard_map/ppermute | solution.py:26
  80.2 6.4 %collective-permute-start.27 = (bf16[32,2048]{1,0:T(8,128)(2,1)S(1)}, bf16[32,2048]{1,0:T(8,128)(2,1)S(1)}, u32[]{:S(2)}, u32[]{:S(2)}) collective-permute-start(bf16[32,2048]{1,0:T(8,128)(2,1)S(1)} %get-tuple-element.10), channel_id=1, source_target_pairs={{0,2},{2,0},{1,3},{3,1},{4,6},{6,4},{5,7},{7,5},{8,10},{10,8},{9,1... | collective-permute-start | bytes 393224 | tf_op jit(solution)/shard_map/ppermute | solution.py:26
  81.8 7.7 %collective-permute-start.25 = (bf16[32,2048]{1,0:T(8,128)(2,1)S(1)}, bf16[32,2048]{1,0:T(8,128)(2,1)S(1)}, u32[]{:S(2)}, u32[]{:S(2)}) collective-permute-start(bf16[32,2048]{1,0:T(8,128)(2,1)S(1)} %get-tuple-element.11), channel_id=1, source_target_pairs={{0,2},{2,0},{1,3},{3,1},{4,6},{6,4},{5,7},{7,5},{8,10},{10,8},{9,1... | collective-permute-start | bytes 393224 | tf_op jit(solution)/shard_map/ppermute | solution.py:26
  82.3 9.9 %collective-permute-start.23 = (bf16[32,2048]{1,0:T(8,128)(2,1)S(1)}, bf16[32,2048]{1,0:T(8,128)(2,1)S(1)}, u32[]{:S(2)}, u32[]{:S(2)}) collective-permute-start(bf16[32,2048]{1,0:T(8,128)(2,1)S(1)} %get-tuple-element.12), channel_id=1, source_target_pairs={{0,2},{2,0},{1,3},{3,1},{4,6},{6,4},{5,7},{7,5},{8,10},{10,8},{9,1... | collective-permute-start | bytes 393224 | tf_op jit(solution)/shard_map/ppermute | solution.py:26
  83.8 12.9 %collective-permute-start.22 = (bf16[32,2048]{1,0:T(8,128)(2,1)S(1)}, bf16[32,2048]{1,0:T(8,128)(2,1)S(1)}, u32[]{:S(2)}, u32[]{:S(2)}) collective-permute-start(bf16[32,2048]{1,0:T(8,128)(2,1)S(1)} %get-tuple-element.9), channel_id=1, source_target_pairs={{0,2},{2,0},{1,3},{3,1},{4,6},{6,4},{5,7},{7,5},{8,10},{10,8},{9,1... | collective-permute-start | bytes 393224 | tf_op jit(solution)/shard_map/ppermute | solution.py:26
  92.3 7.4 %collective-permute-start.24 = (bf16[32,2048]{1,0:T(8,128)(2,1)S(1)}, bf16[32,2048]{1,0:T(8,128)(2,1)S(1)}, u32[]{:S(2)}, u32[]{:S(2)}) collective-permute-start(bf16[32,2048]{1,0:T(8,128)(2,1)S(1)} %get-tuple-element.13), channel_id=1, source_target_pairs={{0,12},{4,0},{8,4},{12,8},{1,13},{5,1},{9,5},{13,9},{2,14},{6,2},{... | collective-permute-start | bytes 393224 | tf_op jit(solution)/shard_map/ppermute | solution.py:26
  93.3 9.0 %collective-permute-start.28 = (bf16[32,2048]{1,0:T(8,128)(2,1)S(1)}, bf16[32,2048]{1,0:T(8,128)(2,1)S(1)}, u32[]{:S(2)}, u32[]{:S(2)}) collective-permute-start(bf16[32,2048]{1,0:T(8,128)(2,1)S(1)} %get-tuple-element.14), channel_id=1, source_target_pairs={{0,4},{4,8},{8,12},{12,0},{1,5},{5,9},{9,13},{13,1},{2,6},{6,10},{... | collective-permute-start | bytes 393224 | tf_op jit(solution)/shard_map/ppermute | solution.py:26
  94.4 11.3 %collective-permute-start.26 = (bf16[32,2048]{1,0:T(8,128)(2,1)S(1)}, bf16[32,2048]{1,0:T(8,128)(2,1)S(1)}, u32[]{:S(2)}, u32[]{:S(2)}) collective-permute-start(bf16[32,2048]{1,0:T(8,128)(2,1)S(1)} %get-tuple-element.15), channel_id=1, source_target_pairs={{0,8},{4,12},{8,0},{12,4},{1,9},{5,13},{9,1},{13,5},{2,10},{6,14},... | collective-permute-start | bytes 393224 | tf_op jit(solution)/shard_map/ppermute | solution.py:26

commit v3 on v2

v3 whole, which is shorter than its diff:
```python
import functools
import math

import jax
import jax.numpy as jnp
from jax import lax
from jax.experimental import pallas as pl
from jax.experimental.pallas import tpu as pltpu
from jax.sharding import PartitionSpec as P

HEAD_DIMENSION = 128
QUERY_HEADS = 32
KEY_VALUE_HEADS = 4
EXPERTS = 64
TOPK = 8
MIB = 1 << 20
BF = jnp.bfloat16
F32 = jnp.float32


def flip(x, axis, bit):
    return lax.ppermute(x, axis, [(i, i ^ bit) for i in range(lax.axis_size(axis))])


def from_earlier(x, axis, steps):
    size = lax.axis_size(axis)
    return lax.ppermute(x, axis, [(i, i + steps) for i in range(size - steps)])


def dot_rows(a, b):
    return lax.dot_general(a, b, (((1,), (1,)), ((), ())), preferred_element_type=F32)


def attention_kernel(n_ctx, n_exp, n_tp, rows, heads, relative, place, *refs):
    kv_refs, (q_hbm, w_hbm, o_ref) = refs[:n_ctx], refs[n_ctx : n_ctx + 3]
    k_all, v_all, q_all, att, att_rel, w_all, q_sem, w_sem = refs[n_ctx + 3 :]
    fetch_q = []
    for h in range(heads):
        columns = slice(h * HEAD_DIMENSION, (h + 1) * HEAD_DIMENSION)
        fetch_q.append(
            pltpu.make_async_copy(q_hbm.at[:, columns], q_all.at[:, columns], q_sem.at[h])
        )
        fetch_q[h].start()
    fetch_w = pltpu.make_async_copy(w_hbm, w_all, w_sem)
    fetch_w.start()
    ctx, exp, tp = place[0], place[1], place[2]
    for z in range(n_ctx):
        k_all[z * rows : (z + 1) * rows, :] = kv_refs[z][:, :HEAD_DIMENSION]
        v_all[z * rows : (z + 1) * rows, :] = kv_refs[z][:, HEAD_DIMENSION:]
    column = lax.broadcasted_iota(jnp.int32, (rows, n_ctx * rows), 1)
    row = lax.broadcasted_iota(jnp.int32, (rows, n_ctx * rows), 0)
    allowed = (column <= row) | ((column >= rows) & (column < (ctx + 1) * rows))
    scale = 1.0 / math.sqrt(HEAD_DIMENSION)
    for h in range(heads):
        columns = slice(h * HEAD_DIMENSION, (h + 1) * HEAD_DIMENSION)
        fetch_q[h].wait()
        s = dot_rows(q_all[:, columns], k_all[...])
        s = jnp.where(allowed, s * scale, -1e30)
        weights = jnp.exp(s - jnp.max(s, axis=1, keepdims=True))
        total = jnp.sum(weights, axis=1, keepdims=True)
        out = jnp.dot(weights.astype(BF), v_all[...], preferred_element_type=F32)
        att[:, columns] = (out / total).astype(BF)
    if relative:
        part = rows // (n_exp * n_tp)
        for t in range(n_tp):
            for x in range(n_exp):
                owner = lax.rem(exp + x, n_exp) * n_tp + lax.rem(tp + t, n_tp)
                source = pl.ds(pl.multiple_of(owner * part, part), part)
                at = (t * n_exp + x) * part
                att_rel[at : at + part, :] = att[source, :]
        att = att_rel
    fetch_w.wait()
    o_ref[...] = jnp.dot(att[...], w_all[...], preferred_element_type=F32).astype(BF)


def attend_project(queries, pieces, out_weight, place, n_exp, n_tp, relative):
    rows, width = queries.shape
    n_ctx, heads = len(pieces), width // HEAD_DIMENSION
    model = out_weight.shape[1]
    vmem = pl.BlockSpec(memory_space=pltpu.VMEM)
    hbm = pl.BlockSpec(memory_space=pltpu.HBM)
    return pl.pallas_call(
        functools.partial(attention_kernel, n_ctx, n_exp, n_tp, rows, heads, relative),
        out_shape=jax.ShapeDtypeStruct((rows, model), BF),
        in_specs=[pl.BlockSpec(memory_space=pltpu.SMEM)] + [vmem] * n_ctx + [hbm] * 2,
        out_specs=vmem,
        scratch_shapes=[
            pltpu.VMEM((n_ctx * rows, HEAD_DIMENSION), BF),
            pltpu.VMEM((n_ctx * rows, HEAD_DIMENSION), BF),
            pltpu.VMEM((rows, width), BF),
            pltpu.VMEM((rows, width), BF),
            pltpu.VMEM((rows, width), BF),
            pltpu.VMEM((width, model), BF),
            pltpu.SemaphoreType.DMA((heads,)),
            pltpu.SemaphoreType.DMA,
        ],
        compiler_params=pltpu.CompilerParams(vmem_limit_bytes=32 * MIB),
        cost_estimate=pl.CostEstimate(
            flops=2 * rows * width * (2 * n_ctx * rows + model),
            bytes_accessed=2 * (rows * width + width * model + rows * model),
            transcendentals=rows * n_ctx * rows * heads,
        ),
        name="attend_project",
    )(
        place,
        *pieces,
        pltpu.with_memory_space_constraint(queries, pltpu.HBM),
        pltpu.with_memory_space_constraint(out_weight, pltpu.HBM),
    )


def expert_kernel(n_pieces, depth, key_ref, weight_ref, *refs):
    pieces, (wg_hbm, wu_hbm, wd_hbm) = refs[:n_pieces], refs[n_pieces : n_pieces + 3]
    outs = refs[n_pieces + 3 : n_pieces + 7]
    x_all, pick_all, scale_all, out_all, wgu, wd, act, sems = refs[n_pieces + 7 :]
    experts, tokens = key_ref.shape
    slots = pick_all.shape[0] // experts
    _, _, halves, hidden, model = wgu.shape
    part = tokens // n_pieces

    def copies(e):
        slot = lax.rem(e, depth)
        rows = pl.ds(e * halves, halves)
        return (
            pltpu.make_async_copy(wg_hbm.at[rows], wgu.at[slot, 0], sems.at[0, slot]),
            pltpu.make_async_copy(wu_hbm.at[rows], wgu.at[slot, 1], sems.at[1, slot]),
            pltpu.make_async_copy(wd_hbm.at[rows], wd.at[slot], sems.at[2, slot]),
        )

    def start(e):
        for copy in copies(e):
            copy.start()

    def wait(e):
        for copy in copies(e):
            copy.wait()

    def gate_up(e):
        x = out_all[pl.ds(pl.multiple_of(e * slots, slots), slots), :]
        weight = wgu[lax.rem(e, depth)].reshape(2 * halves * hidden, model)
        both = dot_rows(weight, x)
        gate, up = both[: halves * hidden], both[halves * hidden :]
        return (gate * jax.nn.sigmoid(gate) * up).astype(BF)

    def down(e):
        here = pl.ds(pl.multiple_of(e * slots, slots), slots)
        weight = wd[lax.rem(e, depth)].reshape(halves * hidden, model)
        out = lax.dot_general(
            act[lax.rem(e, 2)], weight, (((0,), (0,)), ((), ())), preferred_element_type=F32
        )
        return here, (out * scale_all[here, :]).astype(BF)

    for e in range(min(depth - 1, experts)):
        start(e)
    for i, piece in enumerate(pieces):
        x_all[i * part : (i + 1) * part, :] = piece[...]
    slot = lax.broadcasted_iota(jnp.int32, (slots, tokens), 0)
    for e in range(experts):
        chosen = slot == key_ref[e : e + 1, :]
        here = slice(e * slots, (e + 1) * slots)
        pick_all[here, :] = jnp.where(chosen, 1.0, 0.0).astype(BF)
        scale_all[here, :] = jnp.sum(
            jnp.where(chosen, weight_ref[e : e + 1, :], 0.0), axis=1, keepdims=True
        )
    out_all[...] = jnp.dot(pick_all[...], x_all[...], preferred_element_type=F32).astype(BF)
    wait(0)
    act[0] = gate_up(0)

    @pl.loop(0, experts - 1)
    def _(e):
        @pl.when(e + depth - 1 < experts)
        def _():
            start(e + depth - 1)

        wait(e + 1)
        following = gate_up(e + 1)
        here, out = down(e)
        act[lax.rem(e + 1, 2)] = following
        out_all[here, :] = out

    here, out = down(experts - 1)
    out_all[here, :] = out
    quarter = tokens // 4
    for i, o_ref in enumerate(outs):
        o_ref[...] = lax.dot_general(
            pick_all[:, i * quarter : (i + 1) * quarter],
            out_all[...],
            (((0,), (0,)), ((), ())),
            preferred_element_type=F32,
        ).astype(BF)


def run_experts(keys, weights, pieces, w_gate, w_up, w_down, slots):
    experts, tokens = keys.shape
    rows, hidden, model = w_down.shape
    halves = rows // experts
    depth = min(4, experts)
    vmem = pl.BlockSpec(memory_space=pltpu.VMEM)
    hbm = pl.BlockSpec(memory_space=pltpu.HBM)

    def stays(x):
        return pltpu.with_memory_space_constraint(x, pltpu.HBM)

    out = jax.ShapeDtypeStruct((tokens // 4, model), BF)
    return pl.pallas_call(
        functools.partial(expert_kernel, len(pieces), depth),
        out_shape=(out,) * 4,
        in_specs=[vmem] * (2 + len(pieces)) + [hbm] * 3,
        out_specs=(vmem,) * 4,
        scratch_shapes=[
            pltpu.VMEM((tokens, model), BF),
            pltpu.VMEM((experts * slots, tokens), BF),
            pltpu.VMEM((experts * slots, 1), F32),
            pltpu.VMEM((experts * slots, model), BF),
            pltpu.VMEM((depth, 2, halves, hidden, model), BF),
            pltpu.VMEM((depth, halves, hidden, model), BF),
            pltpu.VMEM((2, halves * hidden, slots), BF),
            pltpu.SemaphoreType.DMA((3, depth)),
        ],
        compiler_params=pltpu.CompilerParams(vmem_limit_bytes=44 * MIB),
        cost_estimate=pl.CostEstimate(
            flops=2 * experts * slots * model * (3 * halves * hidden + 2 * tokens),
            bytes_accessed=6 * rows * model * hidden + 4 * tokens * model,
            transcendentals=experts * slots * halves * hidden,
        ),
        name="experts",
    )(
        keys,
        weights,
        *pieces,
        stays(jnp.swapaxes(w_gate, 1, 2)),
        stays(jnp.swapaxes(w_up, 1, 2)),
        stays(w_down),
    )


def experts_plain(keys, weights, x, w_gate, w_up, w_down, slots):
    n_exp = keys.shape[0]
    rows, model, hidden = w_gate.shape
    pick = (keys[:, None, :] == jnp.arange(slots, dtype=jnp.int32)[None, :, None]).astype(BF)
    scale = jnp.sum(pick.astype(F32) * weights[:, None, :], axis=2)
    chosen = jnp.einsum("est,td->esd", pick, x, preferred_element_type=F32).astype(BF)
    chosen = jnp.repeat(chosen, rows // n_exp, axis=0)
    gate = jnp.einsum("rsd,rdf->rsf", chosen, w_gate, preferred_element_type=F32)
    up = jnp.einsum("rsd,rdf->rsf", chosen, w_up, preferred_element_type=F32)
    act = (jax.nn.silu(gate) * up).astype(BF)
    out = jnp.einsum("rsf,rfd->rsd", act, w_down, preferred_element_type=F32)
    out = jnp.sum(out.reshape(n_exp, rows // n_exp, slots, model), axis=1)
    out = (out * scale[:, :, None]).astype(BF)
    return jnp.einsum("est,esd->td", pick, out, preferred_element_type=F32).astype(BF)


def routing_tables(routing, n_ctx, n_exp, n_tp, first, experts_here, cap):
    part = routing.shape[-1]
    routing = routing.transpose(2, 3, 4, 1, 0, 5).astype(F32)
    ids = routing[0].astype(jnp.int32)
    probs = routing[1] + routing[2]
    local = first + jnp.arange(experts_here, dtype=jnp.int32)
    hit = ids[None] == local.reshape(-1, 1, 1, 1, 1, 1)
    named = jnp.any(hit, axis=1)
    weight = jnp.sum(jnp.where(hit, probs[None], 0.0), axis=1)
    block = n_tp * part
    flat = named.transpose(0, 2, 3, 1, 4).reshape(-1, block)
    before = jnp.arange(block)[:, None] < jnp.arange(block)[None, :]
    rank = jnp.dot(flat.astype(BF), before.astype(BF), preferred_element_type=F32)
    rank = rank.astype(jnp.int32).reshape(experts_here, n_exp, n_ctx, n_tp, part)
    rank = rank.transpose(0, 3, 1, 2, 4)
    blocks = jnp.arange(n_ctx * n_exp, dtype=jnp.int32).reshape(1, 1, n_exp, n_ctx, 1)
    cells = jnp.where(named, blocks * cap + rank, -1).reshape(experts_here, -1)
    return cells, weight.reshape(experts_here, -1)


def sums_back(mine, mine_across, other, other_across, part):
    def add(a, *others):
        total = a.astype(F32)
        for b in others:
            total = total + b.astype(F32)
        return total.astype(BF)

    across = add(mine_across, flip(other_across, "tp", 1))
    here = add(mine, flip(other, "tp", 1))
    across = [across[z * part : (z + 1) * part] for z in range(4)]
    here = [here[z * part : (z + 1) * part] for z in range(4)]
    far_across = add(across[2], flip(across[3], "ctx", 1))
    own = flip(across[0], "exp", 1)
    near = flip(across[1], "exp", 1)
    last = flip(here[3], "ctx", 1)
    far_across, here[1] = lax.optimization_barrier((far_across, here[1]))
    far = flip(far_across, "exp", 1)
    near = add(here[1], near)
    near, here[2] = lax.optimization_barrier((near, here[2]))
    near = flip(near, "ctx", 1)
    far = flip(add(here[2], last, far), "ctx", 2)
    return here[0].astype(F32) + own.astype(F32) + near.astype(F32) + far.astype(F32)


def on_device(
    queries, keys, values, out_weight, resid, expert_ids, router_probs, w_gate, w_up, w_down
):
    n_ctx, n_exp, n_tp = (lax.axis_size(a) for a in ("ctx", "exp", "tp"))
    ctx, exp, tp = (lax.axis_index(a) for a in ("ctx", "exp", "tp"))
    place = jnp.stack([ctx, exp, tp]).astype(jnp.int32)
    part, model = resid.shape
    block = expert_ids.shape[0]
    heads_here = queries.shape[1] // HEAD_DIMENSION
    rows_here = w_gate.shape[0]
    experts_here = max(1, rows_here // 2)
    first = (ctx * n_exp + exp) * rows_here // 2
    cap = min(8, block)
    slots = n_ctx * n_exp * cap
    small = (n_ctx, n_exp, n_tp) == (4, 2, 2) and part % 16 == 0 and rows_here % 2 == 0

    shared = (exp * n_tp + tp) * heads_here // (QUERY_HEADS // KEY_VALUE_HEADS)
    key_head = lax.dynamic_slice_in_dim(keys, shared * HEAD_DIMENSION, HEAD_DIMENSION, 1)
    value_head = lax.dynamic_slice_in_dim(values, shared * HEAD_DIMENSION, HEAD_DIMENSION, 1)
    kv = jnp.concatenate([key_head, value_head], axis=1)
    kv_pieces = [kv] + [from_earlier(kv, "ctx", z) for z in range(1, n_ctx)]

    gate_weights = router_probs / jnp.sum(router_probs, axis=1, keepdims=True)
    high = lax.reduce_precision(gate_weights, 8, 7)
    routing = jnp.stack([expert_ids.astype(F32).T, high.T, (gate_weights - high).T]).astype(BF)
    if small:
        routing = routing.reshape(3 * TOPK, block)
        for axis, bit in (("exp", 1), ("ctx", 1), ("ctx", 2)):
            routing = jnp.concatenate([routing, flip(routing, axis, bit)])
        routing = routing.reshape(n_ctx, n_exp, 3, TOPK, n_tp, part)
        routing = jnp.where(tp == 0, routing, routing[:, :, :, :, ::-1])
    else:
        routing = lax.all_gather(routing, ("ctx", "exp"), axis=0)
        routing = routing.reshape(n_ctx, n_exp, 3, TOPK, n_tp, part)
    cells, weight = routing_tables(routing, n_ctx, n_exp, n_tp, first, experts_here, cap)

    projected = attend_project(
        queries, kv_pieces, out_weight, place, n_exp, n_tp, small
    )
    hidden = resid.astype(F32)
    if small:
        mine, other = projected[: n_exp * part], projected[n_exp * part :]
        summed = (mine.astype(F32) + flip(other, "tp", 1).astype(F32)).astype(BF)
        hidden = hidden + summed[:part].astype(F32)
        hidden = hidden + flip(summed[part:], "exp", 1).astype(F32)
    else:
        hidden = hidden + lax.psum_scatter(
            projected, ("exp", "tp"), scatter_dimension=0, tiled=True
        ).astype(F32)
    mean_square = jnp.mean(hidden * hidden, axis=1, keepdims=True)
    normed = (hidden * lax.rsqrt(mean_square + 1e-06)).astype(BF)

    if small:
        far = flip(normed, "ctx", 2)
        across = flip(normed, "exp", 1)
        near = flip(normed, "ctx", 1)
        far_across = flip(far, "exp", 1)
        near_across = flip(near, "exp", 1)
        last = flip(far, "ctx", 1)
        last_across = flip(far_across, "ctx", 1)
        chip = [normed, near, far, last, across, near_across, far_across, last_across]
        pieces = chip + [flip(piece, "tp", 1) for piece in chip]
        sums = run_experts(cells, weight, pieces, w_gate, w_up, w_down, slots)
        return (hidden + sums_back(*sums, part)).astype(BF)
    x = lax.all_gather(normed, ("ctx", "exp", "tp"), axis=0, tiled=True)

    def by_place(table):
        table = table.reshape(experts_here, n_tp, n_exp, n_ctx, part)
        return table.transpose(0, 3, 2, 1, 4).reshape(experts_here, x.shape[0])

    partial = experts_plain(by_place(cells), by_place(weight), x, w_gate, w_up, w_down, slots)
    routed = lax.psum_scatter(partial, ("ctx", "exp", "tp"), scatter_dimension=0, tiled=True)
    return (hidden + routed.astype(F32)).astype(BF)


def solution(mesh):
    in_specs = (
        P(("groups", "ctx"), ("exp", "tp")),
        P(("groups", "ctx"), None),
        P(("groups", "ctx"), None),
        P(("exp", "tp"), None),
        P(("groups", "ctx", "exp", "tp"), None),
        P(("groups", "ctx", "exp"), None),
        P(("groups", "ctx", "exp"), None),
        P(("ctx", "exp"), None, "tp"),
        P(("ctx", "exp"), None, "tp"),
        P(("ctx", "exp"), "tp", None),
    )
    out_specs = P(("groups", "ctx", "exp", "tp"), None)
    return jax.shard_map(
        on_device, mesh=mesh, in_specs=in_specs, out_specs=out_specs, check_vma=False
    )
```

time: 107 us -> 92.9 us (0.87)
  waiting for transfers between devices: 42.9 us -> 31 us
  starting transfers between devices: 27.7 us -> 31.3 us
  local copies, waits for them, and re-layouts: 5.15 us -> 2.06 us
  Pallas kernels: 24.4 us -> 21.5 us
    ppermute x29 -> x32, waiting for transfers between devices: 42.9 us -> 31 us  [the longest x29 31 us: flip(): lax.ppermute(x, axis, [(i, i ^ bit) for i in range(lax.axis_size(axis))])]
    pallas_call x1, Pallas kernels: 20.5 us -> 16.1 us  [run_experts(): pl.pallas_call(functools.partial(expert_kernel, len(pieces), depth), out_...]
    ppermute x29 -> x32, starting transfers between devices: 27.7 us -> 31.3 us  [the longest x29 20.6 us: flip(): lax.ppermute(x, axis, [(i, i ^ bit) for i in range(lax.axis_size(axis))])]
    unnamed x6 -> x2, local copies, waits for them, and re-layouts: 3.14 us -> 0.01 us
    pallas_call x1, Pallas kernels: 3.85 us -> 5.44 us  [attend_project(): pl.pallas_call(functools.partial(attention_kernel, n_ctx, n_exp, n_tp, ro...]
    concatenate x4, other arithmetic: 1.55 us -> 0.04 us  [the longest x3 0.03 us: on_device(): routing = jnp.concatenate([routing, flip(routing, axis, bit)])]
  transfers between devices with their start and end apart: 29 -> 32, of which waited for: 16 -> 15; matrix products, arithmetic and copies ran while one was open for 3% -> 5% of each run, Pallas kernels for 0% -> 6%
where the time goes in v3:
time: 92.9 us; the launch traced here: 92.5 us
  starting transfers between devices  31.3 us (34%)
  waiting for transfers between devices  31 us (33%)
  Pallas kernels  21.5 us (23%)
  other arithmetic  6.26 us (7%)
  local copies, waits for them, and re-layouts  2.06 us (2%)
    ppermute x29, waiting for transfers between devices, flip(): lax.ppermute(x, axis, [(i, i ^ bit) for i in range(lax.axis_size(axis))])  31 us
    ppermute x29, starting transfers between devices, flip(): lax.ppermute(x, axis, [(i, i ^ bit) for i in range(lax.axis_size(axis))])  20.6 us
    pallas_call x1, Pallas kernels, run_experts(): pl.pallas_call(functools.partial(expert_kernel, len(pieces), depth), out_...  16.1 us
    ppermute x3, starting transfers between devices, from_earlier(): return lax.ppermute(x, axis, [(i, i + steps) for i in range(size - steps)])  10.7 us
    pallas_call x1, Pallas kernels, attend_project(): pl.pallas_call(functools.partial(attention_kernel, n_ctx, n_exp, n_tp, ro...  5.44 us
  transfers between devices with their start and end apart: 32, of which 15 were waited for; matrix products, arithmetic and copies ran while one was open for 5% of the time, Pallas kernels for 6%

profile of v3, /device:TPU:0, one launch (start us, length us, event | category | flops | bytes accessed | tf_op | source)
XLA Modules:
  0.0 92.5 jit_solution(12288188816670888794)
XLA Ops:
  0.0 0.8 constant_dynamic-slice_fusion
  0.8 7.0 %collective-permute-start.2 = (bf16[128,256]{1,0:T(8,128)(2,1)S(1)}, bf16[128,256]{1,0:T(8,128)(2,1)S(1)}, u32[]{:S(2)}, u32[]{:S(2)}) collective-permute-start(bf16[128,256]{1,0:T(8,128)(2,1)S(1)} %pad_maximum_fusion.refs_0_), channel_id=1, source_target_pairs={{0,12},{1,13},{2,14},{3,15},{16,28},{17,29},{18,30},{19,31}} | collective-permute-start | bytes 196616 | tf_op jit(solution)/shard_map/ppermute | solution.py:27
  7.8 1.3 %collective-permute-start.1 = (bf16[128,256]{1,0:T(8,128)(2,1)S(1)}, bf16[128,256]{1,0:T(8,128)(2,1)S(1)}, u32[]{:S(2)}, u32[]{:S(2)}) collective-permute-start(bf16[128,256]{1,0:T(8,128)(2,1)S(1)} %pad_maximum_fusion.refs_0_), channel_id=1, source_target_pairs={{0,8},{4,12},{1,9},{5,13},{2,10},{6,14},{3,11},{7,15},{16,24},{20,... | collective-permute-start | bytes 196616 | tf_op jit(solution)/shard_map/ppermute | solution.py:27
  9.1 2.5 %collective-permute-start = (bf16[128,256]{1,0:T(8,128)(2,1)S(1)}, bf16[128,256]{1,0:T(8,128)(2,1)S(1)}, u32[]{:S(2)}, u32[]{:S(2)}) collective-permute-start(bf16[128,256]{1,0:T(8,128)(2,1)S(1)} %pad_maximum_fusion.refs_0_), channel_id=1, source_target_pairs={{0,4},{4,8},{8,12},{1,5},{5,9},{9,13},{2,6},{6,10},{10,14},{3,7},{... | collective-permute-start | bytes 196616 | tf_op jit(solution)/shard_map/ppermute | solution.py:27
  11.5 0.7 fusion.4
  12.2 0.7 reduce_sum.27
  12.9 0.7 fusion.6
  13.6 1.6 %collective-permute-start.5 = (bf16[24,64]{1,0:T(8,128)(2,1)S(1)}, bf16[24,64]{1,0:T(8,128)(2,1)S(1)}, u32[]{:S(2)}, u32[]{:S(2)}) collective-permute-start(bf16[24,64]{1,0:T(8,128)(2,1)S(1)} %maximum_bitcast_fusion), channel_id=1, source_target_pairs={{0,2},{2,0},{1,3},{3,1},{4,6},{6,4},{5,7},{7,5},{8,10},{10,8},{9,1... | collective-permute-start | bytes 9224 | tf_op jit(solution)/shard_map/ppermute | solution.py:22
  15.3 5.4 %attend_project.1 = bf16[128,2048]{1,0:T(8,128)(2,1)S(1)} custom-call(s32[3]{0:T(128)S(1)} %pad_add_fusion.place, bf16[128,256]{1,0:T(8,128)(2,1)S(1)} %pad_maximum_fusion.refs_0_, bf16[128,256]{1,0:T(8,128)(2,1)S(1)} %collective-permute-done.refs_1_, bf16[128,256]{1,0:T(8,128)(2,1)S(1)} %collective-permute-done.1.refs_2_, ...), custom_call_target="tpu_custom_call" | custom-call | flops 805306368 | bytes 4980736 | tf_op jit(solution)/shard_map/attend_project/pallas_call | solution.py:82
  20.9 0.6 collective-permute-start.6
  21.4 3.2 %collective-permute-done.6 = bf16[48,64]{1,0:T(8,128)(2,1)S(1)} collective-permute-done((bf16[48,64]{1,0:T(8,128)(2,1)S(1)}, bf16[48,64]{1,0:T(8,128)(2,1)S(1)}, u32[]{:S(2)}, u32[]{:S(2)}) %collective-permute-start.6) | collective-permute-done | bytes 6176 | tf_op jit(solution)/shard_map/ppermute | solution.py:22
  24.6 1.5 %collective-permute-start.7 = (bf16[96,64]{1,0:T(8,128)(2,1)S(1)}, bf16[96,64]{1,0:T(8,128)(2,1)S(1)}, u32[]{:S(2)}, u32[]{:S(2)}) collective-permute-start(bf16[96,64]{1,0:T(8,128)(2,1)S(1)} %pad_maximum_fusion.2), channel_id=1, source_target_pairs={{0,8},{4,12},{8,0},{12,4},{1,9},{5,13},{9,1},{13,5},{2,10},{6,14},... | collective-permute-start | bytes 36872 | tf_op jit(solution)/shard_map/ppermute | solution.py:22
  26.2 1.6 %collective-permute-start.4 = (bf16[32,2048]{1,0:T(8,128)(2,1)S(1)}, bf16[32,2048]{1,0:T(8,128)(2,1)S(1)}, u32[]{:S(2)}, u32[]{:S(2)}) collective-permute-start(bf16[32,2048]{1,0:T(8,128)(2,1)S(1)} %slice.63), channel_id=1, source_target_pairs={{0,2},{2,0},{1,3},{3,1},{4,6},{6,4},{5,7},{7,5},{8,10},{10,8},{9,1... | collective-permute-start | bytes 393224 | tf_op jit(solution)/shard_map/ppermute | solution.py:22
  27.7 1.9 %collective-permute-done.7 = bf16[96,64]{1,0:T(8,128)(2,1)S(1)} collective-permute-done((bf16[96,64]{1,0:T(8,128)(2,1)S(1)}, bf16[96,64]{1,0:T(8,128)(2,1)S(1)}, u32[]{:S(2)}, u32[]{:S(2)}) %collective-permute-start.7) | collective-permute-done | bytes 12320 | tf_op jit(solution)/shard_map/ppermute | solution.py:22
  29.7 0.6 rev.3
  30.4 0.8 collective-permute-done.4
  31.2 1.1 %multiply_reduce_fusion = f32[32]{0:T(128)S(1)} fusion(bf16[32,2048]{1,0:T(8,128)(2,1)S(1)} %collective-permute-done.4, bf16[64,2048]{1,0:T(8,128)(2,1)S(1)} %add_convert_fusion.2, bf16[32,2048]{1,0:T(8,128)(2,1)} %param.14), kind=kLoop, calls=%fused_computation.12 | loop fusion | flops 458720 | bytes 393344 | tf_op jit(solution)/shard_map/reduce_sum | solution.py:346
  32.3 1.0 %multiply_convert_fusion.refs_0_ = bf16[32,2048]{1,0:T(8,128)(2,1)S(1)} fusion(f32[32]{0:T(128)S(1)} %add_rsqrt_fusion, bf16[32,2048]{1,0:T(8,128)(2,1)S(1)} %collective-permute-done.4, bf16[64,2048]{1,0:T(8,128)(2,1)S(1)} %add_convert_fusion.2, bf16[32,2048]{1,0:T(8,128)(2,1)} %param.14), kind=kLoop, calls=%fused_computation.11 | loop fusion | flops 458752 | bytes 524416 | tf_op jit(solution)/shard_map/convert_element_type | solution.py:347
  33.3 1.6 %collective-permute-start.9 = (bf16[32,2048]{1,0:T(8,128)(2,1)S(1)}, bf16[32,2048]{1,0:T(8,128)(2,1)S(1)}, u32[]{:S(2)}, u32[]{:S(2)}) collective-permute-start(bf16[32,2048]{1,0:T(8,128)(2,1)S(1)} %multiply_convert_fusion.refs_0_), channel_id=1, source_target_pairs={{0,8},{4,12},{8,0},{12,4},{1,9},{5,13},{9,1},{13,5},{2,10},{6,14},... | collective-permute-start | bytes 393224 | tf_op jit(solution)/shard_map/ppermute | solution.py:22
  35.1 0.6 collective-permute-start.11
  35.7 1.4 %collective-permute-start.8 = (bf16[32,2048]{1,0:T(8,128)(2,1)S(1)}, bf16[32,2048]{1,0:T(8,128)(2,1)S(1)}, u32[]{:S(2)}, u32[]{:S(2)}) collective-permute-start(bf16[32,2048]{1,0:T(8,128)(2,1)S(1)} %multiply_convert_fusion.refs_0_), channel_id=1, source_target_pairs={{0,4},{4,0},{8,12},{12,8},{1,5},{5,1},{9,13},{13,9},{2,6},{6,2},{1... | collective-permute-start | bytes 393224 | tf_op jit(solution)/shard_map/ppermute | solution.py:22
  37.1 3.6 %collective-permute-done.9.refs_2_ = bf16[32,2048]{1,0:T(8,128)(2,1)S(1)} collective-permute-done((bf16[32,2048]{1,0:T(8,128)(2,1)S(1)}, bf16[32,2048]{1,0:T(8,128)(2,1)S(1)}, u32[]{:S(2)}, u32[]{:S(2)}) %collective-permute-start.9) | collective-permute-done | bytes 131104 | tf_op jit(solution)/shard_map/ppermute | solution.py:22
  40.7 1.4 %collective-permute-start.13 = (bf16[32,2048]{1,0:T(8,128)(2,1)S(1)}, bf16[32,2048]{1,0:T(8,128)(2,1)S(1)}, u32[]{:S(2)}, u32[]{:S(2)}) collective-permute-start(bf16[32,2048]{1,0:T(8,128)(2,1)S(1)} %collective-permute-done.9.refs_2_), channel_id=1, source_target_pairs={{0,2},{2,0},{1,3},{3,1},{4,6},{6,4},{5,7},{7,5},{8,10},{10,8},{9,1... | collective-permute-start | bytes 393224 | tf_op jit(solution)/shard_map/ppermute | solution.py:22
  42.3 0.3 fusion
  42.7 0.5 collective-permute-start.19
  43.2 0.9 collective-permute-start.12
  44.1 1.6 %collective-permute-done.13.refs_6_ = bf16[32,2048]{1,0:T(8,128)(2,1)S(1)} collective-permute-done((bf16[32,2048]{1,0:T(8,128)(2,1)S(1)}, bf16[32,2048]{1,0:T(8,128)(2,1)S(1)}, u32[]{:S(2)}, u32[]{:S(2)}) %collective-permute-start.13) | collective-permute-done | bytes 131104 | tf_op jit(solution)/shard_map/ppermute | solution.py:22
  46.5 0.5 collective-permute-start.21
  47.0 2.0 %collective-permute-done.10.refs_3_ = bf16[32,2048]{1,0:T(8,128)(2,1)S(1)} collective-permute-done((bf16[32,2048]{1,0:T(8,128)(2,1)S(1)}, bf16[32,2048]{1,0:T(8,128)(2,1)S(1)}, u32[]{:S(2)}, u32[]{:S(2)}) %collective-permute-start.10) | collective-permute-done | bytes 131104 | tf_op jit(solution)/shard_map/ppermute | solution.py:22
  49.0 0.5 collective-permute-start.20
  49.5 1.8 %collective-permute-done.14.refs_7_ = bf16[32,2048]{1,0:T(8,128)(2,1)S(1)} collective-permute-done((bf16[32,2048]{1,0:T(8,128)(2,1)S(1)}, bf16[32,2048]{1,0:T(8,128)(2,1)S(1)}, u32[]{:S(2)}, u32[]{:S(2)}) %collective-permute-start.14) | collective-permute-done | bytes 131104 | tf_op jit(solution)/shard_map/ppermute | solution.py:22
  51.6 1.1 %collective-permute-done.22.refs_15_ = bf16[32,2048]{1,0:T(8,128)(2,1)S(1)} collective-permute-done((bf16[32,2048]{1,0:T(8,128)(2,1)S(1)}, bf16[32,2048]{1,0:T(8,128)(2,1)S(1)}, u32[]{:S(2)}, u32[]{:S(2)}) %collective-permute-start.22) | collective-permute-done | bytes 131104 | tf_op jit(solution)/shard_map/ppermute | solution.py:22
  52.7 16.1 %experts.1 = (bf16[128,2048]{1,0:T(8,128)(2,1)S(1)}, bf16[128,2048]{1,0:T(8,128)(2,1)S(1)}, bf16[128,2048]{1,0:T(8,128)(2,1)S(1)}, bf16[128,2048]{1,0:T(8,128)(2,1)S(1)}) custom-call(s32[8,512]{1,0:T(8,128)S(1)} %reshape.57.key_ref, f32[8,512]{1,0:T(8,128)S(1)} %reshape.58.weight_ref, bf16[32,2048]{1,0:T(8,128)(2,1)S(1)} %multiply_convert_fusion.refs_0_, ...), custom_call_target="tpu_custom_call" | custom-call | flops 4563402752 | bytes 41943040 | tf_op jit(solution)/shard_map/experts/pallas_call | solution.py:205
  69.0 0.4 collective-permute-start.23
  69.3 1.4 %collective-permute-done.24 = bf16[128,2048]{1,0:T(8,128)(2,1)S(1)} collective-permute-done((bf16[128,2048]{1,0:T(8,128)(2,1)S(1)}, bf16[128,2048]{1,0:T(8,128)(2,1)S(1)}, u32[]{:S(2)}, u32[]{:S(2)}) %collective-permute-start.24) | collective-permute-done | bytes 524320 | tf_op jit(solution)/shard_map/ppermute | solution.py:22
  70.9 0.3 collective-permute-start.26
  71.7 1.6 %collective-permute-start.29 = (bf16[32,2048]{1,0:T(8,128)(2,1)S(1)}, bf16[32,2048]{1,0:T(8,128)(2,1)S(1)}, u32[]{:S(2)}, u32[]{:S(2)}) collective-permute-start(bf16[32,2048]{1,0:T(8,128)(2,1)S(1)} %get-tuple-element.25), channel_id=1, source_target_pairs={{0,4},{4,0},{8,12},{12,8},{1,5},{5,1},{9,13},{13,9},{2,6},{6,2},{1... | collective-permute-start | bytes 393224 | tf_op jit(solution)/shard_map/ppermute | solution.py:22
  73.2 1.5 %collective-permute-start.25 = (bf16[32,2048]{1,0:T(8,128)(2,1)S(1)}, bf16[32,2048]{1,0:T(8,128)(2,1)S(1)}, u32[]{:S(2)}, u32[]{:S(2)}) collective-permute-start(bf16[32,2048]{1,0:T(8,128)(2,1)S(1)} %get-tuple-element.21), channel_id=1, source_target_pairs={{0,2},{2,0},{1,3},{3,1},{4,6},{6,4},{5,7},{7,5},{8,10},{10,8},{9,1... | collective-permute-start | bytes 393224 | tf_op jit(solution)/shard_map/ppermute | solution.py:22
  74.8 0.5 collective-permute-start.27
  75.3 2.0 %collective-permute-done.26 = bf16[32,2048]{1,0:T(8,128)(2,1)S(1)} collective-permute-done((bf16[32,2048]{1,0:T(8,128)(2,1)S(1)}, bf16[32,2048]{1,0:T(8,128)(2,1)S(1)}, u32[]{:S(2)}, u32[]{:S(2)}) %collective-permute-start.26) | collective-permute-done | bytes 131104 | tf_op jit(solution)/shard_map/ppermute | solution.py:22
  77.4 1.6 %collective-permute-start.30 = (bf16[32,2048]{1,0:T(8,128)(2,1)S(1)}, bf16[32,2048]{1,0:T(8,128)(2,1)S(1)}, u32[]{:S(2)}, u32[]{:S(2)}) collective-permute-start(bf16[32,2048]{1,0:T(8,128)(2,1)S(1)} %add_convert_fusion.6), channel_id=1, source_target_pairs={{0,2},{2,0},{1,3},{3,1},{4,6},{6,4},{5,7},{7,5},{8,10},{10,8},{9,1... | collective-permute-start | bytes 393224 | tf_op jit(solution)/shard_map/ppermute | solution.py:22
  78.9 3.5 %collective-permute-done.27 = bf16[32,2048]{1,0:T(8,128)(2,1)S(1)} collective-permute-done((bf16[32,2048]{1,0:T(8,128)(2,1)S(1)}, bf16[32,2048]{1,0:T(8,128)(2,1)S(1)}, u32[]{:S(2)}, u32[]{:S(2)}) %collective-permute-start.27) | collective-permute-done | bytes 131104 | tf_op jit(solution)/shard_map/ppermute | solution.py:22
  82.5 0.6 collective-permute-start.28
  83.0 0.8 collective-permute-done.30
  83.9 0.9 collective-permute-start.31
  84.8 4.1 %collective-permute-done.28 = bf16[32,2048]{1,0:T(8,128)(2,1)S(1)} collective-permute-done((bf16[32,2048]{1,0:T(8,128)(2,1)S(1)}, bf16[32,2048]{1,0:T(8,128)(2,1)S(1)}, u32[]{:S(2)}, u32[]{:S(2)}) %collective-permute-start.28) | collective-permute-done | bytes 131104 | tf_op jit(solution)/shard_map/ppermute | solution.py:22
  88.9 2.9 %collective-permute-done.31 = bf16[32,2048]{1,0:T(8,128)(2,1)S(1)} collective-permute-done((bf16[32,2048]{1,0:T(8,128)(2,1)S(1)}, bf16[32,2048]{1,0:T(8,128)(2,1)S(1)}, u32[]{:S(2)}, u32[]{:S(2)}) %collective-permute-start.31) | collective-permute-done | bytes 131104 | tf_op jit(solution)/shard_map/ppermute | solution.py:22
  91.8 0.8 add_convert_fusion.3
  (61 shorter events, 2.7 us)
Async XLA Ops:
  0.8 14.5 %collective-permute-start.2 = (bf16[128,256]{1,0:T(8,128)(2,1)S(1)}, bf16[128,256]{1,0:T(8,128)(2,1)S(1)}, u32[]{:S(2)}, u32[]{:S(2)}) collective-permute-start(bf16[128,256]{1,0:T(8,128)(2,1)S(1)} %pad_maximum_fusion.refs_0_), channel_id=1, source_target_pairs={{0,12},{1,13},{2,14},{3,15},{16,28},{17,29},{18,30},{19,31}} | collective-permute-start | bytes 196616 | tf_op jit(solution)/shard_map/ppermute | solution.py:27
  7.8 7.5 %collective-permute-start.1 = (bf16[128,256]{1,0:T(8,128)(2,1)S(1)}, bf16[128,256]{1,0:T(8,128)(2,1)S(1)}, u32[]{:S(2)}, u32[]{:S(2)}) collective-permute-start(bf16[128,256]{1,0:T(8,128)(2,1)S(1)} %pad_maximum_fusion.refs_0_), channel_id=1, source_target_pairs={{0,8},{4,12},{1,9},{5,13},{2,10},{6,14},{3,11},{7,15},{16,24},{20,... | collective-permute-start | bytes 196616 | tf_op jit(solution)/shard_map/ppermute | solution.py:27
  9.1 6.2 %collective-permute-start = (bf16[128,256]{1,0:T(8,128)(2,1)S(1)}, bf16[128,256]{1,0:T(8,128)(2,1)S(1)}, u32[]{:S(2)}, u32[]{:S(2)}) collective-permute-start(bf16[128,256]{1,0:T(8,128)(2,1)S(1)} %pad_maximum_fusion.refs_0_), channel_id=1, source_target_pairs={{0,4},{4,8},{8,12},{1,5},{5,9},{9,13},{2,6},{6,10},{10,14},{3,7},{... | collective-permute-start | bytes 196616 | tf_op jit(solution)/shard_map/ppermute | solution.py:27
  13.6 7.2 %collective-permute-start.5 = (bf16[24,64]{1,0:T(8,128)(2,1)S(1)}, bf16[24,64]{1,0:T(8,128)(2,1)S(1)}, u32[]{:S(2)}, u32[]{:S(2)}) collective-permute-start(bf16[24,64]{1,0:T(8,128)(2,1)S(1)} %maximum_bitcast_fusion), channel_id=1, source_target_pairs={{0,2},{2,0},{1,3},{3,1},{4,6},{6,4},{5,7},{7,5},{8,10},{10,8},{9,1... | collective-permute-start | bytes 9224 | tf_op jit(solution)/shard_map/ppermute | solution.py:22
  20.8 5.3 %collective-permute-start.3 = (bf16[64,2048]{1,0:T(8,128)(2,1)S(1)}, bf16[64,2048]{1,0:T(8,128)(2,1)S(1)}, u32[]{:S(2)}, u32[]{:S(2)}) collective-permute-start(bf16[64,2048]{1,0:T(8,128)(2,1)S(1)} %slice.61), channel_id=1, source_target_pairs={{0,1},{1,0},{2,3},{3,2},{4,5},{5,4},{6,7},{7,6},{8,9},{9,8},{10,11... | collective-permute-start | bytes 786440 | tf_op jit(solution)/shard_map/ppermute | solution.py:22
  20.9 3.8 %collective-permute-start.6 = (bf16[48,64]{1,0:T(8,128)(2,1)S(1)}, bf16[48,64]{1,0:T(8,128)(2,1)S(1)}, u32[]{:S(2)}, u32[]{:S(2)}) collective-permute-start(bf16[48,64]{1,0:T(8,128)(2,1)S(1)} %pad_maximum_fusion.3), channel_id=1, source_target_pairs={{0,4},{4,0},{8,12},{12,8},{1,5},{5,1},{9,13},{13,9},{2,6},{6,2},{1... | collective-permute-start | bytes 18440 | tf_op jit(solution)/shard_map/ppermute | solution.py:22
  24.6 5.0 %collective-permute-start.7 = (bf16[96,64]{1,0:T(8,128)(2,1)S(1)}, bf16[96,64]{1,0:T(8,128)(2,1)S(1)}, u32[]{:S(2)}, u32[]{:S(2)}) collective-permute-start(bf16[96,64]{1,0:T(8,128)(2,1)S(1)} %pad_maximum_fusion.2), channel_id=1, source_target_pairs={{0,8},{4,12},{8,0},{12,4},{1,9},{5,13},{9,1},{13,5},{2,10},{6,14},... | collective-permute-start | bytes 36872 | tf_op jit(solution)/shard_map/ppermute | solution.py:22
  26.2 5.0 %collective-permute-start.4 = (bf16[32,2048]{1,0:T(8,128)(2,1)S(1)}, bf16[32,2048]{1,0:T(8,128)(2,1)S(1)}, u32[]{:S(2)}, u32[]{:S(2)}) collective-permute-start(bf16[32,2048]{1,0:T(8,128)(2,1)S(1)} %slice.63), channel_id=1, source_target_pairs={{0,2},{2,0},{1,3},{3,1},{4,6},{6,4},{5,7},{7,5},{8,10},{10,8},{9,1... | collective-permute-start | bytes 393224 | tf_op jit(solution)/shard_map/ppermute | solution.py:22
  33.3 7.4 %collective-permute-start.9 = (bf16[32,2048]{1,0:T(8,128)(2,1)S(1)}, bf16[32,2048]{1,0:T(8,128)(2,1)S(1)}, u32[]{:S(2)}, u32[]{:S(2)}) collective-permute-start(bf16[32,2048]{1,0:T(8,128)(2,1)S(1)} %multiply_convert_fusion.refs_0_), channel_id=1, source_target_pairs={{0,8},{4,12},{8,0},{12,4},{1,9},{5,13},{9,1},{13,5},{2,10},{6,14},... | collective-permute-start | bytes 393224 | tf_op jit(solution)/shard_map/ppermute | solution.py:22
  35.0 7.6 %collective-permute-start.15 = (bf16[32,2048]{1,0:T(8,128)(2,1)S(1)}, bf16[32,2048]{1,0:T(8,128)(2,1)S(1)}, u32[]{:S(2)}, u32[]{:S(2)}) collective-permute-start(bf16[32,2048]{1,0:T(8,128)(2,1)S(1)} %multiply_convert_fusion.refs_0_), channel_id=1, source_target_pairs={{0,1},{1,0},{2,3},{3,2},{4,5},{5,4},{6,7},{7,6},{8,9},{9,8},{10,11... | collective-permute-start | bytes 393224 | tf_op jit(solution)/shard_map/ppermute | solution.py:22
  35.1 7.6 %collective-permute-start.11 = (bf16[32,2048]{1,0:T(8,128)(2,1)S(1)}, bf16[32,2048]{1,0:T(8,128)(2,1)S(1)}, u32[]{:S(2)}, u32[]{:S(2)}) collective-permute-start(bf16[32,2048]{1,0:T(8,128)(2,1)S(1)} %multiply_convert_fusion.refs_0_), channel_id=1, source_target_pairs={{0,2},{2,0},{1,3},{3,1},{4,6},{6,4},{5,7},{7,5},{8,10},{10,8},{9,1... | collective-permute-start | bytes 393224 | tf_op jit(solution)/shard_map/ppermute | solution.py:22
  35.7 7.5 %collective-permute-start.8 = (bf16[32,2048]{1,0:T(8,128)(2,1)S(1)}, bf16[32,2048]{1,0:T(8,128)(2,1)S(1)}, u32[]{:S(2)}, u32[]{:S(2)}) collective-permute-start(bf16[32,2048]{1,0:T(8,128)(2,1)S(1)} %multiply_convert_fusion.refs_0_), channel_id=1, source_target_pairs={{0,4},{4,0},{8,12},{12,8},{1,5},{5,1},{9,13},{13,9},{2,6},{6,2},{1... | collective-permute-start | bytes 393224 | tf_op jit(solution)/shard_map/ppermute | solution.py:22
  40.7 5.0 %collective-permute-start.13 = (bf16[32,2048]{1,0:T(8,128)(2,1)S(1)}, bf16[32,2048]{1,0:T(8,128)(2,1)S(1)}, u32[]{:S(2)}, u32[]{:S(2)}) collective-permute-start(bf16[32,2048]{1,0:T(8,128)(2,1)S(1)} %collective-permute-done.9.refs_2_), channel_id=1, source_target_pairs={{0,2},{2,0},{1,3},{3,1},{4,6},{6,4},{5,7},{7,5},{8,10},{10,8},{9,1... | collective-permute-start | bytes 393224 | tf_op jit(solution)/shard_map/ppermute | solution.py:22
  42.5 4.0 %collective-permute-start.17 = (bf16[32,2048]{1,0:T(8,128)(2,1)S(1)}, bf16[32,2048]{1,0:T(8,128)(2,1)S(1)}, u32[]{:S(2)}, u32[]{:S(2)}) collective-permute-start(bf16[32,2048]{1,0:T(8,128)(2,1)S(1)} %collective-permute-done.9.refs_2_), channel_id=1, source_target_pairs={{0,1},{1,0},{2,3},{3,2},{4,5},{5,4},{6,7},{7,6},{8,9},{9,8},{10,11... | collective-permute-start | bytes 393224 | tf_op jit(solution)/shard_map/ppermute | solution.py:22
  42.6 6.4 %collective-permute-start.10 = (bf16[32,2048]{1,0:T(8,128)(2,1)S(1)}, bf16[32,2048]{1,0:T(8,128)(2,1)S(1)}, u32[]{:S(2)}, u32[]{:S(2)}) collective-permute-start(bf16[32,2048]{1,0:T(8,128)(2,1)S(1)} %collective-permute-done.9.refs_2_), channel_id=1, source_target_pairs={{0,4},{4,0},{8,12},{12,8},{1,5},{5,1},{9,13},{13,9},{2,6},{6,2},{1... | collective-permute-start | bytes 393224 | tf_op jit(solution)/shard_map/ppermute | solution.py:22
  42.7 3.7 %collective-permute-start.19 = (bf16[32,2048]{1,0:T(8,128)(2,1)S(1)}, bf16[32,2048]{1,0:T(8,128)(2,1)S(1)}, u32[]{:S(2)}, u32[]{:S(2)}) collective-permute-start(bf16[32,2048]{1,0:T(8,128)(2,1)S(1)} %collective-permute-done.11.refs_4_), channel_id=1, source_target_pairs={{0,1},{1,0},{2,3},{3,2},{4,5},{5,4},{6,7},{7,6},{8,9},{9,8},{10,11... | collective-permute-start | bytes 393224 | tf_op jit(solution)/shard_map/ppermute | solution.py:22
  43.2 5.8 %collective-permute-start.12 = (bf16[32,2048]{1,0:T(8,128)(2,1)S(1)}, bf16[32,2048]{1,0:T(8,128)(2,1)S(1)}, u32[]{:S(2)}, u32[]{:S(2)}) collective-permute-start(bf16[32,2048]{1,0:T(8,128)(2,1)S(1)} %collective-permute-done.8.refs_1_), channel_id=1, source_target_pairs={{0,2},{2,0},{1,3},{3,1},{4,6},{6,4},{5,7},{7,5},{8,10},{10,8},{9,1... | collective-permute-start | bytes 393224 | tf_op jit(solution)/shard_map/ppermute | solution.py:22
  45.7 5.6 %collective-permute-start.14 = (bf16[32,2048]{1,0:T(8,128)(2,1)S(1)}, bf16[32,2048]{1,0:T(8,128)(2,1)S(1)}, u32[]{:S(2)}, u32[]{:S(2)}) collective-permute-start(bf16[32,2048]{1,0:T(8,128)(2,1)S(1)} %collective-permute-done.13.refs_6_), channel_id=1, source_target_pairs={{0,4},{4,0},{8,12},{12,8},{1,5},{5,1},{9,13},{13,9},{2,6},{6,2},{1... | collective-permute-start | bytes 393224 | tf_op jit(solution)/shard_map/ppermute | solution.py:22
  46.4 5.1 %collective-permute-start.16 = (bf16[32,2048]{1,0:T(8,128)(2,1)S(1)}, bf16[32,2048]{1,0:T(8,128)(2,1)S(1)}, u32[]{:S(2)}, u32[]{:S(2)}) collective-permute-start(bf16[32,2048]{1,0:T(8,128)(2,1)S(1)} %collective-permute-done.8.refs_1_), channel_id=1, source_target_pairs={{0,1},{1,0},{2,3},{3,2},{4,5},{5,4},{6,7},{7,6},{8,9},{9,8},{10,11... | collective-permute-start | bytes 393224 | tf_op jit(solution)/shard_map/ppermute | solution.py:22
  46.5 5.0 %collective-permute-start.21 = (bf16[32,2048]{1,0:T(8,128)(2,1)S(1)}, bf16[32,2048]{1,0:T(8,128)(2,1)S(1)}, u32[]{:S(2)}, u32[]{:S(2)}) collective-permute-start(bf16[32,2048]{1,0:T(8,128)(2,1)S(1)} %collective-permute-done.13.refs_6_), channel_id=1, source_target_pairs={{0,1},{1,0},{2,3},{3,2},{4,5},{5,4},{6,7},{7,6},{8,9},{9,8},{10,11... | collective-permute-start | bytes 393224 | tf_op jit(solution)/shard_map/ppermute | solution.py:22
  49.0 2.6 %collective-permute-start.18 = (bf16[32,2048]{1,0:T(8,128)(2,1)S(1)}, bf16[32,2048]{1,0:T(8,128)(2,1)S(1)}, u32[]{:S(2)}, u32[]{:S(2)}) collective-permute-start(bf16[32,2048]{1,0:T(8,128)(2,1)S(1)} %collective-permute-done.10.refs_3_), channel_id=1, source_target_pairs={{0,1},{1,0},{2,3},{3,2},{4,5},{5,4},{6,7},{7,6},{8,9},{9,8},{10,11... | collective-permute-start | bytes 393224 | tf_op jit(solution)/shard_map/ppermute | solution.py:22
  49.0 2.6 %collective-permute-start.20 = (bf16[32,2048]{1,0:T(8,128)(2,1)S(1)}, bf16[32,2048]{1,0:T(8,128)(2,1)S(1)}, u32[]{:S(2)}, u32[]{:S(2)}) collective-permute-start(bf16[32,2048]{1,0:T(8,128)(2,1)S(1)} %collective-permute-done.12.refs_5_), channel_id=1, source_target_pairs={{0,1},{1,0},{2,3},{3,2},{4,5},{5,4},{6,7},{7,6},{8,9},{9,8},{10,11... | collective-permute-start | bytes 393224 | tf_op jit(solution)/shard_map/ppermute | solution.py:22
  51.3 1.3 %collective-permute-start.22 = (bf16[32,2048]{1,0:T(8,128)(2,1)S(1)}, bf16[32,2048]{1,0:T(8,128)(2,1)S(1)}, u32[]{:S(2)}, u32[]{:S(2)}) collective-permute-start(bf16[32,2048]{1,0:T(8,128)(2,1)S(1)} %collective-permute-done.14.refs_7_), channel_id=1, source_target_pairs={{0,1},{1,0},{2,3},{3,2},{4,5},{5,4},{6,7},{7,6},{8,9},{9,8},{10,11... | collective-permute-start | bytes 393224 | tf_op jit(solution)/shard_map/ppermute | solution.py:22
  52.7 39.1 %copy-start = (bf16[32,2048]{1,0:T(8,128)(2,1)S(1)}, bf16[32,2048]{1,0:T(8,128)(2,1)}, u32[]{:S(2)}) copy-start(bf16[32,2048]{1,0:T(8,128)(2,1)} %param.14) | copy-start | bytes 393220
  68.8 2.0 %collective-permute-start.24 = (bf16[128,2048]{1,0:T(8,128)(2,1)S(1)}, bf16[128,2048]{1,0:T(8,128)(2,1)S(1)}, u32[]{:S(2)}, u32[]{:S(2)}) collective-permute-start(bf16[128,2048]{1,0:T(8,128)(2,1)S(1)} %get-tuple-element.16), channel_id=1, source_target_pairs={{0,1},{1,0},{2,3},{3,2},{4,5},{5,4},{6,7},{7,6},{8,9},{9,8},{10,11... | collective-permute-start | bytes 1572872 | tf_op jit(solution)/shard_map/ppermute | solution.py:22
  69.0 2.5 %collective-permute-start.23 = (bf16[128,2048]{1,0:T(8,128)(2,1)S(1)}, bf16[128,2048]{1,0:T(8,128)(2,1)S(1)}, u32[]{:S(2)}, u32[]{:S(2)}) collective-permute-start(bf16[128,2048]{1,0:T(8,128)(2,1)S(1)} %get-tuple-element.14), channel_id=1, source_target_pairs={{0,1},{1,0},{2,3},{3,2},{4,5},{5,4},{6,7},{7,6},{8,9},{9,8},{10,11... | collective-permute-start | bytes 1572872 | tf_op jit(solution)/shard_map/ppermute | solution.py:22
  70.9 6.4 %collective-permute-start.26 = (bf16[32,2048]{1,0:T(8,128)(2,1)S(1)}, bf16[32,2048]{1,0:T(8,128)(2,1)S(1)}, u32[]{:S(2)}, u32[]{:S(2)}) collective-permute-start(bf16[32,2048]{1,0:T(8,128)(2,1)S(1)} %get-tuple-element.23), channel_id=1, source_target_pairs={{0,4},{4,0},{8,12},{12,8},{1,5},{5,1},{9,13},{13,9},{2,6},{6,2},{1... | collective-permute-start | bytes 393224 | tf_op jit(solution)/shard_map/ppermute | solution.py:22
  71.7 11.4 %collective-permute-start.29 = (bf16[32,2048]{1,0:T(8,128)(2,1)S(1)}, bf16[32,2048]{1,0:T(8,128)(2,1)S(1)}, u32[]{:S(2)}, u32[]{:S(2)}) collective-permute-start(bf16[32,2048]{1,0:T(8,128)(2,1)S(1)} %get-tuple-element.25), channel_id=1, source_target_pairs={{0,4},{4,0},{8,12},{12,8},{1,5},{5,1},{9,13},{13,9},{2,6},{6,2},{1... | collective-permute-start | bytes 393224 | tf_op jit(solution)/shard_map/ppermute | solution.py:22
  73.2 11.6 %collective-permute-start.25 = (bf16[32,2048]{1,0:T(8,128)(2,1)S(1)}, bf16[32,2048]{1,0:T(8,128)(2,1)S(1)}, u32[]{:S(2)}, u32[]{:S(2)}) collective-permute-start(bf16[32,2048]{1,0:T(8,128)(2,1)S(1)} %get-tuple-element.21), channel_id=1, source_target_pairs={{0,2},{2,0},{1,3},{3,1},{4,6},{6,4},{5,7},{7,5},{8,10},{10,8},{9,1... | collective-permute-start | bytes 393224 | tf_op jit(solution)/shard_map/ppermute | solution.py:22
  74.8 7.7 %collective-permute-start.27 = (bf16[32,2048]{1,0:T(8,128)(2,1)S(1)}, bf16[32,2048]{1,0:T(8,128)(2,1)S(1)}, u32[]{:S(2)}, u32[]{:S(2)}) collective-permute-start(bf16[32,2048]{1,0:T(8,128)(2,1)S(1)} %get-tuple-element.22), channel_id=1, source_target_pairs={{0,2},{2,0},{1,3},{3,1},{4,6},{6,4},{5,7},{7,5},{8,10},{10,8},{9,1... | collective-permute-start | bytes 393224 | tf_op jit(solution)/shard_map/ppermute | solution.py:22
  77.4 6.5 %collective-permute-start.30 = (bf16[32,2048]{1,0:T(8,128)(2,1)S(1)}, bf16[32,2048]{1,0:T(8,128)(2,1)S(1)}, u32[]{:S(2)}, u32[]{:S(2)}) collective-permute-start(bf16[32,2048]{1,0:T(8,128)(2,1)S(1)} %add_convert_fusion.6), channel_id=1, source_target_pairs={{0,2},{2,0},{1,3},{3,1},{4,6},{6,4},{5,7},{7,5},{8,10},{10,8},{9,1... | collective-permute-start | bytes 393224 | tf_op jit(solution)/shard_map/ppermute | solution.py:22
  82.5 6.4 %collective-permute-start.28 = (bf16[32,2048]{1,0:T(8,128)(2,1)S(1)}, bf16[32,2048]{1,0:T(8,128)(2,1)S(1)}, u32[]{:S(2)}, u32[]{:S(2)}) collective-permute-start(bf16[32,2048]{1,0:T(8,128)(2,1)S(1)} %add_convert_fusion.5), channel_id=1, source_target_pairs={{0,4},{4,0},{8,12},{12,8},{1,5},{5,1},{9,13},{13,9},{2,6},{6,2},{1... | collective-permute-start | bytes 393224 | tf_op jit(solution)/shard_map/ppermute | solution.py:22
  83.9 7.9 %collective-permute-start.31 = (bf16[32,2048]{1,0:T(8,128)(2,1)S(1)}, bf16[32,2048]{1,0:T(8,128)(2,1)S(1)}, u32[]{:S(2)}, u32[]{:S(2)}) collective-permute-start(bf16[32,2048]{1,0:T(8,128)(2,1)S(1)} %add_convert_fusion.4), channel_id=1, source_target_pairs={{0,8},{4,12},{8,0},{12,4},{1,9},{5,13},{9,1},{13,5},{2,10},{6,14},... | collective-permute-start | bytes 393224 | tf_op jit(solution)/shard_map/ppermute | solution.py:22

commit v4 on v0

--- a/solution.py
+++ b/solution.py
@@ -1,8 +1,11 @@
+import functools
 import math
 
 import jax
 import jax.numpy as jnp
 from jax import lax
+from jax.experimental import pallas as pl
+from jax.experimental.pallas import tpu as pltpu
 from jax.sharding import PartitionSpec as P
 
 HEAD_DIMENSION = 128
@@ -10,6 +13,10 @@
 KEY_VALUE_HEADS = 4
 EXPERTS = 64
 TOPK = 8
+MIB = 1 << 20
+LANES = 128
+BF = jnp.bfloat16
+F32 = jnp.float32
 
 
 def attend_blocks(blocks, key_head, value_head, heads_here):
@@ -83,7 +90,7 @@
     )
 
 
-def on_device(
+def on_device_any_size(
     queries, keys, values, out_weight, resid, expert_ids, router_probs, w_gate, w_up, w_down
 ):
     rows_ctx = queries.shape[0]
@@ -159,6 +166,340 @@
     return (hidden + routed).astype(jnp.bfloat16)
 
 
+def flip(x, axis, bit):
+    return lax.ppermute(x, axis, [(i, i ^ bit) for i in range(lax.axis_size(axis))])
+
+
+def from_earlier(x, axis, steps):
+    size = lax.axis_size(axis)
+    return lax.ppermute(x, axis, [(i, i + steps) for i in range(size - steps)])
+
+
+def in_hbm(x):
+    return pltpu.with_memory_space_constraint(x, pltpu.HBM)
+
+
+def dot_rows(a, b):
+    return lax.dot_general(a, b, (((1,), (1,)), ((), ())), preferred_element_type=F32)
+
+
+def attention_kernel(sizes, place, *refs):
+    n_ctx, n_exp, n_tp, heads, part = sizes
+    rows = n_exp * n_tp * part
+    kv_refs, refs = refs[:n_ctx], refs[n_ctx:]
+    ids_ref, probs_ref, resid_hbm, q_hbm, w_hbm = refs[:5]
+    base_ref, across_ref, other_ref, routing_ref = refs[5:9]
+    k_all, v_all, q_all, att, att_rel, w_all, resid, packed, q_sem, sems = refs[9:]
+    fetch_q = []
+    for h in range(heads):
+        columns = slice(h * HEAD_DIMENSION, (h + 1) * HEAD_DIMENSION)
+        fetch_q.append(
+            pltpu.make_async_copy(q_hbm.at[:, columns], q_all.at[:, columns], q_sem.at[h])
+        )
+        fetch_q[h].start()
+    fetch_w = pltpu.make_async_copy(w_hbm, w_all, sems.at[0])
+    fetch_w.start()
+    fetch_resid = pltpu.make_async_copy(resid_hbm, resid, sems.at[1])
+    fetch_resid.start()
+    ctx, exp, tp = place[0], place[1], place[2]
+
+    block = n_tp * part
+    ids = ids_ref[...]
+    probs = probs_ref[...]
+    expert = lax.broadcasted_iota(jnp.int32, (EXPERTS, block), 0)
+    named = jnp.zeros((EXPERTS, block), F32)
+    for k in range(TOPK):
+        named = named + jnp.where(expert == ids[k : k + 1, :], 1.0, 0.0)
+    before = lax.broadcasted_iota(jnp.int32, (block, block), 0) < lax.broadcasted_iota(
+        jnp.int32, (block, block), 1
+    )
+    count = jnp.dot(
+        named.astype(BF), jnp.where(before, 1.0, 0.0).astype(BF), preferred_element_type=F32
+    )
+    ranks = [
+        jnp.sum(jnp.where(expert == ids[k : k + 1, :], count, 0.0), axis=0, keepdims=True)
+        for k in range(TOPK)
+    ]
+    gates = probs / jnp.sum(probs, axis=0, keepdims=True)
+    high = gates.astype(BF).astype(F32)
+    fields = jnp.concatenate([ids.astype(F32)] + ranks + [high, gates - high], axis=0)
+    packed[...] = jnp.zeros_like(packed)
+    packed[: 4 * TOPK, :block] = fields
+    packed[...] = packed[...].T
+    routing_ref[...] = packed[pl.ds(pl.multiple_of(tp * part, part), part), :].astype(BF)
+
+    for z in range(n_ctx):
+        k_all[z * rows : (z + 1) * rows, :] = kv_refs[z][:, :HEAD_DIMENSION]
+        v_all[z * rows : (z + 1) * rows, :HEAD_DIMENSION] = kv_refs[z][:, HEAD_DIMENSION:]
+    v_all[:, HEAD_DIMENSION:] = jnp.ones((n_ctx * rows, HEAD_DIMENSION), BF)
+    column = lax.broadcasted_iota(jnp.int32, (rows, n_ctx * rows), 1)
+    row = lax.broadcasted_iota(jnp.int32, (rows, n_ctx * rows), 0)
+    allowed = (column <= row) | ((column >= rows) & (column < (ctx + 1) * rows))
+    scale = 1.0 / math.sqrt(HEAD_DIMENSION)
+    for h in range(heads):
+        columns = slice(h * HEAD_DIMENSION, (h + 1) * HEAD_DIMENSION)
+        fetch_q[h].wait()
+        s = dot_rows(q_all[:, columns], k_all[...])
+        s = jnp.where(allowed, s * scale, -1e30)
+        weights = jnp.exp(s - jnp.max(s, axis=1, keepdims=True))
+        out = jnp.dot(weights.astype(BF), v_all[...], preferred_element_type=F32)
+        att[:, columns] = (out[:, :HEAD_DIMENSION] / out[:, HEAD_DIMENSION:]).astype(BF)
+    for t in range(n_tp):
+        for x in range(n_exp):
+            owner = lax.rem(exp + x, n_exp) * n_tp + lax.rem(tp + t, n_tp)
+            source = pl.ds(pl.multiple_of(owner * part, part), part)
+            at = (t * n_exp + x) * part
+            att_rel[at : at + part, :] = att[source, :]
+    fetch_w.wait()
+    projected = jnp.dot(att_rel[...], w_all[...], preferred_element_type=F32)
+    fetch_resid.wait()
+    base_ref[...] = resid[...].astype(F32) + projected[:part]
+    across_ref[...] = projected[part : 2 * part].astype(BF)
+    other_ref[...] = projected[2 * part :].astype(BF)
+
+
+def attend_project(place, pieces, expert_ids, router_probs, resid, queries, out_weight, n_exp, n_tp):
+    rows, width = queries.shape
+    n_ctx, heads = len(pieces), width // HEAD_DIMENSION
+    part, model = resid.shape
+    block = expert_ids.shape[0]
+    vmem = pl.BlockSpec(memory_space=pltpu.VMEM)
+    hbm = pl.BlockSpec(memory_space=pltpu.HBM)
+    return pl.pallas_call(
+        functools.partial(attention_kernel, (n_ctx, n_exp, n_tp, heads, part)),
+        out_shape=(
+            jax.ShapeDtypeStruct((part, model), F32),
+            jax.ShapeDtypeStruct((part, model), BF),
+            jax.ShapeDtypeStruct((2 * part, model), BF),
+            jax.ShapeDtypeStruct((part, LANES), BF),
+        ),
+        in_specs=[pl.BlockSpec(memory_space=pltpu.SMEM)] + [vmem] * (n_ctx + 2) + [hbm] * 3,
+        out_specs=(vmem,) * 4,
+        scratch_shapes=[
+            pltpu.VMEM((n_ctx * rows, HEAD_DIMENSION), BF),
+            pltpu.VMEM((n_ctx * rows, 2 * HEAD_DIMENSION), BF),
+            pltpu.VMEM((rows, width), BF),
+            pltpu.VMEM((rows, width), BF),
+            pltpu.VMEM((rows, width), BF),
+            pltpu.VMEM((width, model), BF),
+            pltpu.VMEM((part, model), BF),
+            pltpu.VMEM((LANES, LANES), F32),
+            pltpu.SemaphoreType.DMA((heads,)),
+            pltpu.SemaphoreType.DMA((2,)),
+        ],
+        compiler_params=pltpu.CompilerParams(vmem_limit_bytes=32 * MIB),
+        cost_estimate=pl.CostEstimate(
+            flops=2 * rows * width * (2 * n_ctx * rows + model),
+            bytes_accessed=2 * (rows * width + width * model + rows * model),
+            transcendentals=rows * n_ctx * rows * heads,
+        ),
+        name="attend_project",
+    )(place, *pieces, expert_ids.T, router_probs.T, *map(in_hbm, (resid, queries, out_weight)))
+
+
+def expert_kernel(n_pieces, depth, experts, first_ref, *refs):
+    pieces, (wg_hbm, wu_hbm, wd_hbm) = refs[:n_pieces], refs[n_pieces : n_pieces + 3]
+    outs = refs[n_pieces + 3 : n_pieces + 7]
+    x_all, packed, pick_all, scale_all, out_all, wgu, wd, act, sems = refs[n_pieces + 7 :]
+    tokens = x_all.shape[0]
+    slots = pick_all.shape[0] // experts
+    _, _, halves, hidden, model = wgu.shape
+    part = tokens // n_pieces
+    blocks = n_pieces // 2
+
+    def copies(e):
+        slot = lax.rem(e, depth)
+        rows = pl.ds(e * halves, halves)
+        return (
+            pltpu.make_async_copy(wg_hbm.at[rows], wgu.at[slot, 0], sems.at[0, slot]),
+            pltpu.make_async_copy(wu_hbm.at[rows], wgu.at[slot, 1], sems.at[1, slot]),
+            pltpu.make_async_copy(wd_hbm.at[rows], wd.at[slot], sems.at[2, slot]),
+        )
+
+    def start(e):
+        for copy in copies(e):
+            copy.start()
+
+    def wait(e):
+        for copy in copies(e):
+            copy.wait()
+
+    def gate_up(e):
+        x = out_all[pl.ds(pl.multiple_of(e * slots, slots), slots), :]
+        weight = wgu[lax.rem(e, depth)].reshape(2 * halves * hidden, model)
+        both = dot_rows(weight, x)
+        gate, up = both[: halves * hidden], both[halves * hidden :]
+        return (gate * jax.nn.sigmoid(gate) * up).astype(BF)
+
+    def down(e):
+        here = pl.ds(pl.multiple_of(e * slots, slots), slots)
+        weight = wd[lax.rem(e, depth)].reshape(halves * hidden, model)
+        out = lax.dot_general(
+            act[lax.rem(e, 2)], weight, (((0,), (0,)), ((), ())), preferred_element_type=F32
+        )
+        return here, (out * scale_all[here, :]).astype(BF)
+
+    for e in range(min(depth - 1, experts)):
+        start(e)
+    for i, piece in enumerate(pieces):
+        x_all[i * part : (i + 1) * part, :] = piece[:, :model]
+        packed[i * part : (i + 1) * part, :] = piece[:, model:].astype(F32)
+    fields = packed[...].T
+    ids, ranks = fields[:TOPK], fields[TOPK : 2 * TOPK]
+    gates = fields[2 * TOPK : 3 * TOPK] + fields[3 * TOPK : 4 * TOPK]
+    token = lax.broadcasted_iota(jnp.int32, (TOPK, tokens), 1)
+    places = ranks.astype(jnp.int32) + lax.rem(token // part, blocks) * (slots // blocks)
+    slot = lax.broadcasted_iota(jnp.int32, (slots, tokens), 0)
+    for e in range(experts):
+        hit = ids.astype(jnp.int32) == first_ref[0] + e
+        chosen = slot == jnp.max(jnp.where(hit, places, -1), axis=0, keepdims=True)
+        gate = jnp.sum(jnp.where(hit, gates, 0.0), axis=0, keepdims=True)
+        here = slice(e * slots, (e + 1) * slots)
+        pick_all[here, :] = jnp.where(chosen, 1.0, 0.0).astype(BF)
+        scale_all[here, :] = jnp.sum(jnp.where(chosen, gate, 0.0), axis=1, keepdims=True)
+    out_all[...] = jnp.dot(pick_all[...], x_all[...], preferred_element_type=F32).astype(BF)
+    wait(0)
+    act[0] = gate_up(0)
+
+    @pl.loop(0, experts - 1)
+    def _(e):
+        @pl.when(e + depth - 1 < experts)
+        def _():
+            start(e + depth - 1)
+
+        wait(e + 1)
+        following = gate_up(e + 1)
+        here, out = down(e)
+        act[lax.rem(e + 1, 2)] = following
+        out_all[here, :] = out
+
+    here, out = down(experts - 1)
+    out_all[here, :] = out
+    quarter = tokens // 4
+    for i, o_ref in enumerate(outs):
+        o_ref[...] = lax.dot_general(
+            pick_all[:, i * quarter : (i + 1) * quarter],
+            out_all[...],
+            (((0,), (0,)), ((), ())),
+            preferred_element_type=F32,
+        ).astype(BF)
+
+
+def cube_experts(first, pieces, w_gate, w_up, w_down, slots):
+    rows, hidden, model = w_down.shape
+    halves = 2
+    experts = rows // halves
+    tokens = len(pieces) * pieces[0].shape[0]
+    depth = min(4, experts)
+    vmem = pl.BlockSpec(memory_space=pltpu.VMEM)
+    hbm = pl.BlockSpec(memory_space=pltpu.HBM)
+
+    out = jax.ShapeDtypeStruct((tokens // 4, model), BF)
+    return pl.pallas_call(
+        functools.partial(expert_kernel, len(pieces), depth, experts),
+        out_shape=(out,) * 4,
+        in_specs=[pl.BlockSpec(memory_space=pltpu.SMEM)] + [vmem] * len(pieces) + [hbm] * 3,
+        out_specs=(vmem,) * 4,
+        scratch_shapes=[
+            pltpu.VMEM((tokens, model), BF),
+            pltpu.VMEM((tokens, LANES), F32),
+            pltpu.VMEM((experts * slots, tokens), BF),
+            pltpu.VMEM((experts * slots, 1), F32),
+            pltpu.VMEM((experts * slots, model), BF),
+            pltpu.VMEM((depth, 2, halves, hidden, model), BF),
+            pltpu.VMEM((depth, halves, hidden, model), BF),
+            pltpu.VMEM((2, halves * hidden, slots), BF),
+            pltpu.SemaphoreType.DMA((3, depth)),
+        ],
+        compiler_params=pltpu.CompilerParams(vmem_limit_bytes=44 * MIB),
+        cost_estimate=pl.CostEstimate(
+            flops=2 * experts * slots * model * (3 * halves * hidden + 2 * tokens),
+            bytes_accessed=6 * rows * model * hidden + 4 * tokens * model,
+            transcendentals=experts * slots * halves * hidden,
+        ),
+        name="experts",
+    )(
+        first,
+        *pieces,
+        in_hbm(jnp.swapaxes(w_gate, 1, 2)),
+        in_hbm(jnp.swapaxes(w_up, 1, 2)),
+        in_hbm(w_down),
+    )
+
+
+def sums_back(mine, mine_across, other, other_across, part):
+    def add(a, *others):
+        total = a.astype(F32)
+        for b in others:
+            total = total + b.astype(F32)
+        return total.astype(BF)
+
+    across = add(mine_across, flip(other_across, "tp", 1))
+    here = add(mine, flip(other, "tp", 1))
+    across = [across[z * part : (z + 1) * part] for z in range(4)]
+    here = [here[z * part : (z + 1) * part] for z in range(4)]
+    far_across = add(across[2], flip(across[3], "ctx", 1))
+    own = flip(across[0], "exp", 1)
+    near = flip(across[1], "exp", 1)
+    last = flip(here[3], "ctx", 1)
+    far_across, here[1] = lax.optimization_barrier((far_across, here[1]))
+    far = flip(far_across, "exp", 1)
+    near = add(here[1], near)
+    near, here[2] = lax.optimization_barrier((near, here[2]))
+    near = flip(near, "ctx", 1)
+    far = flip(add(here[2], last, far), "ctx", 2)
+    return here[0].astype(F32) + own.astype(F32) + near.astype(F32) + far.astype(F32)
+
+
+def on_device(
+    queries, keys, values, out_weight, resid, expert_ids, router_probs, w_gate, w_up, w_down
+):
+    n_ctx, n_exp, n_tp = (lax.axis_size(a) for a in ("ctx", "exp", "tp"))
+    part = resid.shape[0]
+    rows_here = w_gate.shape[0]
+    block = expert_ids.shape[0]
+    cube = (n_ctx, n_exp, n_tp) == (4, 2, 2) and block == n_tp * part <= LANES
+    if not cube or part % 16 or rows_here * n_ctx * n_exp != 2 * EXPERTS:
+        return on_device_any_size(
+            queries, keys, values, out_weight, resid, expert_ids, router_probs, w_gate, w_up, w_down
+        )
+    ctx, exp, tp = (lax.axis_index(a) for a in ("ctx", "exp", "tp"))
+    place = jnp.stack([ctx, exp, tp]).astype(jnp.int32)
+    heads_here = queries.shape[1] // HEAD_DIMENSION
+    first = (ctx * n_exp + exp) * rows_here // 2
+    slots = n_ctx * n_exp * min(8, block)
+
+    shared = (exp * n_tp + tp) * heads_here // (QUERY_HEADS // KEY_VALUE_HEADS)
+    key_head = lax.dynamic_slice_in_dim(keys, shared * HEAD_DIMENSION, HEAD_DIMENSION, 1)
+    value_head = lax.dynamic_slice_in_dim(values, shared * HEAD_DIMENSION, HEAD_DIMENSION, 1)
+    kv = jnp.concatenate([key_head, value_head], axis=1)
+    kv_pieces = [kv] + [from_earlier(kv, "ctx", z) for z in range(1, n_ctx)]
+    base, across, other, routing = attend_project(
+        place, kv_pieces, expert_ids, router_probs, resid, queries, out_weight, n_exp, n_tp
+    )
+
+    other = flip(other, "tp", 1).astype(F32)
+    across = flip((across.astype(F32) + other[part:]).astype(BF), "exp", 1)
+    hidden = base + other[:part] + across.astype(F32)
+    mean_square = jnp.mean(hidden * hidden, axis=1, keepdims=True)
+    normed = (hidden * lax.rsqrt(mean_square + 1e-06)).astype(BF)
+    normed = jnp.concatenate([normed, routing], axis=1)
+
+    far = flip(normed, "ctx", 2)
+    across = flip(normed, "exp", 1)
+    near = flip(normed, "ctx", 1)
+    far_across = flip(far, "exp", 1)
+    near_across = flip(near, "exp", 1)
+    last = flip(far, "ctx", 1)
+    last_across = flip(far_across, "ctx", 1)
+    chip = [normed, near, far, last, across, near_across, far_across, last_across]
+    pieces = chip + [flip(piece, "tp", 1) for piece in chip]
+    sums = cube_experts(
+        first.astype(jnp.int32).reshape(1), pieces, w_gate, w_up, w_down, slots
+    )
+    return (hidden + sums_back(*sums, part)).astype(BF)
+
+
 def solution(mesh):
     in_specs = (
         P(("groups", "ctx"), ("exp", "tp")),

time: 358 us -> 91.6 us (0.26)
  blocking collectives: 128 us -> 0 us
  waiting for transfers between devices: 115 us -> 33.6 us
  local copies, waits for them, and re-layouts: 42.9 us -> 2.21 us
  matrix products: 33.4 us -> 0 us
  starting transfers between devices: 4.94 us -> 30.5 us
  Pallas kernels: 0 us -> 23.3 us
  other arithmetic: 18.2 us -> 1.54 us
  between operations: 14.2 us -> 0.19 us
    all_to_all x1 -> x0, blocking collectives: 97.8 us -> none  [on_device(): lax.all_to_all(send_buffer.reshape(rows_here * slot_count, peer_count, mo...]
    all_to_all x1 -> x0, waiting for transfers between devices: 91.9 us -> none  [on_device(): lax.all_to_all(expert_out.reshape(rows_here * slot_count, peer_count, mod...]
    ppermute x0 -> x29, waiting for transfers between devices: none -> 33.6 us  [the longest x26 31.8 us: flip(): lax.ppermute(x, axis, [(i, i ^ bit) for i in range(lax.axis_size(axis))])]
    dot_general x5 -> x0, matrix products: 31.7 us -> none  [the longest x1 14 us: run_experts(): jnp.einsum('rnf,rfd->rnd', activated, w_down, preferred_element_type=jnp....]
    ppermute x0 -> x29, starting transfers between devices: none -> 30.5 us  [the longest x26 19.8 us: flip(): lax.ppermute(x, axis, [(i, i ^ bit) for i in range(lax.axis_size(axis))])]
    all_gather x3 -> x0, blocking collectives: 30.5 us -> none  [the longest x1 15 us: attend_blocks(): lax.all_gather(value_head, 'ctx', axis=0, tiled=True)]
    reduce_scatter x2 -> x0, waiting for transfers between devices: 23.5 us -> none  [the longest x1 16.6 us: on_device(): lax.psum_scatter(jnp.dot(attended, out_weight, preferred_element_type=jnp...]
    pallas_call x0 -> x2, Pallas kernels: none -> 23.3 us  [the longest x1 16.1 us: cube_experts(): pl.pallas_call(functools.partial(expert_kernel, len(pieces), depth, exper...]
  transfers between devices with their start and end apart: 3 -> 29, of which waited for: 3 -> 16; matrix products, arithmetic and copies ran while one was open for 2% -> 1% of each run, Pallas kernels for 0% -> 0%
where the time goes in v4:
time: 91.6 us; the launch traced here: 91.3 us
  waiting for transfers between devices  33.6 us (37%)
  starting transfers between devices  30.5 us (33%)
  Pallas kernels  23.3 us (25%)
  local copies, waits for them, and re-layouts  2.21 us (2%)
  other arithmetic  1.54 us (2%)
    ppermute x26, waiting for transfers between devices, flip(): lax.ppermute(x, axis, [(i, i ^ bit) for i in range(lax.axis_size(axis))])  31.8 us
    ppermute x26, starting transfers between devices, flip(): lax.ppermute(x, axis, [(i, i ^ bit) for i in range(lax.axis_size(axis))])  19.8 us
    pallas_call x1, Pallas kernels, cube_experts(): pl.pallas_call(functools.partial(expert_kernel, len(pieces), depth, exper...  16.1 us
    ppermute x3, starting transfers between devices, from_earlier(): return lax.ppermute(x, axis, [(i, i + steps) for i in range(size - steps)])  10.7 us
    pallas_call x1, Pallas kernels, attend_project(): pl.pallas_call(functools.partial(attention_kernel, (n_ctx, n_exp, n_tp, h...  7.2 us
  transfers between devices with their start and end apart: 29, of which 16 were waited for; matrix products, arithmetic and copies ran while one was open for 1% of the time, Pallas kernels for 0%

profile of v4, /device:TPU:0, one launch (start us, length us, event | category | flops | bytes accessed | tf_op | source)
XLA Modules:
  0.0 91.3 jit_solution(1182675187230212015)
XLA Ops:
  0.0 0.8 constant_dynamic-slice_fusion
  0.8 7.0 %collective-permute-start.2 = (bf16[128,256]{1,0:T(8,128)(2,1)S(1)}, bf16[128,256]{1,0:T(8,128)(2,1)S(1)}, u32[]{:S(2)}, u32[]{:S(2)}) collective-permute-start(bf16[128,256]{1,0:T(8,128)(2,1)S(1)} %pad_maximum_fusion.1.refs_0_), channel_id=1, source_target_pairs={{0,12},{1,13},{2,14},{3,15},{16,28},{17,29},{18,30},{19,31}} | collective-permute-start | bytes 196616 | tf_op jit(solution)/shard_map/ppermute | solution.py:175
  7.8 1.3 %collective-permute-start.1 = (bf16[128,256]{1,0:T(8,128)(2,1)S(1)}, bf16[128,256]{1,0:T(8,128)(2,1)S(1)}, u32[]{:S(2)}, u32[]{:S(2)}) collective-permute-start(bf16[128,256]{1,0:T(8,128)(2,1)S(1)} %pad_maximum_fusion.1.refs_0_), channel_id=1, source_target_pairs={{0,8},{4,12},{1,9},{5,13},{2,10},{6,14},{3,11},{7,15},{16,24},{20,... | collective-permute-start | bytes 196616 | tf_op jit(solution)/shard_map/ppermute | solution.py:175
  9.1 2.5 %collective-permute-start = (bf16[128,256]{1,0:T(8,128)(2,1)S(1)}, bf16[128,256]{1,0:T(8,128)(2,1)S(1)}, u32[]{:S(2)}, u32[]{:S(2)}) collective-permute-start(bf16[128,256]{1,0:T(8,128)(2,1)S(1)} %pad_maximum_fusion.1.refs_0_), channel_id=1, source_target_pairs={{0,4},{4,8},{8,12},{1,5},{5,9},{9,13},{2,6},{6,10},{10,14},{3,7},{... | collective-permute-start | bytes 196616 | tf_op jit(solution)/shard_map/ppermute | solution.py:175
  11.5 0.1 pad_add_fusion.place
  11.6 1.8 %collective-permute-done.refs_1_ = bf16[128,256]{1,0:T(8,128)(2,1)S(1)} collective-permute-done((bf16[128,256]{1,0:T(8,128)(2,1)S(1)}, bf16[128,256]{1,0:T(8,128)(2,1)S(1)}, u32[]{:S(2)}, u32[]{:S(2)}) %collective-permute-start) | collective-permute-done | bytes 65568 | tf_op jit(solution)/shard_map/ppermute | solution.py:175
  13.4 0.7 copy-done
  14.1 0.7 copy-done.1
  14.8 7.2 %attend_project.1 = (f32[32,2048]{1,0:T(8,128)S(1)}, bf16[32,2048]{1,0:T(8,128)(2,1)S(1)}, bf16[64,2048]{1,0:T(8,128)(2,1)S(1)}, bf16[32,128]{1,0:T(8,128)(2,1)S(1)}) custom-call(s32[3]{0:T(128)S(1)} %pad_add_fusion.place, bf16[128,256]{1,0:T(8,128)(2,1)S(1)} %pad_maximum_fusion.1.refs_0_, bf16[128,256]{1,0:T(8,128)(2,1)S(1)} %collective-permute-done.refs_1_, ...), custom_call_target="tpu_custom_call" | custom-call | flops 805306368 | bytes 4980736 | tf_op jit(solution)/shard_map/attend_project/pallas_call | solution.py:268
  22.1 1.5 %collective-permute-done.3 = bf16[64,2048]{1,0:T(8,128)(2,1)S(1)} collective-permute-done((bf16[64,2048]{1,0:T(8,128)(2,1)S(1)}, bf16[64,2048]{1,0:T(8,128)(2,1)S(1)}, u32[]{:S(2)}, u32[]{:S(2)}) %collective-permute-start.3) | collective-permute-done | bytes 262176 | tf_op jit(solution)/shard_map/ppermute | solution.py:170
  23.7 1.6 %collective-permute-start.4 = (bf16[32,2048]{1,0:T(8,128)(2,1)S(1)}, bf16[32,2048]{1,0:T(8,128)(2,1)S(1)}, u32[]{:S(2)}, u32[]{:S(2)}) collective-permute-start(bf16[32,2048]{1,0:T(8,128)(2,1)S(1)} %fusion), channel_id=1, source_target_pairs={{0,2},{2,0},{1,3},{3,1},{4,6},{6,4},{5,7},{7,5},{8,10},{10,8},{9,1... | collective-permute-start | bytes 393224 | tf_op jit(solution)/shard_map/ppermute | solution.py:170
  25.2 4.0 %collective-permute-done.4 = bf16[32,2048]{1,0:T(8,128)(2,1)S(1)} collective-permute-done((bf16[32,2048]{1,0:T(8,128)(2,1)S(1)}, bf16[32,2048]{1,0:T(8,128)(2,1)S(1)}, u32[]{:S(2)}, u32[]{:S(2)}) %collective-permute-start.4) | collective-permute-done | bytes 131104 | tf_op jit(solution)/shard_map/ppermute | solution.py:170
  29.3 0.2 multiply_reduce_fusion
  29.5 0.1 multiply_convert_fusion
  29.6 3.3 %collective-permute-start.6 = (bf16[32,2176]{1,0:T(8,128)(2,1)S(1)}, bf16[32,2176]{1,0:T(8,128)(2,1)S(1)}, u32[]{:S(2)}, u32[]{:S(2)}) collective-permute-start(bf16[32,2176]{1,0:T(8,128)(2,1)S(1)} %pad_maximum_fusion.refs_0_), channel_id=1, source_target_pairs={{0,8},{4,12},{8,0},{12,4},{1,9},{5,13},{9,1},{13,5},{2,10},{6,14},... | collective-permute-start | bytes 417800 | tf_op jit(solution)/shard_map/ppermute | solution.py:170
  32.9 1.5 %collective-permute-start.8 = (bf16[32,2176]{1,0:T(8,128)(2,1)S(1)}, bf16[32,2176]{1,0:T(8,128)(2,1)S(1)}, u32[]{:S(2)}, u32[]{:S(2)}) collective-permute-start(bf16[32,2176]{1,0:T(8,128)(2,1)S(1)} %pad_maximum_fusion.refs_0_), channel_id=1, source_target_pairs={{0,2},{2,0},{1,3},{3,1},{4,6},{6,4},{5,7},{7,5},{8,10},{10,8},{9,1... | collective-permute-start | bytes 417800 | tf_op jit(solution)/shard_map/ppermute | solution.py:170
  34.4 0.5 collective-permute-start.5
  34.9 4.2 %collective-permute-done.6.refs_2_ = bf16[32,2176]{1,0:T(8,128)(2,1)S(1)} collective-permute-done((bf16[32,2176]{1,0:T(8,128)(2,1)S(1)}, bf16[32,2176]{1,0:T(8,128)(2,1)S(1)}, u32[]{:S(2)}, u32[]{:S(2)}) %collective-permute-start.6) | collective-permute-done | bytes 139296 | tf_op jit(solution)/shard_map/ppermute | solution.py:170
  39.1 1.5 %collective-permute-start.10 = (bf16[32,2176]{1,0:T(8,128)(2,1)S(1)}, bf16[32,2176]{1,0:T(8,128)(2,1)S(1)}, u32[]{:S(2)}, u32[]{:S(2)}) collective-permute-start(bf16[32,2176]{1,0:T(8,128)(2,1)S(1)} %collective-permute-done.6.refs_2_), channel_id=1, source_target_pairs={{0,2},{2,0},{1,3},{3,1},{4,6},{6,4},{5,7},{7,5},{8,10},{10,8},{9,1... | collective-permute-start | bytes 417800 | tf_op jit(solution)/shard_map/ppermute | solution.py:170
  40.6 0.5 collective-permute-start.14
  41.2 0.8 collective-permute-done.5.refs_1_
  42.0 0.5 collective-permute-start.9
  42.5 1.7 %collective-permute-done.10.refs_6_ = bf16[32,2176]{1,0:T(8,128)(2,1)S(1)} collective-permute-done((bf16[32,2176]{1,0:T(8,128)(2,1)S(1)}, bf16[32,2176]{1,0:T(8,128)(2,1)S(1)}, u32[]{:S(2)}, u32[]{:S(2)}) %collective-permute-start.10) | collective-permute-done | bytes 139296 | tf_op jit(solution)/shard_map/ppermute | solution.py:170
  44.2 0.5 collective-permute-start.18
  44.7 3.0 %collective-permute-done.7.refs_3_ = bf16[32,2176]{1,0:T(8,128)(2,1)S(1)} collective-permute-done((bf16[32,2176]{1,0:T(8,128)(2,1)S(1)}, bf16[32,2176]{1,0:T(8,128)(2,1)S(1)}, u32[]{:S(2)}, u32[]{:S(2)}) %collective-permute-start.7) | collective-permute-done | bytes 139296 | tf_op jit(solution)/shard_map/ppermute | solution.py:170
  47.7 0.5 collective-permute-start.17
  48.2 1.5 %collective-permute-done.11.refs_7_ = bf16[32,2176]{1,0:T(8,128)(2,1)S(1)} collective-permute-done((bf16[32,2176]{1,0:T(8,128)(2,1)S(1)}, bf16[32,2176]{1,0:T(8,128)(2,1)S(1)}, u32[]{:S(2)}, u32[]{:S(2)}) %collective-permute-start.11) | collective-permute-done | bytes 139296 | tf_op jit(solution)/shard_map/ppermute | solution.py:170
  49.8 1.3 %collective-permute-done.19.refs_15_ = bf16[32,2176]{1,0:T(8,128)(2,1)S(1)} collective-permute-done((bf16[32,2176]{1,0:T(8,128)(2,1)S(1)}, bf16[32,2176]{1,0:T(8,128)(2,1)S(1)}, u32[]{:S(2)}, u32[]{:S(2)}) %collective-permute-start.19) | collective-permute-done | bytes 139296 | tf_op jit(solution)/shard_map/ppermute | solution.py:170
  51.1 16.1 %experts.1 = (bf16[128,2048]{1,0:T(8,128)(2,1)S(1)}, bf16[128,2048]{1,0:T(8,128)(2,1)S(1)}, bf16[128,2048]{1,0:T(8,128)(2,1)S(1)}, bf16[128,2048]{1,0:T(8,128)(2,1)S(1)}) custom-call(s32[1]{0:T(128)} %bitcast.5.first_ref, bf16[32,2176]{1,0:T(8,128)(2,1)S(1)} %pad_maximum_fusion.refs_0_, bf16[32,2176]{1,0:T(8,128)(2,1)S(1)} %collective-permute-done.5.refs_1_, ...), custom_call_target="tpu_custom_call" | custom-call | flops 4563402752 | bytes 41943040 | tf_op jit(solution)/shard_map/experts/pallas_call | solution.py:398
  67.2 0.2 collective-permute-start.21
  67.4 0.4 collective-permute-start.20
  67.8 1.4 %collective-permute-done.21 = bf16[128,2048]{1,0:T(8,128)(2,1)S(1)} collective-permute-done((bf16[128,2048]{1,0:T(8,128)(2,1)S(1)}, bf16[128,2048]{1,0:T(8,128)(2,1)S(1)}, u32[]{:S(2)}, u32[]{:S(2)}) %collective-permute-start.21) | collective-permute-done | bytes 524320 | tf_op jit(solution)/shard_map/ppermute | solution.py:170
  69.2 0.1 add_convert_fusion
  69.3 0.3 collective-permute-start.23
  69.7 0.2 collective-permute-done.20
  69.9 0.1 add_convert_fusion.1
  70.1 1.6 %collective-permute-start.26 = (bf16[32,2048]{1,0:T(8,128)(2,1)S(1)}, bf16[32,2048]{1,0:T(8,128)(2,1)S(1)}, u32[]{:S(2)}, u32[]{:S(2)}) collective-permute-start(bf16[32,2048]{1,0:T(8,128)(2,1)S(1)} %get-tuple-element.35), channel_id=1, source_target_pairs={{0,4},{4,0},{8,12},{12,8},{1,5},{5,1},{9,13},{13,9},{2,6},{6,2},{1... | collective-permute-start | bytes 393224 | tf_op jit(solution)/shard_map/ppermute | solution.py:170
  71.6 1.8 %collective-permute-start.22 = (bf16[32,2048]{1,0:T(8,128)(2,1)S(1)}, bf16[32,2048]{1,0:T(8,128)(2,1)S(1)}, u32[]{:S(2)}, u32[]{:S(2)}) collective-permute-start(bf16[32,2048]{1,0:T(8,128)(2,1)S(1)} %get-tuple-element.31), channel_id=1, source_target_pairs={{0,2},{2,0},{1,3},{3,1},{4,6},{6,4},{5,7},{7,5},{8,10},{10,8},{9,1... | collective-permute-start | bytes 393224 | tf_op jit(solution)/shard_map/ppermute | solution.py:170
  73.5 0.2 collective-permute-start.24
  73.7 2.1 %collective-permute-done.23 = bf16[32,2048]{1,0:T(8,128)(2,1)S(1)} collective-permute-done((bf16[32,2048]{1,0:T(8,128)(2,1)S(1)}, bf16[32,2048]{1,0:T(8,128)(2,1)S(1)}, u32[]{:S(2)}, u32[]{:S(2)}) %collective-permute-start.23) | collective-permute-done | bytes 131104 | tf_op jit(solution)/shard_map/ppermute | solution.py:170
  75.8 1.9 %collective-permute-start.27 = (bf16[32,2048]{1,0:T(8,128)(2,1)S(1)}, bf16[32,2048]{1,0:T(8,128)(2,1)S(1)}, u32[]{:S(2)}, u32[]{:S(2)}) collective-permute-start(bf16[32,2048]{1,0:T(8,128)(2,1)S(1)} %add_convert_fusion.5), channel_id=1, source_target_pairs={{0,2},{2,0},{1,3},{3,1},{4,6},{6,4},{5,7},{7,5},{8,10},{10,8},{9,1... | collective-permute-start | bytes 393224 | tf_op jit(solution)/shard_map/ppermute | solution.py:170
  77.6 3.2 %collective-permute-done.24 = bf16[32,2048]{1,0:T(8,128)(2,1)S(1)} collective-permute-done((bf16[32,2048]{1,0:T(8,128)(2,1)S(1)}, bf16[32,2048]{1,0:T(8,128)(2,1)S(1)}, u32[]{:S(2)}, u32[]{:S(2)}) %collective-permute-start.24) | collective-permute-done | bytes 131104 | tf_op jit(solution)/shard_map/ppermute | solution.py:170
  80.9 0.5 collective-permute-start.25
  81.4 0.9 collective-permute-done.27
  82.4 2.4 %collective-permute-start.28 = (bf16[32,2048]{1,0:T(8,128)(2,1)S(1)}, bf16[32,2048]{1,0:T(8,128)(2,1)S(1)}, u32[]{:S(2)}, u32[]{:S(2)}) collective-permute-start(bf16[32,2048]{1,0:T(8,128)(2,1)S(1)} %add_convert_fusion.3), channel_id=1, source_target_pairs={{0,8},{4,12},{8,0},{12,4},{1,9},{5,13},{9,1},{13,5},{2,10},{6,14},... | collective-permute-start | bytes 393224 | tf_op jit(solution)/shard_map/ppermute | solution.py:170
  84.8 2.1 %collective-permute-done.25 = bf16[32,2048]{1,0:T(8,128)(2,1)S(1)} collective-permute-done((bf16[32,2048]{1,0:T(8,128)(2,1)S(1)}, bf16[32,2048]{1,0:T(8,128)(2,1)S(1)}, u32[]{:S(2)}, u32[]{:S(2)}) %collective-permute-start.25) | collective-permute-done | bytes 131104 | tf_op jit(solution)/shard_map/ppermute | solution.py:170
  86.9 3.7 %collective-permute-done.28 = bf16[32,2048]{1,0:T(8,128)(2,1)S(1)} collective-permute-done((bf16[32,2048]{1,0:T(8,128)(2,1)S(1)}, bf16[32,2048]{1,0:T(8,128)(2,1)S(1)}, u32[]{:S(2)}, u32[]{:S(2)}) %collective-permute-start.28) | collective-permute-done | bytes 131104 | tf_op jit(solution)/shard_map/ppermute | solution.py:170
  90.6 0.7 add_convert_fusion.2
  (33 shorter events, 0.5 us)
Async XLA Ops:
  0.8 10.8 %collective-permute-start.2 = (bf16[128,256]{1,0:T(8,128)(2,1)S(1)}, bf16[128,256]{1,0:T(8,128)(2,1)S(1)}, u32[]{:S(2)}, u32[]{:S(2)}) collective-permute-start(bf16[128,256]{1,0:T(8,128)(2,1)S(1)} %pad_maximum_fusion.1.refs_0_), channel_id=1, source_target_pairs={{0,12},{1,13},{2,14},{3,15},{16,28},{17,29},{18,30},{19,31}} | collective-permute-start | bytes 196616 | tf_op jit(solution)/shard_map/ppermute | solution.py:175
  7.8 3.9 %collective-permute-start.1 = (bf16[128,256]{1,0:T(8,128)(2,1)S(1)}, bf16[128,256]{1,0:T(8,128)(2,1)S(1)}, u32[]{:S(2)}, u32[]{:S(2)}) collective-permute-start(bf16[128,256]{1,0:T(8,128)(2,1)S(1)} %pad_maximum_fusion.1.refs_0_), channel_id=1, source_target_pairs={{0,8},{4,12},{1,9},{5,13},{2,10},{6,14},{3,11},{7,15},{16,24},{20,... | collective-permute-start | bytes 196616 | tf_op jit(solution)/shard_map/ppermute | solution.py:175
  9.1 4.4 %collective-permute-start = (bf16[128,256]{1,0:T(8,128)(2,1)S(1)}, bf16[128,256]{1,0:T(8,128)(2,1)S(1)}, u32[]{:S(2)}, u32[]{:S(2)}) collective-permute-start(bf16[128,256]{1,0:T(8,128)(2,1)S(1)} %pad_maximum_fusion.1.refs_0_), channel_id=1, source_target_pairs={{0,4},{4,8},{8,12},{1,5},{5,9},{9,13},{2,6},{6,10},{10,14},{3,7},{... | collective-permute-start | bytes 196616 | tf_op jit(solution)/shard_map/ppermute | solution.py:175
  13.4 0.7 copy-start
  14.1 0.7 copy-start.1
  22.0 1.6 %collective-permute-start.3 = (bf16[64,2048]{1,0:T(8,128)(2,1)S(1)}, bf16[64,2048]{1,0:T(8,128)(2,1)S(1)}, u32[]{:S(2)}, u32[]{:S(2)}) collective-permute-start(bf16[64,2048]{1,0:T(8,128)(2,1)S(1)} %get-tuple-element.18), channel_id=1, source_target_pairs={{0,1},{1,0},{2,3},{3,2},{4,5},{5,4},{6,7},{7,6},{8,9},{9,8},{10,11... | collective-permute-start | bytes 786440 | tf_op jit(solution)/shard_map/ppermute | solution.py:170
  23.7 5.6 %collective-permute-start.4 = (bf16[32,2048]{1,0:T(8,128)(2,1)S(1)}, bf16[32,2048]{1,0:T(8,128)(2,1)S(1)}, u32[]{:S(2)}, u32[]{:S(2)}) collective-permute-start(bf16[32,2048]{1,0:T(8,128)(2,1)S(1)} %fusion), channel_id=1, source_target_pairs={{0,2},{2,0},{1,3},{3,1},{4,6},{6,4},{5,7},{7,5},{8,10},{10,8},{9,1... | collective-permute-start | bytes 393224 | tf_op jit(solution)/shard_map/ppermute | solution.py:170
  29.6 9.6 %collective-permute-start.6 = (bf16[32,2176]{1,0:T(8,128)(2,1)S(1)}, bf16[32,2176]{1,0:T(8,128)(2,1)S(1)}, u32[]{:S(2)}, u32[]{:S(2)}) collective-permute-start(bf16[32,2176]{1,0:T(8,128)(2,1)S(1)} %pad_maximum_fusion.refs_0_), channel_id=1, source_target_pairs={{0,8},{4,12},{8,0},{12,4},{1,9},{5,13},{9,1},{13,5},{2,10},{6,14},... | collective-permute-start | bytes 417800 | tf_op jit(solution)/shard_map/ppermute | solution.py:170
  32.9 7.7 %collective-permute-start.8 = (bf16[32,2176]{1,0:T(8,128)(2,1)S(1)}, bf16[32,2176]{1,0:T(8,128)(2,1)S(1)}, u32[]{:S(2)}, u32[]{:S(2)}) collective-permute-start(bf16[32,2176]{1,0:T(8,128)(2,1)S(1)} %pad_maximum_fusion.refs_0_), channel_id=1, source_target_pairs={{0,2},{2,0},{1,3},{3,1},{4,6},{6,4},{5,7},{7,5},{8,10},{10,8},{9,1... | collective-permute-start | bytes 417800 | tf_op jit(solution)/shard_map/ppermute | solution.py:170
  34.4 6.8 %collective-permute-start.12 = (bf16[32,2176]{1,0:T(8,128)(2,1)S(1)}, bf16[32,2176]{1,0:T(8,128)(2,1)S(1)}, u32[]{:S(2)}, u32[]{:S(2)}) collective-permute-start(bf16[32,2176]{1,0:T(8,128)(2,1)S(1)} %pad_maximum_fusion.refs_0_), channel_id=1, source_target_pairs={{0,1},{1,0},{2,3},{3,2},{4,5},{5,4},{6,7},{7,6},{8,9},{9,8},{10,11... | collective-permute-start | bytes 417800 | tf_op jit(solution)/shard_map/ppermute | solution.py:170
  34.4 7.6 %collective-permute-start.5 = (bf16[32,2176]{1,0:T(8,128)(2,1)S(1)}, bf16[32,2176]{1,0:T(8,128)(2,1)S(1)}, u32[]{:S(2)}, u32[]{:S(2)}) collective-permute-start(bf16[32,2176]{1,0:T(8,128)(2,1)S(1)} %pad_maximum_fusion.refs_0_), channel_id=1, source_target_pairs={{0,4},{4,0},{8,12},{12,8},{1,5},{5,1},{9,13},{13,9},{2,6},{6,2},{1... | collective-permute-start | bytes 417800 | tf_op jit(solution)/shard_map/ppermute | solution.py:170
  39.1 5.1 %collective-permute-start.10 = (bf16[32,2176]{1,0:T(8,128)(2,1)S(1)}, bf16[32,2176]{1,0:T(8,128)(2,1)S(1)}, u32[]{:S(2)}, u32[]{:S(2)}) collective-permute-start(bf16[32,2176]{1,0:T(8,128)(2,1)S(1)} %collective-permute-done.6.refs_2_), channel_id=1, source_target_pairs={{0,2},{2,0},{1,3},{3,1},{4,6},{6,4},{5,7},{7,5},{8,10},{10,8},{9,1... | collective-permute-start | bytes 417800 | tf_op jit(solution)/shard_map/ppermute | solution.py:170
  40.6 3.6 %collective-permute-start.16 = (bf16[32,2176]{1,0:T(8,128)(2,1)S(1)}, bf16[32,2176]{1,0:T(8,128)(2,1)S(1)}, u32[]{:S(2)}, u32[]{:S(2)}) collective-permute-start(bf16[32,2176]{1,0:T(8,128)(2,1)S(1)} %collective-permute-done.8.refs_4_), channel_id=1, source_target_pairs={{0,1},{1,0},{2,3},{3,2},{4,5},{5,4},{6,7},{7,6},{8,9},{9,8},{10,11... | collective-permute-start | bytes 417800 | tf_op jit(solution)/shard_map/ppermute | solution.py:170
  40.6 3.6 %collective-permute-start.14 = (bf16[32,2176]{1,0:T(8,128)(2,1)S(1)}, bf16[32,2176]{1,0:T(8,128)(2,1)S(1)}, u32[]{:S(2)}, u32[]{:S(2)}) collective-permute-start(bf16[32,2176]{1,0:T(8,128)(2,1)S(1)} %collective-permute-done.6.refs_2_), channel_id=1, source_target_pairs={{0,1},{1,0},{2,3},{3,2},{4,5},{5,4},{6,7},{7,6},{8,9},{9,8},{10,11... | collective-permute-start | bytes 417800 | tf_op jit(solution)/shard_map/ppermute | solution.py:170
  41.2 6.5 %collective-permute-start.7 = (bf16[32,2176]{1,0:T(8,128)(2,1)S(1)}, bf16[32,2176]{1,0:T(8,128)(2,1)S(1)}, u32[]{:S(2)}, u32[]{:S(2)}) collective-permute-start(bf16[32,2176]{1,0:T(8,128)(2,1)S(1)} %collective-permute-done.6.refs_2_), channel_id=1, source_target_pairs={{0,4},{4,0},{8,12},{12,8},{1,5},{5,1},{9,13},{13,9},{2,6},{6,2},{1... | collective-permute-start | bytes 417800 | tf_op jit(solution)/shard_map/ppermute | solution.py:170
  42.0 5.7 %collective-permute-start.9 = (bf16[32,2176]{1,0:T(8,128)(2,1)S(1)}, bf16[32,2176]{1,0:T(8,128)(2,1)S(1)}, u32[]{:S(2)}, u32[]{:S(2)}) collective-permute-start(bf16[32,2176]{1,0:T(8,128)(2,1)S(1)} %collective-permute-done.5.refs_1_), channel_id=1, source_target_pairs={{0,2},{2,0},{1,3},{3,1},{4,6},{6,4},{5,7},{7,5},{8,10},{10,8},{9,1... | collective-permute-start | bytes 417800 | tf_op jit(solution)/shard_map/ppermute | solution.py:170
  44.2 5.5 %collective-permute-start.11 = (bf16[32,2176]{1,0:T(8,128)(2,1)S(1)}, bf16[32,2176]{1,0:T(8,128)(2,1)S(1)}, u32[]{:S(2)}, u32[]{:S(2)}) collective-permute-start(bf16[32,2176]{1,0:T(8,128)(2,1)S(1)} %collective-permute-done.10.refs_6_), channel_id=1, source_target_pairs={{0,4},{4,0},{8,12},{12,8},{1,5},{5,1},{9,13},{13,9},{2,6},{6,2},{1... | collective-permute-start | bytes 417800 | tf_op jit(solution)/shard_map/ppermute | solution.py:170
  44.2 5.5 %collective-permute-start.13 = (bf16[32,2176]{1,0:T(8,128)(2,1)S(1)}, bf16[32,2176]{1,0:T(8,128)(2,1)S(1)}, u32[]{:S(2)}, u32[]{:S(2)}) collective-permute-start(bf16[32,2176]{1,0:T(8,128)(2,1)S(1)} %collective-permute-done.5.refs_1_), channel_id=1, source_target_pairs={{0,1},{1,0},{2,3},{3,2},{4,5},{5,4},{6,7},{7,6},{8,9},{9,8},{10,11... | collective-permute-start | bytes 417800 | tf_op jit(solution)/shard_map/ppermute | solution.py:170
  44.2 5.5 %collective-permute-start.18 = (bf16[32,2176]{1,0:T(8,128)(2,1)S(1)}, bf16[32,2176]{1,0:T(8,128)(2,1)S(1)}, u32[]{:S(2)}, u32[]{:S(2)}) collective-permute-start(bf16[32,2176]{1,0:T(8,128)(2,1)S(1)} %collective-permute-done.10.refs_6_), channel_id=1, source_target_pairs={{0,1},{1,0},{2,3},{3,2},{4,5},{5,4},{6,7},{7,6},{8,9},{9,8},{10,11... | collective-permute-start | bytes 417800 | tf_op jit(solution)/shard_map/ppermute | solution.py:170
  47.7 2.0 %collective-permute-start.15 = (bf16[32,2176]{1,0:T(8,128)(2,1)S(1)}, bf16[32,2176]{1,0:T(8,128)(2,1)S(1)}, u32[]{:S(2)}, u32[]{:S(2)}) collective-permute-start(bf16[32,2176]{1,0:T(8,128)(2,1)S(1)} %collective-permute-done.7.refs_3_), channel_id=1, source_target_pairs={{0,1},{1,0},{2,3},{3,2},{4,5},{5,4},{6,7},{7,6},{8,9},{9,8},{10,11... | collective-permute-start | bytes 417800 | tf_op jit(solution)/shard_map/ppermute | solution.py:170
  47.7 2.0 %collective-permute-start.17 = (bf16[32,2176]{1,0:T(8,128)(2,1)S(1)}, bf16[32,2176]{1,0:T(8,128)(2,1)S(1)}, u32[]{:S(2)}, u32[]{:S(2)}) collective-permute-start(bf16[32,2176]{1,0:T(8,128)(2,1)S(1)} %collective-permute-done.9.refs_5_), channel_id=1, source_target_pairs={{0,1},{1,0},{2,3},{3,2},{4,5},{5,4},{6,7},{7,6},{8,9},{9,8},{10,11... | collective-permute-start | bytes 417800 | tf_op jit(solution)/shard_map/ppermute | solution.py:170
  49.7 1.4 %collective-permute-start.19 = (bf16[32,2176]{1,0:T(8,128)(2,1)S(1)}, bf16[32,2176]{1,0:T(8,128)(2,1)S(1)}, u32[]{:S(2)}, u32[]{:S(2)}) collective-permute-start(bf16[32,2176]{1,0:T(8,128)(2,1)S(1)} %collective-permute-done.11.refs_7_), channel_id=1, source_target_pairs={{0,1},{1,0},{2,3},{3,2},{4,5},{5,4},{6,7},{7,6},{8,9},{9,8},{10,11... | collective-permute-start | bytes 417800 | tf_op jit(solution)/shard_map/ppermute | solution.py:170
  67.2 2.0 %collective-permute-start.21 = (bf16[128,2048]{1,0:T(8,128)(2,1)S(1)}, bf16[128,2048]{1,0:T(8,128)(2,1)S(1)}, u32[]{:S(2)}, u32[]{:S(2)}) collective-permute-start(bf16[128,2048]{1,0:T(8,128)(2,1)S(1)} %get-tuple-element.24), channel_id=1, source_target_pairs={{0,1},{1,0},{2,3},{3,2},{4,5},{5,4},{6,7},{7,6},{8,9},{9,8},{10,11... | collective-permute-start | bytes 1572872 | tf_op jit(solution)/shard_map/ppermute | solution.py:170
  67.4 2.5 %collective-permute-start.20 = (bf16[128,2048]{1,0:T(8,128)(2,1)S(1)}, bf16[128,2048]{1,0:T(8,128)(2,1)S(1)}, u32[]{:S(2)}, u32[]{:S(2)}) collective-permute-start(bf16[128,2048]{1,0:T(8,128)(2,1)S(1)} %get-tuple-element.22), channel_id=1, source_target_pairs={{0,1},{1,0},{2,3},{3,2},{4,5},{5,4},{6,7},{7,6},{8,9},{9,8},{10,11... | collective-permute-start | bytes 1572872 | tf_op jit(solution)/shard_map/ppermute | solution.py:170
  69.3 6.4 %collective-permute-start.23 = (bf16[32,2048]{1,0:T(8,128)(2,1)S(1)}, bf16[32,2048]{1,0:T(8,128)(2,1)S(1)}, u32[]{:S(2)}, u32[]{:S(2)}) collective-permute-start(bf16[32,2048]{1,0:T(8,128)(2,1)S(1)} %get-tuple-element.33), channel_id=1, source_target_pairs={{0,4},{4,0},{8,12},{12,8},{1,5},{5,1},{9,13},{13,9},{2,6},{6,2},{1... | collective-permute-start | bytes 393224 | tf_op jit(solution)/shard_map/ppermute | solution.py:170
  70.1 11.4 %collective-permute-start.26 = (bf16[32,2048]{1,0:T(8,128)(2,1)S(1)}, bf16[32,2048]{1,0:T(8,128)(2,1)S(1)}, u32[]{:S(2)}, u32[]{:S(2)}) collective-permute-start(bf16[32,2048]{1,0:T(8,128)(2,1)S(1)} %get-tuple-element.35), channel_id=1, source_target_pairs={{0,4},{4,0},{8,12},{12,8},{1,5},{5,1},{9,13},{13,9},{2,6},{6,2},{1... | collective-permute-start | bytes 393224 | tf_op jit(solution)/shard_map/ppermute | solution.py:170
  71.6 13.1 %collective-permute-start.22 = (bf16[32,2048]{1,0:T(8,128)(2,1)S(1)}, bf16[32,2048]{1,0:T(8,128)(2,1)S(1)}, u32[]{:S(2)}, u32[]{:S(2)}) collective-permute-start(bf16[32,2048]{1,0:T(8,128)(2,1)S(1)} %get-tuple-element.31), channel_id=1, source_target_pairs={{0,2},{2,0},{1,3},{3,1},{4,6},{6,4},{5,7},{7,5},{8,10},{10,8},{9,1... | collective-permute-start | bytes 393224 | tf_op jit(solution)/shard_map/ppermute | solution.py:170
  73.5 7.4 %collective-permute-start.24 = (bf16[32,2048]{1,0:T(8,128)(2,1)S(1)}, bf16[32,2048]{1,0:T(8,128)(2,1)S(1)}, u32[]{:S(2)}, u32[]{:S(2)}) collective-permute-start(bf16[32,2048]{1,0:T(8,128)(2,1)S(1)} %get-tuple-element.32), channel_id=1, source_target_pairs={{0,2},{2,0},{1,3},{3,1},{4,6},{6,4},{5,7},{7,5},{8,10},{10,8},{9,1... | collective-permute-start | bytes 393224 | tf_op jit(solution)/shard_map/ppermute | solution.py:170
  75.8 6.6 %collective-permute-start.27 = (bf16[32,2048]{1,0:T(8,128)(2,1)S(1)}, bf16[32,2048]{1,0:T(8,128)(2,1)S(1)}, u32[]{:S(2)}, u32[]{:S(2)}) collective-permute-start(bf16[32,2048]{1,0:T(8,128)(2,1)S(1)} %add_convert_fusion.5), channel_id=1, source_target_pairs={{0,2},{2,0},{1,3},{3,1},{4,6},{6,4},{5,7},{7,5},{8,10},{10,8},{9,1... | collective-permute-start | bytes 393224 | tf_op jit(solution)/shard_map/ppermute | solution.py:170
  80.9 6.0 %collective-permute-start.25 = (bf16[32,2048]{1,0:T(8,128)(2,1)S(1)}, bf16[32,2048]{1,0:T(8,128)(2,1)S(1)}, u32[]{:S(2)}, u32[]{:S(2)}) collective-permute-start(bf16[32,2048]{1,0:T(8,128)(2,1)S(1)} %add_convert_fusion.4), channel_id=1, source_target_pairs={{0,4},{4,0},{8,12},{12,8},{1,5},{5,1},{9,13},{13,9},{2,6},{6,2},{1... | collective-permute-start | bytes 393224 | tf_op jit(solution)/shard_map/ppermute | solution.py:170
  82.4 8.2 %collective-permute-start.28 = (bf16[32,2048]{1,0:T(8,128)(2,1)S(1)}, bf16[32,2048]{1,0:T(8,128)(2,1)S(1)}, u32[]{:S(2)}, u32[]{:S(2)}) collective-permute-start(bf16[32,2048]{1,0:T(8,128)(2,1)S(1)} %add_convert_fusion.3), channel_id=1, source_target_pairs={{0,8},{4,12},{8,0},{12,4},{1,9},{5,13},{9,1},{13,5},{2,10},{6,14},... | collective-permute-start | bytes 393224 | tf_op jit(solution)/shard_map/ppermute | solution.py:170

commit v5 on v4

--- a/solution.py
+++ b/solution.py
@@ -183,26 +183,41 @@
     return lax.dot_general(a, b, (((1,), (1,)), ((), ())), preferred_element_type=F32)
 
 
-def attention_kernel(sizes, place, *refs):
-    n_ctx, n_exp, n_tp, heads, part = sizes
+def own_block_kernel(sizes, place, kv_ref, ids_hbm, probs_hbm, q_hbm, w_hbm, resid_hbm, *refs):
+    n_exp, n_tp, heads, part = sizes
     rows = n_exp * n_tp * part
-    kv_refs, refs = refs[:n_ctx], refs[n_ctx:]
-    ids_ref, probs_ref, resid_hbm, q_hbm, w_hbm = refs[:5]
-    base_ref, across_ref, other_ref, routing_ref = refs[5:9]
-    k_all, v_all, q_all, att, att_rel, w_all, resid, packed, q_sem, sems = refs[9:]
-    fetch_q = []
+    q_ref, w_ref, resid_ref, out_ref, sum_ref, max_ref, routing_ref = refs[:7]
+    v_ext, ids_ref, probs_ref, packed, q_sem, sems = refs[7:]
+    fetch = [
+        pltpu.make_async_copy(ids_hbm, ids_ref, sems.at[0]),
+        pltpu.make_async_copy(probs_hbm, probs_ref, sems.at[1]),
+        pltpu.make_async_copy(resid_hbm, resid_ref, sems.at[2]),
+        pltpu.make_async_copy(w_hbm, w_ref, sems.at[3]),
+    ]
+    fetch_q = pltpu.make_async_copy(q_hbm, q_ref, q_sem)
+    fetch_q.start()
+    for copy in fetch:
+        copy.start()
+    tp = place[2]
+    v_ext[:, :HEAD_DIMENSION] = kv_ref[:, HEAD_DIMENSION:]
+    v_ext[:, HEAD_DIMENSION:] = jnp.ones((rows, HEAD_DIMENSION), BF)
+    keys = kv_ref[:, :HEAD_DIMENSION]
+    allowed = lax.broadcasted_iota(jnp.int32, (rows, rows), 1) <= lax.broadcasted_iota(
+        jnp.int32, (rows, rows), 0
+    )
+    scale = 1.0 / math.sqrt(HEAD_DIMENSION)
+    fetch_q.wait()
     for h in range(heads):
         columns = slice(h * HEAD_DIMENSION, (h + 1) * HEAD_DIMENSION)
-        fetch_q.append(
-            pltpu.make_async_copy(q_hbm.at[:, columns], q_all.at[:, columns], q_sem.at[h])
-        )
-        fetch_q[h].start()
-    fetch_w = pltpu.make_async_copy(w_hbm, w_all, sems.at[0])
-    fetch_w.start()
-    fetch_resid = pltpu.make_async_copy(resid_hbm, resid, sems.at[1])
-    fetch_resid.start()
-    ctx, exp, tp = place[0], place[1], place[2]
-
+        s = jnp.where(allowed, dot_rows(q_ref[:, columns], keys) * scale, -1e30)
+        top = jnp.max(s, axis=1, keepdims=True)
+        out = jnp.dot(jnp.exp(s - top).astype(BF), v_ext[...], preferred_element_type=F32)
+        out_ref[:, columns] = out[:, :HEAD_DIMENSION]
+        sum_ref[:, columns] = out[:, HEAD_DIMENSION:]
+        max_ref[:, h : h + 1] = top
+
+    fetch[0].wait()
+    fetch[1].wait()
     block = n_tp * part
     ids = ids_ref[...]
     probs = probs_ref[...]
@@ -227,85 +242,123 @@
     packed[: 4 * TOPK, :block] = fields
     packed[...] = packed[...].T
     routing_ref[...] = packed[pl.ds(pl.multiple_of(tp * part, part), part), :].astype(BF)
-
-    for z in range(n_ctx):
+    fetch[2].wait()
+    fetch[3].wait()
+
+
+def own_block(place, kv, expert_ids, router_probs, queries, out_weight, resid, n_exp, n_tp):
+    rows, width = queries.shape
+    heads = width // HEAD_DIMENSION
+    part, model = resid.shape
+    block = expert_ids.shape[0]
+    vmem = pl.BlockSpec(memory_space=pltpu.VMEM)
+    hbm = pl.BlockSpec(memory_space=pltpu.HBM)
+    return pl.pallas_call(
+        functools.partial(own_block_kernel, (n_exp, n_tp, heads, part)),
+        out_shape=(
+            jax.ShapeDtypeStruct((rows, width), BF),
+            jax.ShapeDtypeStruct((width, model), BF),
+            jax.ShapeDtypeStruct((part, model), BF),
+            jax.ShapeDtypeStruct((rows, width), F32),
+            jax.ShapeDtypeStruct((rows, width), F32),
+            jax.ShapeDtypeStruct((rows, LANES), F32),
+            jax.ShapeDtypeStruct((part, LANES), BF),
+        ),
+        in_specs=[pl.BlockSpec(memory_space=pltpu.SMEM), vmem] + [hbm] * 5,
+        out_specs=(vmem,) * 7,
+        scratch_shapes=[
+            pltpu.VMEM((rows, 2 * HEAD_DIMENSION), BF),
+            pltpu.VMEM((TOPK, block), jnp.int32),
+            pltpu.VMEM((TOPK, block), F32),
+            pltpu.VMEM((LANES, LANES), F32),
+            pltpu.SemaphoreType.DMA,
+            pltpu.SemaphoreType.DMA((4,)),
+        ],
+        compiler_params=pltpu.CompilerParams(vmem_limit_bytes=20 * MIB),
+        cost_estimate=pl.CostEstimate(
+            flops=6 * rows * width * rows,
+            bytes_accessed=2 * (rows * width + width * model + rows * model),
+            transcendentals=rows * rows * heads,
+        ),
+        name="own_block",
+    )(place, kv, *map(in_hbm, (expert_ids.T, router_probs.T, queries, out_weight, resid)))
+
+
+def attention_kernel(sizes, place, *refs):
+    n_ctx, n_exp, n_tp, heads, part = sizes
+    rows = n_exp * n_tp * part
+    kv_refs, refs = refs[: n_ctx - 1], refs[n_ctx - 1 :]
+    q_ref, w_ref, resid_ref, out_ref, sum_ref, max_ref = refs[:6]
+    base_ref, across_ref, other_ref = refs[6:9]
+    k_all, v_all, att, att_rel = refs[9:]
+    ctx, exp, tp = place[0], place[1], place[2]
+    for z in range(n_ctx - 1):
         k_all[z * rows : (z + 1) * rows, :] = kv_refs[z][:, :HEAD_DIMENSION]
         v_all[z * rows : (z + 1) * rows, :HEAD_DIMENSION] = kv_refs[z][:, HEAD_DIMENSION:]
-    v_all[:, HEAD_DIMENSION:] = jnp.ones((n_ctx * rows, HEAD_DIMENSION), BF)
-    column = lax.broadcasted_iota(jnp.int32, (rows, n_ctx * rows), 1)
-    row = lax.broadcasted_iota(jnp.int32, (rows, n_ctx * rows), 0)
-    allowed = (column <= row) | ((column >= rows) & (column < (ctx + 1) * rows))
+    v_all[:, HEAD_DIMENSION:] = jnp.ones(((n_ctx - 1) * rows, HEAD_DIMENSION), BF)
+    allowed = lax.broadcasted_iota(jnp.int32, (1, (n_ctx - 1) * rows), 1) < ctx * rows
     scale = 1.0 / math.sqrt(HEAD_DIMENSION)
     for h in range(heads):
         columns = slice(h * HEAD_DIMENSION, (h + 1) * HEAD_DIMENSION)
-        fetch_q[h].wait()
-        s = dot_rows(q_all[:, columns], k_all[...])
-        s = jnp.where(allowed, s * scale, -1e30)
-        weights = jnp.exp(s - jnp.max(s, axis=1, keepdims=True))
-        out = jnp.dot(weights.astype(BF), v_all[...], preferred_element_type=F32)
-        att[:, columns] = (out[:, :HEAD_DIMENSION] / out[:, HEAD_DIMENSION:]).astype(BF)
+        s = jnp.where(allowed, dot_rows(q_ref[:, columns], k_all[...]) * scale, -1e30)
+        own_top = max_ref[:, h : h + 1]
+        top = jnp.maximum(own_top, jnp.max(s, axis=1, keepdims=True))
+        keep = jnp.exp(own_top - top)
+        out = jnp.dot(jnp.exp(s - top).astype(BF), v_all[...], preferred_element_type=F32)
+        total = sum_ref[:, columns] * keep + out[:, HEAD_DIMENSION:]
+        out = out_ref[:, columns] * keep + out[:, :HEAD_DIMENSION]
+        att[:, columns] = (out / total).astype(BF)
     for t in range(n_tp):
         for x in range(n_exp):
             owner = lax.rem(exp + x, n_exp) * n_tp + lax.rem(tp + t, n_tp)
             source = pl.ds(pl.multiple_of(owner * part, part), part)
             at = (t * n_exp + x) * part
             att_rel[at : at + part, :] = att[source, :]
-    fetch_w.wait()
-    projected = jnp.dot(att_rel[...], w_all[...], preferred_element_type=F32)
-    fetch_resid.wait()
-    base_ref[...] = resid[...].astype(F32) + projected[:part]
+    projected = jnp.dot(att_rel[...], w_ref[...], preferred_element_type=F32)
+    base_ref[...] = resid_ref[...].astype(F32) + projected[:part]
     across_ref[...] = projected[part : 2 * part].astype(BF)
     other_ref[...] = projected[2 * part :].astype(BF)
 
 
-def attend_project(place, pieces, expert_ids, router_probs, resid, queries, out_weight, n_exp, n_tp):
+def attend_project(place, pieces, own, n_exp, n_tp):
+    queries, out_weight, resid = own[:3]
     rows, width = queries.shape
-    n_ctx, heads = len(pieces), width // HEAD_DIMENSION
+    n_ctx, heads = len(pieces) + 1, width // HEAD_DIMENSION
     part, model = resid.shape
-    block = expert_ids.shape[0]
     vmem = pl.BlockSpec(memory_space=pltpu.VMEM)
-    hbm = pl.BlockSpec(memory_space=pltpu.HBM)
     return pl.pallas_call(
         functools.partial(attention_kernel, (n_ctx, n_exp, n_tp, heads, part)),
         out_shape=(
             jax.ShapeDtypeStruct((part, model), F32),
             jax.ShapeDtypeStruct((part, model), BF),
             jax.ShapeDtypeStruct((2 * part, model), BF),
-            jax.ShapeDtypeStruct((part, LANES), BF),
-        ),
-        in_specs=[pl.BlockSpec(memory_space=pltpu.SMEM)] + [vmem] * (n_ctx + 2) + [hbm] * 3,
-        out_specs=(vmem,) * 4,
+        ),
+        in_specs=[pl.BlockSpec(memory_space=pltpu.SMEM)] + [vmem] * (n_ctx - 1 + len(own)),
+        out_specs=(vmem,) * 3,
         scratch_shapes=[
-            pltpu.VMEM((n_ctx * rows, HEAD_DIMENSION), BF),
-            pltpu.VMEM((n_ctx * rows, 2 * HEAD_DIMENSION), BF),
+            pltpu.VMEM(((n_ctx - 1) * rows, HEAD_DIMENSION), BF),
+            pltpu.VMEM(((n_ctx - 1) * rows, 2 * HEAD_DIMENSION), BF),
             pltpu.VMEM((rows, width), BF),
             pltpu.VMEM((rows, width), BF),
-            pltpu.VMEM((rows, width), BF),
-            pltpu.VMEM((width, model), BF),
-            pltpu.VMEM((part, model), BF),
-            pltpu.VMEM((LANES, LANES), F32),
-            pltpu.SemaphoreType.DMA((heads,)),
-            pltpu.SemaphoreType.DMA((2,)),
         ],
-        compiler_params=pltpu.CompilerParams(vmem_limit_bytes=32 * MIB),
+        compiler_params=pltpu.CompilerParams(vmem_limit_bytes=20 * MIB),
         cost_estimate=pl.CostEstimate(
-            flops=2 * rows * width * (2 * n_ctx * rows + model),
+            flops=2 * rows * width * (3 * (n_ctx - 1) * rows + model),
             bytes_accessed=2 * (rows * width + width * model + rows * model),
             transcendentals=rows * n_ctx * rows * heads,
         ),
         name="attend_project",
-    )(place, *pieces, expert_ids.T, router_probs.T, *map(in_hbm, (resid, queries, out_weight)))
-
-
-def expert_kernel(n_pieces, depth, experts, first_ref, *refs):
+    )(place, *pieces, *own)
+
+
+def expert_kernel(n_pieces, order, sizes, depth, experts, first_ref, *refs):
     pieces, (wg_hbm, wu_hbm, wd_hbm) = refs[:n_pieces], refs[n_pieces : n_pieces + 3]
     outs = refs[n_pieces + 3 : n_pieces + 7]
     x_all, packed, pick_all, scale_all, out_all, wgu, wd, act, sems = refs[n_pieces + 7 :]
     tokens = x_all.shape[0]
     slots = pick_all.shape[0] // experts
     _, _, halves, hidden, model = wgu.shape
-    part = tokens // n_pieces
-    blocks = n_pieces // 2
+    part, blocks = sizes
 
     def copies(e):
         slot = lax.rem(e, depth)
@@ -341,9 +394,10 @@
 
     for e in range(min(depth - 1, experts)):
         start(e)
-    for i, piece in enumerate(pieces):
-        x_all[i * part : (i + 1) * part, :] = piece[:, :model]
-        packed[i * part : (i + 1) * part, :] = piece[:, model:].astype(F32)
+    for i, (piece, at) in enumerate(order):
+        rows = slice(at * part, (at + 1) * part)
+        x_all[i * part : (i + 1) * part, :] = pieces[piece][rows, :model]
+        packed[i * part : (i + 1) * part, :] = pieces[piece][rows, model:].astype(F32)
     fields = packed[...].T
     ids, ranks = fields[:TOPK], fields[TOPK : 2 * TOPK]
     gates = fields[2 * TOPK : 3 * TOPK] + fields[3 * TOPK : 4 * TOPK]
@@ -385,18 +439,20 @@
         ).astype(BF)
 
 
-def cube_experts(first, pieces, w_gate, w_up, w_down, slots):
+def cube_experts(first, pieces, order, part, w_gate, w_up, w_down, slots):
     rows, hidden, model = w_down.shape
     halves = 2
     experts = rows // halves
-    tokens = len(pieces) * pieces[0].shape[0]
+    tokens = len(order) * part
     depth = min(4, experts)
     vmem = pl.BlockSpec(memory_space=pltpu.VMEM)
     hbm = pl.BlockSpec(memory_space=pltpu.HBM)
 
     out = jax.ShapeDtypeStruct((tokens // 4, model), BF)
     return pl.pallas_call(
-        functools.partial(expert_kernel, len(pieces), depth, experts),
+        functools.partial(
+            expert_kernel, len(pieces), order, (part, len(order) // 2), depth, experts
+        ),
         out_shape=(out,) * 4,
         in_specs=[pl.BlockSpec(memory_space=pltpu.SMEM)] + [vmem] * len(pieces) + [hbm] * 3,
         out_specs=(vmem,) * 4,
@@ -438,15 +494,15 @@
     here = add(mine, flip(other, "tp", 1))
     across = [across[z * part : (z + 1) * part] for z in range(4)]
     here = [here[z * part : (z + 1) * part] for z in range(4)]
+    near = flip(across[1], "exp", 1)
     far_across = add(across[2], flip(across[3], "ctx", 1))
+    far_across, here[3], here[1] = lax.optimization_barrier((far_across, here[3], here[1]))
+    far = flip(far_across, "exp", 1)
+    last = flip(here[3], "ctx", 1)
+    near = add(here[1], near)
+    near, here[2], across[0] = lax.optimization_barrier((near, here[2], across[0]))
+    near = flip(near, "ctx", 1)
     own = flip(across[0], "exp", 1)
-    near = flip(across[1], "exp", 1)
-    last = flip(here[3], "ctx", 1)
-    far_across, here[1] = lax.optimization_barrier((far_across, here[1]))
-    far = flip(far_across, "exp", 1)
-    near = add(here[1], near)
-    near, here[2] = lax.optimization_barrier((near, here[2]))
-    near = flip(near, "ctx", 1)
     far = flip(add(here[2], last, far), "ctx", 2)
     return here[0].astype(F32) + own.astype(F32) + near.astype(F32) + far.astype(F32)
 
@@ -473,10 +529,11 @@
     key_head = lax.dynamic_slice_in_dim(keys, shared * HEAD_DIMENSION, HEAD_DIMENSION, 1)
     value_head = lax.dynamic_slice_in_dim(values, shared * HEAD_DIMENSION, HEAD_DIMENSION, 1)
     kv = jnp.concatenate([key_head, value_head], axis=1)
-    kv_pieces = [kv] + [from_earlier(kv, "ctx", z) for z in range(1, n_ctx)]
-    base, across, other, routing = attend_project(
-        place, kv_pieces, expert_ids, router_probs, resid, queries, out_weight, n_exp, n_tp
-    )
+    kv_pieces = [from_earlier(kv, "ctx", z) for z in range(1, n_ctx)]
+    *own, routing = own_block(
+        place, kv, expert_ids, router_probs, queries, out_weight, resid, n_exp, n_tp
+    )
+    base, across, other = attend_project(place, kv_pieces, own, n_exp, n_tp)
 
     other = flip(other, "tp", 1).astype(F32)
     across = flip((across.astype(F32) + other[part:]).astype(BF), "exp", 1)
@@ -491,11 +548,18 @@
     far_across = flip(far, "exp", 1)
     near_across = flip(near, "exp", 1)
     last = flip(far, "ctx", 1)
-    last_across = flip(far_across, "ctx", 1)
-    chip = [normed, near, far, last, across, near_across, far_across, last_across]
-    pieces = chip + [flip(piece, "tp", 1) for piece in chip]
+    early = jnp.concatenate([normed, near, far, across, near_across, far_across])
+    early, far_onward = lax.optimization_barrier((early, far_across))
+    last_across = flip(far_onward, "ctx", 1)
+    early_other = flip(early, "tp", 1)
+    late_other = flip(jnp.concatenate([last, last_across]), "tp", 1)
+    pieces = [normed, near, far, last, across, near_across, far_across, last_across]
+    order = [(i, 0) for i in range(8)] + [
+        (8, 0), (8, 1), (8, 2), (9, 0), (8, 3), (8, 4), (8, 5), (9, 1)
+    ]
     sums = cube_experts(
-        first.astype(jnp.int32).reshape(1), pieces, w_gate, w_up, w_down, slots
+        first.astype(jnp.int32).reshape(1), pieces + [early_other, late_other], order, part,
+        w_gate, w_up, w_down, slots,
     )
     return (hidden + sums_back(*sums, part)).astype(BF)
 

time: 91.6 us -> 94 us (1.026)
  waiting for transfers between devices: 33.6 us -> 37.8 us
  starting transfers between devices: 30.5 us -> 26.4 us
  local copies, waits for them, and re-layouts: 2.21 us -> 4.15 us
    ppermute x26 -> x20, waiting for transfers between devices: 31.8 us -> 37.8 us  [flip(): lax.ppermute(x, axis, [(i, i ^ bit) for i in range(lax.axis_size(axis))])]
    pallas_call x1, Pallas kernels: 7.2 us -> 2.96 us  [attend_project(): pl.pallas_call(functools.partial(attention_kernel, (n_ctx, n_exp, n_tp, h...]
    ppermute x26 -> x20, starting transfers between devices: 19.8 us -> 15.6 us  [flip(): lax.ppermute(x, axis, [(i, i ^ bit) for i in range(lax.axis_size(axis))])]
    pallas_call x1 -> x2, Pallas kernels: 16.1 us -> 20.1 us  [the longest x1 16.1 us: cube_experts(): pl.pallas_call(functools.partial(expert_kernel, len(pieces), order, (part...]
    ppermute x3, waiting for transfers between devices: 1.8 us -> 0.01 us  [from_earlier(): return lax.ppermute(x, axis, [(i, i + steps) for i in range(size - steps)])]
    unnamed x4, local copies, waits for them, and re-layouts: 1.37 us -> 2.65 us
  transfers between devices with their start and end apart: 29 -> 23, of which waited for: 16 -> 15; matrix products, arithmetic and copies ran while one was open for 1% -> 3% of each run, Pallas kernels for 0% -> 4%
where the time goes in v5:
time: 94 us; the launch traced here: 93.7 us
  waiting for transfers between devices  37.8 us (40%)
  starting transfers between devices  26.4 us (28%)
  Pallas kernels  23 us (24%)
  local copies, waits for them, and re-layouts  4.15 us (4%)
  other arithmetic  2.23 us (2%)
    ppermute x20, waiting for transfers between devices, flip(): lax.ppermute(x, axis, [(i, i ^ bit) for i in range(lax.axis_size(axis))])  37.8 us
    pallas_call x1, Pallas kernels, cube_experts(): pl.pallas_call(functools.partial(expert_kernel, len(pieces), order, (part...  16.1 us
    ppermute x20, starting transfers between devices, flip(): lax.ppermute(x, axis, [(i, i ^ bit) for i in range(lax.axis_size(axis))])  15.6 us
    ppermute x3, starting transfers between devices, from_earlier(): return lax.ppermute(x, axis, [(i, i + steps) for i in range(size - steps)])  10.7 us
    pallas_call x1, Pallas kernels, own_block(): pl.pallas_call(functools.partial(own_block_kernel, (n_exp, n_tp, heads, p...  3.97 us
    pallas_call x1, Pallas kernels, attend_project(): pl.pallas_call(functools.partial(attention_kernel, (n_ctx, n_exp, n_tp, h...  2.96 us
    unnamed x4, local copies, waits for them, and re-layouts  2.65 us
  transfers between devices with their start and end apart: 23, of which 15 were waited for; matrix products, arithmetic and copies ran while one was open for 3% of the time, Pallas kernels for 4%

profile of v5, /device:TPU:0, one launch (start us, length us, event | category | flops | bytes accessed | tf_op | source)
XLA Modules:
  0.0 93.7 jit_solution(15307822511806613845)
XLA Ops:
  0.0 0.8 constant_dynamic-slice_fusion
  0.8 7.0 %collective-permute-start.2 = (bf16[128,256]{1,0:T(8,128)(2,1)S(1)}, bf16[128,256]{1,0:T(8,128)(2,1)S(1)}, u32[]{:S(2)}, u32[]{:S(2)}) collective-permute-start(bf16[128,256]{1,0:T(8,128)(2,1)S(1)} %pad_maximum_fusion.2.kv_ref), channel_id=1, source_target_pairs={{0,12},{1,13},{2,14},{3,15},{16,28},{17,29},{18,30},{19,31}} | collective-permute-start | bytes 196616 | tf_op jit(solution)/shard_map/ppermute | solution.py:175
  7.8 1.3 %collective-permute-start.1 = (bf16[128,256]{1,0:T(8,128)(2,1)S(1)}, bf16[128,256]{1,0:T(8,128)(2,1)S(1)}, u32[]{:S(2)}, u32[]{:S(2)}) collective-permute-start(bf16[128,256]{1,0:T(8,128)(2,1)S(1)} %pad_maximum_fusion.2.kv_ref), channel_id=1, source_target_pairs={{0,8},{4,12},{1,9},{5,13},{2,10},{6,14},{3,11},{7,15},{16,24},{20,... | collective-permute-start | bytes 196616 | tf_op jit(solution)/shard_map/ppermute | solution.py:175
  9.1 2.5 %collective-permute-start = (bf16[128,256]{1,0:T(8,128)(2,1)S(1)}, bf16[128,256]{1,0:T(8,128)(2,1)S(1)}, u32[]{:S(2)}, u32[]{:S(2)}) collective-permute-start(bf16[128,256]{1,0:T(8,128)(2,1)S(1)} %pad_maximum_fusion.2.kv_ref), channel_id=1, source_target_pairs={{0,4},{4,8},{8,12},{1,5},{5,9},{9,13},{2,6},{6,10},{10,14},{3,7},{... | collective-permute-start | bytes 196616 | tf_op jit(solution)/shard_map/ppermute | solution.py:175
  11.6 4.0 %own_block.1 = (bf16[128,1024]{1,0:T(8,128)(2,1)S(1)}, bf16[1024,2048]{1,0:T(8,128)(2,1)S(1)}, bf16[32,2048]{1,0:T(8,128)(2,1)S(1)}, f32[128,1024]{1,0:T(8,128)S...) custom-call(s32[3]{0:T(128)S(1)} %pad_add_fusion.place, ...), custom_call_target="tpu_custom_call" | custom-call | flops 100663296 | bytes 4980736 | tf_op jit(solution)/shard_map/own_block/pallas_call | solution.py:256
  15.6 3.0 %attend_project.1 = (f32[32,2048]{1,0:T(8,128)S(1)}, bf16[32,2048]{1,0:T(8,128)(2,1)S(1)}, bf16[64,2048]{1,0:T(8,128)(2,1)S(1)}) custom-call(s32[3]{0:T(128)S(1)} %pad_add_fusion.place, bf16[128,256]{1,0:T(8,128)(2,1)S(1)} %collective-permute-done.refs_0_, bf16[128,256]{1,0:T(8,128)(2,1)S(1)} %collective-permute-done.1.refs_1_, ...), custom_call_target="tpu_custom_call" | custom-call | flops 838860800 | bytes 4980736 | tf_op jit(solution)/shard_map/attend_project/pallas_call | solution.py:329
  18.7 1.5 %collective-permute-done.3 = bf16[64,2048]{1,0:T(8,128)(2,1)S(1)} collective-permute-done((bf16[64,2048]{1,0:T(8,128)(2,1)S(1)}, bf16[64,2048]{1,0:T(8,128)(2,1)S(1)}, u32[]{:S(2)}, u32[]{:S(2)}) %collective-permute-start.3) | collective-permute-done | bytes 262176 | tf_op jit(solution)/shard_map/ppermute | solution.py:170
  20.3 1.6 %collective-permute-start.4 = (bf16[32,2048]{1,0:T(8,128)(2,1)S(1)}, bf16[32,2048]{1,0:T(8,128)(2,1)S(1)}, u32[]{:S(2)}, u32[]{:S(2)}) collective-permute-start(bf16[32,2048]{1,0:T(8,128)(2,1)S(1)} %fusion), channel_id=1, source_target_pairs={{0,2},{2,0},{1,3},{3,1},{4,6},{6,4},{5,7},{7,5},{8,10},{10,8},{9,1... | collective-permute-start | bytes 393224 | tf_op jit(solution)/shard_map/ppermute | solution.py:170
  21.8 4.1 %collective-permute-done.4 = bf16[32,2048]{1,0:T(8,128)(2,1)S(1)} collective-permute-done((bf16[32,2048]{1,0:T(8,128)(2,1)S(1)}, bf16[32,2048]{1,0:T(8,128)(2,1)S(1)}, u32[]{:S(2)}, u32[]{:S(2)}) %collective-permute-start.4) | collective-permute-done | bytes 131104 | tf_op jit(solution)/shard_map/ppermute | solution.py:170
  25.9 0.2 multiply_reduce_fusion
  26.1 0.7 constant_dynamic-update-slice_fusion.5
  26.8 1.1 %collective-permute-start.6 = (bf16[32,2176]{1,0:T(8,128)(2,1)S(1)}, bf16[32,2176]{1,0:T(8,128)(2,1)S(1)}, u32[]{:S(2)}, u32[]{:S(2)}) collective-permute-start(bf16[32,2176]{1,0:T(8,128)(2,1)S(1)} %get-tuple-element.58.refs_0_), channel_id=1, source_target_pairs={{0,8},{4,12},{8,0},{12,4},{1,9},{5,13},{9,1},{13,5},{2,10},{6,14},... | collective-permute-start | bytes 417800 | tf_op jit(solution)/shard_map/ppermute | solution.py:170
  27.9 0.5 collective-permute-start.5
  28.4 1.5 %collective-permute-start.8 = (bf16[32,2176]{1,0:T(8,128)(2,1)S(1)}, bf16[32,2176]{1,0:T(8,128)(2,1)S(1)}, u32[]{:S(2)}, u32[]{:S(2)}) collective-permute-start(bf16[32,2176]{1,0:T(8,128)(2,1)S(1)} %get-tuple-element.58.refs_0_), channel_id=1, source_target_pairs={{0,2},{2,0},{1,3},{3,1},{4,6},{6,4},{5,7},{7,5},{8,10},{10,8},{9,1... | collective-permute-start | bytes 417800 | tf_op jit(solution)/shard_map/ppermute | solution.py:170
  29.9 5.4 %collective-permute-done.6.refs_2_ = bf16[32,2176]{1,0:T(8,128)(2,1)S(1)} collective-permute-done((bf16[32,2176]{1,0:T(8,128)(2,1)S(1)}, bf16[32,2176]{1,0:T(8,128)(2,1)S(1)}, u32[]{:S(2)}, u32[]{:S(2)}) %collective-permute-start.6) | collective-permute-done | bytes 139296 | tf_op jit(solution)/shard_map/ppermute | solution.py:170
  35.2 1.5 %collective-permute-start.10 = (bf16[32,2176]{1,0:T(8,128)(2,1)S(1)}, bf16[32,2176]{1,0:T(8,128)(2,1)S(1)}, u32[]{:S(2)}, u32[]{:S(2)}) collective-permute-start(bf16[32,2176]{1,0:T(8,128)(2,1)S(1)} %collective-permute-done.6.refs_2_), channel_id=1, source_target_pairs={{0,2},{2,0},{1,3},{3,1},{4,6},{6,4},{5,7},{7,5},{8,10},{10,8},{9,1... | collective-permute-start | bytes 417800 | tf_op jit(solution)/shard_map/ppermute | solution.py:170
  36.7 0.5 collective-permute-start.9
  37.3 0.7 constant_dynamic-update-slice_fusion.4
  37.9 0.7 constant_dynamic-update-slice_fusion.3
  38.6 0.7 constant_dynamic-update-slice_fusion.2
  39.3 4.1 %collective-permute-done.9.refs_5_ = bf16[32,2176]{1,0:T(8,128)(2,1)S(1)} collective-permute-done((bf16[32,2176]{1,0:T(8,128)(2,1)S(1)}, bf16[32,2176]{1,0:T(8,128)(2,1)S(1)}, u32[]{:S(2)}, u32[]{:S(2)}) %collective-permute-start.9) | collective-permute-done | bytes 139296 | tf_op jit(solution)/shard_map/ppermute | solution.py:170
  43.4 0.7 constant_dynamic-update-slice_fusion.1
  44.1 0.7 constant_dynamic-update-slice_fusion
  44.7 2.0 %collective-permute-start.11 = (bf16[32,2176]{1,0:T(8,128)(2,1)S(1)}, bf16[32,2176]{1,0:T(8,128)(2,1)S(1)}, u32[]{:S(2)}, u32[]{:S(2)}) collective-permute-start(bf16[32,2176]{1,0:T(8,128)(2,1)S(1)} %collective-permute-done.10.refs_6_), channel_id=1, source_target_pairs={{0,4},{4,0},{8,12},{12,8},{1,5},{5,1},{9,13},{13,9},{2,6},{6,2},{1... | collective-permute-start | bytes 417800 | tf_op jit(solution)/shard_map/ppermute | solution.py:170
  46.8 4.4 %collective-permute-done.7.refs_3_ = bf16[32,2176]{1,0:T(8,128)(2,1)S(1)} collective-permute-done((bf16[32,2176]{1,0:T(8,128)(2,1)S(1)}, bf16[32,2176]{1,0:T(8,128)(2,1)S(1)}, u32[]{:S(2)}, u32[]{:S(2)}) %collective-permute-start.7) | collective-permute-done | bytes 139296 | tf_op jit(solution)/shard_map/ppermute | solution.py:170
  51.2 2.6 %collective-permute-done.11.refs_7_ = bf16[32,2176]{1,0:T(8,128)(2,1)S(1)} collective-permute-done((bf16[32,2176]{1,0:T(8,128)(2,1)S(1)}, bf16[32,2176]{1,0:T(8,128)(2,1)S(1)}, u32[]{:S(2)}, u32[]{:S(2)}) %collective-permute-start.11) | collective-permute-done | bytes 139296 | tf_op jit(solution)/shard_map/ppermute | solution.py:170
  53.9 1.5 %collective-permute-done.13.refs_9_ = bf16[64,2176]{1,0:T(8,128)(2,1)S(1)} collective-permute-done((bf16[64,2176]{1,0:T(8,128)(2,1)S(1)}, bf16[64,2176]{1,0:T(8,128)(2,1)S(1)}, u32[]{:S(2)}, u32[]{:S(2)}) %collective-permute-start.13) | collective-permute-done | bytes 278560 | tf_op jit(solution)/shard_map/ppermute | solution.py:170
  55.5 16.1 %experts.1 = (bf16[128,2048]{1,0:T(8,128)(2,1)S(1)}, bf16[128,2048]{1,0:T(8,128)(2,1)S(1)}, bf16[128,2048]{1,0:T(8,128)(2,1)S(1)}, bf16[128,2048]{1,0:T(8,128)(2,1)S(1)}) custom-call(s32[1]{0:T(128)} %bitcast.5.first_ref, bf16[32,2176]{1,0:T(8,128)(2,1)S(1)} %get-tuple-element.58.refs_0_, bf16[32,2176]{1,0:T(8,128)(2,1)S(1)} %collective-permute-done.5.refs_1_, ...), custom_call_target="tpu_custom_call" | custom-call | flops 4563402752 | bytes 41943040 | tf_op jit(solution)/shard_map/experts/pallas_call | solution.py:452
  71.6 0.2 collective-permute-start.15
  71.8 0.4 collective-permute-start.14
  72.1 1.4 %collective-permute-done.15 = bf16[128,2048]{1,0:T(8,128)(2,1)S(1)} collective-permute-done((bf16[128,2048]{1,0:T(8,128)(2,1)S(1)}, bf16[128,2048]{1,0:T(8,128)(2,1)S(1)}, u32[]{:S(2)}, u32[]{:S(2)}) %collective-permute-start.15) | collective-permute-done | bytes 524320 | tf_op jit(solution)/shard_map/ppermute | solution.py:170
  73.5 0.1 add_convert_fusion
  73.7 0.3 collective-permute-start.16
  74.0 0.2 collective-permute-done.14
  74.3 0.1 add_convert_fusion.1
  74.5 1.5 %collective-permute-start.17 = (bf16[32,2048]{1,0:T(8,128)(2,1)S(1)}, bf16[32,2048]{1,0:T(8,128)(2,1)S(1)}, u32[]{:S(2)}, u32[]{:S(2)}) collective-permute-start(bf16[32,2048]{1,0:T(8,128)(2,1)S(1)} %get-tuple-element.52), channel_id=1, source_target_pairs={{0,2},{2,0},{1,3},{3,1},{4,6},{6,4},{5,7},{7,5},{8,10},{10,8},{9,1... | collective-permute-start | bytes 393224 | tf_op jit(solution)/shard_map/ppermute | solution.py:170
  76.0 3.3 %collective-permute-done.16 = bf16[32,2048]{1,0:T(8,128)(2,1)S(1)} collective-permute-done((bf16[32,2048]{1,0:T(8,128)(2,1)S(1)}, bf16[32,2048]{1,0:T(8,128)(2,1)S(1)}, u32[]{:S(2)}, u32[]{:S(2)}) %collective-permute-start.16) | collective-permute-done | bytes 131104 | tf_op jit(solution)/shard_map/ppermute | solution.py:170
  79.3 0.4 collective-permute-start.20
  79.7 1.5 %collective-permute-start.21 = (bf16[32,2048]{1,0:T(8,128)(2,1)S(1)}, bf16[32,2048]{1,0:T(8,128)(2,1)S(1)}, u32[]{:S(2)}, u32[]{:S(2)}) collective-permute-start(bf16[32,2048]{1,0:T(8,128)(2,1)S(1)} %add_convert_fusion.5), channel_id=1, source_target_pairs={{0,2},{2,0},{1,3},{3,1},{4,6},{6,4},{5,7},{7,5},{8,10},{10,8},{9,1... | collective-permute-start | bytes 393224 | tf_op jit(solution)/shard_map/ppermute | solution.py:170
  81.2 0.6 collective-permute-start.18
  81.8 1.7 %collective-permute-start.19 = (bf16[32,2048]{1,0:T(8,128)(2,1)S(1)}, bf16[32,2048]{1,0:T(8,128)(2,1)S(1)}, u32[]{:S(2)}, u32[]{:S(2)}) collective-permute-start(bf16[32,2048]{1,0:T(8,128)(2,1)S(1)} %add_convert_fusion.4), channel_id=1, source_target_pairs={{0,4},{4,0},{8,12},{12,8},{1,5},{5,1},{9,13},{13,9},{2,6},{6,2},{1... | collective-permute-start | bytes 393224 | tf_op jit(solution)/shard_map/ppermute | solution.py:170
  83.6 1.9 %collective-permute-done.20 = bf16[32,2048]{1,0:T(8,128)(2,1)S(1)} collective-permute-done((bf16[32,2048]{1,0:T(8,128)(2,1)S(1)}, bf16[32,2048]{1,0:T(8,128)(2,1)S(1)}, u32[]{:S(2)}, u32[]{:S(2)}) %collective-permute-start.20) | collective-permute-done | bytes 131104 | tf_op jit(solution)/shard_map/ppermute | solution.py:170
  85.5 0.1 collective-permute-done.21
  85.7 0.2 collective-permute-start.22
  85.8 1.2 %collective-permute-done.18 = bf16[32,2048]{1,0:T(8,128)(2,1)S(1)} collective-permute-done((bf16[32,2048]{1,0:T(8,128)(2,1)S(1)}, bf16[32,2048]{1,0:T(8,128)(2,1)S(1)}, u32[]{:S(2)}, u32[]{:S(2)}) %collective-permute-start.18) | collective-permute-done | bytes 131104 | tf_op jit(solution)/shard_map/ppermute | solution.py:170
  87.0 1.6 %collective-permute-done.19 = bf16[32,2048]{1,0:T(8,128)(2,1)S(1)} collective-permute-done((bf16[32,2048]{1,0:T(8,128)(2,1)S(1)}, bf16[32,2048]{1,0:T(8,128)(2,1)S(1)}, u32[]{:S(2)}, u32[]{:S(2)}) %collective-permute-start.19) | collective-permute-done | bytes 131104 | tf_op jit(solution)/shard_map/ppermute | solution.py:170
  88.6 4.4 %collective-permute-done.22 = bf16[32,2048]{1,0:T(8,128)(2,1)S(1)} collective-permute-done((bf16[32,2048]{1,0:T(8,128)(2,1)S(1)}, bf16[32,2048]{1,0:T(8,128)(2,1)S(1)}, u32[]{:S(2)}, u32[]{:S(2)}) %collective-permute-start.22) | collective-permute-done | bytes 131104 | tf_op jit(solution)/shard_map/ppermute | solution.py:170
  93.0 0.7 add_convert_fusion.2
  (24 shorter events, 0.6 us)
Async XLA Ops:
  0.8 14.8 %collective-permute-start.2 = (bf16[128,256]{1,0:T(8,128)(2,1)S(1)}, bf16[128,256]{1,0:T(8,128)(2,1)S(1)}, u32[]{:S(2)}, u32[]{:S(2)}) collective-permute-start(bf16[128,256]{1,0:T(8,128)(2,1)S(1)} %pad_maximum_fusion.2.kv_ref), channel_id=1, source_target_pairs={{0,12},{1,13},{2,14},{3,15},{16,28},{17,29},{18,30},{19,31}} | collective-permute-start | bytes 196616 | tf_op jit(solution)/shard_map/ppermute | solution.py:175
  7.8 7.9 %collective-permute-start.1 = (bf16[128,256]{1,0:T(8,128)(2,1)S(1)}, bf16[128,256]{1,0:T(8,128)(2,1)S(1)}, u32[]{:S(2)}, u32[]{:S(2)}) collective-permute-start(bf16[128,256]{1,0:T(8,128)(2,1)S(1)} %pad_maximum_fusion.2.kv_ref), channel_id=1, source_target_pairs={{0,8},{4,12},{1,9},{5,13},{2,10},{6,14},{3,11},{7,15},{16,24},{20,... | collective-permute-start | bytes 196616 | tf_op jit(solution)/shard_map/ppermute | solution.py:175
  9.1 6.6 %collective-permute-start = (bf16[128,256]{1,0:T(8,128)(2,1)S(1)}, bf16[128,256]{1,0:T(8,128)(2,1)S(1)}, u32[]{:S(2)}, u32[]{:S(2)}) collective-permute-start(bf16[128,256]{1,0:T(8,128)(2,1)S(1)} %pad_maximum_fusion.2.kv_ref), channel_id=1, source_target_pairs={{0,4},{4,8},{8,12},{1,5},{5,9},{9,13},{2,6},{6,10},{10,14},{3,7},{... | collective-permute-start | bytes 196616 | tf_op jit(solution)/shard_map/ppermute | solution.py:175
  18.6 1.6 %collective-permute-start.3 = (bf16[64,2048]{1,0:T(8,128)(2,1)S(1)}, bf16[64,2048]{1,0:T(8,128)(2,1)S(1)}, u32[]{:S(2)}, u32[]{:S(2)}) collective-permute-start(bf16[64,2048]{1,0:T(8,128)(2,1)S(1)} %get-tuple-element.34), channel_id=1, source_target_pairs={{0,1},{1,0},{2,3},{3,2},{4,5},{5,4},{6,7},{7,6},{8,9},{9,8},{10,11... | collective-permute-start | bytes 786440 | tf_op jit(solution)/shard_map/ppermute | solution.py:170
  20.3 5.6 %collective-permute-start.4 = (bf16[32,2048]{1,0:T(8,128)(2,1)S(1)}, bf16[32,2048]{1,0:T(8,128)(2,1)S(1)}, u32[]{:S(2)}, u32[]{:S(2)}) collective-permute-start(bf16[32,2048]{1,0:T(8,128)(2,1)S(1)} %fusion), channel_id=1, source_target_pairs={{0,2},{2,0},{1,3},{3,1},{4,6},{6,4},{5,7},{7,5},{8,10},{10,8},{9,1... | collective-permute-start | bytes 393224 | tf_op jit(solution)/shard_map/ppermute | solution.py:170
  26.8 8.4 %collective-permute-start.6 = (bf16[32,2176]{1,0:T(8,128)(2,1)S(1)}, bf16[32,2176]{1,0:T(8,128)(2,1)S(1)}, u32[]{:S(2)}, u32[]{:S(2)}) collective-permute-start(bf16[32,2176]{1,0:T(8,128)(2,1)S(1)} %get-tuple-element.58.refs_0_), channel_id=1, source_target_pairs={{0,8},{4,12},{8,0},{12,4},{1,9},{5,13},{9,1},{13,5},{2,10},{6,14},... | collective-permute-start | bytes 417800 | tf_op jit(solution)/shard_map/ppermute | solution.py:170
  27.9 8.8 %collective-permute-start.5 = (bf16[32,2176]{1,0:T(8,128)(2,1)S(1)}, bf16[32,2176]{1,0:T(8,128)(2,1)S(1)}, u32[]{:S(2)}, u32[]{:S(2)}) collective-permute-start(bf16[32,2176]{1,0:T(8,128)(2,1)S(1)} %get-tuple-element.58.refs_0_), channel_id=1, source_target_pairs={{0,4},{4,0},{8,12},{12,8},{1,5},{5,1},{9,13},{13,9},{2,6},{6,2},{1... | collective-permute-start | bytes 417800 | tf_op jit(solution)/shard_map/ppermute | solution.py:170
  28.4 10.2 %collective-permute-start.8 = (bf16[32,2176]{1,0:T(8,128)(2,1)S(1)}, bf16[32,2176]{1,0:T(8,128)(2,1)S(1)}, u32[]{:S(2)}, u32[]{:S(2)}) collective-permute-start(bf16[32,2176]{1,0:T(8,128)(2,1)S(1)} %get-tuple-element.58.refs_0_), channel_id=1, source_target_pairs={{0,2},{2,0},{1,3},{3,1},{4,6},{6,4},{5,7},{7,5},{8,10},{10,8},{9,1... | collective-permute-start | bytes 417800 | tf_op jit(solution)/shard_map/ppermute | solution.py:170
  35.2 8.8 %collective-permute-start.10 = (bf16[32,2176]{1,0:T(8,128)(2,1)S(1)}, bf16[32,2176]{1,0:T(8,128)(2,1)S(1)}, u32[]{:S(2)}, u32[]{:S(2)}) collective-permute-start(bf16[32,2176]{1,0:T(8,128)(2,1)S(1)} %collective-permute-done.6.refs_2_), channel_id=1, source_target_pairs={{0,2},{2,0},{1,3},{3,1},{4,6},{6,4},{5,7},{7,5},{8,10},{10,8},{9,1... | collective-permute-start | bytes 417800 | tf_op jit(solution)/shard_map/ppermute | solution.py:170
  36.7 6.7 %collective-permute-start.9 = (bf16[32,2176]{1,0:T(8,128)(2,1)S(1)}, bf16[32,2176]{1,0:T(8,128)(2,1)S(1)}, u32[]{:S(2)}, u32[]{:S(2)}) collective-permute-start(bf16[32,2176]{1,0:T(8,128)(2,1)S(1)} %collective-permute-done.5.refs_1_), channel_id=1, source_target_pairs={{0,2},{2,0},{1,3},{3,1},{4,6},{6,4},{5,7},{7,5},{8,10},{10,8},{9,1... | collective-permute-start | bytes 417800 | tf_op jit(solution)/shard_map/ppermute | solution.py:170
  44.7 10.7 %collective-permute-start.12 = (bf16[192,2176]{1,0:T(8,128)(2,1)}, bf16[192,2176]{1,0:T(8,128)(2,1)S(1)}, u32[]{:S(2)}, u32[]{:S(2)}) collective-permute-start(bf16[192,2176]{1,0:T(8,128)(2,1)} %constant_dynamic-update-slice_fusion), channel_id=1, source_target_pairs={{0,1},{1,0},{2,3},{3,2},{4,5},{5,4},{6,7},{7,6},{8,9},{9,8},{10,11... | collective-permute-start | bytes 2506760 | tf_op jit(solution)/shard_map/ppermute | solution.py:170
  44.7 6.5 %collective-permute-start.7 = (bf16[32,2176]{1,0:T(8,128)(2,1)S(1)}, bf16[32,2176]{1,0:T(8,128)(2,1)S(1)}, u32[]{:S(2)}, u32[]{:S(2)}) collective-permute-start(bf16[32,2176]{1,0:T(8,128)(2,1)S(1)} %collective-permute-done.6.refs_2_), channel_id=1, source_target_pairs={{0,4},{4,0},{8,12},{12,8},{1,5},{5,1},{9,13},{13,9},{2,6},{6,2},{1... | collective-permute-start | bytes 417800 | tf_op jit(solution)/shard_map/ppermute | solution.py:170
  44.7 9.1 %collective-permute-start.11 = (bf16[32,2176]{1,0:T(8,128)(2,1)S(1)}, bf16[32,2176]{1,0:T(8,128)(2,1)S(1)}, u32[]{:S(2)}, u32[]{:S(2)}) collective-permute-start(bf16[32,2176]{1,0:T(8,128)(2,1)S(1)} %collective-permute-done.10.refs_6_), channel_id=1, source_target_pairs={{0,4},{4,0},{8,12},{12,8},{1,5},{5,1},{9,13},{13,9},{2,6},{6,2},{1... | collective-permute-start | bytes 417800 | tf_op jit(solution)/shard_map/ppermute | solution.py:170
  53.8 1.6 %collective-permute-start.13 = (bf16[64,2176]{1,0:T(8,128)(2,1)S(1)}, bf16[64,2176]{1,0:T(8,128)(2,1)S(1)}, u32[]{:S(2)}, u32[]{:S(2)}) collective-permute-start(bf16[64,2176]{1,0:T(8,128)(2,1)S(1)} %pad_maximum_fusion), channel_id=1, source_target_pairs={{0,1},{1,0},{2,3},{3,2},{4,5},{5,4},{6,7},{7,6},{8,9},{9,8},{10,11... | collective-permute-start | bytes 835592 | tf_op jit(solution)/shard_map/ppermute | solution.py:170
  71.6 2.0 %collective-permute-start.15 = (bf16[128,2048]{1,0:T(8,128)(2,1)S(1)}, bf16[128,2048]{1,0:T(8,128)(2,1)S(1)}, u32[]{:S(2)}, u32[]{:S(2)}) collective-permute-start(bf16[128,2048]{1,0:T(8,128)(2,1)S(1)} %get-tuple-element.42), channel_id=1, source_target_pairs={{0,1},{1,0},{2,3},{3,2},{4,5},{5,4},{6,7},{7,6},{8,9},{9,8},{10,11... | collective-permute-start | bytes 1572872 | tf_op jit(solution)/shard_map/ppermute | solution.py:170
  71.8 2.5 %collective-permute-start.14 = (bf16[128,2048]{1,0:T(8,128)(2,1)S(1)}, bf16[128,2048]{1,0:T(8,128)(2,1)S(1)}, u32[]{:S(2)}, u32[]{:S(2)}) collective-permute-start(bf16[128,2048]{1,0:T(8,128)(2,1)S(1)} %get-tuple-element.40), channel_id=1, source_target_pairs={{0,1},{1,0},{2,3},{3,2},{4,5},{5,4},{6,7},{7,6},{8,9},{9,8},{10,11... | collective-permute-start | bytes 1572872 | tf_op jit(solution)/shard_map/ppermute | solution.py:170
  73.7 5.6 %collective-permute-start.16 = (bf16[32,2048]{1,0:T(8,128)(2,1)S(1)}, bf16[32,2048]{1,0:T(8,128)(2,1)S(1)}, u32[]{:S(2)}, u32[]{:S(2)}) collective-permute-start(bf16[32,2048]{1,0:T(8,128)(2,1)S(1)} %get-tuple-element.53), channel_id=1, source_target_pairs={{0,4},{4,0},{8,12},{12,8},{1,5},{5,1},{9,13},{13,9},{2,6},{6,2},{1... | collective-permute-start | bytes 393224 | tf_op jit(solution)/shard_map/ppermute | solution.py:170
  74.5 6.7 %collective-permute-start.17 = (bf16[32,2048]{1,0:T(8,128)(2,1)S(1)}, bf16[32,2048]{1,0:T(8,128)(2,1)S(1)}, u32[]{:S(2)}, u32[]{:S(2)}) collective-permute-start(bf16[32,2048]{1,0:T(8,128)(2,1)S(1)} %get-tuple-element.52), channel_id=1, source_target_pairs={{0,2},{2,0},{1,3},{3,1},{4,6},{6,4},{5,7},{7,5},{8,10},{10,8},{9,1... | collective-permute-start | bytes 393224 | tf_op jit(solution)/shard_map/ppermute | solution.py:170
  79.3 6.1 %collective-permute-start.20 = (bf16[32,2048]{1,0:T(8,128)(2,1)S(1)}, bf16[32,2048]{1,0:T(8,128)(2,1)S(1)}, u32[]{:S(2)}, u32[]{:S(2)}) collective-permute-start(bf16[32,2048]{1,0:T(8,128)(2,1)S(1)} %get-tuple-element.47), channel_id=1, source_target_pairs={{0,4},{4,0},{8,12},{12,8},{1,5},{5,1},{9,13},{13,9},{2,6},{6,2},{1... | collective-permute-start | bytes 393224 | tf_op jit(solution)/shard_map/ppermute | solution.py:170
  79.7 5.9 %collective-permute-start.21 = (bf16[32,2048]{1,0:T(8,128)(2,1)S(1)}, bf16[32,2048]{1,0:T(8,128)(2,1)S(1)}, u32[]{:S(2)}, u32[]{:S(2)}) collective-permute-start(bf16[32,2048]{1,0:T(8,128)(2,1)S(1)} %add_convert_fusion.5), channel_id=1, source_target_pairs={{0,2},{2,0},{1,3},{3,1},{4,6},{6,4},{5,7},{7,5},{8,10},{10,8},{9,1... | collective-permute-start | bytes 393224 | tf_op jit(solution)/shard_map/ppermute | solution.py:170
  81.2 5.8 %collective-permute-start.18 = (bf16[32,2048]{1,0:T(8,128)(2,1)S(1)}, bf16[32,2048]{1,0:T(8,128)(2,1)S(1)}, u32[]{:S(2)}, u32[]{:S(2)}) collective-permute-start(bf16[32,2048]{1,0:T(8,128)(2,1)S(1)} %get-tuple-element.44), channel_id=1, source_target_pairs={{0,2},{2,0},{1,3},{3,1},{4,6},{6,4},{5,7},{7,5},{8,10},{10,8},{9,1... | collective-permute-start | bytes 393224 | tf_op jit(solution)/shard_map/ppermute | solution.py:170
  81.8 6.8 %collective-permute-start.19 = (bf16[32,2048]{1,0:T(8,128)(2,1)S(1)}, bf16[32,2048]{1,0:T(8,128)(2,1)S(1)}, u32[]{:S(2)}, u32[]{:S(2)}) collective-permute-start(bf16[32,2048]{1,0:T(8,128)(2,1)S(1)} %add_convert_fusion.4), channel_id=1, source_target_pairs={{0,4},{4,0},{8,12},{12,8},{1,5},{5,1},{9,13},{13,9},{2,6},{6,2},{1... | collective-permute-start | bytes 393224 | tf_op jit(solution)/shard_map/ppermute | solution.py:170
  85.7 7.3 %collective-permute-start.22 = (bf16[32,2048]{1,0:T(8,128)(2,1)S(1)}, bf16[32,2048]{1,0:T(8,128)(2,1)S(1)}, u32[]{:S(2)}, u32[]{:S(2)}) collective-permute-start(bf16[32,2048]{1,0:T(8,128)(2,1)S(1)} %add_convert_fusion.3), channel_id=1, source_target_pairs={{0,8},{4,12},{8,0},{12,4},{1,9},{5,13},{9,1},{13,5},{2,10},{6,14},... | collective-permute-start | bytes 393224 | tf_op jit(solution)/shard_map/ppermute | solution.py:170

commit v6 on v5

--- a/solution.py
+++ b/solution.py
@@ -170,6 +170,13 @@
     return lax.ppermute(x, axis, [(i, i ^ bit) for i in range(lax.axis_size(axis))])
 
 
+def flip_both(x):
+    n_exp = lax.axis_size("exp")
+    mask = n_exp + 1
+    size = lax.axis_size("ctx") * n_exp
+    return lax.ppermute(x, ("ctx", "exp"), [(i, i ^ mask) for i in range(size)])
+
+
 def from_earlier(x, axis, steps):
     size = lax.axis_size(axis)
     return lax.ppermute(x, axis, [(i, i + steps) for i in range(size - steps)])
@@ -351,14 +358,15 @@
     )(place, *pieces, *own)
 
 
-def expert_kernel(n_pieces, order, sizes, depth, experts, first_ref, *refs):
+def expert_kernel(n_pieces, depth, experts, first_ref, *refs):
     pieces, (wg_hbm, wu_hbm, wd_hbm) = refs[:n_pieces], refs[n_pieces : n_pieces + 3]
     outs = refs[n_pieces + 3 : n_pieces + 7]
     x_all, packed, pick_all, scale_all, out_all, wgu, wd, act, sems = refs[n_pieces + 7 :]
     tokens = x_all.shape[0]
     slots = pick_all.shape[0] // experts
     _, _, halves, hidden, model = wgu.shape
-    part, blocks = sizes
+    part = tokens // n_pieces
+    blocks = n_pieces // 2
 
     def copies(e):
         slot = lax.rem(e, depth)
@@ -394,10 +402,9 @@
 
     for e in range(min(depth - 1, experts)):
         start(e)
-    for i, (piece, at) in enumerate(order):
-        rows = slice(at * part, (at + 1) * part)
-        x_all[i * part : (i + 1) * part, :] = pieces[piece][rows, :model]
-        packed[i * part : (i + 1) * part, :] = pieces[piece][rows, model:].astype(F32)
+    for i, piece in enumerate(pieces):
+        x_all[i * part : (i + 1) * part, :] = piece[:, :model]
+        packed[i * part : (i + 1) * part, :] = piece[:, model:].astype(F32)
     fields = packed[...].T
     ids, ranks = fields[:TOPK], fields[TOPK : 2 * TOPK]
     gates = fields[2 * TOPK : 3 * TOPK] + fields[3 * TOPK : 4 * TOPK]
@@ -439,20 +446,18 @@
         ).astype(BF)
 
 
-def cube_experts(first, pieces, order, part, w_gate, w_up, w_down, slots):
+def cube_experts(first, pieces, w_gate, w_up, w_down, slots):
     rows, hidden, model = w_down.shape
     halves = 2
     experts = rows // halves
-    tokens = len(order) * part
+    tokens = len(pieces) * pieces[0].shape[0]
     depth = min(4, experts)
     vmem = pl.BlockSpec(memory_space=pltpu.VMEM)
     hbm = pl.BlockSpec(memory_space=pltpu.HBM)
 
     out = jax.ShapeDtypeStruct((tokens // 4, model), BF)
     return pl.pallas_call(
-        functools.partial(
-            expert_kernel, len(pieces), order, (part, len(order) // 2), depth, experts
-        ),
+        functools.partial(expert_kernel, len(pieces), depth, experts),
         out_shape=(out,) * 4,
         in_specs=[pl.BlockSpec(memory_space=pltpu.SMEM)] + [vmem] * len(pieces) + [hbm] * 3,
         out_specs=(vmem,) * 4,
@@ -494,17 +499,17 @@
     here = add(mine, flip(other, "tp", 1))
     across = [across[z * part : (z + 1) * part] for z in range(4)]
     here = [here[z * part : (z + 1) * part] for z in range(4)]
-    near = flip(across[1], "exp", 1)
-    far_across = add(across[2], flip(across[3], "ctx", 1))
-    far_across, here[3], here[1] = lax.optimization_barrier((far_across, here[3], here[1]))
-    far = flip(far_across, "exp", 1)
+    far_across = flip(across[2], "exp", 1)
+    last_across = flip_both(across[3])
     last = flip(here[3], "ctx", 1)
-    near = add(here[1], near)
-    near, here[2], across[0] = lax.optimization_barrier((near, here[2], across[0]))
-    near = flip(near, "ctx", 1)
     own = flip(across[0], "exp", 1)
-    far = flip(add(here[2], last, far), "ctx", 2)
-    return here[0].astype(F32) + own.astype(F32) + near.astype(F32) + far.astype(F32)
+    near = flip(here[1], "ctx", 1)
+    near_across = flip_both(across[1])
+    far = flip(add(here[2], last, far_across, last_across), "ctx", 2)
+    total = here[0].astype(F32)
+    for term in (own, near, near_across, far):
+        total = total + term.astype(F32)
+    return total
 
 
 def on_device(
@@ -545,21 +550,16 @@
     far = flip(normed, "ctx", 2)
     across = flip(normed, "exp", 1)
     near = flip(normed, "ctx", 1)
+    near_across = flip_both(normed)
     far_across = flip(far, "exp", 1)
-    near_across = flip(near, "exp", 1)
+    last_across = flip_both(far)
     last = flip(far, "ctx", 1)
-    early = jnp.concatenate([normed, near, far, across, near_across, far_across])
-    early, far_onward = lax.optimization_barrier((early, far_across))
-    last_across = flip(far_onward, "ctx", 1)
-    early_other = flip(early, "tp", 1)
-    late_other = flip(jnp.concatenate([last, last_across]), "tp", 1)
+    early = lax.optimization_barrier((normed, near, far, across, near_across))
     pieces = [normed, near, far, last, across, near_across, far_across, last_across]
-    order = [(i, 0) for i in range(8)] + [
-        (8, 0), (8, 1), (8, 2), (9, 0), (8, 3), (8, 4), (8, 5), (9, 1)
-    ]
+    pieces += [flip(piece, "tp", 1) for piece in early[:3] + (last,)]
+    pieces += [flip(piece, "tp", 1) for piece in early[3:] + (far_across, last_across)]
     sums = cube_experts(
-        first.astype(jnp.int32).reshape(1), pieces + [early_other, late_other], order, part,
-        w_gate, w_up, w_down, slots,
+        first.astype(jnp.int32).reshape(1), pieces, w_gate, w_up, w_down, slots
     )
     return (hidden + sums_back(*sums, part)).astype(BF)
 

time: 94 us -> 85 us (0.904)
  waiting for transfers between devices: 37.8 us -> 32.1 us
  local copies, waits for them, and re-layouts: 4.15 us -> 0.84 us
    ppermute x20 -> x22, waiting for transfers between devices: 37.8 us -> 26.5 us  [flip(): lax.ppermute(x, axis, [(i, i ^ bit) for i in range(lax.axis_size(axis))])]
    ppermute x0 -> x4, waiting for transfers between devices: none -> 5.64 us  [flip_both(): return lax.ppermute(x, ('ctx', 'exp'), [(i, i ^ mask) for i in range(size)])]
    ppermute x0 -> x4, starting transfers between devices: none -> 4.11 us  [flip_both(): return lax.ppermute(x, ('ctx', 'exp'), [(i, i ^ mask) for i in range(size)])]
    ppermute x20 -> x22, starting transfers between devices: 15.6 us -> 12.3 us  [flip(): lax.ppermute(x, axis, [(i, i ^ bit) for i in range(lax.axis_size(axis))])]
    unnamed x4 -> x0, local copies, waits for them, and re-layouts: 2.65 us -> none
  transfers between devices with their start and end apart: 23 -> 29, of which waited for: 15 -> 19; matrix products, arithmetic and copies ran while one was open for 3% -> 1% of each run, Pallas kernels for 4% -> 5%
where the time goes in v6:
time: 85 us; the launch traced here: 84.8 us
  waiting for transfers between devices  32.1 us (38%)
  starting transfers between devices  27.1 us (32%)
  Pallas kernels  23 us (27%)
  other arithmetic  1.51 us (2%)
    ppermute x22, waiting for transfers between devices, flip(): lax.ppermute(x, axis, [(i, i ^ bit) for i in range(lax.axis_size(axis))])  26.5 us
    pallas_call x1, Pallas kernels, cube_experts(): pl.pallas_call(functools.partial(expert_kernel, len(pieces), depth, exper...  16.1 us
    ppermute x22, starting transfers between devices, flip(): lax.ppermute(x, axis, [(i, i ^ bit) for i in range(lax.axis_size(axis))])  12.3 us
    ppermute x3, starting transfers between devices, from_earlier(): return lax.ppermute(x, axis, [(i, i + steps) for i in range(size - steps)])  10.7 us
    ppermute x4, waiting for transfers between devices, flip_both(): return lax.ppermute(x, ('ctx', 'exp'), [(i, i ^ mask) for i in range(size)])  5.64 us
    ppermute x4, starting transfers between devices, flip_both(): return lax.ppermute(x, ('ctx', 'exp'), [(i, i ^ mask) for i in range(size)])  4.11 us
    pallas_call x1, Pallas kernels, own_block(): pl.pallas_call(functools.partial(own_block_kernel, (n_exp, n_tp, heads, p...  3.97 us
    pallas_call x1, Pallas kernels, attend_project(): pl.pallas_call(functools.partial(attention_kernel, (n_ctx, n_exp, n_tp, h...  2.96 us
  transfers between devices with their start and end apart: 29, of which 19 were waited for; matrix products, arithmetic and copies ran while one was open for 1% of the time, Pallas kernels for 5%

profile of v6, /device:TPU:0, one launch (start us, length us, event | category | flops | bytes accessed | tf_op | source)
XLA Modules:
  0.0 84.8 jit_solution(9786548661528068603)
XLA Ops:
  0.0 0.8 constant_dynamic-slice_fusion
  0.8 7.0 %collective-permute-start.2 = (bf16[128,256]{1,0:T(8,128)(2,1)S(1)}, bf16[128,256]{1,0:T(8,128)(2,1)S(1)}, u32[]{:S(2)}, u32[]{:S(2)}) collective-permute-start(bf16[128,256]{1,0:T(8,128)(2,1)S(1)} %pad_maximum_fusion.1.kv_ref), channel_id=1, source_target_pairs={{0,12},{1,13},{2,14},{3,15},{16,28},{17,29},{18,30},{19,31}} | collective-permute-start | bytes 196616 | tf_op jit(solution)/shard_map/ppermute | solution.py:182
  7.8 1.3 %collective-permute-start.1 = (bf16[128,256]{1,0:T(8,128)(2,1)S(1)}, bf16[128,256]{1,0:T(8,128)(2,1)S(1)}, u32[]{:S(2)}, u32[]{:S(2)}) collective-permute-start(bf16[128,256]{1,0:T(8,128)(2,1)S(1)} %pad_maximum_fusion.1.kv_ref), channel_id=1, source_target_pairs={{0,8},{4,12},{1,9},{5,13},{2,10},{6,14},{3,11},{7,15},{16,24},{20,... | collective-permute-start | bytes 196616 | tf_op jit(solution)/shard_map/ppermute | solution.py:182
  9.1 2.5 %collective-permute-start = (bf16[128,256]{1,0:T(8,128)(2,1)S(1)}, bf16[128,256]{1,0:T(8,128)(2,1)S(1)}, u32[]{:S(2)}, u32[]{:S(2)}) collective-permute-start(bf16[128,256]{1,0:T(8,128)(2,1)S(1)} %pad_maximum_fusion.1.kv_ref), channel_id=1, source_target_pairs={{0,4},{4,8},{8,12},{1,5},{5,9},{9,13},{2,6},{6,10},{10,14},{3,7},{... | collective-permute-start | bytes 196616 | tf_op jit(solution)/shard_map/ppermute | solution.py:182
  11.6 4.0 %own_block.1 = (bf16[128,1024]{1,0:T(8,128)(2,1)S(1)}, bf16[1024,2048]{1,0:T(8,128)(2,1)S(1)}, bf16[32,2048]{1,0:T(8,128)(2,1)S(1)}, f32[128,1024]{1,0:T(8,128)S...) custom-call(s32[3]{0:T(128)S(1)} %pad_add_fusion.place, ...), custom_call_target="tpu_custom_call" | custom-call | flops 100663296 | bytes 4980736 | tf_op jit(solution)/shard_map/own_block/pallas_call | solution.py:263
  15.6 3.0 %attend_project.1 = (f32[32,2048]{1,0:T(8,128)S(1)}, bf16[32,2048]{1,0:T(8,128)(2,1)S(1)}, bf16[64,2048]{1,0:T(8,128)(2,1)S(1)}) custom-call(s32[3]{0:T(128)S(1)} %pad_add_fusion.place, bf16[128,256]{1,0:T(8,128)(2,1)S(1)} %collective-permute-done.refs_0_, bf16[128,256]{1,0:T(8,128)(2,1)S(1)} %collective-permute-done.1.refs_1_, ...), custom_call_target="tpu_custom_call" | custom-call | flops 838860800 | bytes 4980736 | tf_op jit(solution)/shard_map/attend_project/pallas_call | solution.py:336
  18.7 1.5 %collective-permute-done.3 = bf16[64,2048]{1,0:T(8,128)(2,1)S(1)} collective-permute-done((bf16[64,2048]{1,0:T(8,128)(2,1)S(1)}, bf16[64,2048]{1,0:T(8,128)(2,1)S(1)}, u32[]{:S(2)}, u32[]{:S(2)}) %collective-permute-start.3) | collective-permute-done | bytes 262176 | tf_op jit(solution)/shard_map/ppermute | solution.py:170
  20.3 1.6 %collective-permute-start.4 = (bf16[32,2048]{1,0:T(8,128)(2,1)S(1)}, bf16[32,2048]{1,0:T(8,128)(2,1)S(1)}, u32[]{:S(2)}, u32[]{:S(2)}) collective-permute-start(bf16[32,2048]{1,0:T(8,128)(2,1)S(1)} %fusion), channel_id=1, source_target_pairs={{0,2},{2,0},{1,3},{3,1},{4,6},{6,4},{5,7},{7,5},{8,10},{10,8},{9,1... | collective-permute-start | bytes 393224 | tf_op jit(solution)/shard_map/ppermute | solution.py:170
  21.8 4.1 %collective-permute-done.4 = bf16[32,2048]{1,0:T(8,128)(2,1)S(1)} collective-permute-done((bf16[32,2048]{1,0:T(8,128)(2,1)S(1)}, bf16[32,2048]{1,0:T(8,128)(2,1)S(1)}, u32[]{:S(2)}, u32[]{:S(2)}) %collective-permute-start.4) | collective-permute-done | bytes 131104 | tf_op jit(solution)/shard_map/ppermute | solution.py:170
  25.9 0.2 multiply_reduce_fusion
  26.2 1.1 %collective-permute-start.6 = (bf16[32,2176]{1,0:T(8,128)(2,1)S(1)}, bf16[32,2176]{1,0:T(8,128)(2,1)S(1)}, u32[]{:S(2)}, u32[]{:S(2)}) collective-permute-start(bf16[32,2176]{1,0:T(8,128)(2,1)S(1)} %pad_maximum_fusion.refs_0_), channel_id=1, source_target_pairs={{0,8},{4,12},{8,0},{12,4},{1,9},{5,13},{9,1},{13,5},{2,10},{6,14},... | collective-permute-start | bytes 417800 | tf_op jit(solution)/shard_map/ppermute | solution.py:170
  27.3 1.4 %collective-permute-start.9 = (bf16[32,2176]{1,0:T(8,128)(2,1)S(1)}, bf16[32,2176]{1,0:T(8,128)(2,1)S(1)}, u32[]{:S(2)}, u32[]{:S(2)}) collective-permute-start(bf16[32,2176]{1,0:T(8,128)(2,1)S(1)} %pad_maximum_fusion.refs_0_), channel_id=1, source_target_pairs={{0,6},{2,4},{4,2},{6,0},{8,14},{10,12},{12,10},{14,8},{1,7},{3,5},... | collective-permute-start | bytes 417800 | tf_op jit(solution)/shard_map/ppermute | solution.py:177
  28.7 0.5 collective-permute-start.8
  29.3 1.5 %collective-permute-start.5 = (bf16[32,2176]{1,0:T(8,128)(2,1)S(1)}, bf16[32,2176]{1,0:T(8,128)(2,1)S(1)}, u32[]{:S(2)}, u32[]{:S(2)}) collective-permute-start(bf16[32,2176]{1,0:T(8,128)(2,1)S(1)} %pad_maximum_fusion.refs_0_), channel_id=1, source_target_pairs={{0,4},{4,0},{8,12},{12,8},{1,5},{5,1},{9,13},{13,9},{2,6},{6,2},{1... | collective-permute-start | bytes 417800 | tf_op jit(solution)/shard_map/ppermute | solution.py:170
  30.8 3.8 %collective-permute-done.6.refs_2_ = bf16[32,2176]{1,0:T(8,128)(2,1)S(1)} collective-permute-done((bf16[32,2176]{1,0:T(8,128)(2,1)S(1)}, bf16[32,2176]{1,0:T(8,128)(2,1)S(1)}, u32[]{:S(2)}, u32[]{:S(2)}) %collective-permute-start.6) | collective-permute-done | bytes 139296 | tf_op jit(solution)/shard_map/ppermute | solution.py:170
  34.6 0.2 collective-permute-start.11
  34.8 1.3 %collective-permute-start.10 = (bf16[32,2176]{1,0:T(8,128)(2,1)S(1)}, bf16[32,2176]{1,0:T(8,128)(2,1)S(1)}, u32[]{:S(2)}, u32[]{:S(2)}) collective-permute-start(bf16[32,2176]{1,0:T(8,128)(2,1)S(1)} %collective-permute-done.6.refs_2_), channel_id=1, source_target_pairs={{0,2},{2,0},{1,3},{3,1},{4,6},{6,4},{5,7},{7,5},{8,10},{10,8},{9,1... | collective-permute-start | bytes 417800 | tf_op jit(solution)/shard_map/ppermute | solution.py:170
  36.1 1.3 %collective-permute-done.9.refs_5_ = bf16[32,2176]{1,0:T(8,128)(2,1)S(1)} collective-permute-done((bf16[32,2176]{1,0:T(8,128)(2,1)S(1)}, bf16[32,2176]{1,0:T(8,128)(2,1)S(1)}, u32[]{:S(2)}, u32[]{:S(2)}) %collective-permute-start.9) | collective-permute-done | bytes 139296 | tf_op jit(solution)/shard_map/ppermute | solution.py:177
  37.4 2.2 %collective-permute-done.5.refs_1_ = bf16[32,2176]{1,0:T(8,128)(2,1)S(1)} collective-permute-done((bf16[32,2176]{1,0:T(8,128)(2,1)S(1)}, bf16[32,2176]{1,0:T(8,128)(2,1)S(1)}, u32[]{:S(2)}, u32[]{:S(2)}) %collective-permute-start.5) | collective-permute-done | bytes 139296 | tf_op jit(solution)/shard_map/ppermute | solution.py:170
  39.6 0.5 collective-permute-start.13
  40.1 2.4 %collective-permute-done.11.refs_7_ = bf16[32,2176]{1,0:T(8,128)(2,1)S(1)} collective-permute-done((bf16[32,2176]{1,0:T(8,128)(2,1)S(1)}, bf16[32,2176]{1,0:T(8,128)(2,1)S(1)}, u32[]{:S(2)}, u32[]{:S(2)}) %collective-permute-start.11) | collective-permute-done | bytes 139296 | tf_op jit(solution)/shard_map/ppermute | solution.py:177
  42.5 0.7 collective-permute-done.10.refs_6_
  43.2 1.5 %collective-permute-done.7.refs_3_ = bf16[32,2176]{1,0:T(8,128)(2,1)S(1)} collective-permute-done((bf16[32,2176]{1,0:T(8,128)(2,1)S(1)}, bf16[32,2176]{1,0:T(8,128)(2,1)S(1)}, u32[]{:S(2)}, u32[]{:S(2)}) %collective-permute-start.7) | collective-permute-done | bytes 139296 | tf_op jit(solution)/shard_map/ppermute | solution.py:170
  44.7 0.5 collective-permute-start.19
  45.3 0.4 collective-permute-start.15
  45.8 0.3 collective-permute-done.17.refs_13_
  46.1 0.2 collective-permute-done.19.refs_15_
  46.3 0.3 collective-permute-done.18.refs_14_
  46.6 0.2 collective-permute-done.15.refs_11_
  46.8 16.1 %experts.1 = (bf16[128,2048]{1,0:T(8,128)(2,1)S(1)}, bf16[128,2048]{1,0:T(8,128)(2,1)S(1)}, bf16[128,2048]{1,0:T(8,128)(2,1)S(1)}, bf16[128,2048]{1,0:T(8,128)(2,1)S(1)}) custom-call(s32[1]{0:T(128)} %bitcast.5.first_ref, bf16[32,2176]{1,0:T(8,128)(2,1)S(1)} %pad_maximum_fusion.refs_0_, bf16[32,2176]{1,0:T(8,128)(2,1)S(1)} %collective-permute-done.5.refs_1_, ...), custom_call_target="tpu_custom_call" | custom-call | flops 4563402752 | bytes 41943040 | tf_op jit(solution)/shard_map/experts/pallas_call | solution.py:459
  62.9 0.4 collective-permute-start.20
  63.3 0.2 collective-permute-start.21
  63.5 1.4 %collective-permute-done.20 = bf16[128,2048]{1,0:T(8,128)(2,1)S(1)} collective-permute-done((bf16[128,2048]{1,0:T(8,128)(2,1)S(1)}, bf16[128,2048]{1,0:T(8,128)(2,1)S(1)}, u32[]{:S(2)}, u32[]{:S(2)}) %collective-permute-start.20) | collective-permute-done | bytes 524320 | tf_op jit(solution)/shard_map/ppermute | solution.py:170
  64.9 0.1 add_convert_fusion.1
  65.0 0.4 collective-permute-start.25
  65.5 0.1 collective-permute-done.21
  65.8 1.6 %collective-permute-start.27 = (bf16[32,2048]{1,0:T(8,128)(2,1)S(1)}, bf16[32,2048]{1,0:T(8,128)(2,1)S(1)}, u32[]{:S(2)}, u32[]{:S(2)}) collective-permute-start(bf16[32,2048]{1,0:T(8,128)(2,1)S(1)} %get-tuple-element.46), channel_id=1, source_target_pairs={{0,6},{2,4},{4,2},{6,0},{8,14},{10,12},{12,10},{14,8},{1,7},{3,5},... | collective-permute-start | bytes 393224 | tf_op jit(solution)/shard_map/ppermute | solution.py:177
  67.4 1.4 %collective-permute-start.26 = (bf16[32,2048]{1,0:T(8,128)(2,1)S(1)}, bf16[32,2048]{1,0:T(8,128)(2,1)S(1)}, u32[]{:S(2)}, u32[]{:S(2)}) collective-permute-start(bf16[32,2048]{1,0:T(8,128)(2,1)S(1)} %get-tuple-element.47), channel_id=1, source_target_pairs={{0,2},{2,0},{1,3},{3,1},{4,6},{6,4},{5,7},{7,5},{8,10},{10,8},{9,1... | collective-permute-start | bytes 393224 | tf_op jit(solution)/shard_map/ppermute | solution.py:170
  68.9 0.5 collective-permute-start.23
  69.4 0.7 collective-permute-start.22
  70.0 1.4 %collective-permute-done.25 = bf16[32,2048]{1,0:T(8,128)(2,1)S(1)} collective-permute-done((bf16[32,2048]{1,0:T(8,128)(2,1)S(1)}, bf16[32,2048]{1,0:T(8,128)(2,1)S(1)}, u32[]{:S(2)}, u32[]{:S(2)}) %collective-permute-start.25) | collective-permute-done | bytes 131104 | tf_op jit(solution)/shard_map/ppermute | solution.py:170
  71.4 0.9 %collective-permute-start.24 = (bf16[32,2048]{1,0:T(8,128)(2,1)S(1)}, bf16[32,2048]{1,0:T(8,128)(2,1)S(1)}, u32[]{:S(2)}, u32[]{:S(2)}) collective-permute-start(bf16[32,2048]{1,0:T(8,128)(2,1)S(1)} %get-tuple-element.48), channel_id=1, source_target_pairs={{0,6},{2,4},{4,2},{6,0},{8,14},{10,12},{12,10},{14,8},{1,7},{3,5},... | collective-permute-start | bytes 393224 | tf_op jit(solution)/shard_map/ppermute | solution.py:177
  72.3 2.0 %collective-permute-done.27 = bf16[32,2048]{1,0:T(8,128)(2,1)S(1)} collective-permute-done((bf16[32,2048]{1,0:T(8,128)(2,1)S(1)}, bf16[32,2048]{1,0:T(8,128)(2,1)S(1)}, u32[]{:S(2)}, u32[]{:S(2)}) %collective-permute-start.27) | collective-permute-done | bytes 131104 | tf_op jit(solution)/shard_map/ppermute | solution.py:177
  74.3 2.3 %collective-permute-done.26 = bf16[32,2048]{1,0:T(8,128)(2,1)S(1)} collective-permute-done((bf16[32,2048]{1,0:T(8,128)(2,1)S(1)}, bf16[32,2048]{1,0:T(8,128)(2,1)S(1)}, u32[]{:S(2)}, u32[]{:S(2)}) %collective-permute-start.26) | collective-permute-done | bytes 131104 | tf_op jit(solution)/shard_map/ppermute | solution.py:170
  76.7 1.0 %collective-permute-start.28 = (bf16[32,2048]{1,0:T(8,128)(2,1)S(1)}, bf16[32,2048]{1,0:T(8,128)(2,1)S(1)}, u32[]{:S(2)}, u32[]{:S(2)}) collective-permute-start(bf16[32,2048]{1,0:T(8,128)(2,1)S(1)} %add_convert_fusion.3), channel_id=1, source_target_pairs={{0,8},{4,12},{8,0},{12,4},{1,9},{5,13},{9,1},{13,5},{2,10},{6,14},... | collective-permute-start | bytes 393224 | tf_op jit(solution)/shard_map/ppermute | solution.py:170
  77.7 3.3 %collective-permute-done.22 = bf16[32,2048]{1,0:T(8,128)(2,1)S(1)} collective-permute-done((bf16[32,2048]{1,0:T(8,128)(2,1)S(1)}, bf16[32,2048]{1,0:T(8,128)(2,1)S(1)}, u32[]{:S(2)}, u32[]{:S(2)}) %collective-permute-start.22) | collective-permute-done | bytes 131104 | tf_op jit(solution)/shard_map/ppermute | solution.py:170
  81.0 3.0 %collective-permute-done.28 = bf16[32,2048]{1,0:T(8,128)(2,1)S(1)} collective-permute-done((bf16[32,2048]{1,0:T(8,128)(2,1)S(1)}, bf16[32,2048]{1,0:T(8,128)(2,1)S(1)}, u32[]{:S(2)}, u32[]{:S(2)}) %collective-permute-start.28) | collective-permute-done | bytes 131104 | tf_op jit(solution)/shard_map/ppermute | solution.py:170
  84.0 0.8 add_convert_fusion.2
  (28 shorter events, 0.7 us)
Async XLA Ops:
  0.8 14.8 %collective-permute-start.2 = (bf16[128,256]{1,0:T(8,128)(2,1)S(1)}, bf16[128,256]{1,0:T(8,128)(2,1)S(1)}, u32[]{:S(2)}, u32[]{:S(2)}) collective-permute-start(bf16[128,256]{1,0:T(8,128)(2,1)S(1)} %pad_maximum_fusion.1.kv_ref), channel_id=1, source_target_pairs={{0,12},{1,13},{2,14},{3,15},{16,28},{17,29},{18,30},{19,31}} | collective-permute-start | bytes 196616 | tf_op jit(solution)/shard_map/ppermute | solution.py:182
  7.8 7.9 %collective-permute-start.1 = (bf16[128,256]{1,0:T(8,128)(2,1)S(1)}, bf16[128,256]{1,0:T(8,128)(2,1)S(1)}, u32[]{:S(2)}, u32[]{:S(2)}) collective-permute-start(bf16[128,256]{1,0:T(8,128)(2,1)S(1)} %pad_maximum_fusion.1.kv_ref), channel_id=1, source_target_pairs={{0,8},{4,12},{1,9},{5,13},{2,10},{6,14},{3,11},{7,15},{16,24},{20,... | collective-permute-start | bytes 196616 | tf_op jit(solution)/shard_map/ppermute | solution.py:182
  9.1 6.6 %collective-permute-start = (bf16[128,256]{1,0:T(8,128)(2,1)S(1)}, bf16[128,256]{1,0:T(8,128)(2,1)S(1)}, u32[]{:S(2)}, u32[]{:S(2)}) collective-permute-start(bf16[128,256]{1,0:T(8,128)(2,1)S(1)} %pad_maximum_fusion.1.kv_ref), channel_id=1, source_target_pairs={{0,4},{4,8},{8,12},{1,5},{5,9},{9,13},{2,6},{6,10},{10,14},{3,7},{... | collective-permute-start | bytes 196616 | tf_op jit(solution)/shard_map/ppermute | solution.py:182
  18.6 1.6 %collective-permute-start.3 = (bf16[64,2048]{1,0:T(8,128)(2,1)S(1)}, bf16[64,2048]{1,0:T(8,128)(2,1)S(1)}, u32[]{:S(2)}, u32[]{:S(2)}) collective-permute-start(bf16[64,2048]{1,0:T(8,128)(2,1)S(1)} %get-tuple-element.31), channel_id=1, source_target_pairs={{0,1},{1,0},{2,3},{3,2},{4,5},{5,4},{6,7},{7,6},{8,9},{9,8},{10,11... | collective-permute-start | bytes 786440 | tf_op jit(solution)/shard_map/ppermute | solution.py:170
  20.3 5.6 %collective-permute-start.4 = (bf16[32,2048]{1,0:T(8,128)(2,1)S(1)}, bf16[32,2048]{1,0:T(8,128)(2,1)S(1)}, u32[]{:S(2)}, u32[]{:S(2)}) collective-permute-start(bf16[32,2048]{1,0:T(8,128)(2,1)S(1)} %fusion), channel_id=1, source_target_pairs={{0,2},{2,0},{1,3},{3,1},{4,6},{6,4},{5,7},{7,5},{8,10},{10,8},{9,1... | collective-permute-start | bytes 393224 | tf_op jit(solution)/shard_map/ppermute | solution.py:170
  26.2 8.4 %collective-permute-start.6 = (bf16[32,2176]{1,0:T(8,128)(2,1)S(1)}, bf16[32,2176]{1,0:T(8,128)(2,1)S(1)}, u32[]{:S(2)}, u32[]{:S(2)}) collective-permute-start(bf16[32,2176]{1,0:T(8,128)(2,1)S(1)} %pad_maximum_fusion.refs_0_), channel_id=1, source_target_pairs={{0,8},{4,12},{8,0},{12,4},{1,9},{5,13},{9,1},{13,5},{2,10},{6,14},... | collective-permute-start | bytes 417800 | tf_op jit(solution)/shard_map/ppermute | solution.py:170
  27.3 10.1 %collective-permute-start.9 = (bf16[32,2176]{1,0:T(8,128)(2,1)S(1)}, bf16[32,2176]{1,0:T(8,128)(2,1)S(1)}, u32[]{:S(2)}, u32[]{:S(2)}) collective-permute-start(bf16[32,2176]{1,0:T(8,128)(2,1)S(1)} %pad_maximum_fusion.refs_0_), channel_id=1, source_target_pairs={{0,6},{2,4},{4,2},{6,0},{8,14},{10,12},{12,10},{14,8},{1,7},{3,5},... | collective-permute-start | bytes 417800 | tf_op jit(solution)/shard_map/ppermute | solution.py:177
  28.7 8.7 %collective-permute-start.8 = (bf16[32,2176]{1,0:T(8,128)(2,1)S(1)}, bf16[32,2176]{1,0:T(8,128)(2,1)S(1)}, u32[]{:S(2)}, u32[]{:S(2)}) collective-permute-start(bf16[32,2176]{1,0:T(8,128)(2,1)S(1)} %pad_maximum_fusion.refs_0_), channel_id=1, source_target_pairs={{0,2},{2,0},{1,3},{3,1},{4,6},{6,4},{5,7},{7,5},{8,10},{10,8},{9,1... | collective-permute-start | bytes 417800 | tf_op jit(solution)/shard_map/ppermute | solution.py:170
  29.3 10.3 %collective-permute-start.5 = (bf16[32,2176]{1,0:T(8,128)(2,1)S(1)}, bf16[32,2176]{1,0:T(8,128)(2,1)S(1)}, u32[]{:S(2)}, u32[]{:S(2)}) collective-permute-start(bf16[32,2176]{1,0:T(8,128)(2,1)S(1)} %pad_maximum_fusion.refs_0_), channel_id=1, source_target_pairs={{0,4},{4,0},{8,12},{12,8},{1,5},{5,1},{9,13},{13,9},{2,6},{6,2},{1... | collective-permute-start | bytes 417800 | tf_op jit(solution)/shard_map/ppermute | solution.py:170
  34.6 7.9 %collective-permute-start.11 = (bf16[32,2176]{1,0:T(8,128)(2,1)S(1)}, bf16[32,2176]{1,0:T(8,128)(2,1)S(1)}, u32[]{:S(2)}, u32[]{:S(2)}) collective-permute-start(bf16[32,2176]{1,0:T(8,128)(2,1)S(1)} %collective-permute-done.6.refs_2_), channel_id=1, source_target_pairs={{0,6},{2,4},{4,2},{6,0},{8,14},{10,12},{12,10},{14,8},{1,7},{3,5},... | collective-permute-start | bytes 417800 | tf_op jit(solution)/shard_map/ppermute | solution.py:177
  34.8 8.4 %collective-permute-start.10 = (bf16[32,2176]{1,0:T(8,128)(2,1)S(1)}, bf16[32,2176]{1,0:T(8,128)(2,1)S(1)}, u32[]{:S(2)}, u32[]{:S(2)}) collective-permute-start(bf16[32,2176]{1,0:T(8,128)(2,1)S(1)} %collective-permute-done.6.refs_2_), channel_id=1, source_target_pairs={{0,2},{2,0},{1,3},{3,1},{4,6},{6,4},{5,7},{7,5},{8,10},{10,8},{9,1... | collective-permute-start | bytes 417800 | tf_op jit(solution)/shard_map/ppermute | solution.py:170
  39.6 5.1 %collective-permute-start.7 = (bf16[32,2176]{1,0:T(8,128)(2,1)S(1)}, bf16[32,2176]{1,0:T(8,128)(2,1)S(1)}, u32[]{:S(2)}, u32[]{:S(2)}) collective-permute-start(bf16[32,2176]{1,0:T(8,128)(2,1)S(1)} %collective-permute-done.6.refs_2_), channel_id=1, source_target_pairs={{0,4},{4,0},{8,12},{12,8},{1,5},{5,1},{9,13},{13,9},{2,6},{6,2},{1... | collective-permute-start | bytes 417800 | tf_op jit(solution)/shard_map/ppermute | solution.py:170
  39.6 5.1 %collective-permute-start.12 = (bf16[32,2176]{1,0:T(8,128)(2,1)S(1)}, bf16[32,2176]{1,0:T(8,128)(2,1)S(1)}, u32[]{:S(2)}, u32[]{:S(2)}) collective-permute-start(bf16[32,2176]{1,0:T(8,128)(2,1)S(1)} %pad_maximum_fusion.refs_0_), channel_id=1, source_target_pairs={{0,1},{1,0},{2,3},{3,2},{4,5},{5,4},{6,7},{7,6},{8,9},{9,8},{10,11... | collective-permute-start | bytes 417800 | tf_op jit(solution)/shard_map/ppermute | solution.py:170
  39.6 5.7 %collective-permute-start.13 = (bf16[32,2176]{1,0:T(8,128)(2,1)S(1)}, bf16[32,2176]{1,0:T(8,128)(2,1)S(1)}, u32[]{:S(2)}, u32[]{:S(2)}) collective-permute-start(bf16[32,2176]{1,0:T(8,128)(2,1)S(1)} %collective-permute-done.5.refs_1_), channel_id=1, source_target_pairs={{0,1},{1,0},{2,3},{3,2},{4,5},{5,4},{6,7},{7,6},{8,9},{9,8},{10,11... | collective-permute-start | bytes 417800 | tf_op jit(solution)/shard_map/ppermute | solution.py:170
  42.5 2.9 %collective-permute-start.14 = (bf16[32,2176]{1,0:T(8,128)(2,1)S(1)}, bf16[32,2176]{1,0:T(8,128)(2,1)S(1)}, u32[]{:S(2)}, u32[]{:S(2)}) collective-permute-start(bf16[32,2176]{1,0:T(8,128)(2,1)S(1)} %collective-permute-done.6.refs_2_), channel_id=1, source_target_pairs={{0,1},{1,0},{2,3},{3,2},{4,5},{5,4},{6,7},{7,6},{8,9},{9,8},{10,11... | collective-permute-start | bytes 417800 | tf_op jit(solution)/shard_map/ppermute | solution.py:170
  43.2 2.6 %collective-permute-start.16 = (bf16[32,2176]{1,0:T(8,128)(2,1)S(1)}, bf16[32,2176]{1,0:T(8,128)(2,1)S(1)}, u32[]{:S(2)}, u32[]{:S(2)}) collective-permute-start(bf16[32,2176]{1,0:T(8,128)(2,1)S(1)} %collective-permute-done.8.refs_4_), channel_id=1, source_target_pairs={{0,1},{1,0},{2,3},{3,2},{4,5},{5,4},{6,7},{7,6},{8,9},{9,8},{10,11... | collective-permute-start | bytes 417800 | tf_op jit(solution)/shard_map/ppermute | solution.py:170
  44.7 1.4 %collective-permute-start.17 = (bf16[32,2176]{1,0:T(8,128)(2,1)S(1)}, bf16[32,2176]{1,0:T(8,128)(2,1)S(1)}, u32[]{:S(2)}, u32[]{:S(2)}) collective-permute-start(bf16[32,2176]{1,0:T(8,128)(2,1)S(1)} %collective-permute-done.9.refs_5_), channel_id=1, source_target_pairs={{0,1},{1,0},{2,3},{3,2},{4,5},{5,4},{6,7},{7,6},{8,9},{9,8},{10,11... | collective-permute-start | bytes 417800 | tf_op jit(solution)/shard_map/ppermute | solution.py:170
  44.7 1.6 %collective-permute-start.19 = (bf16[32,2176]{1,0:T(8,128)(2,1)S(1)}, bf16[32,2176]{1,0:T(8,128)(2,1)S(1)}, u32[]{:S(2)}, u32[]{:S(2)}) collective-permute-start(bf16[32,2176]{1,0:T(8,128)(2,1)S(1)} %collective-permute-done.11.refs_7_), channel_id=1, source_target_pairs={{0,1},{1,0},{2,3},{3,2},{4,5},{5,4},{6,7},{7,6},{8,9},{9,8},{10,11... | collective-permute-start | bytes 417800 | tf_op jit(solution)/shard_map/ppermute | solution.py:170
  45.2 1.4 %collective-permute-start.18 = (bf16[32,2176]{1,0:T(8,128)(2,1)S(1)}, bf16[32,2176]{1,0:T(8,128)(2,1)S(1)}, u32[]{:S(2)}, u32[]{:S(2)}) collective-permute-start(bf16[32,2176]{1,0:T(8,128)(2,1)S(1)} %collective-permute-done.10.refs_6_), channel_id=1, source_target_pairs={{0,1},{1,0},{2,3},{3,2},{4,5},{5,4},{6,7},{7,6},{8,9},{9,8},{10,11... | collective-permute-start | bytes 417800 | tf_op jit(solution)/shard_map/ppermute | solution.py:170
  45.3 1.5 %collective-permute-start.15 = (bf16[32,2176]{1,0:T(8,128)(2,1)S(1)}, bf16[32,2176]{1,0:T(8,128)(2,1)S(1)}, u32[]{:S(2)}, u32[]{:S(2)}) collective-permute-start(bf16[32,2176]{1,0:T(8,128)(2,1)S(1)} %collective-permute-done.7.refs_3_), channel_id=1, source_target_pairs={{0,1},{1,0},{2,3},{3,2},{4,5},{5,4},{6,7},{7,6},{8,9},{9,8},{10,11... | collective-permute-start | bytes 417800 | tf_op jit(solution)/shard_map/ppermute | solution.py:170
  62.9 2.0 %collective-permute-start.20 = (bf16[128,2048]{1,0:T(8,128)(2,1)S(1)}, bf16[128,2048]{1,0:T(8,128)(2,1)S(1)}, u32[]{:S(2)}, u32[]{:S(2)}) collective-permute-start(bf16[128,2048]{1,0:T(8,128)(2,1)S(1)} %get-tuple-element.40), channel_id=1, source_target_pairs={{0,1},{1,0},{2,3},{3,2},{4,5},{5,4},{6,7},{7,6},{8,9},{9,8},{10,11... | collective-permute-start | bytes 1572872 | tf_op jit(solution)/shard_map/ppermute | solution.py:170
  63.3 2.4 %collective-permute-start.21 = (bf16[128,2048]{1,0:T(8,128)(2,1)S(1)}, bf16[128,2048]{1,0:T(8,128)(2,1)S(1)}, u32[]{:S(2)}, u32[]{:S(2)}) collective-permute-start(bf16[128,2048]{1,0:T(8,128)(2,1)S(1)} %get-tuple-element.42), channel_id=1, source_target_pairs={{0,1},{1,0},{2,3},{3,2},{4,5},{5,4},{6,7},{7,6},{8,9},{9,8},{10,11... | collective-permute-start | bytes 1572872 | tf_op jit(solution)/shard_map/ppermute | solution.py:170
  65.0 6.4 %collective-permute-start.25 = (bf16[32,2048]{1,0:T(8,128)(2,1)S(1)}, bf16[32,2048]{1,0:T(8,128)(2,1)S(1)}, u32[]{:S(2)}, u32[]{:S(2)}) collective-permute-start(bf16[32,2048]{1,0:T(8,128)(2,1)S(1)} %get-tuple-element.50), channel_id=1, source_target_pairs={{0,4},{4,0},{8,12},{12,8},{1,5},{5,1},{9,13},{13,9},{2,6},{6,2},{1... | collective-permute-start | bytes 393224 | tf_op jit(solution)/shard_map/ppermute | solution.py:170
  65.8 8.5 %collective-permute-start.27 = (bf16[32,2048]{1,0:T(8,128)(2,1)S(1)}, bf16[32,2048]{1,0:T(8,128)(2,1)S(1)}, u32[]{:S(2)}, u32[]{:S(2)}) collective-permute-start(bf16[32,2048]{1,0:T(8,128)(2,1)S(1)} %get-tuple-element.46), channel_id=1, source_target_pairs={{0,6},{2,4},{4,2},{6,0},{8,14},{10,12},{12,10},{14,8},{1,7},{3,5},... | collective-permute-start | bytes 393224 | tf_op jit(solution)/shard_map/ppermute | solution.py:177
  67.4 9.2 %collective-permute-start.26 = (bf16[32,2048]{1,0:T(8,128)(2,1)S(1)}, bf16[32,2048]{1,0:T(8,128)(2,1)S(1)}, u32[]{:S(2)}, u32[]{:S(2)}) collective-permute-start(bf16[32,2048]{1,0:T(8,128)(2,1)S(1)} %get-tuple-element.47), channel_id=1, source_target_pairs={{0,2},{2,0},{1,3},{3,1},{4,6},{6,4},{5,7},{7,5},{8,10},{10,8},{9,1... | collective-permute-start | bytes 393224 | tf_op jit(solution)/shard_map/ppermute | solution.py:170
  68.9 8.8 %collective-permute-start.23 = (bf16[32,2048]{1,0:T(8,128)(2,1)S(1)}, bf16[32,2048]{1,0:T(8,128)(2,1)S(1)}, u32[]{:S(2)}, u32[]{:S(2)}) collective-permute-start(bf16[32,2048]{1,0:T(8,128)(2,1)S(1)} %get-tuple-element.49), channel_id=1, source_target_pairs={{0,4},{4,0},{8,12},{12,8},{1,5},{5,1},{9,13},{13,9},{2,6},{6,2},{1... | collective-permute-start | bytes 393224 | tf_op jit(solution)/shard_map/ppermute | solution.py:170
  69.4 11.6 %collective-permute-start.22 = (bf16[32,2048]{1,0:T(8,128)(2,1)S(1)}, bf16[32,2048]{1,0:T(8,128)(2,1)S(1)}, u32[]{:S(2)}, u32[]{:S(2)}) collective-permute-start(bf16[32,2048]{1,0:T(8,128)(2,1)S(1)} %get-tuple-element.45), channel_id=1, source_target_pairs={{0,2},{2,0},{1,3},{3,1},{4,6},{6,4},{5,7},{7,5},{8,10},{10,8},{9,1... | collective-permute-start | bytes 393224 | tf_op jit(solution)/shard_map/ppermute | solution.py:170
  71.4 9.6 %collective-permute-start.24 = (bf16[32,2048]{1,0:T(8,128)(2,1)S(1)}, bf16[32,2048]{1,0:T(8,128)(2,1)S(1)}, u32[]{:S(2)}, u32[]{:S(2)}) collective-permute-start(bf16[32,2048]{1,0:T(8,128)(2,1)S(1)} %get-tuple-element.48), channel_id=1, source_target_pairs={{0,6},{2,4},{4,2},{6,0},{8,14},{10,12},{12,10},{14,8},{1,7},{3,5},... | collective-permute-start | bytes 393224 | tf_op jit(solution)/shard_map/ppermute | solution.py:177
  76.7 7.3 %collective-permute-start.28 = (bf16[32,2048]{1,0:T(8,128)(2,1)S(1)}, bf16[32,2048]{1,0:T(8,128)(2,1)S(1)}, u32[]{:S(2)}, u32[]{:S(2)}) collective-permute-start(bf16[32,2048]{1,0:T(8,128)(2,1)S(1)} %add_convert_fusion.3), channel_id=1, source_target_pairs={{0,8},{4,12},{8,0},{12,4},{1,9},{5,13},{9,1},{13,5},{2,10},{6,14},... | collective-permute-start | bytes 393224 | tf_op jit(solution)/shard_map/ppermute | solution.py:170

commit v7 on v6

--- a/solution.py
+++ b/solution.py
@@ -291,6 +291,10 @@
     )(place, kv, *map(in_hbm, (expert_ids.T, router_probs.T, queries, out_weight, resid)))
 
 
+def dot_columns(a, b):
+    return lax.dot_general(a, b, (((0,), (0,)), ((), ())), preferred_element_type=F32)
+
+
 def attention_kernel(sizes, place, *refs):
     n_ctx, n_exp, n_tp, heads, part = sizes
     rows = n_exp * n_tp * part
@@ -360,13 +364,13 @@
 
 def expert_kernel(n_pieces, depth, experts, first_ref, *refs):
     pieces, (wg_hbm, wu_hbm, wd_hbm) = refs[:n_pieces], refs[n_pieces : n_pieces + 3]
-    outs = refs[n_pieces + 3 : n_pieces + 7]
-    x_all, packed, pick_all, scale_all, out_all, wgu, wd, act, sems = refs[n_pieces + 7 :]
-    tokens = x_all.shape[0]
-    slots = pick_all.shape[0] // experts
-    _, _, halves, hidden, model = wgu.shape
-    part = tokens // n_pieces
-    blocks = n_pieces // 2
+    outs = refs[n_pieces + 3 : n_pieces + 9]
+    x_all, packed, pick_all, scale_all, out_all, wgu, wd, act, sems = refs[n_pieces + 9 :]
+    sides, tokens, model = x_all.shape
+    slots = pick_all.shape[1] // experts
+    _, _, halves, hidden, _ = wgu.shape
+    blocks = n_pieces // (2 * sides)
+    part = tokens // (2 * blocks)
 
     def copies(e):
         slot = lax.rem(e, depth)
@@ -385,40 +389,53 @@
         for copy in copies(e):
             copy.wait()
 
+    def of_expert(e):
+        return pl.ds(pl.multiple_of(e * slots, slots), slots)
+
     def gate_up(e):
-        x = out_all[pl.ds(pl.multiple_of(e * slots, slots), slots), :]
+        x = jnp.concatenate([out_all[side, of_expert(e), :] for side in range(sides)])
         weight = wgu[lax.rem(e, depth)].reshape(2 * halves * hidden, model)
         both = dot_rows(weight, x)
         gate, up = both[: halves * hidden], both[halves * hidden :]
         return (gate * jax.nn.sigmoid(gate) * up).astype(BF)
 
     def down(e):
-        here = pl.ds(pl.multiple_of(e * slots, slots), slots)
         weight = wd[lax.rem(e, depth)].reshape(halves * hidden, model)
-        out = lax.dot_general(
-            act[lax.rem(e, 2)], weight, (((0,), (0,)), ((), ())), preferred_element_type=F32
-        )
-        return here, (out * scale_all[here, :]).astype(BF)
+        out = dot_columns(act[lax.rem(e, 2)], weight)
+        scale = jnp.concatenate([scale_all[side, of_expert(e), :] for side in range(sides)])
+        return (out * scale).astype(BF)
+
+    def keep(e, out):
+        for side in range(sides):
+            out_all[side, of_expert(e), :] = out[side * slots : (side + 1) * slots]
 
     for e in range(min(depth - 1, experts)):
         start(e)
     for i, piece in enumerate(pieces):
-        x_all[i * part : (i + 1) * part, :] = piece[:, :model]
-        packed[i * part : (i + 1) * part, :] = piece[:, model:].astype(F32)
-    fields = packed[...].T
-    ids, ranks = fields[:TOPK], fields[TOPK : 2 * TOPK]
-    gates = fields[2 * TOPK : 3 * TOPK] + fields[3 * TOPK : 4 * TOPK]
+        core, side, block = i // (sides * blocks), i // blocks % sides, i % blocks
+        rows = slice((core * blocks + block) * part, (core * blocks + block + 1) * part)
+        x_all[side, rows, :] = piece[:, :model]
+        packed[side, rows, :] = piece[:, model:].astype(F32)
+    slot = lax.broadcasted_iota(jnp.int32, (slots, tokens), 0)
     token = lax.broadcasted_iota(jnp.int32, (TOPK, tokens), 1)
-    places = ranks.astype(jnp.int32) + lax.rem(token // part, blocks) * (slots // blocks)
-    slot = lax.broadcasted_iota(jnp.int32, (slots, tokens), 0)
-    for e in range(experts):
-        hit = ids.astype(jnp.int32) == first_ref[0] + e
-        chosen = slot == jnp.max(jnp.where(hit, places, -1), axis=0, keepdims=True)
-        gate = jnp.sum(jnp.where(hit, gates, 0.0), axis=0, keepdims=True)
-        here = slice(e * slots, (e + 1) * slots)
-        pick_all[here, :] = jnp.where(chosen, 1.0, 0.0).astype(BF)
-        scale_all[here, :] = jnp.sum(jnp.where(chosen, gate, 0.0), axis=1, keepdims=True)
-    out_all[...] = jnp.dot(pick_all[...], x_all[...], preferred_element_type=F32).astype(BF)
+    offset = lax.rem(token // part, blocks) * (slots // blocks)
+    for side in range(sides):
+        fields = packed[side].T
+        ids, ranks = fields[:TOPK].astype(jnp.int32), fields[TOPK : 2 * TOPK]
+        gates = fields[2 * TOPK : 3 * TOPK] + fields[3 * TOPK : 4 * TOPK]
+        places = ranks.astype(jnp.int32) + offset
+        for e in range(experts):
+            hit = ids == first_ref[0] + e
+            chosen = slot == jnp.max(jnp.where(hit, places, -1), axis=0, keepdims=True)
+            gate = jnp.sum(jnp.where(hit, gates, 0.0), axis=0, keepdims=True)
+            here = slice(e * slots, (e + 1) * slots)
+            pick_all[side, here, :] = jnp.where(chosen, 1.0, 0.0).astype(BF)
+            scale_all[side, here, :] = jnp.sum(
+                jnp.where(chosen, gate, 0.0), axis=1, keepdims=True
+            )
+        out_all[side] = jnp.dot(
+            pick_all[side], x_all[side], preferred_element_type=F32
+        ).astype(BF)
     wait(0)
     act[0] = gate_up(0)
 
@@ -430,53 +447,52 @@
 
         wait(e + 1)
         following = gate_up(e + 1)
-        here, out = down(e)
+        out = down(e)
         act[lax.rem(e + 1, 2)] = following
-        out_all[here, :] = out
-
-    here, out = down(experts - 1)
-    out_all[here, :] = out
-    quarter = tokens // 4
-    for i, o_ref in enumerate(outs):
-        o_ref[...] = lax.dot_general(
-            pick_all[:, i * quarter : (i + 1) * quarter],
-            out_all[...],
-            (((0,), (0,)), ((), ())),
-            preferred_element_type=F32,
-        ).astype(BF)
+        keep(e, out)
+
+    keep(experts - 1, down(experts - 1))
+    half = blocks * part // 2
+    for side in (1, 0):
+        routed = dot_columns(pick_all[side], out_all[side]).astype(BF)
+        for core in range(2):
+            near, far = routed[2 * core * half :][:half], routed[(2 * core + 1) * half :][:half]
+            outs[3 * core + 1 - side][...] = far
+            outs[3 * core + 2][(1 - side) * half : (2 - side) * half, :] = near
 
 
 def cube_experts(first, pieces, w_gate, w_up, w_down, slots):
     rows, hidden, model = w_down.shape
-    halves = 2
+    halves, sides = 2, 2
     experts = rows // halves
-    tokens = len(pieces) * pieces[0].shape[0]
+    tokens = len(pieces) * pieces[0].shape[0] // sides
     depth = min(4, experts)
     vmem = pl.BlockSpec(memory_space=pltpu.VMEM)
     hbm = pl.BlockSpec(memory_space=pltpu.HBM)
 
-    out = jax.ShapeDtypeStruct((tokens // 4, model), BF)
+    half = jax.ShapeDtypeStruct((tokens // 4, model), BF)
+    whole = jax.ShapeDtypeStruct((tokens // 2, model), BF)
     return pl.pallas_call(
         functools.partial(expert_kernel, len(pieces), depth, experts),
-        out_shape=(out,) * 4,
+        out_shape=(half, half, whole) * 2,
         in_specs=[pl.BlockSpec(memory_space=pltpu.SMEM)] + [vmem] * len(pieces) + [hbm] * 3,
-        out_specs=(vmem,) * 4,
+        out_specs=(vmem,) * 6,
         scratch_shapes=[
-            pltpu.VMEM((tokens, model), BF),
-            pltpu.VMEM((tokens, LANES), F32),
-            pltpu.VMEM((experts * slots, tokens), BF),
-            pltpu.VMEM((experts * slots, 1), F32),
-            pltpu.VMEM((experts * slots, model), BF),
+            pltpu.VMEM((sides, tokens, model), BF),
+            pltpu.VMEM((sides, tokens, LANES), F32),
+            pltpu.VMEM((sides, experts * slots, tokens), BF),
+            pltpu.VMEM((sides, experts * slots, 1), F32),
+            pltpu.VMEM((sides, experts * slots, model), BF),
             pltpu.VMEM((depth, 2, halves, hidden, model), BF),
             pltpu.VMEM((depth, halves, hidden, model), BF),
-            pltpu.VMEM((2, halves * hidden, slots), BF),
+            pltpu.VMEM((2, halves * hidden, sides * slots), BF),
             pltpu.SemaphoreType.DMA((3, depth)),
         ],
         compiler_params=pltpu.CompilerParams(vmem_limit_bytes=44 * MIB),
         cost_estimate=pl.CostEstimate(
-            flops=2 * experts * slots * model * (3 * halves * hidden + 2 * tokens),
+            flops=2 * experts * sides * slots * model * (3 * halves * hidden + 2 * tokens),
             bytes_accessed=6 * rows * model * hidden + 4 * tokens * model,
-            transcendentals=experts * slots * halves * hidden,
+            transcendentals=experts * sides * slots * halves * hidden,
         ),
         name="experts",
     )(
@@ -488,17 +504,18 @@
     )
 
 
-def sums_back(mine, mine_across, other, other_across, part):
+def sums_back(mine, other, part):
     def add(a, *others):
         total = a.astype(F32)
         for b in others:
             total = total + b.astype(F32)
         return total.astype(BF)
 
-    across = add(mine_across, flip(other_across, "tp", 1))
-    here = add(mine, flip(other, "tp", 1))
-    across = [across[z * part : (z + 1) * part] for z in range(4)]
-    here = [here[z * part : (z + 1) * part] for z in range(4)]
+    sums = [add(a, flip(b, "tp", 1)) for a, b in zip(mine, other)]
+    sums[1], sums[2] = lax.optimization_barrier((sums[1], sums[2]))
+    sums = [[x[at : at + part] for at in range(0, x.shape[0], part)] for x in sums]
+    across = sums[2][:2] + sums[0]
+    here = sums[2][2:] + sums[1]
     far_across = flip(across[2], "exp", 1)
     last_across = flip_both(across[3])
     last = flip(here[3], "ctx", 1)
@@ -528,7 +545,7 @@
     place = jnp.stack([ctx, exp, tp]).astype(jnp.int32)
     heads_here = queries.shape[1] // HEAD_DIMENSION
     first = (ctx * n_exp + exp) * rows_here // 2
-    slots = n_ctx * n_exp * min(8, block)
+    slots = n_ctx * min(8, block)
 
     shared = (exp * n_tp + tp) * heads_here // (QUERY_HEADS // KEY_VALUE_HEADS)
     key_head = lax.dynamic_slice_in_dim(keys, shared * HEAD_DIMENSION, HEAD_DIMENSION, 1)
@@ -554,14 +571,12 @@
     far_across = flip(far, "exp", 1)
     last_across = flip_both(far)
     last = flip(far, "ctx", 1)
-    early = lax.optimization_barrier((normed, near, far, across, near_across))
     pieces = [normed, near, far, last, across, near_across, far_across, last_across]
-    pieces += [flip(piece, "tp", 1) for piece in early[:3] + (last,)]
-    pieces += [flip(piece, "tp", 1) for piece in early[3:] + (far_across, last_across)]
+    pieces += [flip(piece, "tp", 1) for piece in pieces]
     sums = cube_experts(
         first.astype(jnp.int32).reshape(1), pieces, w_gate, w_up, w_down, slots
     )
-    return (hidden + sums_back(*sums, part)).astype(BF)
+    return (hidden + sums_back(sums[:3], sums[3:], part)).astype(BF)
 
 
 def solution(mesh):

time: 85 us -> 84.2 us (level)
  starting transfers between devices: 27.1 us -> 28.7 us
  waiting for transfers between devices: 32.1 us -> 30.8 us
  Pallas kernels: 23 us -> 21.9 us
    ppermute x22 -> x23, waiting for transfers between devices: 26.5 us -> 24.1 us  [flip(): lax.ppermute(x, axis, [(i, i ^ bit) for i in range(lax.axis_size(axis))])]
    ppermute x4, starting transfers between devices: 4.11 us -> 5.54 us  [flip_both(): return lax.ppermute(x, ('ctx', 'exp'), [(i, i ^ mask) for i in range(size)])]
    pallas_call x1, Pallas kernels: 16.1 us -> 15 us  [cube_experts(): pl.pallas_call(functools.partial(expert_kernel, len(pieces), depth, exper...]
    ppermute x4, waiting for transfers between devices: 5.64 us -> 6.75 us  [flip_both(): return lax.ppermute(x, ('ctx', 'exp'), [(i, i ^ mask) for i in range(size)])]
    ppermute x22 -> x23, starting transfers between devices: 12.3 us -> 12.4 us  [flip(): lax.ppermute(x, axis, [(i, i ^ bit) for i in range(lax.axis_size(axis))])]
  transfers between devices with their start and end apart: 29 -> 30, of which waited for: 19 -> 16; matrix products, arithmetic and copies ran while one was open for 1% -> 1% of each run, Pallas kernels for 5% -> 5%
where the time goes in v7:
time: 84.2 us; the launch traced here: 84 us
  waiting for transfers between devices  30.8 us (37%)
  starting transfers between devices  28.7 us (34%)
  Pallas kernels  21.9 us (26%)
  other arithmetic  1.52 us (2%)
    ppermute x23, waiting for transfers between devices, flip(): lax.ppermute(x, axis, [(i, i ^ bit) for i in range(lax.axis_size(axis))])  24.1 us
    pallas_call x1, Pallas kernels, cube_experts(): pl.pallas_call(functools.partial(expert_kernel, len(pieces), depth, exper...  15 us
    ppermute x23, starting transfers between devices, flip(): lax.ppermute(x, axis, [(i, i ^ bit) for i in range(lax.axis_size(axis))])  12.4 us
    ppermute x3, starting transfers between devices, from_earlier(): return lax.ppermute(x, axis, [(i, i + steps) for i in range(size - steps)])  10.7 us
    ppermute x4, waiting for transfers between devices, flip_both(): return lax.ppermute(x, ('ctx', 'exp'), [(i, i ^ mask) for i in range(size)])  6.75 us
    ppermute x4, starting transfers between devices, flip_both(): return lax.ppermute(x, ('ctx', 'exp'), [(i, i ^ mask) for i in range(size)])  5.54 us
    pallas_call x1, Pallas kernels, own_block(): pl.pallas_call(functools.partial(own_block_kernel, (n_exp, n_tp, heads, p...  3.97 us
    pallas_call x1, Pallas kernels, attend_project(): pl.pallas_call(functools.partial(attention_kernel, (n_ctx, n_exp, n_tp, h...  2.96 us
  transfers between devices with their start and end apart: 30, of which 16 were waited for; matrix products, arithmetic and copies ran while one was open for 1% of the time, Pallas kernels for 5%

profile of v7, /device:TPU:0, one launch (start us, length us, event | category | flops | bytes accessed | tf_op | source)
XLA Modules:
  0.0 84.0 jit_solution(4887806107385974004)
XLA Ops:
  0.0 0.8 constant_dynamic-slice_fusion
  0.8 7.0 %collective-permute-start.2 = (bf16[128,256]{1,0:T(8,128)(2,1)S(1)}, bf16[128,256]{1,0:T(8,128)(2,1)S(1)}, u32[]{:S(2)}, u32[]{:S(2)}) collective-permute-start(bf16[128,256]{1,0:T(8,128)(2,1)S(1)} %pad_maximum_fusion.1.kv_ref), channel_id=1, source_target_pairs={{0,12},{1,13},{2,14},{3,15},{16,28},{17,29},{18,30},{19,31}} | collective-permute-start | bytes 196616 | tf_op jit(solution)/shard_map/ppermute | solution.py:182
  7.8 1.3 %collective-permute-start.1 = (bf16[128,256]{1,0:T(8,128)(2,1)S(1)}, bf16[128,256]{1,0:T(8,128)(2,1)S(1)}, u32[]{:S(2)}, u32[]{:S(2)}) collective-permute-start(bf16[128,256]{1,0:T(8,128)(2,1)S(1)} %pad_maximum_fusion.1.kv_ref), channel_id=1, source_target_pairs={{0,8},{4,12},{1,9},{5,13},{2,10},{6,14},{3,11},{7,15},{16,24},{20,... | collective-permute-start | bytes 196616 | tf_op jit(solution)/shard_map/ppermute | solution.py:182
  9.1 2.5 %collective-permute-start = (bf16[128,256]{1,0:T(8,128)(2,1)S(1)}, bf16[128,256]{1,0:T(8,128)(2,1)S(1)}, u32[]{:S(2)}, u32[]{:S(2)}) collective-permute-start(bf16[128,256]{1,0:T(8,128)(2,1)S(1)} %pad_maximum_fusion.1.kv_ref), channel_id=1, source_target_pairs={{0,4},{4,8},{8,12},{1,5},{5,9},{9,13},{2,6},{6,10},{10,14},{3,7},{... | collective-permute-start | bytes 196616 | tf_op jit(solution)/shard_map/ppermute | solution.py:182
  11.5 0.1 pad_add_fusion.place
  11.6 4.0 %own_block.1 = (bf16[128,1024]{1,0:T(8,128)(2,1)S(1)}, bf16[1024,2048]{1,0:T(8,128)(2,1)S(1)}, bf16[32,2048]{1,0:T(8,128)(2,1)S(1)}, f32[128,1024]{1,0:T(8,128)S...) custom-call(s32[3]{0:T(128)S(1)} %pad_add_fusion.place, ...), custom_call_target="tpu_custom_call" | custom-call | flops 100663296 | bytes 4980736 | tf_op jit(solution)/shard_map/own_block/pallas_call | solution.py:263
  15.6 3.0 %attend_project.1 = (f32[32,2048]{1,0:T(8,128)S(1)}, bf16[32,2048]{1,0:T(8,128)(2,1)S(1)}, bf16[64,2048]{1,0:T(8,128)(2,1)S(1)}) custom-call(s32[3]{0:T(128)S(1)} %pad_add_fusion.place, bf16[128,256]{1,0:T(8,128)(2,1)S(1)} %collective-permute-done.refs_0_, bf16[128,256]{1,0:T(8,128)(2,1)S(1)} %collective-permute-done.1.refs_1_, ...), custom_call_target="tpu_custom_call" | custom-call | flops 838860800 | bytes 4980736 | tf_op jit(solution)/shard_map/attend_project/pallas_call | solution.py:340
  18.6 0.1 collective-permute-start.3
  18.7 1.5 %collective-permute-done.3 = bf16[64,2048]{1,0:T(8,128)(2,1)S(1)} collective-permute-done((bf16[64,2048]{1,0:T(8,128)(2,1)S(1)}, bf16[64,2048]{1,0:T(8,128)(2,1)S(1)}, u32[]{:S(2)}, u32[]{:S(2)}) %collective-permute-start.3) | collective-permute-done | bytes 262176 | tf_op jit(solution)/shard_map/ppermute | solution.py:170
  20.3 1.6 %collective-permute-start.4 = (bf16[32,2048]{1,0:T(8,128)(2,1)S(1)}, bf16[32,2048]{1,0:T(8,128)(2,1)S(1)}, u32[]{:S(2)}, u32[]{:S(2)}) collective-permute-start(bf16[32,2048]{1,0:T(8,128)(2,1)S(1)} %fusion), channel_id=1, source_target_pairs={{0,2},{2,0},{1,3},{3,1},{4,6},{6,4},{5,7},{7,5},{8,10},{10,8},{9,1... | collective-permute-start | bytes 393224 | tf_op jit(solution)/shard_map/ppermute | solution.py:170
  21.8 4.1 %collective-permute-done.4 = bf16[32,2048]{1,0:T(8,128)(2,1)S(1)} collective-permute-done((bf16[32,2048]{1,0:T(8,128)(2,1)S(1)}, bf16[32,2048]{1,0:T(8,128)(2,1)S(1)}, u32[]{:S(2)}, u32[]{:S(2)}) %collective-permute-start.4) | collective-permute-done | bytes 131104 | tf_op jit(solution)/shard_map/ppermute | solution.py:170
  25.9 0.2 multiply_reduce_fusion
  26.1 0.1 multiply_convert_fusion
  26.2 1.1 %collective-permute-start.9 = (bf16[32,2176]{1,0:T(8,128)(2,1)S(1)}, bf16[32,2176]{1,0:T(8,128)(2,1)S(1)}, u32[]{:S(2)}, u32[]{:S(2)}) collective-permute-start(bf16[32,2176]{1,0:T(8,128)(2,1)S(1)} %pad_maximum_fusion.refs_0_), channel_id=1, source_target_pairs={{0,6},{2,4},{4,2},{6,0},{8,14},{10,12},{12,10},{14,8},{1,7},{3,5},... | collective-permute-start | bytes 417800 | tf_op jit(solution)/shard_map/ppermute | solution.py:177
  27.3 0.5 collective-permute-start.8
  27.8 1.4 %collective-permute-start.6 = (bf16[32,2176]{1,0:T(8,128)(2,1)S(1)}, bf16[32,2176]{1,0:T(8,128)(2,1)S(1)}, u32[]{:S(2)}, u32[]{:S(2)}) collective-permute-start(bf16[32,2176]{1,0:T(8,128)(2,1)S(1)} %pad_maximum_fusion.refs_0_), channel_id=1, source_target_pairs={{0,8},{4,12},{8,0},{12,4},{1,9},{5,13},{9,1},{13,5},{2,10},{6,14},... | collective-permute-start | bytes 417800 | tf_op jit(solution)/shard_map/ppermute | solution.py:170
  29.3 1.5 %collective-permute-start.5 = (bf16[32,2176]{1,0:T(8,128)(2,1)S(1)}, bf16[32,2176]{1,0:T(8,128)(2,1)S(1)}, u32[]{:S(2)}, u32[]{:S(2)}) collective-permute-start(bf16[32,2176]{1,0:T(8,128)(2,1)S(1)} %pad_maximum_fusion.refs_0_), channel_id=1, source_target_pairs={{0,4},{4,0},{8,12},{12,8},{1,5},{5,1},{9,13},{13,9},{2,6},{6,2},{1... | collective-permute-start | bytes 417800 | tf_op jit(solution)/shard_map/ppermute | solution.py:170
  30.8 3.3 %collective-permute-done.9.refs_5_ = bf16[32,2176]{1,0:T(8,128)(2,1)S(1)} collective-permute-done((bf16[32,2176]{1,0:T(8,128)(2,1)S(1)}, bf16[32,2176]{1,0:T(8,128)(2,1)S(1)}, u32[]{:S(2)}, u32[]{:S(2)}) %collective-permute-start.9) | collective-permute-done | bytes 139296 | tf_op jit(solution)/shard_map/ppermute | solution.py:177
  34.1 0.8 collective-permute-done.8.refs_4_
  34.9 0.8 collective-permute-done.6.refs_2_
  35.7 2.2 %collective-permute-start.11 = (bf16[32,2176]{1,0:T(8,128)(2,1)S(1)}, bf16[32,2176]{1,0:T(8,128)(2,1)S(1)}, u32[]{:S(2)}, u32[]{:S(2)}) collective-permute-start(bf16[32,2176]{1,0:T(8,128)(2,1)S(1)} %collective-permute-done.6.refs_2_), channel_id=1, source_target_pairs={{0,6},{2,4},{4,2},{6,0},{8,14},{10,12},{12,10},{14,8},{1,7},{3,5},... | collective-permute-start | bytes 417800 | tf_op jit(solution)/shard_map/ppermute | solution.py:177
  37.9 1.1 %collective-permute-start.10 = (bf16[32,2176]{1,0:T(8,128)(2,1)S(1)}, bf16[32,2176]{1,0:T(8,128)(2,1)S(1)}, u32[]{:S(2)}, u32[]{:S(2)}) collective-permute-start(bf16[32,2176]{1,0:T(8,128)(2,1)S(1)} %collective-permute-done.6.refs_2_), channel_id=1, source_target_pairs={{0,2},{2,0},{1,3},{3,1},{4,6},{6,4},{5,7},{7,5},{8,10},{10,8},{9,1... | collective-permute-start | bytes 417800 | tf_op jit(solution)/shard_map/ppermute | solution.py:170
  39.0 0.8 collective-permute-start.7
  39.9 0.5 collective-permute-start.13
  40.4 1.8 %collective-permute-done.11.refs_7_ = bf16[32,2176]{1,0:T(8,128)(2,1)S(1)} collective-permute-done((bf16[32,2176]{1,0:T(8,128)(2,1)S(1)}, bf16[32,2176]{1,0:T(8,128)(2,1)S(1)}, u32[]{:S(2)}, u32[]{:S(2)}) %collective-permute-start.11) | collective-permute-done | bytes 139296 | tf_op jit(solution)/shard_map/ppermute | solution.py:177
  42.2 2.7 %collective-permute-done.10.refs_6_ = bf16[32,2176]{1,0:T(8,128)(2,1)S(1)} collective-permute-done((bf16[32,2176]{1,0:T(8,128)(2,1)S(1)}, bf16[32,2176]{1,0:T(8,128)(2,1)S(1)}, u32[]{:S(2)}, u32[]{:S(2)}) %collective-permute-start.10) | collective-permute-done | bytes 139296 | tf_op jit(solution)/shard_map/ppermute | solution.py:170
  44.9 1.5 %collective-permute-done.7.refs_3_ = bf16[32,2176]{1,0:T(8,128)(2,1)S(1)} collective-permute-done((bf16[32,2176]{1,0:T(8,128)(2,1)S(1)}, bf16[32,2176]{1,0:T(8,128)(2,1)S(1)}, u32[]{:S(2)}, u32[]{:S(2)}) %collective-permute-start.7) | collective-permute-done | bytes 139296 | tf_op jit(solution)/shard_map/ppermute | solution.py:170
  46.5 1.3 %collective-permute-done.15.refs_11_ = bf16[32,2176]{1,0:T(8,128)(2,1)S(1)} collective-permute-done((bf16[32,2176]{1,0:T(8,128)(2,1)S(1)}, bf16[32,2176]{1,0:T(8,128)(2,1)S(1)}, u32[]{:S(2)}, u32[]{:S(2)}) %collective-permute-start.15) | collective-permute-done | bytes 139296 | tf_op jit(solution)/shard_map/ppermute | solution.py:170
  47.8 15.0 %experts.1 = (bf16[64,2048]{1,0:T(8,128)(2,1)S(1)}, bf16[64,2048]{1,0:T(8,128)(2,1)S(1)}, bf16[128,2048]{1,0:T(8,128)(2,1)S(1)}, bf16[64,2048]{1,0:T(8,128)(2,1)...) custom-call(s32[1]{0:T(128)} %bitcast.5.first_ref, bf16[32,2176]{1,0:T(8,128)(2,1)S(1)} %pad_maximum_fusion.refs_0_, ...), custom_call_target="tpu_custom_call" | custom-call | flops 3489660928 | bytes 39845888 | tf_op jit(solution)/shard_map/experts/pallas_call | solution.py:475
  62.7 0.2 collective-permute-start.26
  63.0 0.4 collective-permute-start.20
  63.3 0.2 collective-permute-start.21
  63.5 0.9 %collective-permute-done.26 = bf16[64,2048]{1,0:T(8,128)(2,1)S(1)} collective-permute-done((bf16[64,2048]{1,0:T(8,128)(2,1)S(1)}, bf16[64,2048]{1,0:T(8,128)(2,1)S(1)}, u32[]{:S(2)}, u32[]{:S(2)}) %collective-permute-start.26) | collective-permute-done | bytes 262176 | tf_op jit(solution)/shard_map/ppermute | solution.py:170
  64.4 0.9 %collective-permute-start.27 = (bf16[32,2048]{1,0:T(8,128)(2,1)S(1)}, bf16[32,2048]{1,0:T(8,128)(2,1)S(1)}, u32[]{:S(2)}, u32[]{:S(2)}) collective-permute-start(bf16[32,2048]{1,0:T(8,128)(2,1)S(1)} %get-tuple-element.46), channel_id=1, source_target_pairs={{0,2},{2,0},{1,3},{3,1},{4,6},{6,4},{5,7},{7,5},{8,10},{10,8},{9,1... | collective-permute-start | bytes 393224 | tf_op jit(solution)/shard_map/ppermute | solution.py:170
  65.3 1.1 %collective-permute-start.28 = (bf16[32,2048]{1,0:T(8,128)(2,1)S(1)}, bf16[32,2048]{1,0:T(8,128)(2,1)S(1)}, u32[]{:S(2)}, u32[]{:S(2)}) collective-permute-start(bf16[32,2048]{1,0:T(8,128)(2,1)S(1)} %get-tuple-element.47), channel_id=1, source_target_pairs={{0,6},{2,4},{4,2},{6,0},{8,14},{10,12},{12,10},{14,8},{1,7},{3,5},... | collective-permute-start | bytes 393224 | tf_op jit(solution)/shard_map/ppermute | solution.py:177
  66.5 0.1 add_convert_fusion
  66.6 1.7 %collective-permute-start.25 = (bf16[32,2048]{1,0:T(8,128)(2,1)S(1)}, bf16[32,2048]{1,0:T(8,128)(2,1)S(1)}, u32[]{:S(2)}, u32[]{:S(2)}) collective-permute-start(bf16[32,2048]{1,0:T(8,128)(2,1)S(1)} %slice.37), channel_id=1, source_target_pairs={{0,4},{4,0},{8,12},{12,8},{1,5},{5,1},{9,13},{13,9},{2,6},{6,2},{1... | collective-permute-start | bytes 393224 | tf_op jit(solution)/shard_map/ppermute | solution.py:170
  68.3 0.9 %collective-permute-start.22 = (bf16[32,2048]{1,0:T(8,128)(2,1)S(1)}, bf16[32,2048]{1,0:T(8,128)(2,1)S(1)}, u32[]{:S(2)}, u32[]{:S(2)}) collective-permute-start(bf16[32,2048]{1,0:T(8,128)(2,1)S(1)} %get-tuple-element.43), channel_id=1, source_target_pairs={{0,2},{2,0},{1,3},{3,1},{4,6},{6,4},{5,7},{7,5},{8,10},{10,8},{9,1... | collective-permute-start | bytes 393224 | tf_op jit(solution)/shard_map/ppermute | solution.py:170
  69.2 1.1 %collective-permute-start.24 = (bf16[32,2048]{1,0:T(8,128)(2,1)S(1)}, bf16[32,2048]{1,0:T(8,128)(2,1)S(1)}, u32[]{:S(2)}, u32[]{:S(2)}) collective-permute-start(bf16[32,2048]{1,0:T(8,128)(2,1)S(1)} %get-tuple-element.44), channel_id=1, source_target_pairs={{0,6},{2,4},{4,2},{6,0},{8,14},{10,12},{12,10},{14,8},{1,7},{3,5},... | collective-permute-start | bytes 393224 | tf_op jit(solution)/shard_map/ppermute | solution.py:177
  70.3 3.5 %collective-permute-done.27 = bf16[32,2048]{1,0:T(8,128)(2,1)S(1)} collective-permute-done((bf16[32,2048]{1,0:T(8,128)(2,1)S(1)}, bf16[32,2048]{1,0:T(8,128)(2,1)S(1)}, u32[]{:S(2)}, u32[]{:S(2)}) %collective-permute-start.27) | collective-permute-done | bytes 131104 | tf_op jit(solution)/shard_map/ppermute | solution.py:170
  73.8 0.7 collective-permute-start.23
  74.5 0.7 collective-permute-done.25
  75.2 0.1 collective-permute-start.29
  75.3 2.7 %collective-permute-done.22 = bf16[32,2048]{1,0:T(8,128)(2,1)S(1)} collective-permute-done((bf16[32,2048]{1,0:T(8,128)(2,1)S(1)}, bf16[32,2048]{1,0:T(8,128)(2,1)S(1)}, u32[]{:S(2)}, u32[]{:S(2)}) %collective-permute-start.22) | collective-permute-done | bytes 131104 | tf_op jit(solution)/shard_map/ppermute | solution.py:170
  78.1 1.6 %collective-permute-done.24 = bf16[32,2048]{1,0:T(8,128)(2,1)S(1)} collective-permute-done((bf16[32,2048]{1,0:T(8,128)(2,1)S(1)}, bf16[32,2048]{1,0:T(8,128)(2,1)S(1)}, u32[]{:S(2)}, u32[]{:S(2)}) %collective-permute-start.24) | collective-permute-done | bytes 131104 | tf_op jit(solution)/shard_map/ppermute | solution.py:177
  79.7 1.7 %collective-permute-done.23 = bf16[32,2048]{1,0:T(8,128)(2,1)S(1)} collective-permute-done((bf16[32,2048]{1,0:T(8,128)(2,1)S(1)}, bf16[32,2048]{1,0:T(8,128)(2,1)S(1)}, u32[]{:S(2)}, u32[]{:S(2)}) %collective-permute-start.23) | collective-permute-done | bytes 131104 | tf_op jit(solution)/shard_map/ppermute | solution.py:170
  81.4 1.8 %collective-permute-done.29 = bf16[32,2048]{1,0:T(8,128)(2,1)S(1)} collective-permute-done((bf16[32,2048]{1,0:T(8,128)(2,1)S(1)}, bf16[32,2048]{1,0:T(8,128)(2,1)S(1)}, u32[]{:S(2)}, u32[]{:S(2)}) %collective-permute-start.29) | collective-permute-done | bytes 131104 | tf_op jit(solution)/shard_map/ppermute | solution.py:170
  83.2 0.8 add_convert_fusion.3
  (32 shorter events, 0.4 us)
Async XLA Ops:
  0.8 14.8 %collective-permute-start.2 = (bf16[128,256]{1,0:T(8,128)(2,1)S(1)}, bf16[128,256]{1,0:T(8,128)(2,1)S(1)}, u32[]{:S(2)}, u32[]{:S(2)}) collective-permute-start(bf16[128,256]{1,0:T(8,128)(2,1)S(1)} %pad_maximum_fusion.1.kv_ref), channel_id=1, source_target_pairs={{0,12},{1,13},{2,14},{3,15},{16,28},{17,29},{18,30},{19,31}} | collective-permute-start | bytes 196616 | tf_op jit(solution)/shard_map/ppermute | solution.py:182
  7.8 7.9 %collective-permute-start.1 = (bf16[128,256]{1,0:T(8,128)(2,1)S(1)}, bf16[128,256]{1,0:T(8,128)(2,1)S(1)}, u32[]{:S(2)}, u32[]{:S(2)}) collective-permute-start(bf16[128,256]{1,0:T(8,128)(2,1)S(1)} %pad_maximum_fusion.1.kv_ref), channel_id=1, source_target_pairs={{0,8},{4,12},{1,9},{5,13},{2,10},{6,14},{3,11},{7,15},{16,24},{20,... | collective-permute-start | bytes 196616 | tf_op jit(solution)/shard_map/ppermute | solution.py:182
  9.1 6.6 %collective-permute-start = (bf16[128,256]{1,0:T(8,128)(2,1)S(1)}, bf16[128,256]{1,0:T(8,128)(2,1)S(1)}, u32[]{:S(2)}, u32[]{:S(2)}) collective-permute-start(bf16[128,256]{1,0:T(8,128)(2,1)S(1)} %pad_maximum_fusion.1.kv_ref), channel_id=1, source_target_pairs={{0,4},{4,8},{8,12},{1,5},{5,9},{9,13},{2,6},{6,10},{10,14},{3,7},{... | collective-permute-start | bytes 196616 | tf_op jit(solution)/shard_map/ppermute | solution.py:182
  18.6 1.6 %collective-permute-start.3 = (bf16[64,2048]{1,0:T(8,128)(2,1)S(1)}, bf16[64,2048]{1,0:T(8,128)(2,1)S(1)}, u32[]{:S(2)}, u32[]{:S(2)}) collective-permute-start(bf16[64,2048]{1,0:T(8,128)(2,1)S(1)} %get-tuple-element.30), channel_id=1, source_target_pairs={{0,1},{1,0},{2,3},{3,2},{4,5},{5,4},{6,7},{7,6},{8,9},{9,8},{10,11... | collective-permute-start | bytes 786440 | tf_op jit(solution)/shard_map/ppermute | solution.py:170
  20.3 5.6 %collective-permute-start.4 = (bf16[32,2048]{1,0:T(8,128)(2,1)S(1)}, bf16[32,2048]{1,0:T(8,128)(2,1)S(1)}, u32[]{:S(2)}, u32[]{:S(2)}) collective-permute-start(bf16[32,2048]{1,0:T(8,128)(2,1)S(1)} %fusion), channel_id=1, source_target_pairs={{0,2},{2,0},{1,3},{3,1},{4,6},{6,4},{5,7},{7,5},{8,10},{10,8},{9,1... | collective-permute-start | bytes 393224 | tf_op jit(solution)/shard_map/ppermute | solution.py:170
  26.2 7.9 %collective-permute-start.9 = (bf16[32,2176]{1,0:T(8,128)(2,1)S(1)}, bf16[32,2176]{1,0:T(8,128)(2,1)S(1)}, u32[]{:S(2)}, u32[]{:S(2)}) collective-permute-start(bf16[32,2176]{1,0:T(8,128)(2,1)S(1)} %pad_maximum_fusion.refs_0_), channel_id=1, source_target_pairs={{0,6},{2,4},{4,2},{6,0},{8,14},{10,12},{12,10},{14,8},{1,7},{3,5},... | collective-permute-start | bytes 417800 | tf_op jit(solution)/shard_map/ppermute | solution.py:177
  27.3 7.6 %collective-permute-start.8 = (bf16[32,2176]{1,0:T(8,128)(2,1)S(1)}, bf16[32,2176]{1,0:T(8,128)(2,1)S(1)}, u32[]{:S(2)}, u32[]{:S(2)}) collective-permute-start(bf16[32,2176]{1,0:T(8,128)(2,1)S(1)} %pad_maximum_fusion.refs_0_), channel_id=1, source_target_pairs={{0,2},{2,0},{1,3},{3,1},{4,6},{6,4},{5,7},{7,5},{8,10},{10,8},{9,1... | collective-permute-start | bytes 417800 | tf_op jit(solution)/shard_map/ppermute | solution.py:170
  27.8 7.8 %collective-permute-start.6 = (bf16[32,2176]{1,0:T(8,128)(2,1)S(1)}, bf16[32,2176]{1,0:T(8,128)(2,1)S(1)}, u32[]{:S(2)}, u32[]{:S(2)}) collective-permute-start(bf16[32,2176]{1,0:T(8,128)(2,1)S(1)} %pad_maximum_fusion.refs_0_), channel_id=1, source_target_pairs={{0,8},{4,12},{8,0},{12,4},{1,9},{5,13},{9,1},{13,5},{2,10},{6,14},... | collective-permute-start | bytes 417800 | tf_op jit(solution)/shard_map/ppermute | solution.py:170
  29.3 8.7 %collective-permute-start.12 = (bf16[32,2176]{1,0:T(8,128)(2,1)S(1)}, bf16[32,2176]{1,0:T(8,128)(2,1)S(1)}, u32[]{:S(2)}, u32[]{:S(2)}) collective-permute-start(bf16[32,2176]{1,0:T(8,128)(2,1)S(1)} %pad_maximum_fusion.refs_0_), channel_id=1, source_target_pairs={{0,1},{1,0},{2,3},{3,2},{4,5},{5,4},{6,7},{7,6},{8,9},{9,8},{10,11... | collective-permute-start | bytes 417800 | tf_op jit(solution)/shard_map/ppermute | solution.py:170
  29.3 9.8 %collective-permute-start.5 = (bf16[32,2176]{1,0:T(8,128)(2,1)S(1)}, bf16[32,2176]{1,0:T(8,128)(2,1)S(1)}, u32[]{:S(2)}, u32[]{:S(2)}) collective-permute-start(bf16[32,2176]{1,0:T(8,128)(2,1)S(1)} %pad_maximum_fusion.refs_0_), channel_id=1, source_target_pairs={{0,4},{4,0},{8,12},{12,8},{1,5},{5,1},{9,13},{13,9},{2,6},{6,2},{1... | collective-permute-start | bytes 417800 | tf_op jit(solution)/shard_map/ppermute | solution.py:170
  34.1 5.8 %collective-permute-start.17 = (bf16[32,2176]{1,0:T(8,128)(2,1)S(1)}, bf16[32,2176]{1,0:T(8,128)(2,1)S(1)}, u32[]{:S(2)}, u32[]{:S(2)}) collective-permute-start(bf16[32,2176]{1,0:T(8,128)(2,1)S(1)} %collective-permute-done.9.refs_5_), channel_id=1, source_target_pairs={{0,1},{1,0},{2,3},{3,2},{4,5},{5,4},{6,7},{7,6},{8,9},{9,8},{10,11... | collective-permute-start | bytes 417800 | tf_op jit(solution)/shard_map/ppermute | solution.py:170
  34.9 5.0 %collective-permute-start.16 = (bf16[32,2176]{1,0:T(8,128)(2,1)S(1)}, bf16[32,2176]{1,0:T(8,128)(2,1)S(1)}, u32[]{:S(2)}, u32[]{:S(2)}) collective-permute-start(bf16[32,2176]{1,0:T(8,128)(2,1)S(1)} %collective-permute-done.8.refs_4_), channel_id=1, source_target_pairs={{0,1},{1,0},{2,3},{3,2},{4,5},{5,4},{6,7},{7,6},{8,9},{9,8},{10,11... | collective-permute-start | bytes 417800 | tf_op jit(solution)/shard_map/ppermute | solution.py:170
  35.7 6.5 %collective-permute-start.11 = (bf16[32,2176]{1,0:T(8,128)(2,1)S(1)}, bf16[32,2176]{1,0:T(8,128)(2,1)S(1)}, u32[]{:S(2)}, u32[]{:S(2)}) collective-permute-start(bf16[32,2176]{1,0:T(8,128)(2,1)S(1)} %collective-permute-done.6.refs_2_), channel_id=1, source_target_pairs={{0,6},{2,4},{4,2},{6,0},{8,14},{10,12},{12,10},{14,8},{1,7},{3,5},... | collective-permute-start | bytes 417800 | tf_op jit(solution)/shard_map/ppermute | solution.py:177
  37.9 6.9 %collective-permute-start.10 = (bf16[32,2176]{1,0:T(8,128)(2,1)S(1)}, bf16[32,2176]{1,0:T(8,128)(2,1)S(1)}, u32[]{:S(2)}, u32[]{:S(2)}) collective-permute-start(bf16[32,2176]{1,0:T(8,128)(2,1)S(1)} %collective-permute-done.6.refs_2_), channel_id=1, source_target_pairs={{0,2},{2,0},{1,3},{3,1},{4,6},{6,4},{5,7},{7,5},{8,10},{10,8},{9,1... | collective-permute-start | bytes 417800 | tf_op jit(solution)/shard_map/ppermute | solution.py:170
  39.0 7.4 %collective-permute-start.7 = (bf16[32,2176]{1,0:T(8,128)(2,1)S(1)}, bf16[32,2176]{1,0:T(8,128)(2,1)S(1)}, u32[]{:S(2)}, u32[]{:S(2)}) collective-permute-start(bf16[32,2176]{1,0:T(8,128)(2,1)S(1)} %collective-permute-done.6.refs_2_), channel_id=1, source_target_pairs={{0,4},{4,0},{8,12},{12,8},{1,5},{5,1},{9,13},{13,9},{2,6},{6,2},{1... | collective-permute-start | bytes 417800 | tf_op jit(solution)/shard_map/ppermute | solution.py:170
  39.8 6.6 %collective-permute-start.14 = (bf16[32,2176]{1,0:T(8,128)(2,1)S(1)}, bf16[32,2176]{1,0:T(8,128)(2,1)S(1)}, u32[]{:S(2)}, u32[]{:S(2)}) collective-permute-start(bf16[32,2176]{1,0:T(8,128)(2,1)S(1)} %collective-permute-done.6.refs_2_), channel_id=1, source_target_pairs={{0,1},{1,0},{2,3},{3,2},{4,5},{5,4},{6,7},{7,6},{8,9},{9,8},{10,11... | collective-permute-start | bytes 417800 | tf_op jit(solution)/shard_map/ppermute | solution.py:170
  39.9 6.6 %collective-permute-start.13 = (bf16[32,2176]{1,0:T(8,128)(2,1)S(1)}, bf16[32,2176]{1,0:T(8,128)(2,1)S(1)}, u32[]{:S(2)}, u32[]{:S(2)}) collective-permute-start(bf16[32,2176]{1,0:T(8,128)(2,1)S(1)} %collective-permute-done.5.refs_1_), channel_id=1, source_target_pairs={{0,1},{1,0},{2,3},{3,2},{4,5},{5,4},{6,7},{7,6},{8,9},{9,8},{10,11... | collective-permute-start | bytes 417800 | tf_op jit(solution)/shard_map/ppermute | solution.py:170
  42.2 4.2 %collective-permute-start.19 = (bf16[32,2176]{1,0:T(8,128)(2,1)S(1)}, bf16[32,2176]{1,0:T(8,128)(2,1)S(1)}, u32[]{:S(2)}, u32[]{:S(2)}) collective-permute-start(bf16[32,2176]{1,0:T(8,128)(2,1)S(1)} %collective-permute-done.11.refs_7_), channel_id=1, source_target_pairs={{0,1},{1,0},{2,3},{3,2},{4,5},{5,4},{6,7},{7,6},{8,9},{9,8},{10,11... | collective-permute-start | bytes 417800 | tf_op jit(solution)/shard_map/ppermute | solution.py:170
  44.9 1.6 %collective-permute-start.18 = (bf16[32,2176]{1,0:T(8,128)(2,1)S(1)}, bf16[32,2176]{1,0:T(8,128)(2,1)S(1)}, u32[]{:S(2)}, u32[]{:S(2)}) collective-permute-start(bf16[32,2176]{1,0:T(8,128)(2,1)S(1)} %collective-permute-done.10.refs_6_), channel_id=1, source_target_pairs={{0,1},{1,0},{2,3},{3,2},{4,5},{5,4},{6,7},{7,6},{8,9},{9,8},{10,11... | collective-permute-start | bytes 417800 | tf_op jit(solution)/shard_map/ppermute | solution.py:170
  46.4 1.4 %collective-permute-start.15 = (bf16[32,2176]{1,0:T(8,128)(2,1)S(1)}, bf16[32,2176]{1,0:T(8,128)(2,1)S(1)}, u32[]{:S(2)}, u32[]{:S(2)}) collective-permute-start(bf16[32,2176]{1,0:T(8,128)(2,1)S(1)} %collective-permute-done.7.refs_3_), channel_id=1, source_target_pairs={{0,1},{1,0},{2,3},{3,2},{4,5},{5,4},{6,7},{7,6},{8,9},{9,8},{10,11... | collective-permute-start | bytes 417800 | tf_op jit(solution)/shard_map/ppermute | solution.py:170
  62.7 1.6 %collective-permute-start.26 = (bf16[64,2048]{1,0:T(8,128)(2,1)S(1)}, bf16[64,2048]{1,0:T(8,128)(2,1)S(1)}, u32[]{:S(2)}, u32[]{:S(2)}) collective-permute-start(bf16[64,2048]{1,0:T(8,128)(2,1)S(1)} %get-tuple-element.40), channel_id=1, source_target_pairs={{0,1},{1,0},{2,3},{3,2},{4,5},{5,4},{6,7},{7,6},{8,9},{9,8},{10,11... | collective-permute-start | bytes 786440 | tf_op jit(solution)/shard_map/ppermute | solution.py:170
  63.0 3.4 %collective-permute-start.20 = (bf16[64,2048]{1,0:T(8,128)(2,1)S(1)}, bf16[64,2048]{1,0:T(8,128)(2,1)S(1)}, u32[]{:S(2)}, u32[]{:S(2)}) collective-permute-start(bf16[64,2048]{1,0:T(8,128)(2,1)S(1)} %get-tuple-element.34), channel_id=1, source_target_pairs={{0,1},{1,0},{2,3},{3,2},{4,5},{5,4},{6,7},{7,6},{8,9},{9,8},{10,11... | collective-permute-start | bytes 786440 | tf_op jit(solution)/shard_map/ppermute | solution.py:170
  63.3 3.2 %collective-permute-start.21 = (bf16[128,2048]{1,0:T(8,128)(2,1)S(1)}, bf16[128,2048]{1,0:T(8,128)(2,1)S(1)}, u32[]{:S(2)}, u32[]{:S(2)}) collective-permute-start(bf16[128,2048]{1,0:T(8,128)(2,1)S(1)} %get-tuple-element.36), channel_id=1, source_target_pairs={{0,1},{1,0},{2,3},{3,2},{4,5},{5,4},{6,7},{7,6},{8,9},{9,8},{10,11... | collective-permute-start | bytes 1572872 | tf_op jit(solution)/shard_map/ppermute | solution.py:170
  64.4 9.3 %collective-permute-start.27 = (bf16[32,2048]{1,0:T(8,128)(2,1)S(1)}, bf16[32,2048]{1,0:T(8,128)(2,1)S(1)}, u32[]{:S(2)}, u32[]{:S(2)}) collective-permute-start(bf16[32,2048]{1,0:T(8,128)(2,1)S(1)} %get-tuple-element.46), channel_id=1, source_target_pairs={{0,2},{2,0},{1,3},{3,1},{4,6},{6,4},{5,7},{7,5},{8,10},{10,8},{9,1... | collective-permute-start | bytes 393224 | tf_op jit(solution)/shard_map/ppermute | solution.py:170
  65.3 9.1 %collective-permute-start.28 = (bf16[32,2048]{1,0:T(8,128)(2,1)S(1)}, bf16[32,2048]{1,0:T(8,128)(2,1)S(1)}, u32[]{:S(2)}, u32[]{:S(2)}) collective-permute-start(bf16[32,2048]{1,0:T(8,128)(2,1)S(1)} %get-tuple-element.47), channel_id=1, source_target_pairs={{0,6},{2,4},{4,2},{6,0},{8,14},{10,12},{12,10},{14,8},{1,7},{3,5},... | collective-permute-start | bytes 393224 | tf_op jit(solution)/shard_map/ppermute | solution.py:177
  66.6 8.5 %collective-permute-start.25 = (bf16[32,2048]{1,0:T(8,128)(2,1)S(1)}, bf16[32,2048]{1,0:T(8,128)(2,1)S(1)}, u32[]{:S(2)}, u32[]{:S(2)}) collective-permute-start(bf16[32,2048]{1,0:T(8,128)(2,1)S(1)} %slice.37), channel_id=1, source_target_pairs={{0,4},{4,0},{8,12},{12,8},{1,5},{5,1},{9,13},{13,9},{2,6},{6,2},{1... | collective-permute-start | bytes 393224 | tf_op jit(solution)/shard_map/ppermute | solution.py:170
  68.3 9.7 %collective-permute-start.22 = (bf16[32,2048]{1,0:T(8,128)(2,1)S(1)}, bf16[32,2048]{1,0:T(8,128)(2,1)S(1)}, u32[]{:S(2)}, u32[]{:S(2)}) collective-permute-start(bf16[32,2048]{1,0:T(8,128)(2,1)S(1)} %get-tuple-element.43), channel_id=1, source_target_pairs={{0,2},{2,0},{1,3},{3,1},{4,6},{6,4},{5,7},{7,5},{8,10},{10,8},{9,1... | collective-permute-start | bytes 393224 | tf_op jit(solution)/shard_map/ppermute | solution.py:170
  69.2 10.4 %collective-permute-start.24 = (bf16[32,2048]{1,0:T(8,128)(2,1)S(1)}, bf16[32,2048]{1,0:T(8,128)(2,1)S(1)}, u32[]{:S(2)}, u32[]{:S(2)}) collective-permute-start(bf16[32,2048]{1,0:T(8,128)(2,1)S(1)} %get-tuple-element.44), channel_id=1, source_target_pairs={{0,6},{2,4},{4,2},{6,0},{8,14},{10,12},{12,10},{14,8},{1,7},{3,5},... | collective-permute-start | bytes 393224 | tf_op jit(solution)/shard_map/ppermute | solution.py:177
  73.8 7.6 %collective-permute-start.23 = (bf16[32,2048]{1,0:T(8,128)(2,1)S(1)}, bf16[32,2048]{1,0:T(8,128)(2,1)S(1)}, u32[]{:S(2)}, u32[]{:S(2)}) collective-permute-start(bf16[32,2048]{1,0:T(8,128)(2,1)S(1)} %get-tuple-element.45), channel_id=1, source_target_pairs={{0,4},{4,0},{8,12},{12,8},{1,5},{5,1},{9,13},{13,9},{2,6},{6,2},{1... | collective-permute-start | bytes 393224 | tf_op jit(solution)/shard_map/ppermute | solution.py:170
  75.2 8.0 %collective-permute-start.29 = (bf16[32,2048]{1,0:T(8,128)(2,1)S(1)}, bf16[32,2048]{1,0:T(8,128)(2,1)S(1)}, u32[]{:S(2)}, u32[]{:S(2)}) collective-permute-start(bf16[32,2048]{1,0:T(8,128)(2,1)S(1)} %add_convert_fusion.4), channel_id=1, source_target_pairs={{0,8},{4,12},{8,0},{12,4},{1,9},{5,13},{9,1},{13,5},{2,10},{6,14},... | collective-permute-start | bytes 393224 | tf_op jit(solution)/shard_map/ppermute | solution.py:170

commit v8 on v7

--- a/solution.py
+++ b/solution.py
@@ -307,7 +307,8 @@
         k_all[z * rows : (z + 1) * rows, :] = kv_refs[z][:, :HEAD_DIMENSION]
         v_all[z * rows : (z + 1) * rows, :HEAD_DIMENSION] = kv_refs[z][:, HEAD_DIMENSION:]
     v_all[:, HEAD_DIMENSION:] = jnp.ones(((n_ctx - 1) * rows, HEAD_DIMENSION), BF)
-    allowed = lax.broadcasted_iota(jnp.int32, (1, (n_ctx - 1) * rows), 1) < ctx * rows
+    column = lax.broadcasted_iota(jnp.int32, (1, (n_ctx - 1) * rows), 1)
+    allowed = column >= (n_ctx - 1 - ctx) * rows
     scale = 1.0 / math.sqrt(HEAD_DIMENSION)
     for h in range(heads):
         columns = slice(h * HEAD_DIMENSION, (h + 1) * HEAD_DIMENSION)
@@ -372,21 +373,23 @@
     blocks = n_pieces // (2 * sides)
     part = tokens // (2 * blocks)
 
-    def copies(e):
-        slot = lax.rem(e, depth)
-        rows = pl.ds(e * halves, halves)
+    def gate_up_copies(e):
+        slot, rows = lax.rem(e, depth), pl.ds(e * halves, halves)
         return (
             pltpu.make_async_copy(wg_hbm.at[rows], wgu.at[slot, 0], sems.at[0, slot]),
             pltpu.make_async_copy(wu_hbm.at[rows], wgu.at[slot, 1], sems.at[1, slot]),
-            pltpu.make_async_copy(wd_hbm.at[rows], wd.at[slot], sems.at[2, slot]),
         )
 
-    def start(e):
-        for copy in copies(e):
+    def down_copies(e):
+        slot, rows = lax.rem(e, depth), pl.ds(e * halves, halves)
+        return (pltpu.make_async_copy(wd_hbm.at[rows], wd.at[slot], sems.at[2, slot]),)
+
+    def start(copies):
+        for copy in copies:
             copy.start()
 
-    def wait(e):
-        for copy in copies(e):
+    def wait(copies):
+        for copy in copies:
             copy.wait()
 
     def of_expert(e):
@@ -409,8 +412,10 @@
         for side in range(sides):
             out_all[side, of_expert(e), :] = out[side * slots : (side + 1) * slots]
 
-    for e in range(min(depth - 1, experts)):
-        start(e)
+    for e in range(depth - 1):
+        start(gate_up_copies(e))
+        if e:
+            start(down_copies(e - 1))
     for i, piece in enumerate(pieces):
         core, side, block = i // (sides * blocks), i // blocks % sides, i % blocks
         rows = slice((core * blocks + block) * part, (core * blocks + block + 1) * part)
@@ -436,21 +441,27 @@
         out_all[side] = jnp.dot(
             pick_all[side], x_all[side], preferred_element_type=F32
         ).astype(BF)
-    wait(0)
+    wait(gate_up_copies(0))
     act[0] = gate_up(0)
 
     @pl.loop(0, experts - 1)
     def _(e):
         @pl.when(e + depth - 1 < experts)
         def _():
-            start(e + depth - 1)
-
-        wait(e + 1)
+            start(gate_up_copies(e + depth - 1))
+
+        @pl.when(e + depth - 2 < experts)
+        def _():
+            start(down_copies(e + depth - 2))
+
+        wait(down_copies(e))
+        wait(gate_up_copies(e + 1))
         following = gate_up(e + 1)
         out = down(e)
         act[lax.rem(e + 1, 2)] = following
         keep(e, out)
 
+    wait(down_copies(experts - 1))
     keep(experts - 1, down(experts - 1))
     half = blocks * part // 2
     for side in (1, 0):
@@ -466,7 +477,7 @@
     halves, sides = 2, 2
     experts = rows // halves
     tokens = len(pieces) * pieces[0].shape[0] // sides
-    depth = min(4, experts)
+    depth = 4
     vmem = pl.BlockSpec(memory_space=pltpu.VMEM)
     hbm = pl.BlockSpec(memory_space=pltpu.HBM)
 
@@ -551,7 +562,7 @@
     key_head = lax.dynamic_slice_in_dim(keys, shared * HEAD_DIMENSION, HEAD_DIMENSION, 1)
     value_head = lax.dynamic_slice_in_dim(values, shared * HEAD_DIMENSION, HEAD_DIMENSION, 1)
     kv = jnp.concatenate([key_head, value_head], axis=1)
-    kv_pieces = [from_earlier(kv, "ctx", z) for z in range(1, n_ctx)]
+    kv_pieces = [from_earlier(kv, "ctx", z) for z in range(n_ctx - 1, 0, -1)]
     *own, routing = own_block(
         place, kv, expert_ids, router_probs, queries, out_weight, resid, n_exp, n_tp
     )
@@ -571,8 +582,10 @@
     far_across = flip(far, "exp", 1)
     last_across = flip_both(far)
     last = flip(far, "ctx", 1)
+    early = lax.optimization_barrier((normed, near, far, across, near_across))
     pieces = [normed, near, far, last, across, near_across, far_across, last_across]
-    pieces += [flip(piece, "tp", 1) for piece in pieces]
+    pieces += [flip(piece, "tp", 1) for piece in early[:3] + (last,)]
+    pieces += [flip(piece, "tp", 1) for piece in early[3:] + (far_across, last_across)]
     sums = cube_experts(
         first.astype(jnp.int32).reshape(1), pieces, w_gate, w_up, w_down, slots
     )

time: 84.2 us -> 82.8 us (0.983)
  starting transfers between devices: 28.7 us -> 27.2 us
    ppermute x23, waiting for transfers between devices: 24.1 us -> 26.7 us  [flip(): lax.ppermute(x, axis, [(i, i ^ bit) for i in range(lax.axis_size(axis))])]
    ppermute x4, waiting for transfers between devices: 6.75 us -> 4.65 us  [flip_both(): return lax.ppermute(x, ('ctx', 'exp'), [(i, i ^ mask) for i in range(size)])]
    ppermute x23, starting transfers between devices: 12.4 us -> 11.2 us  [flip(): lax.ppermute(x, axis, [(i, i ^ bit) for i in range(lax.axis_size(axis))])]
  transfers between devices with their start and end apart: 30 -> 30, of which waited for: 16 -> 19; matrix products, arithmetic and copies ran while one was open for 1% -> 1% of each run, Pallas kernels for 5% -> 5%
where the time goes in v8:
time: 82.8 us; the launch traced here: 82.6 us
  waiting for transfers between devices  31.4 us (38%)
  starting transfers between devices  27.2 us (33%)
  Pallas kernels  21.4 us (26%)
  other arithmetic  1.52 us (2%)
  local copies, waits for them, and re-layouts  0.84 us (1%)
    ppermute x23, waiting for transfers between devices, flip(): lax.ppermute(x, axis, [(i, i ^ bit) for i in range(lax.axis_size(axis))])  26.7 us
    pallas_call x1, Pallas kernels, cube_experts(): pl.pallas_call(functools.partial(expert_kernel, len(pieces), depth, exper...  14.5 us
    ppermute x23, starting transfers between devices, flip(): lax.ppermute(x, axis, [(i, i ^ bit) for i in range(lax.axis_size(axis))])  11.2 us
    ppermute x3, starting transfers between devices, from_earlier(): return lax.ppermute(x, axis, [(i, i + steps) for i in range(size - steps)])  10.7 us
    ppermute x4, starting transfers between devices, flip_both(): return lax.ppermute(x, ('ctx', 'exp'), [(i, i ^ mask) for i in range(size)])  5.34 us
    ppermute x4, waiting for transfers between devices, flip_both(): return lax.ppermute(x, ('ctx', 'exp'), [(i, i ^ mask) for i in range(size)])  4.65 us
    pallas_call x1, Pallas kernels, own_block(): pl.pallas_call(functools.partial(own_block_kernel, (n_exp, n_tp, heads, p...  3.97 us
    pallas_call x1, Pallas kernels, attend_project(): pl.pallas_call(functools.partial(attention_kernel, (n_ctx, n_exp, n_tp, h...  2.95 us
  transfers between devices with their start and end apart: 30, of which 19 were waited for; matrix products, arithmetic and copies ran while one was open for 1% of the time, Pallas kernels for 5%

profile of v8, /device:TPU:0, one launch (start us, length us, event | category | flops | bytes accessed | tf_op | source)
XLA Modules:
  0.0 82.6 jit_solution(5931938028954542387)
XLA Ops:
  0.0 0.8 constant_dynamic-slice_fusion
  0.8 4.9 %collective-permute-start.2 = (bf16[128,256]{1,0:T(8,128)(2,1)S(1)}, bf16[128,256]{1,0:T(8,128)(2,1)S(1)}, u32[]{:S(2)}, u32[]{:S(2)}) collective-permute-start(bf16[128,256]{1,0:T(8,128)(2,1)S(1)} %pad_maximum_fusion.1.kv_ref), channel_id=1, source_target_pairs={{0,4},{4,8},{8,12},{1,5},{5,9},{9,13},{2,6},{6,10},{10,14},{3,7},{... | collective-permute-start | bytes 196616 | tf_op jit(solution)/shard_map/ppermute | solution.py:182
  5.7 4.5 %collective-permute-start.1 = (bf16[128,256]{1,0:T(8,128)(2,1)S(1)}, bf16[128,256]{1,0:T(8,128)(2,1)S(1)}, u32[]{:S(2)}, u32[]{:S(2)}) collective-permute-start(bf16[128,256]{1,0:T(8,128)(2,1)S(1)} %pad_maximum_fusion.1.kv_ref), channel_id=1, source_target_pairs={{0,8},{4,12},{1,9},{5,13},{2,10},{6,14},{3,11},{7,15},{16,24},{20,... | collective-permute-start | bytes 196616 | tf_op jit(solution)/shard_map/ppermute | solution.py:182
  10.2 1.3 %collective-permute-start = (bf16[128,256]{1,0:T(8,128)(2,1)S(1)}, bf16[128,256]{1,0:T(8,128)(2,1)S(1)}, u32[]{:S(2)}, u32[]{:S(2)}) collective-permute-start(bf16[128,256]{1,0:T(8,128)(2,1)S(1)} %pad_maximum_fusion.1.kv_ref), channel_id=1, source_target_pairs={{0,12},{1,13},{2,14},{3,15},{16,28},{17,29},{18,30},{19,31}} | collective-permute-start | bytes 196616 | tf_op jit(solution)/shard_map/ppermute | solution.py:182
  11.6 4.0 %own_block.1 = (bf16[128,1024]{1,0:T(8,128)(2,1)S(1)}, bf16[1024,2048]{1,0:T(8,128)(2,1)S(1)}, bf16[32,2048]{1,0:T(8,128)(2,1)S(1)}, f32[128,1024]{1,0:T(8,128)S...) custom-call(s32[3]{0:T(128)S(1)} %pad_add_fusion.place, ...), custom_call_target="tpu_custom_call" | custom-call | flops 100663296 | bytes 4980736 | tf_op jit(solution)/shard_map/own_block/pallas_call | solution.py:263
  15.6 3.0 %attend_project.1 = (f32[32,2048]{1,0:T(8,128)S(1)}, bf16[32,2048]{1,0:T(8,128)(2,1)S(1)}, bf16[64,2048]{1,0:T(8,128)(2,1)S(1)}) custom-call(s32[3]{0:T(128)S(1)} %pad_add_fusion.place, bf16[128,256]{1,0:T(8,128)(2,1)S(1)} %collective-permute-done.refs_0_, bf16[128,256]{1,0:T(8,128)(2,1)S(1)} %collective-permute-done.1.refs_1_, ...), custom_call_target="tpu_custom_call" | custom-call | flops 838860800 | bytes 4980736 | tf_op jit(solution)/shard_map/attend_project/pallas_call | solution.py:341
  18.7 1.5 %collective-permute-done.3 = bf16[64,2048]{1,0:T(8,128)(2,1)S(1)} collective-permute-done((bf16[64,2048]{1,0:T(8,128)(2,1)S(1)}, bf16[64,2048]{1,0:T(8,128)(2,1)S(1)}, u32[]{:S(2)}, u32[]{:S(2)}) %collective-permute-start.3) | collective-permute-done | bytes 262176 | tf_op jit(solution)/shard_map/ppermute | solution.py:170
  20.3 1.6 %collective-permute-start.4 = (bf16[32,2048]{1,0:T(8,128)(2,1)S(1)}, bf16[32,2048]{1,0:T(8,128)(2,1)S(1)}, u32[]{:S(2)}, u32[]{:S(2)}) collective-permute-start(bf16[32,2048]{1,0:T(8,128)(2,1)S(1)} %fusion), channel_id=1, source_target_pairs={{0,2},{2,0},{1,3},{3,1},{4,6},{6,4},{5,7},{7,5},{8,10},{10,8},{9,1... | collective-permute-start | bytes 393224 | tf_op jit(solution)/shard_map/ppermute | solution.py:170
  21.8 4.0 %collective-permute-done.4 = bf16[32,2048]{1,0:T(8,128)(2,1)S(1)} collective-permute-done((bf16[32,2048]{1,0:T(8,128)(2,1)S(1)}, bf16[32,2048]{1,0:T(8,128)(2,1)S(1)}, u32[]{:S(2)}, u32[]{:S(2)}) %collective-permute-start.4) | collective-permute-done | bytes 131104 | tf_op jit(solution)/shard_map/ppermute | solution.py:170
  25.9 0.2 multiply_reduce_fusion
  26.1 0.1 multiply_convert_fusion
  26.2 0.4 collective-permute-start.6
  26.6 3.1 %collective-permute-start.9 = (bf16[32,2176]{1,0:T(8,128)(2,1)S(1)}, bf16[32,2176]{1,0:T(8,128)(2,1)S(1)}, u32[]{:S(2)}, u32[]{:S(2)}) collective-permute-start(bf16[32,2176]{1,0:T(8,128)(2,1)S(1)} %pad_maximum_fusion.refs_0_), channel_id=1, source_target_pairs={{0,6},{2,4},{4,2},{6,0},{8,14},{10,12},{12,10},{14,8},{1,7},{3,5},... | collective-permute-start | bytes 417800 | tf_op jit(solution)/shard_map/ppermute | solution.py:177
  29.7 0.5 collective-permute-start.8
  30.2 4.2 %collective-permute-done.6.refs_2_ = bf16[32,2176]{1,0:T(8,128)(2,1)S(1)} collective-permute-done((bf16[32,2176]{1,0:T(8,128)(2,1)S(1)}, bf16[32,2176]{1,0:T(8,128)(2,1)S(1)}, u32[]{:S(2)}, u32[]{:S(2)}) %collective-permute-start.6) | collective-permute-done | bytes 139296 | tf_op jit(solution)/shard_map/ppermute | solution.py:170
  34.4 1.5 %collective-permute-start.10 = (bf16[32,2176]{1,0:T(8,128)(2,1)S(1)}, bf16[32,2176]{1,0:T(8,128)(2,1)S(1)}, u32[]{:S(2)}, u32[]{:S(2)}) collective-permute-start(bf16[32,2176]{1,0:T(8,128)(2,1)S(1)} %collective-permute-done.6.refs_2_), channel_id=1, source_target_pairs={{0,2},{2,0},{1,3},{3,1},{4,6},{6,4},{5,7},{7,5},{8,10},{10,8},{9,1... | collective-permute-start | bytes 417800 | tf_op jit(solution)/shard_map/ppermute | solution.py:170
  35.9 0.7 collective-permute-done.9.refs_5_
  36.6 2.5 %collective-permute-done.5.refs_1_ = bf16[32,2176]{1,0:T(8,128)(2,1)S(1)} collective-permute-done((bf16[32,2176]{1,0:T(8,128)(2,1)S(1)}, bf16[32,2176]{1,0:T(8,128)(2,1)S(1)}, u32[]{:S(2)}, u32[]{:S(2)}) %collective-permute-start.5) | collective-permute-done | bytes 139296 | tf_op jit(solution)/shard_map/ppermute | solution.py:170
  39.1 0.5 collective-permute-start.13
  39.6 2.6 %collective-permute-done.11.refs_7_ = bf16[32,2176]{1,0:T(8,128)(2,1)S(1)} collective-permute-done((bf16[32,2176]{1,0:T(8,128)(2,1)S(1)}, bf16[32,2176]{1,0:T(8,128)(2,1)S(1)}, u32[]{:S(2)}, u32[]{:S(2)}) %collective-permute-start.11) | collective-permute-done | bytes 139296 | tf_op jit(solution)/shard_map/ppermute | solution.py:177
  42.2 0.7 collective-permute-done.10.refs_6_
  42.9 1.5 %collective-permute-done.7.refs_3_ = bf16[32,2176]{1,0:T(8,128)(2,1)S(1)} collective-permute-done((bf16[32,2176]{1,0:T(8,128)(2,1)S(1)}, bf16[32,2176]{1,0:T(8,128)(2,1)S(1)}, u32[]{:S(2)}, u32[]{:S(2)}) %collective-permute-start.7) | collective-permute-done | bytes 139296 | tf_op jit(solution)/shard_map/ppermute | solution.py:170
  44.5 0.5 collective-permute-start.19
  45.0 0.4 collective-permute-start.15
  45.5 0.3 collective-permute-done.17.refs_13_
  45.8 0.2 collective-permute-done.19.refs_15_
  46.0 0.3 collective-permute-done.18.refs_14_
  46.3 0.2 collective-permute-done.15.refs_11_
  46.5 14.5 %experts.1 = (bf16[64,2048]{1,0:T(8,128)(2,1)S(1)}, bf16[64,2048]{1,0:T(8,128)(2,1)S(1)}, bf16[128,2048]{1,0:T(8,128)(2,1)S(1)}, bf16[64,2048]{1,0:T(8,128)(2,1)...) custom-call(s32[1]{0:T(128)} %bitcast.5.first_ref, bf16[32,2176]{1,0:T(8,128)(2,1)S(1)} %pad_maximum_fusion.refs_0_, ...), custom_call_target="tpu_custom_call" | custom-call | flops 3489660928 | bytes 39845888 | tf_op jit(solution)/shard_map/experts/pallas_call | solution.py:486
  61.1 0.4 collective-permute-start.26
  61.4 0.2 collective-permute-start.20
  61.6 0.3 collective-permute-start.21
  61.9 0.7 collective-permute-done.26
  62.8 0.8 collective-permute-start.27
  63.5 1.1 %collective-permute-start.28 = (bf16[32,2048]{1,0:T(8,128)(2,1)S(1)}, bf16[32,2048]{1,0:T(8,128)(2,1)S(1)}, u32[]{:S(2)}, u32[]{:S(2)}) collective-permute-start(bf16[32,2048]{1,0:T(8,128)(2,1)S(1)} %get-tuple-element.57), channel_id=1, source_target_pairs={{0,6},{2,4},{4,2},{6,0},{8,14},{10,12},{12,10},{14,8},{1,7},{3,5},... | collective-permute-start | bytes 393224 | tf_op jit(solution)/shard_map/ppermute | solution.py:177
  64.7 0.1 add_convert_fusion
  64.9 1.7 %collective-permute-start.25 = (bf16[32,2048]{1,0:T(8,128)(2,1)S(1)}, bf16[32,2048]{1,0:T(8,128)(2,1)S(1)}, u32[]{:S(2)}, u32[]{:S(2)}) collective-permute-start(bf16[32,2048]{1,0:T(8,128)(2,1)S(1)} %slice.37), channel_id=1, source_target_pairs={{0,4},{4,0},{8,12},{12,8},{1,5},{5,1},{9,13},{13,9},{2,6},{6,2},{1... | collective-permute-start | bytes 393224 | tf_op jit(solution)/shard_map/ppermute | solution.py:170
  66.6 0.8 collective-permute-start.22
  67.4 1.1 %collective-permute-start.24 = (bf16[32,2048]{1,0:T(8,128)(2,1)S(1)}, bf16[32,2048]{1,0:T(8,128)(2,1)S(1)}, u32[]{:S(2)}, u32[]{:S(2)}) collective-permute-start(bf16[32,2048]{1,0:T(8,128)(2,1)S(1)} %get-tuple-element.54), channel_id=1, source_target_pairs={{0,6},{2,4},{4,2},{6,0},{8,14},{10,12},{12,10},{14,8},{1,7},{3,5},... | collective-permute-start | bytes 393224 | tf_op jit(solution)/shard_map/ppermute | solution.py:177
  68.5 3.6 %collective-permute-done.27 = bf16[32,2048]{1,0:T(8,128)(2,1)S(1)} collective-permute-done((bf16[32,2048]{1,0:T(8,128)(2,1)S(1)}, bf16[32,2048]{1,0:T(8,128)(2,1)S(1)}, u32[]{:S(2)}, u32[]{:S(2)}) %collective-permute-start.27) | collective-permute-done | bytes 131104 | tf_op jit(solution)/shard_map/ppermute | solution.py:170
  72.1 0.6 collective-permute-start.23
  72.8 0.7 collective-permute-done.25
  73.6 0.7 collective-permute-start.29
  74.3 2.2 %collective-permute-done.22 = bf16[32,2048]{1,0:T(8,128)(2,1)S(1)} collective-permute-done((bf16[32,2048]{1,0:T(8,128)(2,1)S(1)}, bf16[32,2048]{1,0:T(8,128)(2,1)S(1)}, u32[]{:S(2)}, u32[]{:S(2)}) %collective-permute-start.22) | collective-permute-done | bytes 131104 | tf_op jit(solution)/shard_map/ppermute | solution.py:170
  76.5 1.3 %collective-permute-done.24 = bf16[32,2048]{1,0:T(8,128)(2,1)S(1)} collective-permute-done((bf16[32,2048]{1,0:T(8,128)(2,1)S(1)}, bf16[32,2048]{1,0:T(8,128)(2,1)S(1)}, u32[]{:S(2)}, u32[]{:S(2)}) %collective-permute-start.24) | collective-permute-done | bytes 131104 | tf_op jit(solution)/shard_map/ppermute | solution.py:177
  77.9 2.4 %collective-permute-done.23 = bf16[32,2048]{1,0:T(8,128)(2,1)S(1)} collective-permute-done((bf16[32,2048]{1,0:T(8,128)(2,1)S(1)}, bf16[32,2048]{1,0:T(8,128)(2,1)S(1)}, u32[]{:S(2)}, u32[]{:S(2)}) %collective-permute-start.23) | collective-permute-done | bytes 131104 | tf_op jit(solution)/shard_map/ppermute | solution.py:170
  80.2 1.6 %collective-permute-done.29 = bf16[32,2048]{1,0:T(8,128)(2,1)S(1)} collective-permute-done((bf16[32,2048]{1,0:T(8,128)(2,1)S(1)}, bf16[32,2048]{1,0:T(8,128)(2,1)S(1)}, u32[]{:S(2)}, u32[]{:S(2)}) %collective-permute-start.29) | collective-permute-done | bytes 131104 | tf_op jit(solution)/shard_map/ppermute | solution.py:170
  81.8 0.8 add_convert_fusion.3
  (32 shorter events, 0.6 us)
Async XLA Ops:
  0.8 14.8 %collective-permute-start.2 = (bf16[128,256]{1,0:T(8,128)(2,1)S(1)}, bf16[128,256]{1,0:T(8,128)(2,1)S(1)}, u32[]{:S(2)}, u32[]{:S(2)}) collective-permute-start(bf16[128,256]{1,0:T(8,128)(2,1)S(1)} %pad_maximum_fusion.1.kv_ref), channel_id=1, source_target_pairs={{0,4},{4,8},{8,12},{1,5},{5,9},{9,13},{2,6},{6,10},{10,14},{3,7},{... | collective-permute-start | bytes 196616 | tf_op jit(solution)/shard_map/ppermute | solution.py:182
  5.7 9.9 %collective-permute-start.1 = (bf16[128,256]{1,0:T(8,128)(2,1)S(1)}, bf16[128,256]{1,0:T(8,128)(2,1)S(1)}, u32[]{:S(2)}, u32[]{:S(2)}) collective-permute-start(bf16[128,256]{1,0:T(8,128)(2,1)S(1)} %pad_maximum_fusion.1.kv_ref), channel_id=1, source_target_pairs={{0,8},{4,12},{1,9},{5,13},{2,10},{6,14},{3,11},{7,15},{16,24},{20,... | collective-permute-start | bytes 196616 | tf_op jit(solution)/shard_map/ppermute | solution.py:182
  10.2 5.4 %collective-permute-start = (bf16[128,256]{1,0:T(8,128)(2,1)S(1)}, bf16[128,256]{1,0:T(8,128)(2,1)S(1)}, u32[]{:S(2)}, u32[]{:S(2)}) collective-permute-start(bf16[128,256]{1,0:T(8,128)(2,1)S(1)} %pad_maximum_fusion.1.kv_ref), channel_id=1, source_target_pairs={{0,12},{1,13},{2,14},{3,15},{16,28},{17,29},{18,30},{19,31}} | collective-permute-start | bytes 196616 | tf_op jit(solution)/shard_map/ppermute | solution.py:182
  18.6 1.6 %collective-permute-start.3 = (bf16[64,2048]{1,0:T(8,128)(2,1)S(1)}, bf16[64,2048]{1,0:T(8,128)(2,1)S(1)}, u32[]{:S(2)}, u32[]{:S(2)}) collective-permute-start(bf16[64,2048]{1,0:T(8,128)(2,1)S(1)} %get-tuple-element.35), channel_id=1, source_target_pairs={{0,1},{1,0},{2,3},{3,2},{4,5},{5,4},{6,7},{7,6},{8,9},{9,8},{10,11... | collective-permute-start | bytes 786440 | tf_op jit(solution)/shard_map/ppermute | solution.py:170
  20.3 5.6 %collective-permute-start.4 = (bf16[32,2048]{1,0:T(8,128)(2,1)S(1)}, bf16[32,2048]{1,0:T(8,128)(2,1)S(1)}, u32[]{:S(2)}, u32[]{:S(2)}) collective-permute-start(bf16[32,2048]{1,0:T(8,128)(2,1)S(1)} %fusion), channel_id=1, source_target_pairs={{0,2},{2,0},{1,3},{3,1},{4,6},{6,4},{5,7},{7,5},{8,10},{10,8},{9,1... | collective-permute-start | bytes 393224 | tf_op jit(solution)/shard_map/ppermute | solution.py:170
  26.2 8.2 %collective-permute-start.6 = (bf16[32,2176]{1,0:T(8,128)(2,1)S(1)}, bf16[32,2176]{1,0:T(8,128)(2,1)S(1)}, u32[]{:S(2)}, u32[]{:S(2)}) collective-permute-start(bf16[32,2176]{1,0:T(8,128)(2,1)S(1)} %pad_maximum_fusion.refs_0_), channel_id=1, source_target_pairs={{0,8},{4,12},{8,0},{12,4},{1,9},{5,13},{9,1},{13,5},{2,10},{6,14},... | collective-permute-start | bytes 417800 | tf_op jit(solution)/shard_map/ppermute | solution.py:170
  26.6 10.0 %collective-permute-start.9 = (bf16[32,2176]{1,0:T(8,128)(2,1)S(1)}, bf16[32,2176]{1,0:T(8,128)(2,1)S(1)}, u32[]{:S(2)}, u32[]{:S(2)}) collective-permute-start(bf16[32,2176]{1,0:T(8,128)(2,1)S(1)} %pad_maximum_fusion.refs_0_), channel_id=1, source_target_pairs={{0,6},{2,4},{4,2},{6,0},{8,14},{10,12},{12,10},{14,8},{1,7},{3,5},... | collective-permute-start | bytes 417800 | tf_op jit(solution)/shard_map/ppermute | solution.py:177
  29.7 6.9 %collective-permute-start.8 = (bf16[32,2176]{1,0:T(8,128)(2,1)S(1)}, bf16[32,2176]{1,0:T(8,128)(2,1)S(1)}, u32[]{:S(2)}, u32[]{:S(2)}) collective-permute-start(bf16[32,2176]{1,0:T(8,128)(2,1)S(1)} %pad_maximum_fusion.refs_0_), channel_id=1, source_target_pairs={{0,2},{2,0},{1,3},{3,1},{4,6},{6,4},{5,7},{7,5},{8,10},{10,8},{9,1... | collective-permute-start | bytes 417800 | tf_op jit(solution)/shard_map/ppermute | solution.py:170
  30.2 8.9 %collective-permute-start.5 = (bf16[32,2176]{1,0:T(8,128)(2,1)S(1)}, bf16[32,2176]{1,0:T(8,128)(2,1)S(1)}, u32[]{:S(2)}, u32[]{:S(2)}) collective-permute-start(bf16[32,2176]{1,0:T(8,128)(2,1)S(1)} %pad_maximum_fusion.refs_0_), channel_id=1, source_target_pairs={{0,4},{4,0},{8,12},{12,8},{1,5},{5,1},{9,13},{13,9},{2,6},{6,2},{1... | collective-permute-start | bytes 417800 | tf_op jit(solution)/shard_map/ppermute | solution.py:170
  34.4 7.8 %collective-permute-start.11 = (bf16[32,2176]{1,0:T(8,128)(2,1)S(1)}, bf16[32,2176]{1,0:T(8,128)(2,1)S(1)}, u32[]{:S(2)}, u32[]{:S(2)}) collective-permute-start(bf16[32,2176]{1,0:T(8,128)(2,1)S(1)} %collective-permute-done.6.refs_2_), channel_id=1, source_target_pairs={{0,6},{2,4},{4,2},{6,0},{8,14},{10,12},{12,10},{14,8},{1,7},{3,5},... | collective-permute-start | bytes 417800 | tf_op jit(solution)/shard_map/ppermute | solution.py:177
  34.4 8.5 %collective-permute-start.10 = (bf16[32,2176]{1,0:T(8,128)(2,1)S(1)}, bf16[32,2176]{1,0:T(8,128)(2,1)S(1)}, u32[]{:S(2)}, u32[]{:S(2)}) collective-permute-start(bf16[32,2176]{1,0:T(8,128)(2,1)S(1)} %collective-permute-done.6.refs_2_), channel_id=1, source_target_pairs={{0,2},{2,0},{1,3},{3,1},{4,6},{6,4},{5,7},{7,5},{8,10},{10,8},{9,1... | collective-permute-start | bytes 417800 | tf_op jit(solution)/shard_map/ppermute | solution.py:170
  39.1 5.4 %collective-permute-start.7 = (bf16[32,2176]{1,0:T(8,128)(2,1)S(1)}, bf16[32,2176]{1,0:T(8,128)(2,1)S(1)}, u32[]{:S(2)}, u32[]{:S(2)}) collective-permute-start(bf16[32,2176]{1,0:T(8,128)(2,1)S(1)} %collective-permute-done.6.refs_2_), channel_id=1, source_target_pairs={{0,4},{4,0},{8,12},{12,8},{1,5},{5,1},{9,13},{13,9},{2,6},{6,2},{1... | collective-permute-start | bytes 417800 | tf_op jit(solution)/shard_map/ppermute | solution.py:170
  39.1 5.4 %collective-permute-start.12 = (bf16[32,2176]{1,0:T(8,128)(2,1)S(1)}, bf16[32,2176]{1,0:T(8,128)(2,1)S(1)}, u32[]{:S(2)}, u32[]{:S(2)}) collective-permute-start(bf16[32,2176]{1,0:T(8,128)(2,1)S(1)} %pad_maximum_fusion.refs_0_), channel_id=1, source_target_pairs={{0,1},{1,0},{2,3},{3,2},{4,5},{5,4},{6,7},{7,6},{8,9},{9,8},{10,11... | collective-permute-start | bytes 417800 | tf_op jit(solution)/shard_map/ppermute | solution.py:170
  39.1 5.9 %collective-permute-start.13 = (bf16[32,2176]{1,0:T(8,128)(2,1)S(1)}, bf16[32,2176]{1,0:T(8,128)(2,1)S(1)}, u32[]{:S(2)}, u32[]{:S(2)}) collective-permute-start(bf16[32,2176]{1,0:T(8,128)(2,1)S(1)} %collective-permute-done.5.refs_1_), channel_id=1, source_target_pairs={{0,1},{1,0},{2,3},{3,2},{4,5},{5,4},{6,7},{7,6},{8,9},{9,8},{10,11... | collective-permute-start | bytes 417800 | tf_op jit(solution)/shard_map/ppermute | solution.py:170
  42.2 2.8 %collective-permute-start.14 = (bf16[32,2176]{1,0:T(8,128)(2,1)S(1)}, bf16[32,2176]{1,0:T(8,128)(2,1)S(1)}, u32[]{:S(2)}, u32[]{:S(2)}) collective-permute-start(bf16[32,2176]{1,0:T(8,128)(2,1)S(1)} %collective-permute-done.6.refs_2_), channel_id=1, source_target_pairs={{0,1},{1,0},{2,3},{3,2},{4,5},{5,4},{6,7},{7,6},{8,9},{9,8},{10,11... | collective-permute-start | bytes 417800 | tf_op jit(solution)/shard_map/ppermute | solution.py:170
  42.9 2.5 %collective-permute-start.16 = (bf16[32,2176]{1,0:T(8,128)(2,1)S(1)}, bf16[32,2176]{1,0:T(8,128)(2,1)S(1)}, u32[]{:S(2)}, u32[]{:S(2)}) collective-permute-start(bf16[32,2176]{1,0:T(8,128)(2,1)S(1)} %collective-permute-done.8.refs_4_), channel_id=1, source_target_pairs={{0,1},{1,0},{2,3},{3,2},{4,5},{5,4},{6,7},{7,6},{8,9},{9,8},{10,11... | collective-permute-start | bytes 417800 | tf_op jit(solution)/shard_map/ppermute | solution.py:170
  44.4 1.4 %collective-permute-start.17 = (bf16[32,2176]{1,0:T(8,128)(2,1)S(1)}, bf16[32,2176]{1,0:T(8,128)(2,1)S(1)}, u32[]{:S(2)}, u32[]{:S(2)}) collective-permute-start(bf16[32,2176]{1,0:T(8,128)(2,1)S(1)} %collective-permute-done.9.refs_5_), channel_id=1, source_target_pairs={{0,1},{1,0},{2,3},{3,2},{4,5},{5,4},{6,7},{7,6},{8,9},{9,8},{10,11... | collective-permute-start | bytes 417800 | tf_op jit(solution)/shard_map/ppermute | solution.py:170
  44.5 1.6 %collective-permute-start.19 = (bf16[32,2176]{1,0:T(8,128)(2,1)S(1)}, bf16[32,2176]{1,0:T(8,128)(2,1)S(1)}, u32[]{:S(2)}, u32[]{:S(2)}) collective-permute-start(bf16[32,2176]{1,0:T(8,128)(2,1)S(1)} %collective-permute-done.11.refs_7_), channel_id=1, source_target_pairs={{0,1},{1,0},{2,3},{3,2},{4,5},{5,4},{6,7},{7,6},{8,9},{9,8},{10,11... | collective-permute-start | bytes 417800 | tf_op jit(solution)/shard_map/ppermute | solution.py:170
  45.0 1.4 %collective-permute-start.18 = (bf16[32,2176]{1,0:T(8,128)(2,1)S(1)}, bf16[32,2176]{1,0:T(8,128)(2,1)S(1)}, u32[]{:S(2)}, u32[]{:S(2)}) collective-permute-start(bf16[32,2176]{1,0:T(8,128)(2,1)S(1)} %collective-permute-done.10.refs_6_), channel_id=1, source_target_pairs={{0,1},{1,0},{2,3},{3,2},{4,5},{5,4},{6,7},{7,6},{8,9},{9,8},{10,11... | collective-permute-start | bytes 417800 | tf_op jit(solution)/shard_map/ppermute | solution.py:170
  45.0 1.5 %collective-permute-start.15 = (bf16[32,2176]{1,0:T(8,128)(2,1)S(1)}, bf16[32,2176]{1,0:T(8,128)(2,1)S(1)}, u32[]{:S(2)}, u32[]{:S(2)}) collective-permute-start(bf16[32,2176]{1,0:T(8,128)(2,1)S(1)} %collective-permute-done.7.refs_3_), channel_id=1, source_target_pairs={{0,1},{1,0},{2,3},{3,2},{4,5},{5,4},{6,7},{7,6},{8,9},{9,8},{10,11... | collective-permute-start | bytes 417800 | tf_op jit(solution)/shard_map/ppermute | solution.py:170
  61.1 1.6 %collective-permute-start.26 = (bf16[64,2048]{1,0:T(8,128)(2,1)S(1)}, bf16[64,2048]{1,0:T(8,128)(2,1)S(1)}, u32[]{:S(2)}, u32[]{:S(2)}) collective-permute-start(bf16[64,2048]{1,0:T(8,128)(2,1)S(1)} %get-tuple-element.50), channel_id=1, source_target_pairs={{0,1},{1,0},{2,3},{3,2},{4,5},{5,4},{6,7},{7,6},{8,9},{9,8},{10,11... | collective-permute-start | bytes 786440 | tf_op jit(solution)/shard_map/ppermute | solution.py:170
  61.4 3.2 %collective-permute-start.20 = (bf16[64,2048]{1,0:T(8,128)(2,1)S(1)}, bf16[64,2048]{1,0:T(8,128)(2,1)S(1)}, u32[]{:S(2)}, u32[]{:S(2)}) collective-permute-start(bf16[64,2048]{1,0:T(8,128)(2,1)S(1)} %get-tuple-element.44), channel_id=1, source_target_pairs={{0,1},{1,0},{2,3},{3,2},{4,5},{5,4},{6,7},{7,6},{8,9},{9,8},{10,11... | collective-permute-start | bytes 786440 | tf_op jit(solution)/shard_map/ppermute | solution.py:170
  61.6 3.1 %collective-permute-start.21 = (bf16[128,2048]{1,0:T(8,128)(2,1)S(1)}, bf16[128,2048]{1,0:T(8,128)(2,1)S(1)}, u32[]{:S(2)}, u32[]{:S(2)}) collective-permute-start(bf16[128,2048]{1,0:T(8,128)(2,1)S(1)} %get-tuple-element.46), channel_id=1, source_target_pairs={{0,1},{1,0},{2,3},{3,2},{4,5},{5,4},{6,7},{7,6},{8,9},{9,8},{10,11... | collective-permute-start | bytes 1572872 | tf_op jit(solution)/shard_map/ppermute | solution.py:170
  62.8 9.4 %collective-permute-start.27 = (bf16[32,2048]{1,0:T(8,128)(2,1)S(1)}, bf16[32,2048]{1,0:T(8,128)(2,1)S(1)}, u32[]{:S(2)}, u32[]{:S(2)}) collective-permute-start(bf16[32,2048]{1,0:T(8,128)(2,1)S(1)} %get-tuple-element.56), channel_id=1, source_target_pairs={{0,2},{2,0},{1,3},{3,1},{4,6},{6,4},{5,7},{7,5},{8,10},{10,8},{9,1... | collective-permute-start | bytes 393224 | tf_op jit(solution)/shard_map/ppermute | solution.py:170
  63.5 9.2 %collective-permute-start.28 = (bf16[32,2048]{1,0:T(8,128)(2,1)S(1)}, bf16[32,2048]{1,0:T(8,128)(2,1)S(1)}, u32[]{:S(2)}, u32[]{:S(2)}) collective-permute-start(bf16[32,2048]{1,0:T(8,128)(2,1)S(1)} %get-tuple-element.57), channel_id=1, source_target_pairs={{0,6},{2,4},{4,2},{6,0},{8,14},{10,12},{12,10},{14,8},{1,7},{3,5},... | collective-permute-start | bytes 393224 | tf_op jit(solution)/shard_map/ppermute | solution.py:177
  64.9 8.6 %collective-permute-start.25 = (bf16[32,2048]{1,0:T(8,128)(2,1)S(1)}, bf16[32,2048]{1,0:T(8,128)(2,1)S(1)}, u32[]{:S(2)}, u32[]{:S(2)}) collective-permute-start(bf16[32,2048]{1,0:T(8,128)(2,1)S(1)} %slice.37), channel_id=1, source_target_pairs={{0,4},{4,0},{8,12},{12,8},{1,5},{5,1},{9,13},{13,9},{2,6},{6,2},{1... | collective-permute-start | bytes 393224 | tf_op jit(solution)/shard_map/ppermute | solution.py:170
  66.6 9.9 %collective-permute-start.22 = (bf16[32,2048]{1,0:T(8,128)(2,1)S(1)}, bf16[32,2048]{1,0:T(8,128)(2,1)S(1)}, u32[]{:S(2)}, u32[]{:S(2)}) collective-permute-start(bf16[32,2048]{1,0:T(8,128)(2,1)S(1)} %get-tuple-element.53), channel_id=1, source_target_pairs={{0,2},{2,0},{1,3},{3,1},{4,6},{6,4},{5,7},{7,5},{8,10},{10,8},{9,1... | collective-permute-start | bytes 393224 | tf_op jit(solution)/shard_map/ppermute | solution.py:170
  67.4 10.5 %collective-permute-start.24 = (bf16[32,2048]{1,0:T(8,128)(2,1)S(1)}, bf16[32,2048]{1,0:T(8,128)(2,1)S(1)}, u32[]{:S(2)}, u32[]{:S(2)}) collective-permute-start(bf16[32,2048]{1,0:T(8,128)(2,1)S(1)} %get-tuple-element.54), channel_id=1, source_target_pairs={{0,6},{2,4},{4,2},{6,0},{8,14},{10,12},{12,10},{14,8},{1,7},{3,5},... | collective-permute-start | bytes 393224 | tf_op jit(solution)/shard_map/ppermute | solution.py:177
  72.1 8.1 %collective-permute-start.23 = (bf16[32,2048]{1,0:T(8,128)(2,1)S(1)}, bf16[32,2048]{1,0:T(8,128)(2,1)S(1)}, u32[]{:S(2)}, u32[]{:S(2)}) collective-permute-start(bf16[32,2048]{1,0:T(8,128)(2,1)S(1)} %get-tuple-element.55), channel_id=1, source_target_pairs={{0,4},{4,0},{8,12},{12,8},{1,5},{5,1},{9,13},{13,9},{2,6},{6,2},{1... | collective-permute-start | bytes 393224 | tf_op jit(solution)/shard_map/ppermute | solution.py:170
  73.6 8.3 %collective-permute-start.29 = (bf16[32,2048]{1,0:T(8,128)(2,1)S(1)}, bf16[32,2048]{1,0:T(8,128)(2,1)S(1)}, u32[]{:S(2)}, u32[]{:S(2)}) collective-permute-start(bf16[32,2048]{1,0:T(8,128)(2,1)S(1)} %add_convert_fusion.4), channel_id=1, source_target_pairs={{0,8},{4,12},{8,0},{12,4},{1,9},{5,13},{9,1},{13,5},{2,10},{6,14},... | collective-permute-start | bytes 393224 | tf_op jit(solution)/shard_map/ppermute | solution.py:170

commit v9 on v8

--- a/solution.py
+++ b/solution.py
@@ -177,9 +177,8 @@
     return lax.ppermute(x, ("ctx", "exp"), [(i, i ^ mask) for i in range(size)])
 
 
-def from_earlier(x, axis, steps):
-    size = lax.axis_size(axis)
-    return lax.ppermute(x, axis, [(i, i + steps) for i in range(size - steps)])
+def from_earlier(x, axis, bits):
+    return lax.ppermute(x, axis, [(i, i ^ bits) for i in range(lax.axis_size(axis)) if i < i ^ bits])
 
 
 def in_hbm(x):
@@ -188,6 +187,9 @@
 
 def dot_rows(a, b):
     return lax.dot_general(a, b, (((1,), (1,)), ((), ())), preferred_element_type=F32)
+
+
+KV_ORDER = (1, 2, 3)
 
 
 def own_block_kernel(sizes, place, kv_ref, ids_hbm, probs_hbm, q_hbm, w_hbm, resid_hbm, *refs):
@@ -201,27 +203,33 @@
         pltpu.make_async_copy(resid_hbm, resid_ref, sems.at[2]),
         pltpu.make_async_copy(w_hbm, w_ref, sems.at[3]),
     ]
-    fetch_q = pltpu.make_async_copy(q_hbm, q_ref, q_sem)
-    fetch_q.start()
+    fetch_q = []
+    for h in range(heads):
+        columns = slice(h * HEAD_DIMENSION, (h + 1) * HEAD_DIMENSION)
+        fetch_q.append(
+            pltpu.make_async_copy(
+                q_hbm.at[:, columns], q_ref.at[pl.ds(h * rows, rows)], q_sem.at[h]
+            )
+        )
+        fetch_q[h].start()
     for copy in fetch:
         copy.start()
     tp = place[2]
     v_ext[:, :HEAD_DIMENSION] = kv_ref[:, HEAD_DIMENSION:]
     v_ext[:, HEAD_DIMENSION:] = jnp.ones((rows, HEAD_DIMENSION), BF)
     keys = kv_ref[:, :HEAD_DIMENSION]
-    allowed = lax.broadcasted_iota(jnp.int32, (rows, rows), 1) <= lax.broadcasted_iota(
-        jnp.int32, (rows, rows), 0
-    )
+    column = lax.broadcasted_iota(jnp.int32, (rows, rows), 1)
+    allowed = column <= lax.broadcasted_iota(jnp.int32, (rows, rows), 0)
     scale = 1.0 / math.sqrt(HEAD_DIMENSION)
-    fetch_q.wait()
-    for h in range(heads):
-        columns = slice(h * HEAD_DIMENSION, (h + 1) * HEAD_DIMENSION)
-        s = jnp.where(allowed, dot_rows(q_ref[:, columns], keys) * scale, -1e30)
-        top = jnp.max(s, axis=1, keepdims=True)
-        out = jnp.dot(jnp.exp(s - top).astype(BF), v_ext[...], preferred_element_type=F32)
-        out_ref[:, columns] = out[:, :HEAD_DIMENSION]
-        sum_ref[:, columns] = out[:, HEAD_DIMENSION:]
-        max_ref[:, h : h + 1] = top
+    for copy in fetch_q:
+        copy.wait()
+    s = dot_rows(q_ref[...], keys).reshape(heads, rows, rows)
+    s = jnp.where(allowed, s * scale, -1e30).reshape(heads * rows, rows)
+    top = jnp.max(s, axis=1, keepdims=True)
+    out = jnp.dot(jnp.exp(s - top).astype(BF), v_ext[...], preferred_element_type=F32)
+    out_ref[...] = out[:, :HEAD_DIMENSION]
+    sum_ref[...] = out[:, HEAD_DIMENSION:]
+    max_ref[...] = jnp.broadcast_to(top, max_ref.shape)
 
     fetch[0].wait()
     fetch[1].wait()
@@ -263,12 +271,12 @@
     return pl.pallas_call(
         functools.partial(own_block_kernel, (n_exp, n_tp, heads, part)),
         out_shape=(
-            jax.ShapeDtypeStruct((rows, width), BF),
+            jax.ShapeDtypeStruct((heads * rows, HEAD_DIMENSION), BF),
             jax.ShapeDtypeStruct((width, model), BF),
             jax.ShapeDtypeStruct((part, model), BF),
-            jax.ShapeDtypeStruct((rows, width), F32),
-            jax.ShapeDtypeStruct((rows, width), F32),
-            jax.ShapeDtypeStruct((rows, LANES), F32),
+            jax.ShapeDtypeStruct((heads * rows, HEAD_DIMENSION), F32),
+            jax.ShapeDtypeStruct((heads * rows, HEAD_DIMENSION), F32),
+            jax.ShapeDtypeStruct((heads * rows, LANES), F32),
             jax.ShapeDtypeStruct((part, LANES), BF),
         ),
         in_specs=[pl.BlockSpec(memory_space=pltpu.SMEM), vmem] + [hbm] * 5,
@@ -278,7 +286,7 @@
             pltpu.VMEM((TOPK, block), jnp.int32),
             pltpu.VMEM((TOPK, block), F32),
             pltpu.VMEM((LANES, LANES), F32),
-            pltpu.SemaphoreType.DMA,
+            pltpu.SemaphoreType.DMA((heads,)),
             pltpu.SemaphoreType.DMA((4,)),
         ],
         compiler_params=pltpu.CompilerParams(vmem_limit_bytes=20 * MIB),
@@ -303,29 +311,34 @@
     base_ref, across_ref, other_ref = refs[6:9]
     k_all, v_all, att, att_rel = refs[9:]
     ctx, exp, tp = place[0], place[1], place[2]
-    for z in range(n_ctx - 1):
-        k_all[z * rows : (z + 1) * rows, :] = kv_refs[z][:, :HEAD_DIMENSION]
-        v_all[z * rows : (z + 1) * rows, :HEAD_DIMENSION] = kv_refs[z][:, HEAD_DIMENSION:]
+    for i, kv_ref in enumerate(kv_refs):
+        at = slice(i * rows, (i + 1) * rows)
+        k_all[at, :] = kv_ref[:, :HEAD_DIMENSION]
+        v_all[at, :HEAD_DIMENSION] = kv_ref[:, HEAD_DIMENSION:]
     v_all[:, HEAD_DIMENSION:] = jnp.ones(((n_ctx - 1) * rows, HEAD_DIMENSION), BF)
-    column = lax.broadcasted_iota(jnp.int32, (1, (n_ctx - 1) * rows), 1)
-    allowed = column >= (n_ctx - 1 - ctx) * rows
+    piece = lax.broadcasted_iota(jnp.int32, (1, (n_ctx - 1) * rows), 1) // rows
+    earlier = jnp.zeros_like(piece)
+    for i, bits in enumerate(KV_ORDER):
+        there = jnp.where(lax.bitwise_xor(ctx, bits) < ctx, 1, 0)
+        earlier = earlier + jnp.where(piece == i, there, 0)
+    allowed = earlier == 1
     scale = 1.0 / math.sqrt(HEAD_DIMENSION)
-    for h in range(heads):
-        columns = slice(h * HEAD_DIMENSION, (h + 1) * HEAD_DIMENSION)
-        s = jnp.where(allowed, dot_rows(q_ref[:, columns], k_all[...]) * scale, -1e30)
-        own_top = max_ref[:, h : h + 1]
-        top = jnp.maximum(own_top, jnp.max(s, axis=1, keepdims=True))
-        keep = jnp.exp(own_top - top)
-        out = jnp.dot(jnp.exp(s - top).astype(BF), v_all[...], preferred_element_type=F32)
-        total = sum_ref[:, columns] * keep + out[:, HEAD_DIMENSION:]
-        out = out_ref[:, columns] * keep + out[:, :HEAD_DIMENSION]
-        att[:, columns] = (out / total).astype(BF)
+    s = jnp.where(allowed, dot_rows(q_ref[...], k_all[...]) * scale, -1e30)
+    own_top = max_ref[...]
+    top = jnp.maximum(own_top, jnp.max(s, axis=1, keepdims=True))
+    keep = jnp.exp(own_top - top)
+    out = jnp.dot(jnp.exp(s - top[:, :1]).astype(BF), v_all[...], preferred_element_type=F32)
+    total = sum_ref[...] * keep + out[:, HEAD_DIMENSION:]
+    out = out_ref[...] * keep + out[:, :HEAD_DIMENSION]
+    att[...] = (out / total).astype(BF)
     for t in range(n_tp):
         for x in range(n_exp):
             owner = lax.rem(exp + x, n_exp) * n_tp + lax.rem(tp + t, n_tp)
-            source = pl.ds(pl.multiple_of(owner * part, part), part)
             at = (t * n_exp + x) * part
-            att_rel[at : at + part, :] = att[source, :]
+            for h in range(heads):
+                source = pl.ds(pl.multiple_of(h * rows + owner * part, part), part)
+                columns = slice(h * HEAD_DIMENSION, (h + 1) * HEAD_DIMENSION)
+                att_rel[at : at + part, columns] = att[source, :]
     projected = jnp.dot(att_rel[...], w_ref[...], preferred_element_type=F32)
     base_ref[...] = resid_ref[...].astype(F32) + projected[:part]
     across_ref[...] = projected[part : 2 * part].astype(BF)
@@ -334,9 +347,10 @@
 
 def attend_project(place, pieces, own, n_exp, n_tp):
     queries, out_weight, resid = own[:3]
-    rows, width = queries.shape
+    width, model = out_weight.shape
     n_ctx, heads = len(pieces) + 1, width // HEAD_DIMENSION
-    part, model = resid.shape
+    rows = queries.shape[0] // heads
+    part = resid.shape[0]
     vmem = pl.BlockSpec(memory_space=pltpu.VMEM)
     return pl.pallas_call(
         functools.partial(attention_kernel, (n_ctx, n_exp, n_tp, heads, part)),
@@ -350,7 +364,7 @@
         scratch_shapes=[
             pltpu.VMEM(((n_ctx - 1) * rows, HEAD_DIMENSION), BF),
             pltpu.VMEM(((n_ctx - 1) * rows, 2 * HEAD_DIMENSION), BF),
-            pltpu.VMEM((rows, width), BF),
+            pltpu.VMEM((heads * rows, HEAD_DIMENSION), BF),
             pltpu.VMEM((rows, width), BF),
         ],
         compiler_params=pltpu.CompilerParams(vmem_limit_bytes=20 * MIB),
@@ -533,9 +547,9 @@
     own = flip(across[0], "exp", 1)
     near = flip(here[1], "ctx", 1)
     near_across = flip_both(across[1])
-    far = flip(add(here[2], last, far_across, last_across), "ctx", 2)
+    far = flip(add(here[2], last_across, far_across, last), "ctx", 2)
     total = here[0].astype(F32)
-    for term in (own, near, near_across, far):
+    for term in (far, near, near_across, own):
         total = total + term.astype(F32)
     return total
 
@@ -562,7 +576,7 @@
     key_head = lax.dynamic_slice_in_dim(keys, shared * HEAD_DIMENSION, HEAD_DIMENSION, 1)
     value_head = lax.dynamic_slice_in_dim(values, shared * HEAD_DIMENSION, HEAD_DIMENSION, 1)
     kv = jnp.concatenate([key_head, value_head], axis=1)
-    kv_pieces = [from_earlier(kv, "ctx", z) for z in range(n_ctx - 1, 0, -1)]
+    kv_pieces = [from_earlier(kv, "ctx", bits) for bits in KV_ORDER]
     *own, routing = own_block(
         place, kv, expert_ids, router_probs, queries, out_weight, resid, n_exp, n_tp
     )

time: 82.8 us -> 80.2 us (0.969)
  waiting for transfers between devices: 31.4 us -> 29.1 us
  Pallas kernels: 21.4 us -> 20.4 us
    ppermute x23, waiting for transfers between devices: 26.7 us -> 17.8 us  [flip(): lax.ppermute(x, axis, [(i, i ^ bit) for i in range(lax.axis_size(axis))])]
    ppermute x4, waiting for transfers between devices: 4.65 us -> 11.3 us  [flip_both(): return lax.ppermute(x, ('ctx', 'exp'), [(i, i ^ mask) for i in range(size)])]
    ppermute x23, starting transfers between devices: 11.2 us -> 12.9 us  [flip(): lax.ppermute(x, axis, [(i, i ^ bit) for i in range(lax.axis_size(axis))])]
    ppermute x4, starting transfers between devices: 5.34 us -> 4.33 us  [flip_both(): return lax.ppermute(x, ('ctx', 'exp'), [(i, i ^ mask) for i in range(size)])]
    pallas_call x1, Pallas kernels: 3.97 us -> 3.09 us  [own_block(): pl.pallas_call(functools.partial(own_block_kernel, (n_exp, n_tp, heads, p...]
  transfers between devices with their start and end apart: 30 -> 30, of which waited for: 19 -> 16; matrix products, arithmetic and copies ran while one was open for 1% -> 1% of each run, Pallas kernels for 5% -> 4%
where the time goes in v9:
time: 80.2 us; the launch traced here: 80 us
  waiting for transfers between devices  29.1 us (36%)
  starting transfers between devices  27.9 us (35%)
  Pallas kernels  20.4 us (25%)
  other arithmetic  1.52 us (2%)
  local copies, waits for them, and re-layouts  0.84 us (1%)
    ppermute x23, waiting for transfers between devices, flip(): lax.ppermute(x, axis, [(i, i ^ bit) for i in range(lax.axis_size(axis))])  17.8 us
    pallas_call x1, Pallas kernels, cube_experts(): pl.pallas_call(functools.partial(expert_kernel, len(pieces), depth, exper...  14.5 us
    ppermute x23, starting transfers between devices, flip(): lax.ppermute(x, axis, [(i, i ^ bit) for i in range(lax.axis_size(axis))])  12.9 us
    ppermute x4, waiting for transfers between devices, flip_both(): return lax.ppermute(x, ('ctx', 'exp'), [(i, i ^ mask) for i in range(size)])  11.3 us
    ppermute x3, starting transfers between devices, from_earlier(): lax.ppermute(x, axis, [(i, i ^ bits) for i in range(lax.axis_size(axis))...  10.7 us
    ppermute x4, starting transfers between devices, flip_both(): return lax.ppermute(x, ('ctx', 'exp'), [(i, i ^ mask) for i in range(size)])  4.33 us
    pallas_call x1, Pallas kernels, own_block(): pl.pallas_call(functools.partial(own_block_kernel, (n_exp, n_tp, heads, p...  3.09 us
    pallas_call x1, Pallas kernels, attend_project(): pl.pallas_call(functools.partial(attention_kernel, (n_ctx, n_exp, n_tp, h...  2.76 us
  transfers between devices with their start and end apart: 30, of which 16 were waited for; matrix products, arithmetic and copies ran while one was open for 1% of the time, Pallas kernels for 4%

profile of v9, /device:TPU:0, one launch (start us, length us, event | category | flops | bytes accessed | tf_op | source)
XLA Modules:
  0.0 80.0 jit_solution(12224531757344068332)
XLA Ops:
  0.0 0.8 constant_dynamic-slice_fusion
  0.8 7.0 %collective-permute-start.2 = (bf16[128,256]{1,0:T(8,128)(2,1)S(1)}, bf16[128,256]{1,0:T(8,128)(2,1)S(1)}, u32[]{:S(2)}, u32[]{:S(2)}) collective-permute-start(bf16[128,256]{1,0:T(8,128)(2,1)S(1)} %pad_maximum_fusion.1.kv_ref), channel_id=1, source_target_pairs={{0,12},{4,8},{1,13},{5,9},{2,14},{6,10},{3,15},{7,11},{16,28},{20,... | collective-permute-start | bytes 196616 | tf_op jit(solution)/shard_map/ppermute | solution.py:181
  7.8 1.3 %collective-permute-start.1 = (bf16[128,256]{1,0:T(8,128)(2,1)S(1)}, bf16[128,256]{1,0:T(8,128)(2,1)S(1)}, u32[]{:S(2)}, u32[]{:S(2)}) collective-permute-start(bf16[128,256]{1,0:T(8,128)(2,1)S(1)} %pad_maximum_fusion.1.kv_ref), channel_id=1, source_target_pairs={{0,8},{4,12},{1,9},{5,13},{2,10},{6,14},{3,11},{7,15},{16,24},{20,... | collective-permute-start | bytes 196616 | tf_op jit(solution)/shard_map/ppermute | solution.py:181
  9.1 2.5 %collective-permute-start = (bf16[128,256]{1,0:T(8,128)(2,1)S(1)}, bf16[128,256]{1,0:T(8,128)(2,1)S(1)}, u32[]{:S(2)}, u32[]{:S(2)}) collective-permute-start(bf16[128,256]{1,0:T(8,128)(2,1)S(1)} %pad_maximum_fusion.1.kv_ref), channel_id=1, source_target_pairs={{0,4},{8,12},{1,5},{9,13},{2,6},{10,14},{3,7},{11,15},{16,20},{24,... | collective-permute-start | bytes 196616 | tf_op jit(solution)/shard_map/ppermute | solution.py:181
  11.5 0.1 pad_add_fusion.place
  11.6 3.1 %own_block.1 = (bf16[1024,128]{1,0:T(8,128)(2,1)S(1)}, bf16[1024,2048]{1,0:T(8,128)(2,1)S(1)}, bf16[32,2048]{1,0:T(8,128)(2,1)S(1)}, f32[1024,128]{1,0:T(8,128)S...) custom-call(s32[3]{0:T(128)S(1)} %pad_add_fusion.place, ...), custom_call_target="tpu_custom_call" | custom-call | flops 100663296 | bytes 4980736 | tf_op jit(solution)/shard_map/own_block/pallas_call | solution.py:271
  14.7 2.8 %attend_project.1 = (f32[32,2048]{1,0:T(8,128)S(1)}, bf16[32,2048]{1,0:T(8,128)(2,1)S(1)}, bf16[64,2048]{1,0:T(8,128)(2,1)S(1)}) custom-call(s32[3]{0:T(128)S(1)} %pad_add_fusion.place, bf16[128,256]{1,0:T(8,128)(2,1)S(1)} %collective-permute-done.refs_0_, bf16[128,256]{1,0:T(8,128)(2,1)S(1)} %collective-permute-done.1.refs_1_, ...), custom_call_target="tpu_custom_call" | custom-call | flops 838860800 | bytes 4980736 | tf_op jit(solution)/shard_map/attend_project/pallas_call | solution.py:355
  17.5 0.1 collective-permute-start.3
  17.6 1.5 %collective-permute-done.3 = bf16[64,2048]{1,0:T(8,128)(2,1)S(1)} collective-permute-done((bf16[64,2048]{1,0:T(8,128)(2,1)S(1)}, bf16[64,2048]{1,0:T(8,128)(2,1)S(1)}, u32[]{:S(2)}, u32[]{:S(2)}) %collective-permute-start.3) | collective-permute-done | bytes 262176 | tf_op jit(solution)/shard_map/ppermute | solution.py:170
  19.2 1.6 %collective-permute-start.4 = (bf16[32,2048]{1,0:T(8,128)(2,1)S(1)}, bf16[32,2048]{1,0:T(8,128)(2,1)S(1)}, u32[]{:S(2)}, u32[]{:S(2)}) collective-permute-start(bf16[32,2048]{1,0:T(8,128)(2,1)S(1)} %fusion), channel_id=1, source_target_pairs={{0,2},{2,0},{1,3},{3,1},{4,6},{6,4},{5,7},{7,5},{8,10},{10,8},{9,1... | collective-permute-start | bytes 393224 | tf_op jit(solution)/shard_map/ppermute | solution.py:170
  20.7 4.0 %collective-permute-done.4 = bf16[32,2048]{1,0:T(8,128)(2,1)S(1)} collective-permute-done((bf16[32,2048]{1,0:T(8,128)(2,1)S(1)}, bf16[32,2048]{1,0:T(8,128)(2,1)S(1)}, u32[]{:S(2)}, u32[]{:S(2)}) %collective-permute-start.4) | collective-permute-done | bytes 131104 | tf_op jit(solution)/shard_map/ppermute | solution.py:170
  24.8 0.2 multiply_reduce_fusion
  25.0 0.1 multiply_convert_fusion
  25.2 2.9 %collective-permute-start.9 = (bf16[32,2176]{1,0:T(8,128)(2,1)S(1)}, bf16[32,2176]{1,0:T(8,128)(2,1)S(1)}, u32[]{:S(2)}, u32[]{:S(2)}) collective-permute-start(bf16[32,2176]{1,0:T(8,128)(2,1)S(1)} %pad_maximum_fusion.refs_0_), channel_id=1, source_target_pairs={{0,6},{2,4},{4,2},{6,0},{8,14},{10,12},{12,10},{14,8},{1,7},{3,5},... | collective-permute-start | bytes 417800 | tf_op jit(solution)/shard_map/ppermute | solution.py:177
  28.1 0.5 collective-permute-start.8
  28.6 0.1 collective-permute-start.5
  28.7 5.2 %collective-permute-done.6.refs_2_ = bf16[32,2176]{1,0:T(8,128)(2,1)S(1)} collective-permute-done((bf16[32,2176]{1,0:T(8,128)(2,1)S(1)}, bf16[32,2176]{1,0:T(8,128)(2,1)S(1)}, u32[]{:S(2)}, u32[]{:S(2)}) %collective-permute-start.6) | collective-permute-done | bytes 139296 | tf_op jit(solution)/shard_map/ppermute | solution.py:170
  33.9 0.7 collective-permute-start.11
  34.6 0.8 %collective-permute-start.10 = (bf16[32,2176]{1,0:T(8,128)(2,1)S(1)}, bf16[32,2176]{1,0:T(8,128)(2,1)S(1)}, u32[]{:S(2)}, u32[]{:S(2)}) collective-permute-start(bf16[32,2176]{1,0:T(8,128)(2,1)S(1)} %collective-permute-done.6.refs_2_), channel_id=1, source_target_pairs={{0,2},{2,0},{1,3},{3,1},{4,6},{6,4},{5,7},{7,5},{8,10},{10,8},{9,1... | collective-permute-start | bytes 417800 | tf_op jit(solution)/shard_map/ppermute | solution.py:170
  35.4 1.5 %collective-permute-done.5.refs_1_ = bf16[32,2176]{1,0:T(8,128)(2,1)S(1)} collective-permute-done((bf16[32,2176]{1,0:T(8,128)(2,1)S(1)}, bf16[32,2176]{1,0:T(8,128)(2,1)S(1)}, u32[]{:S(2)}, u32[]{:S(2)}) %collective-permute-start.5) | collective-permute-done | bytes 139296 | tf_op jit(solution)/shard_map/ppermute | solution.py:170
  37.0 0.5 collective-permute-start.7
  37.5 0.5 collective-permute-start.13
  38.0 3.4 %collective-permute-done.11.refs_7_ = bf16[32,2176]{1,0:T(8,128)(2,1)S(1)} collective-permute-done((bf16[32,2176]{1,0:T(8,128)(2,1)S(1)}, bf16[32,2176]{1,0:T(8,128)(2,1)S(1)}, u32[]{:S(2)}, u32[]{:S(2)}) %collective-permute-start.11) | collective-permute-done | bytes 139296 | tf_op jit(solution)/shard_map/ppermute | solution.py:177
  41.4 0.5 collective-permute-done.10.refs_6_
  42.0 1.0 %collective-permute-done.7.refs_3_ = bf16[32,2176]{1,0:T(8,128)(2,1)S(1)} collective-permute-done((bf16[32,2176]{1,0:T(8,128)(2,1)S(1)}, bf16[32,2176]{1,0:T(8,128)(2,1)S(1)}, u32[]{:S(2)}, u32[]{:S(2)}) %collective-permute-start.7) | collective-permute-done | bytes 139296 | tf_op jit(solution)/shard_map/ppermute | solution.py:170
  43.0 0.5 collective-permute-start.19
  43.6 0.4 collective-permute-start.15
  44.0 0.3 collective-permute-done.17.refs_13_
  44.3 0.2 collective-permute-done.19.refs_15_
  44.5 0.3 collective-permute-done.18.refs_14_
  44.8 0.2 collective-permute-done.15.refs_11_
  45.0 14.5 %experts.1 = (bf16[64,2048]{1,0:T(8,128)(2,1)S(1)}, bf16[64,2048]{1,0:T(8,128)(2,1)S(1)}, bf16[128,2048]{1,0:T(8,128)(2,1)S(1)}, bf16[64,2048]{1,0:T(8,128)(2,1)...) custom-call(s32[1]{0:T(128)} %bitcast.5.first_ref, bf16[32,2176]{1,0:T(8,128)(2,1)S(1)} %pad_maximum_fusion.refs_0_, ...), custom_call_target="tpu_custom_call" | custom-call | flops 3489660928 | bytes 39845888 | tf_op jit(solution)/shard_map/experts/pallas_call | solution.py:500
  59.6 0.4 collective-permute-start.22
  60.0 0.2 collective-permute-start.20
  60.2 0.3 collective-permute-start.21
  60.5 0.7 collective-permute-done.22
  61.3 0.6 collective-permute-start.23
  61.9 1.4 %collective-permute-start.24 = (bf16[32,2048]{1,0:T(8,128)(2,1)S(1)}, bf16[32,2048]{1,0:T(8,128)(2,1)S(1)}, u32[]{:S(2)}, u32[]{:S(2)}) collective-permute-start(bf16[32,2048]{1,0:T(8,128)(2,1)S(1)} %get-tuple-element.57), channel_id=1, source_target_pairs={{0,2},{2,0},{1,3},{3,1},{4,6},{6,4},{5,7},{7,5},{8,10},{10,8},{9,1... | collective-permute-start | bytes 393224 | tf_op jit(solution)/shard_map/ppermute | solution.py:170
  63.4 0.1 add_convert_fusion
  63.6 1.6 %collective-permute-start.25 = (bf16[32,2048]{1,0:T(8,128)(2,1)S(1)}, bf16[32,2048]{1,0:T(8,128)(2,1)S(1)}, u32[]{:S(2)}, u32[]{:S(2)}) collective-permute-start(bf16[32,2048]{1,0:T(8,128)(2,1)S(1)} %slice.36), channel_id=1, source_target_pairs={{0,4},{4,0},{8,12},{12,8},{1,5},{5,1},{9,13},{13,9},{2,6},{6,2},{1... | collective-permute-start | bytes 393224 | tf_op jit(solution)/shard_map/ppermute | solution.py:170
  65.2 0.6 collective-permute-start.27
  65.8 0.6 collective-permute-start.29
  66.3 2.3 %collective-permute-done.23 = bf16[32,2048]{1,0:T(8,128)(2,1)S(1)} collective-permute-done((bf16[32,2048]{1,0:T(8,128)(2,1)S(1)}, bf16[32,2048]{1,0:T(8,128)(2,1)S(1)}, u32[]{:S(2)}, u32[]{:S(2)}) %collective-permute-start.23) | collective-permute-done | bytes 131104 | tf_op jit(solution)/shard_map/ppermute | solution.py:177
  68.6 0.1 collective-permute-start.28
  68.7 2.1 %collective-permute-done.24 = bf16[32,2048]{1,0:T(8,128)(2,1)S(1)} collective-permute-done((bf16[32,2048]{1,0:T(8,128)(2,1)S(1)}, bf16[32,2048]{1,0:T(8,128)(2,1)S(1)}, u32[]{:S(2)}, u32[]{:S(2)}) %collective-permute-start.24) | collective-permute-done | bytes 131104 | tf_op jit(solution)/shard_map/ppermute | solution.py:170
  70.9 2.6 %collective-permute-start.26 = (bf16[32,2048]{1,0:T(8,128)(2,1)S(1)}, bf16[32,2048]{1,0:T(8,128)(2,1)S(1)}, u32[]{:S(2)}, u32[]{:S(2)}) collective-permute-start(bf16[32,2048]{1,0:T(8,128)(2,1)S(1)} %add_convert_fusion.4), channel_id=1, source_target_pairs={{0,8},{4,12},{8,0},{12,4},{1,9},{5,13},{9,1},{13,5},{2,10},{6,14},... | collective-permute-start | bytes 393224 | tf_op jit(solution)/shard_map/ppermute | solution.py:170
  73.6 5.6 %collective-permute-done.28 = bf16[32,2048]{1,0:T(8,128)(2,1)S(1)} collective-permute-done((bf16[32,2048]{1,0:T(8,128)(2,1)S(1)}, bf16[32,2048]{1,0:T(8,128)(2,1)S(1)}, u32[]{:S(2)}, u32[]{:S(2)}) %collective-permute-start.28) | collective-permute-done | bytes 131104 | tf_op jit(solution)/shard_map/ppermute | solution.py:177
  79.2 0.8 add_convert_fusion.3
  (32 shorter events, 0.6 us)
Async XLA Ops:
  0.8 13.9 %collective-permute-start.2 = (bf16[128,256]{1,0:T(8,128)(2,1)S(1)}, bf16[128,256]{1,0:T(8,128)(2,1)S(1)}, u32[]{:S(2)}, u32[]{:S(2)}) collective-permute-start(bf16[128,256]{1,0:T(8,128)(2,1)S(1)} %pad_maximum_fusion.1.kv_ref), channel_id=1, source_target_pairs={{0,12},{4,8},{1,13},{5,9},{2,14},{6,10},{3,15},{7,11},{16,28},{20,... | collective-permute-start | bytes 196616 | tf_op jit(solution)/shard_map/ppermute | solution.py:181
  7.8 7.0 %collective-permute-start.1 = (bf16[128,256]{1,0:T(8,128)(2,1)S(1)}, bf16[128,256]{1,0:T(8,128)(2,1)S(1)}, u32[]{:S(2)}, u32[]{:S(2)}) collective-permute-start(bf16[128,256]{1,0:T(8,128)(2,1)S(1)} %pad_maximum_fusion.1.kv_ref), channel_id=1, source_target_pairs={{0,8},{4,12},{1,9},{5,13},{2,10},{6,14},{3,11},{7,15},{16,24},{20,... | collective-permute-start | bytes 196616 | tf_op jit(solution)/shard_map/ppermute | solution.py:181
  9.1 5.7 %collective-permute-start = (bf16[128,256]{1,0:T(8,128)(2,1)S(1)}, bf16[128,256]{1,0:T(8,128)(2,1)S(1)}, u32[]{:S(2)}, u32[]{:S(2)}) collective-permute-start(bf16[128,256]{1,0:T(8,128)(2,1)S(1)} %pad_maximum_fusion.1.kv_ref), channel_id=1, source_target_pairs={{0,4},{8,12},{1,5},{9,13},{2,6},{10,14},{3,7},{11,15},{16,20},{24,... | collective-permute-start | bytes 196616 | tf_op jit(solution)/shard_map/ppermute | solution.py:181
  17.5 1.6 %collective-permute-start.3 = (bf16[64,2048]{1,0:T(8,128)(2,1)S(1)}, bf16[64,2048]{1,0:T(8,128)(2,1)S(1)}, u32[]{:S(2)}, u32[]{:S(2)}) collective-permute-start(bf16[64,2048]{1,0:T(8,128)(2,1)S(1)} %get-tuple-element.35), channel_id=1, source_target_pairs={{0,1},{1,0},{2,3},{3,2},{4,5},{5,4},{6,7},{7,6},{8,9},{9,8},{10,11... | collective-permute-start | bytes 786440 | tf_op jit(solution)/shard_map/ppermute | solution.py:170
  19.2 5.6 %collective-permute-start.4 = (bf16[32,2048]{1,0:T(8,128)(2,1)S(1)}, bf16[32,2048]{1,0:T(8,128)(2,1)S(1)}, u32[]{:S(2)}, u32[]{:S(2)}) collective-permute-start(bf16[32,2048]{1,0:T(8,128)(2,1)S(1)} %fusion), channel_id=1, source_target_pairs={{0,2},{2,0},{1,3},{3,1},{4,6},{6,4},{5,7},{7,5},{8,10},{10,8},{9,1... | collective-permute-start | bytes 393224 | tf_op jit(solution)/shard_map/ppermute | solution.py:170
  25.1 8.8 %collective-permute-start.6 = (bf16[32,2176]{1,0:T(8,128)(2,1)S(1)}, bf16[32,2176]{1,0:T(8,128)(2,1)S(1)}, u32[]{:S(2)}, u32[]{:S(2)}) collective-permute-start(bf16[32,2176]{1,0:T(8,128)(2,1)S(1)} %pad_maximum_fusion.refs_0_), channel_id=1, source_target_pairs={{0,8},{4,12},{8,0},{12,4},{1,9},{5,13},{9,1},{13,5},{2,10},{6,14},... | collective-permute-start | bytes 417800 | tf_op jit(solution)/shard_map/ppermute | solution.py:170
  25.2 10.3 %collective-permute-start.9 = (bf16[32,2176]{1,0:T(8,128)(2,1)S(1)}, bf16[32,2176]{1,0:T(8,128)(2,1)S(1)}, u32[]{:S(2)}, u32[]{:S(2)}) collective-permute-start(bf16[32,2176]{1,0:T(8,128)(2,1)S(1)} %pad_maximum_fusion.refs_0_), channel_id=1, source_target_pairs={{0,6},{2,4},{4,2},{6,0},{8,14},{10,12},{12,10},{14,8},{1,7},{3,5},... | collective-permute-start | bytes 417800 | tf_op jit(solution)/shard_map/ppermute | solution.py:177
  28.1 7.4 %collective-permute-start.8 = (bf16[32,2176]{1,0:T(8,128)(2,1)S(1)}, bf16[32,2176]{1,0:T(8,128)(2,1)S(1)}, u32[]{:S(2)}, u32[]{:S(2)}) collective-permute-start(bf16[32,2176]{1,0:T(8,128)(2,1)S(1)} %pad_maximum_fusion.refs_0_), channel_id=1, source_target_pairs={{0,2},{2,0},{1,3},{3,1},{4,6},{6,4},{5,7},{7,5},{8,10},{10,8},{9,1... | collective-permute-start | bytes 417800 | tf_op jit(solution)/shard_map/ppermute | solution.py:170
  28.6 8.4 %collective-permute-start.5 = (bf16[32,2176]{1,0:T(8,128)(2,1)S(1)}, bf16[32,2176]{1,0:T(8,128)(2,1)S(1)}, u32[]{:S(2)}, u32[]{:S(2)}) collective-permute-start(bf16[32,2176]{1,0:T(8,128)(2,1)S(1)} %pad_maximum_fusion.refs_0_), channel_id=1, source_target_pairs={{0,4},{4,0},{8,12},{12,8},{1,5},{5,1},{9,13},{13,9},{2,6},{6,2},{1... | collective-permute-start | bytes 417800 | tf_op jit(solution)/shard_map/ppermute | solution.py:170
  33.9 7.5 %collective-permute-start.11 = (bf16[32,2176]{1,0:T(8,128)(2,1)S(1)}, bf16[32,2176]{1,0:T(8,128)(2,1)S(1)}, u32[]{:S(2)}, u32[]{:S(2)}) collective-permute-start(bf16[32,2176]{1,0:T(8,128)(2,1)S(1)} %collective-permute-done.6.refs_2_), channel_id=1, source_target_pairs={{0,6},{2,4},{4,2},{6,0},{8,14},{10,12},{12,10},{14,8},{1,7},{3,5},... | collective-permute-start | bytes 417800 | tf_op jit(solution)/shard_map/ppermute | solution.py:177
  34.6 7.3 %collective-permute-start.10 = (bf16[32,2176]{1,0:T(8,128)(2,1)S(1)}, bf16[32,2176]{1,0:T(8,128)(2,1)S(1)}, u32[]{:S(2)}, u32[]{:S(2)}) collective-permute-start(bf16[32,2176]{1,0:T(8,128)(2,1)S(1)} %collective-permute-done.6.refs_2_), channel_id=1, source_target_pairs={{0,2},{2,0},{1,3},{3,1},{4,6},{6,4},{5,7},{7,5},{8,10},{10,8},{9,1... | collective-permute-start | bytes 417800 | tf_op jit(solution)/shard_map/ppermute | solution.py:170
  37.0 6.0 %collective-permute-start.7 = (bf16[32,2176]{1,0:T(8,128)(2,1)S(1)}, bf16[32,2176]{1,0:T(8,128)(2,1)S(1)}, u32[]{:S(2)}, u32[]{:S(2)}) collective-permute-start(bf16[32,2176]{1,0:T(8,128)(2,1)S(1)} %collective-permute-done.6.refs_2_), channel_id=1, source_target_pairs={{0,4},{4,0},{8,12},{12,8},{1,5},{5,1},{9,13},{13,9},{2,6},{6,2},{1... | collective-permute-start | bytes 417800 | tf_op jit(solution)/shard_map/ppermute | solution.py:170
  37.5 5.5 %collective-permute-start.12 = (bf16[32,2176]{1,0:T(8,128)(2,1)S(1)}, bf16[32,2176]{1,0:T(8,128)(2,1)S(1)}, u32[]{:S(2)}, u32[]{:S(2)}) collective-permute-start(bf16[32,2176]{1,0:T(8,128)(2,1)S(1)} %pad_maximum_fusion.refs_0_), channel_id=1, source_target_pairs={{0,1},{1,0},{2,3},{3,2},{4,5},{5,4},{6,7},{7,6},{8,9},{9,8},{10,11... | collective-permute-start | bytes 417800 | tf_op jit(solution)/shard_map/ppermute | solution.py:170
  37.5 6.0 %collective-permute-start.13 = (bf16[32,2176]{1,0:T(8,128)(2,1)S(1)}, bf16[32,2176]{1,0:T(8,128)(2,1)S(1)}, u32[]{:S(2)}, u32[]{:S(2)}) collective-permute-start(bf16[32,2176]{1,0:T(8,128)(2,1)S(1)} %collective-permute-done.5.refs_1_), channel_id=1, source_target_pairs={{0,1},{1,0},{2,3},{3,2},{4,5},{5,4},{6,7},{7,6},{8,9},{9,8},{10,11... | collective-permute-start | bytes 417800 | tf_op jit(solution)/shard_map/ppermute | solution.py:170
  41.4 2.1 %collective-permute-start.14 = (bf16[32,2176]{1,0:T(8,128)(2,1)S(1)}, bf16[32,2176]{1,0:T(8,128)(2,1)S(1)}, u32[]{:S(2)}, u32[]{:S(2)}) collective-permute-start(bf16[32,2176]{1,0:T(8,128)(2,1)S(1)} %collective-permute-done.6.refs_2_), channel_id=1, source_target_pairs={{0,1},{1,0},{2,3},{3,2},{4,5},{5,4},{6,7},{7,6},{8,9},{9,8},{10,11... | collective-permute-start | bytes 417800 | tf_op jit(solution)/shard_map/ppermute | solution.py:170
  42.0 2.0 %collective-permute-start.16 = (bf16[32,2176]{1,0:T(8,128)(2,1)S(1)}, bf16[32,2176]{1,0:T(8,128)(2,1)S(1)}, u32[]{:S(2)}, u32[]{:S(2)}) collective-permute-start(bf16[32,2176]{1,0:T(8,128)(2,1)S(1)} %collective-permute-done.8.refs_4_), channel_id=1, source_target_pairs={{0,1},{1,0},{2,3},{3,2},{4,5},{5,4},{6,7},{7,6},{8,9},{9,8},{10,11... | collective-permute-start | bytes 417800 | tf_op jit(solution)/shard_map/ppermute | solution.py:170
  43.0 1.4 %collective-permute-start.17 = (bf16[32,2176]{1,0:T(8,128)(2,1)S(1)}, bf16[32,2176]{1,0:T(8,128)(2,1)S(1)}, u32[]{:S(2)}, u32[]{:S(2)}) collective-permute-start(bf16[32,2176]{1,0:T(8,128)(2,1)S(1)} %collective-permute-done.9.refs_5_), channel_id=1, source_target_pairs={{0,1},{1,0},{2,3},{3,2},{4,5},{5,4},{6,7},{7,6},{8,9},{9,8},{10,11... | collective-permute-start | bytes 417800 | tf_op jit(solution)/shard_map/ppermute | solution.py:170
  43.0 1.6 %collective-permute-start.19 = (bf16[32,2176]{1,0:T(8,128)(2,1)S(1)}, bf16[32,2176]{1,0:T(8,128)(2,1)S(1)}, u32[]{:S(2)}, u32[]{:S(2)}) collective-permute-start(bf16[32,2176]{1,0:T(8,128)(2,1)S(1)} %collective-permute-done.11.refs_7_), channel_id=1, source_target_pairs={{0,1},{1,0},{2,3},{3,2},{4,5},{5,4},{6,7},{7,6},{8,9},{9,8},{10,11... | collective-permute-start | bytes 417800 | tf_op jit(solution)/shard_map/ppermute | solution.py:170
  43.5 1.4 %collective-permute-start.18 = (bf16[32,2176]{1,0:T(8,128)(2,1)S(1)}, bf16[32,2176]{1,0:T(8,128)(2,1)S(1)}, u32[]{:S(2)}, u32[]{:S(2)}) collective-permute-start(bf16[32,2176]{1,0:T(8,128)(2,1)S(1)} %collective-permute-done.10.refs_6_), channel_id=1, source_target_pairs={{0,1},{1,0},{2,3},{3,2},{4,5},{5,4},{6,7},{7,6},{8,9},{9,8},{10,11... | collective-permute-start | bytes 417800 | tf_op jit(solution)/shard_map/ppermute | solution.py:170
  43.6 1.5 %collective-permute-start.15 = (bf16[32,2176]{1,0:T(8,128)(2,1)S(1)}, bf16[32,2176]{1,0:T(8,128)(2,1)S(1)}, u32[]{:S(2)}, u32[]{:S(2)}) collective-permute-start(bf16[32,2176]{1,0:T(8,128)(2,1)S(1)} %collective-permute-done.7.refs_3_), channel_id=1, source_target_pairs={{0,1},{1,0},{2,3},{3,2},{4,5},{5,4},{6,7},{7,6},{8,9},{9,8},{10,11... | collective-permute-start | bytes 417800 | tf_op jit(solution)/shard_map/ppermute | solution.py:170
  59.6 1.6 %collective-permute-start.22 = (bf16[64,2048]{1,0:T(8,128)(2,1)S(1)}, bf16[64,2048]{1,0:T(8,128)(2,1)S(1)}, u32[]{:S(2)}, u32[]{:S(2)}) collective-permute-start(bf16[64,2048]{1,0:T(8,128)(2,1)S(1)} %get-tuple-element.50), channel_id=1, source_target_pairs={{0,1},{1,0},{2,3},{3,2},{4,5},{5,4},{6,7},{7,6},{8,9},{9,8},{10,11... | collective-permute-start | bytes 786440 | tf_op jit(solution)/shard_map/ppermute | solution.py:170
  60.0 3.4 %collective-permute-start.20 = (bf16[64,2048]{1,0:T(8,128)(2,1)S(1)}, bf16[64,2048]{1,0:T(8,128)(2,1)S(1)}, u32[]{:S(2)}, u32[]{:S(2)}) collective-permute-start(bf16[64,2048]{1,0:T(8,128)(2,1)S(1)} %get-tuple-element.44), channel_id=1, source_target_pairs={{0,1},{1,0},{2,3},{3,2},{4,5},{5,4},{6,7},{7,6},{8,9},{9,8},{10,11... | collective-permute-start | bytes 786440 | tf_op jit(solution)/shard_map/ppermute | solution.py:170
  60.2 3.3 %collective-permute-start.21 = (bf16[128,2048]{1,0:T(8,128)(2,1)S(1)}, bf16[128,2048]{1,0:T(8,128)(2,1)S(1)}, u32[]{:S(2)}, u32[]{:S(2)}) collective-permute-start(bf16[128,2048]{1,0:T(8,128)(2,1)S(1)} %get-tuple-element.46), channel_id=1, source_target_pairs={{0,1},{1,0},{2,3},{3,2},{4,5},{5,4},{6,7},{7,6},{8,9},{9,8},{10,11... | collective-permute-start | bytes 1572872 | tf_op jit(solution)/shard_map/ppermute | solution.py:170
  61.3 7.3 %collective-permute-start.23 = (bf16[32,2048]{1,0:T(8,128)(2,1)S(1)}, bf16[32,2048]{1,0:T(8,128)(2,1)S(1)}, u32[]{:S(2)}, u32[]{:S(2)}) collective-permute-start(bf16[32,2048]{1,0:T(8,128)(2,1)S(1)} %get-tuple-element.56), channel_id=1, source_target_pairs={{0,6},{2,4},{4,2},{6,0},{8,14},{10,12},{12,10},{14,8},{1,7},{3,5},... | collective-permute-start | bytes 393224 | tf_op jit(solution)/shard_map/ppermute | solution.py:177
  61.9 9.0 %collective-permute-start.24 = (bf16[32,2048]{1,0:T(8,128)(2,1)S(1)}, bf16[32,2048]{1,0:T(8,128)(2,1)S(1)}, u32[]{:S(2)}, u32[]{:S(2)}) collective-permute-start(bf16[32,2048]{1,0:T(8,128)(2,1)S(1)} %get-tuple-element.57), channel_id=1, source_target_pairs={{0,2},{2,0},{1,3},{3,1},{4,6},{6,4},{5,7},{7,5},{8,10},{10,8},{9,1... | collective-permute-start | bytes 393224 | tf_op jit(solution)/shard_map/ppermute | solution.py:170
  63.6 7.3 %collective-permute-start.25 = (bf16[32,2048]{1,0:T(8,128)(2,1)S(1)}, bf16[32,2048]{1,0:T(8,128)(2,1)S(1)}, u32[]{:S(2)}, u32[]{:S(2)}) collective-permute-start(bf16[32,2048]{1,0:T(8,128)(2,1)S(1)} %slice.36), channel_id=1, source_target_pairs={{0,4},{4,0},{8,12},{12,8},{1,5},{5,1},{9,13},{13,9},{2,6},{6,2},{1... | collective-permute-start | bytes 393224 | tf_op jit(solution)/shard_map/ppermute | solution.py:170
  65.2 8.4 %collective-permute-start.27 = (bf16[32,2048]{1,0:T(8,128)(2,1)S(1)}, bf16[32,2048]{1,0:T(8,128)(2,1)S(1)}, u32[]{:S(2)}, u32[]{:S(2)}) collective-permute-start(bf16[32,2048]{1,0:T(8,128)(2,1)S(1)} %get-tuple-element.53), channel_id=1, source_target_pairs={{0,4},{4,0},{8,12},{12,8},{1,5},{5,1},{9,13},{13,9},{2,6},{6,2},{1... | collective-permute-start | bytes 393224 | tf_op jit(solution)/shard_map/ppermute | solution.py:170
  65.8 7.8 %collective-permute-start.29 = (bf16[32,2048]{1,0:T(8,128)(2,1)S(1)}, bf16[32,2048]{1,0:T(8,128)(2,1)S(1)}, u32[]{:S(2)}, u32[]{:S(2)}) collective-permute-start(bf16[32,2048]{1,0:T(8,128)(2,1)S(1)} %get-tuple-element.54), channel_id=1, source_target_pairs={{0,2},{2,0},{1,3},{3,1},{4,6},{6,4},{5,7},{7,5},{8,10},{10,8},{9,1... | collective-permute-start | bytes 393224 | tf_op jit(solution)/shard_map/ppermute | solution.py:170
  68.6 10.6 %collective-permute-start.28 = (bf16[32,2048]{1,0:T(8,128)(2,1)S(1)}, bf16[32,2048]{1,0:T(8,128)(2,1)S(1)}, u32[]{:S(2)}, u32[]{:S(2)}) collective-permute-start(bf16[32,2048]{1,0:T(8,128)(2,1)S(1)} %get-tuple-element.55), channel_id=1, source_target_pairs={{0,6},{2,4},{4,2},{6,0},{8,14},{10,12},{12,10},{14,8},{1,7},{3,5},... | collective-permute-start | bytes 393224 | tf_op jit(solution)/shard_map/ppermute | solution.py:177
  70.9 8.3 %collective-permute-start.26 = (bf16[32,2048]{1,0:T(8,128)(2,1)S(1)}, bf16[32,2048]{1,0:T(8,128)(2,1)S(1)}, u32[]{:S(2)}, u32[]{:S(2)}) collective-permute-start(bf16[32,2048]{1,0:T(8,128)(2,1)S(1)} %add_convert_fusion.4), channel_id=1, source_target_pairs={{0,8},{4,12},{8,0},{12,4},{1,9},{5,13},{9,1},{13,5},{2,10},{6,14},... | collective-permute-start | bytes 393224 | tf_op jit(solution)/shard_map/ppermute | solution.py:170

commit v10 on v9

--- a/solution.py
+++ b/solution.py
@@ -438,7 +438,8 @@
     slot = lax.broadcasted_iota(jnp.int32, (slots, tokens), 0)
     token = lax.broadcasted_iota(jnp.int32, (TOPK, tokens), 1)
     offset = lax.rem(token // part, blocks) * (slots // blocks)
-    for side in range(sides):
+    @pl.loop(0, sides)
+    def _(side):
         fields = packed[side].T
         ids, ranks = fields[:TOPK].astype(jnp.int32), fields[TOPK : 2 * TOPK]
         gates = fields[2 * TOPK : 3 * TOPK] + fields[3 * TOPK : 4 * TOPK]

time: 80.2 us -> 79.6 us (level)
  transfers between devices with their start and end apart: 30 -> 30, of which waited for: 16 -> 15; matrix products, arithmetic and copies ran while one was open for 1% -> 1% of each run, Pallas kernels for 4% -> 4%
where the time goes in v10:
time: 79.6 us; the launch traced here: 79.4 us
  waiting for transfers between devices  29.1 us (37%)
  starting transfers between devices  27.9 us (35%)
  Pallas kernels  19.8 us (25%)
  other arithmetic  1.52 us (2%)
  local copies, waits for them, and re-layouts  0.84 us (1%)
    ppermute x23, waiting for transfers between devices, flip(): lax.ppermute(x, axis, [(i, i ^ bit) for i in range(lax.axis_size(axis))])  17.8 us
    pallas_call x1, Pallas kernels, cube_experts(): pl.pallas_call(functools.partial(expert_kernel, len(pieces), depth, exper...  13.9 us
    ppermute x23, starting transfers between devices, flip(): lax.ppermute(x, axis, [(i, i ^ bit) for i in range(lax.axis_size(axis))])  12.9 us
    ppermute x4, waiting for transfers between devices, flip_both(): return lax.ppermute(x, ('ctx', 'exp'), [(i, i ^ mask) for i in range(size)])  11.3 us
    ppermute x3, starting transfers between devices, from_earlier(): lax.ppermute(x, axis, [(i, i ^ bits) for i in range(lax.axis_size(axis))...  10.7 us
    ppermute x4, starting transfers between devices, flip_both(): return lax.ppermute(x, ('ctx', 'exp'), [(i, i ^ mask) for i in range(size)])  4.33 us
    pallas_call x1, Pallas kernels, own_block(): pl.pallas_call(functools.partial(own_block_kernel, (n_exp, n_tp, heads, p...  3.09 us
    pallas_call x1, Pallas kernels, attend_project(): pl.pallas_call(functools.partial(attention_kernel, (n_ctx, n_exp, n_tp, h...  2.76 us
  transfers between devices with their start and end apart: 30, of which 15 were waited for; matrix products, arithmetic and copies ran while one was open for 1% of the time, Pallas kernels for 4%

profile of v10, /device:TPU:0, one launch (start us, length us, event | category | flops | bytes accessed | tf_op | source)
XLA Modules:
  0.0 79.4 jit_solution(16013298176195482311)
XLA Ops:
  0.0 0.8 constant_dynamic-slice_fusion
  0.8 7.0 %collective-permute-start.2 = (bf16[128,256]{1,0:T(8,128)(2,1)S(1)}, bf16[128,256]{1,0:T(8,128)(2,1)S(1)}, u32[]{:S(2)}, u32[]{:S(2)}) collective-permute-start(bf16[128,256]{1,0:T(8,128)(2,1)S(1)} %pad_maximum_fusion.1.kv_ref), channel_id=1, source_target_pairs={{0,12},{4,8},{1,13},{5,9},{2,14},{6,10},{3,15},{7,11},{16,28},{20,... | collective-permute-start | bytes 196616 | tf_op jit(solution)/shard_map/ppermute | solution.py:181
  7.8 1.3 %collective-permute-start.1 = (bf16[128,256]{1,0:T(8,128)(2,1)S(1)}, bf16[128,256]{1,0:T(8,128)(2,1)S(1)}, u32[]{:S(2)}, u32[]{:S(2)}) collective-permute-start(bf16[128,256]{1,0:T(8,128)(2,1)S(1)} %pad_maximum_fusion.1.kv_ref), channel_id=1, source_target_pairs={{0,8},{4,12},{1,9},{5,13},{2,10},{6,14},{3,11},{7,15},{16,24},{20,... | collective-permute-start | bytes 196616 | tf_op jit(solution)/shard_map/ppermute | solution.py:181
  9.1 2.5 %collective-permute-start = (bf16[128,256]{1,0:T(8,128)(2,1)S(1)}, bf16[128,256]{1,0:T(8,128)(2,1)S(1)}, u32[]{:S(2)}, u32[]{:S(2)}) collective-permute-start(bf16[128,256]{1,0:T(8,128)(2,1)S(1)} %pad_maximum_fusion.1.kv_ref), channel_id=1, source_target_pairs={{0,4},{8,12},{1,5},{9,13},{2,6},{10,14},{3,7},{11,15},{16,20},{24,... | collective-permute-start | bytes 196616 | tf_op jit(solution)/shard_map/ppermute | solution.py:181
  11.5 0.1 pad_add_fusion.place
  11.6 3.1 %own_block.1 = (bf16[1024,128]{1,0:T(8,128)(2,1)S(1)}, bf16[1024,2048]{1,0:T(8,128)(2,1)S(1)}, bf16[32,2048]{1,0:T(8,128)(2,1)S(1)}, f32[1024,128]{1,0:T(8,128)S...) custom-call(s32[3]{0:T(128)S(1)} %pad_add_fusion.place, ...), custom_call_target="tpu_custom_call" | custom-call | flops 100663296 | bytes 4980736 | tf_op jit(solution)/shard_map/own_block/pallas_call | solution.py:271
  14.7 2.8 %attend_project.1 = (f32[32,2048]{1,0:T(8,128)S(1)}, bf16[32,2048]{1,0:T(8,128)(2,1)S(1)}, bf16[64,2048]{1,0:T(8,128)(2,1)S(1)}) custom-call(s32[3]{0:T(128)S(1)} %pad_add_fusion.place, bf16[128,256]{1,0:T(8,128)(2,1)S(1)} %collective-permute-done.refs_0_, bf16[128,256]{1,0:T(8,128)(2,1)S(1)} %collective-permute-done.1.refs_1_, ...), custom_call_target="tpu_custom_call" | custom-call | flops 838860800 | bytes 4980736 | tf_op jit(solution)/shard_map/attend_project/pallas_call | solution.py:355
  17.5 0.1 collective-permute-start.3
  17.6 1.5 %collective-permute-done.3 = bf16[64,2048]{1,0:T(8,128)(2,1)S(1)} collective-permute-done((bf16[64,2048]{1,0:T(8,128)(2,1)S(1)}, bf16[64,2048]{1,0:T(8,128)(2,1)S(1)}, u32[]{:S(2)}, u32[]{:S(2)}) %collective-permute-start.3) | collective-permute-done | bytes 262176 | tf_op jit(solution)/shard_map/ppermute | solution.py:170
  19.2 1.6 %collective-permute-start.4 = (bf16[32,2048]{1,0:T(8,128)(2,1)S(1)}, bf16[32,2048]{1,0:T(8,128)(2,1)S(1)}, u32[]{:S(2)}, u32[]{:S(2)}) collective-permute-start(bf16[32,2048]{1,0:T(8,128)(2,1)S(1)} %fusion), channel_id=1, source_target_pairs={{0,2},{2,0},{1,3},{3,1},{4,6},{6,4},{5,7},{7,5},{8,10},{10,8},{9,1... | collective-permute-start | bytes 393224 | tf_op jit(solution)/shard_map/ppermute | solution.py:170
  20.7 4.0 %collective-permute-done.4 = bf16[32,2048]{1,0:T(8,128)(2,1)S(1)} collective-permute-done((bf16[32,2048]{1,0:T(8,128)(2,1)S(1)}, bf16[32,2048]{1,0:T(8,128)(2,1)S(1)}, u32[]{:S(2)}, u32[]{:S(2)}) %collective-permute-start.4) | collective-permute-done | bytes 131104 | tf_op jit(solution)/shard_map/ppermute | solution.py:170
  24.8 0.2 multiply_reduce_fusion
  25.0 0.1 multiply_convert_fusion
  25.2 2.9 %collective-permute-start.9 = (bf16[32,2176]{1,0:T(8,128)(2,1)S(1)}, bf16[32,2176]{1,0:T(8,128)(2,1)S(1)}, u32[]{:S(2)}, u32[]{:S(2)}) collective-permute-start(bf16[32,2176]{1,0:T(8,128)(2,1)S(1)} %pad_maximum_fusion.refs_0_), channel_id=1, source_target_pairs={{0,6},{2,4},{4,2},{6,0},{8,14},{10,12},{12,10},{14,8},{1,7},{3,5},... | collective-permute-start | bytes 417800 | tf_op jit(solution)/shard_map/ppermute | solution.py:177
  28.1 0.5 collective-permute-start.8
  28.6 0.1 collective-permute-start.5
  28.7 5.2 %collective-permute-done.6.refs_2_ = bf16[32,2176]{1,0:T(8,128)(2,1)S(1)} collective-permute-done((bf16[32,2176]{1,0:T(8,128)(2,1)S(1)}, bf16[32,2176]{1,0:T(8,128)(2,1)S(1)}, u32[]{:S(2)}, u32[]{:S(2)}) %collective-permute-start.6) | collective-permute-done | bytes 139296 | tf_op jit(solution)/shard_map/ppermute | solution.py:170
  33.9 0.7 collective-permute-start.11
  34.6 0.8 %collective-permute-start.10 = (bf16[32,2176]{1,0:T(8,128)(2,1)S(1)}, bf16[32,2176]{1,0:T(8,128)(2,1)S(1)}, u32[]{:S(2)}, u32[]{:S(2)}) collective-permute-start(bf16[32,2176]{1,0:T(8,128)(2,1)S(1)} %collective-permute-done.6.refs_2_), channel_id=1, source_target_pairs={{0,2},{2,0},{1,3},{3,1},{4,6},{6,4},{5,7},{7,5},{8,10},{10,8},{9,1... | collective-permute-start | bytes 417800 | tf_op jit(solution)/shard_map/ppermute | solution.py:170
  35.4 1.5 %collective-permute-done.5.refs_1_ = bf16[32,2176]{1,0:T(8,128)(2,1)S(1)} collective-permute-done((bf16[32,2176]{1,0:T(8,128)(2,1)S(1)}, bf16[32,2176]{1,0:T(8,128)(2,1)S(1)}, u32[]{:S(2)}, u32[]{:S(2)}) %collective-permute-start.5) | collective-permute-done | bytes 139296 | tf_op jit(solution)/shard_map/ppermute | solution.py:170
  37.0 0.5 collective-permute-start.7
  37.5 0.5 collective-permute-start.13
  38.0 3.4 %collective-permute-done.11.refs_7_ = bf16[32,2176]{1,0:T(8,128)(2,1)S(1)} collective-permute-done((bf16[32,2176]{1,0:T(8,128)(2,1)S(1)}, bf16[32,2176]{1,0:T(8,128)(2,1)S(1)}, u32[]{:S(2)}, u32[]{:S(2)}) %collective-permute-start.11) | collective-permute-done | bytes 139296 | tf_op jit(solution)/shard_map/ppermute | solution.py:177
  41.4 0.5 collective-permute-done.10.refs_6_
  42.0 1.0 %collective-permute-done.7.refs_3_ = bf16[32,2176]{1,0:T(8,128)(2,1)S(1)} collective-permute-done((bf16[32,2176]{1,0:T(8,128)(2,1)S(1)}, bf16[32,2176]{1,0:T(8,128)(2,1)S(1)}, u32[]{:S(2)}, u32[]{:S(2)}) %collective-permute-start.7) | collective-permute-done | bytes 139296 | tf_op jit(solution)/shard_map/ppermute | solution.py:170
  43.0 0.5 collective-permute-start.19
  43.6 0.4 collective-permute-start.15
  44.0 0.3 collective-permute-done.17.refs_13_
  44.3 0.2 collective-permute-done.19.refs_15_
  44.5 0.3 collective-permute-done.18.refs_14_
  44.8 0.2 collective-permute-done.15.refs_11_
  45.0 13.9 %experts.1 = (bf16[64,2048]{1,0:T(8,128)(2,1)S(1)}, bf16[64,2048]{1,0:T(8,128)(2,1)S(1)}, bf16[128,2048]{1,0:T(8,128)(2,1)S(1)}, bf16[64,2048]{1,0:T(8,128)(2,1)...) custom-call(s32[1]{0:T(128)} %bitcast.5.first_ref, bf16[32,2176]{1,0:T(8,128)(2,1)S(1)} %pad_maximum_fusion.refs_0_, ...), custom_call_target="tpu_custom_call" | custom-call | flops 3489660928 | bytes 39845888 | tf_op jit(solution)/shard_map/experts/pallas_call | solution.py:501
  59.0 0.4 collective-permute-start.22
  59.3 0.2 collective-permute-start.20
  59.5 0.3 collective-permute-start.21
  59.8 0.7 collective-permute-done.22
  60.7 0.6 collective-permute-start.23
  61.3 1.4 %collective-permute-start.24 = (bf16[32,2048]{1,0:T(8,128)(2,1)S(1)}, bf16[32,2048]{1,0:T(8,128)(2,1)S(1)}, u32[]{:S(2)}, u32[]{:S(2)}) collective-permute-start(bf16[32,2048]{1,0:T(8,128)(2,1)S(1)} %get-tuple-element.57), channel_id=1, source_target_pairs={{0,2},{2,0},{1,3},{3,1},{4,6},{6,4},{5,7},{7,5},{8,10},{10,8},{9,1... | collective-permute-start | bytes 393224 | tf_op jit(solution)/shard_map/ppermute | solution.py:170
  62.8 0.1 add_convert_fusion
  63.0 1.5 %collective-permute-start.25 = (bf16[32,2048]{1,0:T(8,128)(2,1)S(1)}, bf16[32,2048]{1,0:T(8,128)(2,1)S(1)}, u32[]{:S(2)}, u32[]{:S(2)}) collective-permute-start(bf16[32,2048]{1,0:T(8,128)(2,1)S(1)} %slice.36), channel_id=1, source_target_pairs={{0,4},{4,0},{8,12},{12,8},{1,5},{5,1},{9,13},{13,9},{2,6},{6,2},{1... | collective-permute-start | bytes 393224 | tf_op jit(solution)/shard_map/ppermute | solution.py:170
  64.5 0.6 collective-permute-start.27
  65.1 0.6 collective-permute-start.29
  65.7 2.3 %collective-permute-done.23 = bf16[32,2048]{1,0:T(8,128)(2,1)S(1)} collective-permute-done((bf16[32,2048]{1,0:T(8,128)(2,1)S(1)}, bf16[32,2048]{1,0:T(8,128)(2,1)S(1)}, u32[]{:S(2)}, u32[]{:S(2)}) %collective-permute-start.23) | collective-permute-done | bytes 131104 | tf_op jit(solution)/shard_map/ppermute | solution.py:177
  68.0 0.1 collective-permute-start.28
  68.1 2.1 %collective-permute-done.24 = bf16[32,2048]{1,0:T(8,128)(2,1)S(1)} collective-permute-done((bf16[32,2048]{1,0:T(8,128)(2,1)S(1)}, bf16[32,2048]{1,0:T(8,128)(2,1)S(1)}, u32[]{:S(2)}, u32[]{:S(2)}) %collective-permute-start.24) | collective-permute-done | bytes 131104 | tf_op jit(solution)/shard_map/ppermute | solution.py:170
  70.3 2.6 %collective-permute-start.26 = (bf16[32,2048]{1,0:T(8,128)(2,1)S(1)}, bf16[32,2048]{1,0:T(8,128)(2,1)S(1)}, u32[]{:S(2)}, u32[]{:S(2)}) collective-permute-start(bf16[32,2048]{1,0:T(8,128)(2,1)S(1)} %add_convert_fusion.4), channel_id=1, source_target_pairs={{0,8},{4,12},{8,0},{12,4},{1,9},{5,13},{9,1},{13,5},{2,10},{6,14},... | collective-permute-start | bytes 393224 | tf_op jit(solution)/shard_map/ppermute | solution.py:170
  73.0 5.7 %collective-permute-done.28 = bf16[32,2048]{1,0:T(8,128)(2,1)S(1)} collective-permute-done((bf16[32,2048]{1,0:T(8,128)(2,1)S(1)}, bf16[32,2048]{1,0:T(8,128)(2,1)S(1)}, u32[]{:S(2)}, u32[]{:S(2)}) %collective-permute-start.28) | collective-permute-done | bytes 131104 | tf_op jit(solution)/shard_map/ppermute | solution.py:177
  78.6 0.8 add_convert_fusion.3
  (32 shorter events, 0.6 us)
Async XLA Ops:
  0.8 13.9 %collective-permute-start.2 = (bf16[128,256]{1,0:T(8,128)(2,1)S(1)}, bf16[128,256]{1,0:T(8,128)(2,1)S(1)}, u32[]{:S(2)}, u32[]{:S(2)}) collective-permute-start(bf16[128,256]{1,0:T(8,128)(2,1)S(1)} %pad_maximum_fusion.1.kv_ref), channel_id=1, source_target_pairs={{0,12},{4,8},{1,13},{5,9},{2,14},{6,10},{3,15},{7,11},{16,28},{20,... | collective-permute-start | bytes 196616 | tf_op jit(solution)/shard_map/ppermute | solution.py:181
  7.8 7.0 %collective-permute-start.1 = (bf16[128,256]{1,0:T(8,128)(2,1)S(1)}, bf16[128,256]{1,0:T(8,128)(2,1)S(1)}, u32[]{:S(2)}, u32[]{:S(2)}) collective-permute-start(bf16[128,256]{1,0:T(8,128)(2,1)S(1)} %pad_maximum_fusion.1.kv_ref), channel_id=1, source_target_pairs={{0,8},{4,12},{1,9},{5,13},{2,10},{6,14},{3,11},{7,15},{16,24},{20,... | collective-permute-start | bytes 196616 | tf_op jit(solution)/shard_map/ppermute | solution.py:181
  9.1 5.7 %collective-permute-start = (bf16[128,256]{1,0:T(8,128)(2,1)S(1)}, bf16[128,256]{1,0:T(8,128)(2,1)S(1)}, u32[]{:S(2)}, u32[]{:S(2)}) collective-permute-start(bf16[128,256]{1,0:T(8,128)(2,1)S(1)} %pad_maximum_fusion.1.kv_ref), channel_id=1, source_target_pairs={{0,4},{8,12},{1,5},{9,13},{2,6},{10,14},{3,7},{11,15},{16,20},{24,... | collective-permute-start | bytes 196616 | tf_op jit(solution)/shard_map/ppermute | solution.py:181
  17.5 1.6 %collective-permute-start.3 = (bf16[64,2048]{1,0:T(8,128)(2,1)S(1)}, bf16[64,2048]{1,0:T(8,128)(2,1)S(1)}, u32[]{:S(2)}, u32[]{:S(2)}) collective-permute-start(bf16[64,2048]{1,0:T(8,128)(2,1)S(1)} %get-tuple-element.35), channel_id=1, source_target_pairs={{0,1},{1,0},{2,3},{3,2},{4,5},{5,4},{6,7},{7,6},{8,9},{9,8},{10,11... | collective-permute-start | bytes 786440 | tf_op jit(solution)/shard_map/ppermute | solution.py:170
  19.2 5.6 %collective-permute-start.4 = (bf16[32,2048]{1,0:T(8,128)(2,1)S(1)}, bf16[32,2048]{1,0:T(8,128)(2,1)S(1)}, u32[]{:S(2)}, u32[]{:S(2)}) collective-permute-start(bf16[32,2048]{1,0:T(8,128)(2,1)S(1)} %fusion), channel_id=1, source_target_pairs={{0,2},{2,0},{1,3},{3,1},{4,6},{6,4},{5,7},{7,5},{8,10},{10,8},{9,1... | collective-permute-start | bytes 393224 | tf_op jit(solution)/shard_map/ppermute | solution.py:170
  25.1 8.8 %collective-permute-start.6 = (bf16[32,2176]{1,0:T(8,128)(2,1)S(1)}, bf16[32,2176]{1,0:T(8,128)(2,1)S(1)}, u32[]{:S(2)}, u32[]{:S(2)}) collective-permute-start(bf16[32,2176]{1,0:T(8,128)(2,1)S(1)} %pad_maximum_fusion.refs_0_), channel_id=1, source_target_pairs={{0,8},{4,12},{8,0},{12,4},{1,9},{5,13},{9,1},{13,5},{2,10},{6,14},... | collective-permute-start | bytes 417800 | tf_op jit(solution)/shard_map/ppermute | solution.py:170
  25.2 10.3 %collective-permute-start.9 = (bf16[32,2176]{1,0:T(8,128)(2,1)S(1)}, bf16[32,2176]{1,0:T(8,128)(2,1)S(1)}, u32[]{:S(2)}, u32[]{:S(2)}) collective-permute-start(bf16[32,2176]{1,0:T(8,128)(2,1)S(1)} %pad_maximum_fusion.refs_0_), channel_id=1, source_target_pairs={{0,6},{2,4},{4,2},{6,0},{8,14},{10,12},{12,10},{14,8},{1,7},{3,5},... | collective-permute-start | bytes 417800 | tf_op jit(solution)/shard_map/ppermute | solution.py:177
  28.1 7.4 %collective-permute-start.8 = (bf16[32,2176]{1,0:T(8,128)(2,1)S(1)}, bf16[32,2176]{1,0:T(8,128)(2,1)S(1)}, u32[]{:S(2)}, u32[]{:S(2)}) collective-permute-start(bf16[32,2176]{1,0:T(8,128)(2,1)S(1)} %pad_maximum_fusion.refs_0_), channel_id=1, source_target_pairs={{0,2},{2,0},{1,3},{3,1},{4,6},{6,4},{5,7},{7,5},{8,10},{10,8},{9,1... | collective-permute-start | bytes 417800 | tf_op jit(solution)/shard_map/ppermute | solution.py:170
  28.6 8.4 %collective-permute-start.5 = (bf16[32,2176]{1,0:T(8,128)(2,1)S(1)}, bf16[32,2176]{1,0:T(8,128)(2,1)S(1)}, u32[]{:S(2)}, u32[]{:S(2)}) collective-permute-start(bf16[32,2176]{1,0:T(8,128)(2,1)S(1)} %pad_maximum_fusion.refs_0_), channel_id=1, source_target_pairs={{0,4},{4,0},{8,12},{12,8},{1,5},{5,1},{9,13},{13,9},{2,6},{6,2},{1... | collective-permute-start | bytes 417800 | tf_op jit(solution)/shard_map/ppermute | solution.py:170
  33.9 7.5 %collective-permute-start.11 = (bf16[32,2176]{1,0:T(8,128)(2,1)S(1)}, bf16[32,2176]{1,0:T(8,128)(2,1)S(1)}, u32[]{:S(2)}, u32[]{:S(2)}) collective-permute-start(bf16[32,2176]{1,0:T(8,128)(2,1)S(1)} %collective-permute-done.6.refs_2_), channel_id=1, source_target_pairs={{0,6},{2,4},{4,2},{6,0},{8,14},{10,12},{12,10},{14,8},{1,7},{3,5},... | collective-permute-start | bytes 417800 | tf_op jit(solution)/shard_map/ppermute | solution.py:177
  34.6 7.3 %collective-permute-start.10 = (bf16[32,2176]{1,0:T(8,128)(2,1)S(1)}, bf16[32,2176]{1,0:T(8,128)(2,1)S(1)}, u32[]{:S(2)}, u32[]{:S(2)}) collective-permute-start(bf16[32,2176]{1,0:T(8,128)(2,1)S(1)} %collective-permute-done.6.refs_2_), channel_id=1, source_target_pairs={{0,2},{2,0},{1,3},{3,1},{4,6},{6,4},{5,7},{7,5},{8,10},{10,8},{9,1... | collective-permute-start | bytes 417800 | tf_op jit(solution)/shard_map/ppermute | solution.py:170
  37.0 6.0 %collective-permute-start.7 = (bf16[32,2176]{1,0:T(8,128)(2,1)S(1)}, bf16[32,2176]{1,0:T(8,128)(2,1)S(1)}, u32[]{:S(2)}, u32[]{:S(2)}) collective-permute-start(bf16[32,2176]{1,0:T(8,128)(2,1)S(1)} %collective-permute-done.6.refs_2_), channel_id=1, source_target_pairs={{0,4},{4,0},{8,12},{12,8},{1,5},{5,1},{9,13},{13,9},{2,6},{6,2},{1... | collective-permute-start | bytes 417800 | tf_op jit(solution)/shard_map/ppermute | solution.py:170
  37.5 5.5 %collective-permute-start.12 = (bf16[32,2176]{1,0:T(8,128)(2,1)S(1)}, bf16[32,2176]{1,0:T(8,128)(2,1)S(1)}, u32[]{:S(2)}, u32[]{:S(2)}) collective-permute-start(bf16[32,2176]{1,0:T(8,128)(2,1)S(1)} %pad_maximum_fusion.refs_0_), channel_id=1, source_target_pairs={{0,1},{1,0},{2,3},{3,2},{4,5},{5,4},{6,7},{7,6},{8,9},{9,8},{10,11... | collective-permute-start | bytes 417800 | tf_op jit(solution)/shard_map/ppermute | solution.py:170
  37.5 6.0 %collective-permute-start.13 = (bf16[32,2176]{1,0:T(8,128)(2,1)S(1)}, bf16[32,2176]{1,0:T(8,128)(2,1)S(1)}, u32[]{:S(2)}, u32[]{:S(2)}) collective-permute-start(bf16[32,2176]{1,0:T(8,128)(2,1)S(1)} %collective-permute-done.5.refs_1_), channel_id=1, source_target_pairs={{0,1},{1,0},{2,3},{3,2},{4,5},{5,4},{6,7},{7,6},{8,9},{9,8},{10,11... | collective-permute-start | bytes 417800 | tf_op jit(solution)/shard_map/ppermute | solution.py:170
  41.4 2.1 %collective-permute-start.14 = (bf16[32,2176]{1,0:T(8,128)(2,1)S(1)}, bf16[32,2176]{1,0:T(8,128)(2,1)S(1)}, u32[]{:S(2)}, u32[]{:S(2)}) collective-permute-start(bf16[32,2176]{1,0:T(8,128)(2,1)S(1)} %collective-permute-done.6.refs_2_), channel_id=1, source_target_pairs={{0,1},{1,0},{2,3},{3,2},{4,5},{5,4},{6,7},{7,6},{8,9},{9,8},{10,11... | collective-permute-start | bytes 417800 | tf_op jit(solution)/shard_map/ppermute | solution.py:170
  42.0 2.0 %collective-permute-start.16 = (bf16[32,2176]{1,0:T(8,128)(2,1)S(1)}, bf16[32,2176]{1,0:T(8,128)(2,1)S(1)}, u32[]{:S(2)}, u32[]{:S(2)}) collective-permute-start(bf16[32,2176]{1,0:T(8,128)(2,1)S(1)} %collective-permute-done.8.refs_4_), channel_id=1, source_target_pairs={{0,1},{1,0},{2,3},{3,2},{4,5},{5,4},{6,7},{7,6},{8,9},{9,8},{10,11... | collective-permute-start | bytes 417800 | tf_op jit(solution)/shard_map/ppermute | solution.py:170
  43.0 1.4 %collective-permute-start.17 = (bf16[32,2176]{1,0:T(8,128)(2,1)S(1)}, bf16[32,2176]{1,0:T(8,128)(2,1)S(1)}, u32[]{:S(2)}, u32[]{:S(2)}) collective-permute-start(bf16[32,2176]{1,0:T(8,128)(2,1)S(1)} %collective-permute-done.9.refs_5_), channel_id=1, source_target_pairs={{0,1},{1,0},{2,3},{3,2},{4,5},{5,4},{6,7},{7,6},{8,9},{9,8},{10,11... | collective-permute-start | bytes 417800 | tf_op jit(solution)/shard_map/ppermute | solution.py:170
  43.0 1.6 %collective-permute-start.19 = (bf16[32,2176]{1,0:T(8,128)(2,1)S(1)}, bf16[32,2176]{1,0:T(8,128)(2,1)S(1)}, u32[]{:S(2)}, u32[]{:S(2)}) collective-permute-start(bf16[32,2176]{1,0:T(8,128)(2,1)S(1)} %collective-permute-done.11.refs_7_), channel_id=1, source_target_pairs={{0,1},{1,0},{2,3},{3,2},{4,5},{5,4},{6,7},{7,6},{8,9},{9,8},{10,11... | collective-permute-start | bytes 417800 | tf_op jit(solution)/shard_map/ppermute | solution.py:170
  43.5 1.4 %collective-permute-start.18 = (bf16[32,2176]{1,0:T(8,128)(2,1)S(1)}, bf16[32,2176]{1,0:T(8,128)(2,1)S(1)}, u32[]{:S(2)}, u32[]{:S(2)}) collective-permute-start(bf16[32,2176]{1,0:T(8,128)(2,1)S(1)} %collective-permute-done.10.refs_6_), channel_id=1, source_target_pairs={{0,1},{1,0},{2,3},{3,2},{4,5},{5,4},{6,7},{7,6},{8,9},{9,8},{10,11... | collective-permute-start | bytes 417800 | tf_op jit(solution)/shard_map/ppermute | solution.py:170
  43.6 1.5 %collective-permute-start.15 = (bf16[32,2176]{1,0:T(8,128)(2,1)S(1)}, bf16[32,2176]{1,0:T(8,128)(2,1)S(1)}, u32[]{:S(2)}, u32[]{:S(2)}) collective-permute-start(bf16[32,2176]{1,0:T(8,128)(2,1)S(1)} %collective-permute-done.7.refs_3_), channel_id=1, source_target_pairs={{0,1},{1,0},{2,3},{3,2},{4,5},{5,4},{6,7},{7,6},{8,9},{9,8},{10,11... | collective-permute-start | bytes 417800 | tf_op jit(solution)/shard_map/ppermute | solution.py:170
  59.0 1.6 %collective-permute-start.22 = (bf16[64,2048]{1,0:T(8,128)(2,1)S(1)}, bf16[64,2048]{1,0:T(8,128)(2,1)S(1)}, u32[]{:S(2)}, u32[]{:S(2)}) collective-permute-start(bf16[64,2048]{1,0:T(8,128)(2,1)S(1)} %get-tuple-element.50), channel_id=1, source_target_pairs={{0,1},{1,0},{2,3},{3,2},{4,5},{5,4},{6,7},{7,6},{8,9},{9,8},{10,11... | collective-permute-start | bytes 786440 | tf_op jit(solution)/shard_map/ppermute | solution.py:170
  59.3 3.4 %collective-permute-start.20 = (bf16[64,2048]{1,0:T(8,128)(2,1)S(1)}, bf16[64,2048]{1,0:T(8,128)(2,1)S(1)}, u32[]{:S(2)}, u32[]{:S(2)}) collective-permute-start(bf16[64,2048]{1,0:T(8,128)(2,1)S(1)} %get-tuple-element.44), channel_id=1, source_target_pairs={{0,1},{1,0},{2,3},{3,2},{4,5},{5,4},{6,7},{7,6},{8,9},{9,8},{10,11... | collective-permute-start | bytes 786440 | tf_op jit(solution)/shard_map/ppermute | solution.py:170
  59.5 3.3 %collective-permute-start.21 = (bf16[128,2048]{1,0:T(8,128)(2,1)S(1)}, bf16[128,2048]{1,0:T(8,128)(2,1)S(1)}, u32[]{:S(2)}, u32[]{:S(2)}) collective-permute-start(bf16[128,2048]{1,0:T(8,128)(2,1)S(1)} %get-tuple-element.46), channel_id=1, source_target_pairs={{0,1},{1,0},{2,3},{3,2},{4,5},{5,4},{6,7},{7,6},{8,9},{9,8},{10,11... | collective-permute-start | bytes 1572872 | tf_op jit(solution)/shard_map/ppermute | solution.py:170
  60.7 7.3 %collective-permute-start.23 = (bf16[32,2048]{1,0:T(8,128)(2,1)S(1)}, bf16[32,2048]{1,0:T(8,128)(2,1)S(1)}, u32[]{:S(2)}, u32[]{:S(2)}) collective-permute-start(bf16[32,2048]{1,0:T(8,128)(2,1)S(1)} %get-tuple-element.56), channel_id=1, source_target_pairs={{0,6},{2,4},{4,2},{6,0},{8,14},{10,12},{12,10},{14,8},{1,7},{3,5},... | collective-permute-start | bytes 393224 | tf_op jit(solution)/shard_map/ppermute | solution.py:177
  61.3 9.0 %collective-permute-start.24 = (bf16[32,2048]{1,0:T(8,128)(2,1)S(1)}, bf16[32,2048]{1,0:T(8,128)(2,1)S(1)}, u32[]{:S(2)}, u32[]{:S(2)}) collective-permute-start(bf16[32,2048]{1,0:T(8,128)(2,1)S(1)} %get-tuple-element.57), channel_id=1, source_target_pairs={{0,2},{2,0},{1,3},{3,1},{4,6},{6,4},{5,7},{7,5},{8,10},{10,8},{9,1... | collective-permute-start | bytes 393224 | tf_op jit(solution)/shard_map/ppermute | solution.py:170
  63.0 7.3 %collective-permute-start.25 = (bf16[32,2048]{1,0:T(8,128)(2,1)S(1)}, bf16[32,2048]{1,0:T(8,128)(2,1)S(1)}, u32[]{:S(2)}, u32[]{:S(2)}) collective-permute-start(bf16[32,2048]{1,0:T(8,128)(2,1)S(1)} %slice.36), channel_id=1, source_target_pairs={{0,4},{4,0},{8,12},{12,8},{1,5},{5,1},{9,13},{13,9},{2,6},{6,2},{1... | collective-permute-start | bytes 393224 | tf_op jit(solution)/shard_map/ppermute | solution.py:170
  64.5 8.4 %collective-permute-start.27 = (bf16[32,2048]{1,0:T(8,128)(2,1)S(1)}, bf16[32,2048]{1,0:T(8,128)(2,1)S(1)}, u32[]{:S(2)}, u32[]{:S(2)}) collective-permute-start(bf16[32,2048]{1,0:T(8,128)(2,1)S(1)} %get-tuple-element.53), channel_id=1, source_target_pairs={{0,4},{4,0},{8,12},{12,8},{1,5},{5,1},{9,13},{13,9},{2,6},{6,2},{1... | collective-permute-start | bytes 393224 | tf_op jit(solution)/shard_map/ppermute | solution.py:170
  65.1 7.8 %collective-permute-start.29 = (bf16[32,2048]{1,0:T(8,128)(2,1)S(1)}, bf16[32,2048]{1,0:T(8,128)(2,1)S(1)}, u32[]{:S(2)}, u32[]{:S(2)}) collective-permute-start(bf16[32,2048]{1,0:T(8,128)(2,1)S(1)} %get-tuple-element.54), channel_id=1, source_target_pairs={{0,2},{2,0},{1,3},{3,1},{4,6},{6,4},{5,7},{7,5},{8,10},{10,8},{9,1... | collective-permute-start | bytes 393224 | tf_op jit(solution)/shard_map/ppermute | solution.py:170
  68.0 10.6 %collective-permute-start.28 = (bf16[32,2048]{1,0:T(8,128)(2,1)S(1)}, bf16[32,2048]{1,0:T(8,128)(2,1)S(1)}, u32[]{:S(2)}, u32[]{:S(2)}) collective-permute-start(bf16[32,2048]{1,0:T(8,128)(2,1)S(1)} %get-tuple-element.55), channel_id=1, source_target_pairs={{0,6},{2,4},{4,2},{6,0},{8,14},{10,12},{12,10},{14,8},{1,7},{3,5},... | collective-permute-start | bytes 393224 | tf_op jit(solution)/shard_map/ppermute | solution.py:177
  70.3 8.3 %collective-permute-start.26 = (bf16[32,2048]{1,0:T(8,128)(2,1)S(1)}, bf16[32,2048]{1,0:T(8,128)(2,1)S(1)}, u32[]{:S(2)}, u32[]{:S(2)}) collective-permute-start(bf16[32,2048]{1,0:T(8,128)(2,1)S(1)} %add_convert_fusion.4), channel_id=1, source_target_pairs={{0,8},{4,12},{8,0},{12,4},{1,9},{5,13},{9,1},{13,5},{2,10},{6,14},... | collective-permute-start | bytes 393224 | tf_op jit(solution)/shard_map/ppermute | solution.py:170

commit v11 on v10

--- a/solution.py
+++ b/solution.py
@@ -598,9 +598,9 @@
     last_across = flip_both(far)
     last = flip(far, "ctx", 1)
     early = lax.optimization_barrier((normed, near, far, across, near_across))
+    late = lax.optimization_barrier((far_across, last_across, last))
     pieces = [normed, near, far, last, across, near_across, far_across, last_across]
-    pieces += [flip(piece, "tp", 1) for piece in early[:3] + (last,)]
-    pieces += [flip(piece, "tp", 1) for piece in early[3:] + (far_across, last_across)]
+    pieces += [flip(piece, "tp", 1) for piece in early[:3] + late[2:] + early[3:] + late[:2]]
     sums = cube_experts(
         first.astype(jnp.int32).reshape(1), pieces, w_gate, w_up, w_down, slots
     )

time: 79.6 us -> 79.5 us (level)
  starting transfers between devices: 27.9 us -> 29 us
  waiting for transfers between devices: 29.1 us -> 28 us
    ppermute x4, waiting for transfers between devices: 11.3 us -> 9.92 us  [flip_both(): return lax.ppermute(x, ('ctx', 'exp'), [(i, i ^ mask) for i in range(size)])]
    ppermute x23, starting transfers between devices: 12.9 us -> 13.9 us  [flip(): lax.ppermute(x, axis, [(i, i ^ bit) for i in range(lax.axis_size(axis))])]
where the time goes in v11:
time: 79.5 us; the launch traced here: 79.3 us
  starting transfers between devices  29 us (36%)
  waiting for transfers between devices  28 us (35%)
  Pallas kernels  19.8 us (25%)
  other arithmetic  1.52 us (2%)
  local copies, waits for them, and re-layouts  0.84 us (1%)
    ppermute x23, waiting for transfers between devices, flip(): lax.ppermute(x, axis, [(i, i ^ bit) for i in range(lax.axis_size(axis))])  18.1 us
    ppermute x23, starting transfers between devices, flip(): lax.ppermute(x, axis, [(i, i ^ bit) for i in range(lax.axis_size(axis))])  13.9 us
    pallas_call x1, Pallas kernels, cube_experts(): pl.pallas_call(functools.partial(expert_kernel, len(pieces), depth, exper...  13.9 us
    ppermute x3, starting transfers between devices, from_earlier(): lax.ppermute(x, axis, [(i, i ^ bits) for i in range(lax.axis_size(axis))...  10.7 us
    ppermute x4, waiting for transfers between devices, flip_both(): return lax.ppermute(x, ('ctx', 'exp'), [(i, i ^ mask) for i in range(size)])  9.92 us
    ppermute x4, starting transfers between devices, flip_both(): return lax.ppermute(x, ('ctx', 'exp'), [(i, i ^ mask) for i in range(size)])  4.33 us
    pallas_call x1, Pallas kernels, own_block(): pl.pallas_call(functools.partial(own_block_kernel, (n_exp, n_tp, heads, p...  3.09 us
    pallas_call x1, Pallas kernels, attend_project(): pl.pallas_call(functools.partial(attention_kernel, (n_ctx, n_exp, n_tp, h...  2.76 us
  transfers between devices with their start and end apart: 30, of which 15 were waited for; matrix products, arithmetic and copies ran while one was open for 1% of the time, Pallas kernels for 4%

profile of v11, /device:TPU:0, one launch (start us, length us, event | category | flops | bytes accessed | tf_op | source)
XLA Modules:
  0.0 79.3 jit_solution(3972359310410091212)
XLA Ops:
  0.0 0.8 constant_dynamic-slice_fusion
  0.8 7.0 %collective-permute-start.2 = (bf16[128,256]{1,0:T(8,128)(2,1)S(1)}, bf16[128,256]{1,0:T(8,128)(2,1)S(1)}, u32[]{:S(2)}, u32[]{:S(2)}) collective-permute-start(bf16[128,256]{1,0:T(8,128)(2,1)S(1)} %pad_maximum_fusion.1.kv_ref), channel_id=1, source_target_pairs={{0,12},{4,8},{1,13},{5,9},{2,14},{6,10},{3,15},{7,11},{16,28},{20,... | collective-permute-start | bytes 196616 | tf_op jit(solution)/shard_map/ppermute | solution.py:181
  7.8 1.3 %collective-permute-start.1 = (bf16[128,256]{1,0:T(8,128)(2,1)S(1)}, bf16[128,256]{1,0:T(8,128)(2,1)S(1)}, u32[]{:S(2)}, u32[]{:S(2)}) collective-permute-start(bf16[128,256]{1,0:T(8,128)(2,1)S(1)} %pad_maximum_fusion.1.kv_ref), channel_id=1, source_target_pairs={{0,8},{4,12},{1,9},{5,13},{2,10},{6,14},{3,11},{7,15},{16,24},{20,... | collective-permute-start | bytes 196616 | tf_op jit(solution)/shard_map/ppermute | solution.py:181
  9.1 2.5 %collective-permute-start = (bf16[128,256]{1,0:T(8,128)(2,1)S(1)}, bf16[128,256]{1,0:T(8,128)(2,1)S(1)}, u32[]{:S(2)}, u32[]{:S(2)}) collective-permute-start(bf16[128,256]{1,0:T(8,128)(2,1)S(1)} %pad_maximum_fusion.1.kv_ref), channel_id=1, source_target_pairs={{0,4},{8,12},{1,5},{9,13},{2,6},{10,14},{3,7},{11,15},{16,20},{24,... | collective-permute-start | bytes 196616 | tf_op jit(solution)/shard_map/ppermute | solution.py:181
  11.5 0.1 pad_add_fusion.place
  11.6 3.1 %own_block.1 = (bf16[1024,128]{1,0:T(8,128)(2,1)S(1)}, bf16[1024,2048]{1,0:T(8,128)(2,1)S(1)}, bf16[32,2048]{1,0:T(8,128)(2,1)S(1)}, f32[1024,128]{1,0:T(8,128)S...) custom-call(s32[3]{0:T(128)S(1)} %pad_add_fusion.place, ...), custom_call_target="tpu_custom_call" | custom-call | flops 100663296 | bytes 4980736 | tf_op jit(solution)/shard_map/own_block/pallas_call | solution.py:271
  14.7 2.8 %attend_project.1 = (f32[32,2048]{1,0:T(8,128)S(1)}, bf16[32,2048]{1,0:T(8,128)(2,1)S(1)}, bf16[64,2048]{1,0:T(8,128)(2,1)S(1)}) custom-call(s32[3]{0:T(128)S(1)} %pad_add_fusion.place, bf16[128,256]{1,0:T(8,128)(2,1)S(1)} %collective-permute-done.refs_0_, bf16[128,256]{1,0:T(8,128)(2,1)S(1)} %collective-permute-done.1.refs_1_, ...), custom_call_target="tpu_custom_call" | custom-call | flops 838860800 | bytes 4980736 | tf_op jit(solution)/shard_map/attend_project/pallas_call | solution.py:355
  17.6 1.5 %collective-permute-done.3 = bf16[64,2048]{1,0:T(8,128)(2,1)S(1)} collective-permute-done((bf16[64,2048]{1,0:T(8,128)(2,1)S(1)}, bf16[64,2048]{1,0:T(8,128)(2,1)S(1)}, u32[]{:S(2)}, u32[]{:S(2)}) %collective-permute-start.3) | collective-permute-done | bytes 262176 | tf_op jit(solution)/shard_map/ppermute | solution.py:170
  19.2 1.6 %collective-permute-start.4 = (bf16[32,2048]{1,0:T(8,128)(2,1)S(1)}, bf16[32,2048]{1,0:T(8,128)(2,1)S(1)}, u32[]{:S(2)}, u32[]{:S(2)}) collective-permute-start(bf16[32,2048]{1,0:T(8,128)(2,1)S(1)} %fusion), channel_id=1, source_target_pairs={{0,2},{2,0},{1,3},{3,1},{4,6},{6,4},{5,7},{7,5},{8,10},{10,8},{9,1... | collective-permute-start | bytes 393224 | tf_op jit(solution)/shard_map/ppermute | solution.py:170
  20.7 4.0 %collective-permute-done.4 = bf16[32,2048]{1,0:T(8,128)(2,1)S(1)} collective-permute-done((bf16[32,2048]{1,0:T(8,128)(2,1)S(1)}, bf16[32,2048]{1,0:T(8,128)(2,1)S(1)}, u32[]{:S(2)}, u32[]{:S(2)}) %collective-permute-start.4) | collective-permute-done | bytes 131104 | tf_op jit(solution)/shard_map/ppermute | solution.py:170
  24.8 0.2 multiply_reduce_fusion
  25.0 0.1 multiply_convert_fusion
  25.1 0.1 collective-permute-start.6
  25.2 2.9 %collective-permute-start.9 = (bf16[32,2176]{1,0:T(8,128)(2,1)S(1)}, bf16[32,2176]{1,0:T(8,128)(2,1)S(1)}, u32[]{:S(2)}, u32[]{:S(2)}) collective-permute-start(bf16[32,2176]{1,0:T(8,128)(2,1)S(1)} %pad_maximum_fusion.refs_0_), channel_id=1, source_target_pairs={{0,6},{2,4},{4,2},{6,0},{8,14},{10,12},{12,10},{14,8},{1,7},{3,5},... | collective-permute-start | bytes 417800 | tf_op jit(solution)/shard_map/ppermute | solution.py:177
  28.1 0.5 collective-permute-start.8
  28.6 0.1 collective-permute-start.5
  28.7 5.2 %collective-permute-done.6.refs_2_ = bf16[32,2176]{1,0:T(8,128)(2,1)S(1)} collective-permute-done((bf16[32,2176]{1,0:T(8,128)(2,1)S(1)}, bf16[32,2176]{1,0:T(8,128)(2,1)S(1)}, u32[]{:S(2)}, u32[]{:S(2)}) %collective-permute-start.6) | collective-permute-done | bytes 139296 | tf_op jit(solution)/shard_map/ppermute | solution.py:170
  33.9 0.7 collective-permute-start.11
  34.6 0.8 %collective-permute-start.10 = (bf16[32,2176]{1,0:T(8,128)(2,1)S(1)}, bf16[32,2176]{1,0:T(8,128)(2,1)S(1)}, u32[]{:S(2)}, u32[]{:S(2)}) collective-permute-start(bf16[32,2176]{1,0:T(8,128)(2,1)S(1)} %collective-permute-done.6.refs_2_), channel_id=1, source_target_pairs={{0,2},{2,0},{1,3},{3,1},{4,6},{6,4},{5,7},{7,5},{8,10},{10,8},{9,1... | collective-permute-start | bytes 417800 | tf_op jit(solution)/shard_map/ppermute | solution.py:170
  35.4 2.0 %collective-permute-start.7 = (bf16[32,2176]{1,0:T(8,128)(2,1)S(1)}, bf16[32,2176]{1,0:T(8,128)(2,1)S(1)}, u32[]{:S(2)}, u32[]{:S(2)}) collective-permute-start(bf16[32,2176]{1,0:T(8,128)(2,1)S(1)} %collective-permute-done.6.refs_2_), channel_id=1, source_target_pairs={{0,4},{4,0},{8,12},{12,8},{1,5},{5,1},{9,13},{13,9},{2,6},{6,2},{1... | collective-permute-start | bytes 417800 | tf_op jit(solution)/shard_map/ppermute | solution.py:170
  37.4 0.5 collective-permute-start.13
  37.9 3.5 %collective-permute-done.11.refs_7_ = bf16[32,2176]{1,0:T(8,128)(2,1)S(1)} collective-permute-done((bf16[32,2176]{1,0:T(8,128)(2,1)S(1)}, bf16[32,2176]{1,0:T(8,128)(2,1)S(1)}, u32[]{:S(2)}, u32[]{:S(2)}) %collective-permute-start.11) | collective-permute-done | bytes 139296 | tf_op jit(solution)/shard_map/ppermute | solution.py:177
  41.4 0.5 collective-permute-done.10.refs_6_
  42.0 1.0 %collective-permute-done.7.refs_3_ = bf16[32,2176]{1,0:T(8,128)(2,1)S(1)} collective-permute-done((bf16[32,2176]{1,0:T(8,128)(2,1)S(1)}, bf16[32,2176]{1,0:T(8,128)(2,1)S(1)}, u32[]{:S(2)}, u32[]{:S(2)}) %collective-permute-start.7) | collective-permute-done | bytes 139296 | tf_op jit(solution)/shard_map/ppermute | solution.py:170
  43.0 0.5 collective-permute-start.15
  43.6 0.4 collective-permute-start.19
  44.0 0.3 collective-permute-done.17.refs_13_
  44.3 0.2 collective-permute-done.15.refs_11_
  44.5 0.3 collective-permute-done.18.refs_14_
  44.8 0.2 collective-permute-done.19.refs_15_
  45.0 13.9 %experts.1 = (bf16[64,2048]{1,0:T(8,128)(2,1)S(1)}, bf16[64,2048]{1,0:T(8,128)(2,1)S(1)}, bf16[128,2048]{1,0:T(8,128)(2,1)S(1)}, bf16[64,2048]{1,0:T(8,128)(2,1)...) custom-call(s32[1]{0:T(128)} %bitcast.5.first_ref, bf16[32,2176]{1,0:T(8,128)(2,1)S(1)} %pad_maximum_fusion.refs_0_, ...), custom_call_target="tpu_custom_call" | custom-call | flops 3489660928 | bytes 39845888 | tf_op jit(solution)/shard_map/experts/pallas_call | solution.py:501
  59.0 0.4 collective-permute-start.22
  59.3 0.2 collective-permute-start.20
  59.5 0.3 collective-permute-start.21
  59.8 0.7 collective-permute-done.22
  60.7 0.6 collective-permute-start.23
  61.3 1.4 %collective-permute-start.24 = (bf16[32,2048]{1,0:T(8,128)(2,1)S(1)}, bf16[32,2048]{1,0:T(8,128)(2,1)S(1)}, u32[]{:S(2)}, u32[]{:S(2)}) collective-permute-start(bf16[32,2048]{1,0:T(8,128)(2,1)S(1)} %get-tuple-element.63), channel_id=1, source_target_pairs={{0,2},{2,0},{1,3},{3,1},{4,6},{6,4},{5,7},{7,5},{8,10},{10,8},{9,1... | collective-permute-start | bytes 393224 | tf_op jit(solution)/shard_map/ppermute | solution.py:170
  62.8 0.1 add_convert_fusion
  63.0 1.5 %collective-permute-start.25 = (bf16[32,2048]{1,0:T(8,128)(2,1)S(1)}, bf16[32,2048]{1,0:T(8,128)(2,1)S(1)}, u32[]{:S(2)}, u32[]{:S(2)}) collective-permute-start(bf16[32,2048]{1,0:T(8,128)(2,1)S(1)} %slice.36), channel_id=1, source_target_pairs={{0,4},{4,0},{8,12},{12,8},{1,5},{5,1},{9,13},{13,9},{2,6},{6,2},{1... | collective-permute-start | bytes 393224 | tf_op jit(solution)/shard_map/ppermute | solution.py:170
  64.5 0.6 collective-permute-start.27
  65.1 0.6 collective-permute-start.29
  65.7 2.3 %collective-permute-done.23 = bf16[32,2048]{1,0:T(8,128)(2,1)S(1)} collective-permute-done((bf16[32,2048]{1,0:T(8,128)(2,1)S(1)}, bf16[32,2048]{1,0:T(8,128)(2,1)S(1)}, u32[]{:S(2)}, u32[]{:S(2)}) %collective-permute-start.23) | collective-permute-done | bytes 131104 | tf_op jit(solution)/shard_map/ppermute | solution.py:177
  68.0 0.1 collective-permute-start.28
  68.1 2.1 %collective-permute-done.24 = bf16[32,2048]{1,0:T(8,128)(2,1)S(1)} collective-permute-done((bf16[32,2048]{1,0:T(8,128)(2,1)S(1)}, bf16[32,2048]{1,0:T(8,128)(2,1)S(1)}, u32[]{:S(2)}, u32[]{:S(2)}) %collective-permute-start.24) | collective-permute-done | bytes 131104 | tf_op jit(solution)/shard_map/ppermute | solution.py:170
  70.3 2.2 %collective-permute-start.26 = (bf16[32,2048]{1,0:T(8,128)(2,1)S(1)}, bf16[32,2048]{1,0:T(8,128)(2,1)S(1)}, u32[]{:S(2)}, u32[]{:S(2)}) collective-permute-start(bf16[32,2048]{1,0:T(8,128)(2,1)S(1)} %add_convert_fusion.4), channel_id=1, source_target_pairs={{0,8},{4,12},{8,0},{12,4},{1,9},{5,13},{9,1},{13,5},{2,10},{6,14},... | collective-permute-start | bytes 393224 | tf_op jit(solution)/shard_map/ppermute | solution.py:170
  72.5 1.8 %collective-permute-done.27 = bf16[32,2048]{1,0:T(8,128)(2,1)S(1)} collective-permute-done((bf16[32,2048]{1,0:T(8,128)(2,1)S(1)}, bf16[32,2048]{1,0:T(8,128)(2,1)S(1)}, u32[]{:S(2)}, u32[]{:S(2)}) %collective-permute-start.27) | collective-permute-done | bytes 131104 | tf_op jit(solution)/shard_map/ppermute | solution.py:170
  74.4 4.2 %collective-permute-done.28 = bf16[32,2048]{1,0:T(8,128)(2,1)S(1)} collective-permute-done((bf16[32,2048]{1,0:T(8,128)(2,1)S(1)}, bf16[32,2048]{1,0:T(8,128)(2,1)S(1)}, u32[]{:S(2)}, u32[]{:S(2)}) %collective-permute-start.28) | collective-permute-done | bytes 131104 | tf_op jit(solution)/shard_map/ppermute | solution.py:177
  78.5 0.8 add_convert_fusion.3
  (32 shorter events, 0.5 us)
Async XLA Ops:
  0.8 13.9 %collective-permute-start.2 = (bf16[128,256]{1,0:T(8,128)(2,1)S(1)}, bf16[128,256]{1,0:T(8,128)(2,1)S(1)}, u32[]{:S(2)}, u32[]{:S(2)}) collective-permute-start(bf16[128,256]{1,0:T(8,128)(2,1)S(1)} %pad_maximum_fusion.1.kv_ref), channel_id=1, source_target_pairs={{0,12},{4,8},{1,13},{5,9},{2,14},{6,10},{3,15},{7,11},{16,28},{20,... | collective-permute-start | bytes 196616 | tf_op jit(solution)/shard_map/ppermute | solution.py:181
  7.8 7.0 %collective-permute-start.1 = (bf16[128,256]{1,0:T(8,128)(2,1)S(1)}, bf16[128,256]{1,0:T(8,128)(2,1)S(1)}, u32[]{:S(2)}, u32[]{:S(2)}) collective-permute-start(bf16[128,256]{1,0:T(8,128)(2,1)S(1)} %pad_maximum_fusion.1.kv_ref), channel_id=1, source_target_pairs={{0,8},{4,12},{1,9},{5,13},{2,10},{6,14},{3,11},{7,15},{16,24},{20,... | collective-permute-start | bytes 196616 | tf_op jit(solution)/shard_map/ppermute | solution.py:181
  9.1 5.7 %collective-permute-start = (bf16[128,256]{1,0:T(8,128)(2,1)S(1)}, bf16[128,256]{1,0:T(8,128)(2,1)S(1)}, u32[]{:S(2)}, u32[]{:S(2)}) collective-permute-start(bf16[128,256]{1,0:T(8,128)(2,1)S(1)} %pad_maximum_fusion.1.kv_ref), channel_id=1, source_target_pairs={{0,4},{8,12},{1,5},{9,13},{2,6},{10,14},{3,7},{11,15},{16,20},{24,... | collective-permute-start | bytes 196616 | tf_op jit(solution)/shard_map/ppermute | solution.py:181
  17.5 1.6 %collective-permute-start.3 = (bf16[64,2048]{1,0:T(8,128)(2,1)S(1)}, bf16[64,2048]{1,0:T(8,128)(2,1)S(1)}, u32[]{:S(2)}, u32[]{:S(2)}) collective-permute-start(bf16[64,2048]{1,0:T(8,128)(2,1)S(1)} %get-tuple-element.38), channel_id=1, source_target_pairs={{0,1},{1,0},{2,3},{3,2},{4,5},{5,4},{6,7},{7,6},{8,9},{9,8},{10,11... | collective-permute-start | bytes 786440 | tf_op jit(solution)/shard_map/ppermute | solution.py:170
  19.2 5.6 %collective-permute-start.4 = (bf16[32,2048]{1,0:T(8,128)(2,1)S(1)}, bf16[32,2048]{1,0:T(8,128)(2,1)S(1)}, u32[]{:S(2)}, u32[]{:S(2)}) collective-permute-start(bf16[32,2048]{1,0:T(8,128)(2,1)S(1)} %fusion), channel_id=1, source_target_pairs={{0,2},{2,0},{1,3},{3,1},{4,6},{6,4},{5,7},{7,5},{8,10},{10,8},{9,1... | collective-permute-start | bytes 393224 | tf_op jit(solution)/shard_map/ppermute | solution.py:170
  25.1 8.8 %collective-permute-start.6 = (bf16[32,2176]{1,0:T(8,128)(2,1)S(1)}, bf16[32,2176]{1,0:T(8,128)(2,1)S(1)}, u32[]{:S(2)}, u32[]{:S(2)}) collective-permute-start(bf16[32,2176]{1,0:T(8,128)(2,1)S(1)} %pad_maximum_fusion.refs_0_), channel_id=1, source_target_pairs={{0,8},{4,12},{8,0},{12,4},{1,9},{5,13},{9,1},{13,5},{2,10},{6,14},... | collective-permute-start | bytes 417800 | tf_op jit(solution)/shard_map/ppermute | solution.py:170
  25.2 10.3 %collective-permute-start.9 = (bf16[32,2176]{1,0:T(8,128)(2,1)S(1)}, bf16[32,2176]{1,0:T(8,128)(2,1)S(1)}, u32[]{:S(2)}, u32[]{:S(2)}) collective-permute-start(bf16[32,2176]{1,0:T(8,128)(2,1)S(1)} %pad_maximum_fusion.refs_0_), channel_id=1, source_target_pairs={{0,6},{2,4},{4,2},{6,0},{8,14},{10,12},{12,10},{14,8},{1,7},{3,5},... | collective-permute-start | bytes 417800 | tf_op jit(solution)/shard_map/ppermute | solution.py:177
  28.1 9.3 %collective-permute-start.8 = (bf16[32,2176]{1,0:T(8,128)(2,1)S(1)}, bf16[32,2176]{1,0:T(8,128)(2,1)S(1)}, u32[]{:S(2)}, u32[]{:S(2)}) collective-permute-start(bf16[32,2176]{1,0:T(8,128)(2,1)S(1)} %pad_maximum_fusion.refs_0_), channel_id=1, source_target_pairs={{0,2},{2,0},{1,3},{3,1},{4,6},{6,4},{5,7},{7,5},{8,10},{10,8},{9,1... | collective-permute-start | bytes 417800 | tf_op jit(solution)/shard_map/ppermute | solution.py:170
  28.6 8.8 %collective-permute-start.5 = (bf16[32,2176]{1,0:T(8,128)(2,1)S(1)}, bf16[32,2176]{1,0:T(8,128)(2,1)S(1)}, u32[]{:S(2)}, u32[]{:S(2)}) collective-permute-start(bf16[32,2176]{1,0:T(8,128)(2,1)S(1)} %pad_maximum_fusion.refs_0_), channel_id=1, source_target_pairs={{0,4},{4,0},{8,12},{12,8},{1,5},{5,1},{9,13},{13,9},{2,6},{6,2},{1... | collective-permute-start | bytes 417800 | tf_op jit(solution)/shard_map/ppermute | solution.py:170
  33.9 7.5 %collective-permute-start.11 = (bf16[32,2176]{1,0:T(8,128)(2,1)S(1)}, bf16[32,2176]{1,0:T(8,128)(2,1)S(1)}, u32[]{:S(2)}, u32[]{:S(2)}) collective-permute-start(bf16[32,2176]{1,0:T(8,128)(2,1)S(1)} %collective-permute-done.6.refs_2_), channel_id=1, source_target_pairs={{0,6},{2,4},{4,2},{6,0},{8,14},{10,12},{12,10},{14,8},{1,7},{3,5},... | collective-permute-start | bytes 417800 | tf_op jit(solution)/shard_map/ppermute | solution.py:177
  34.6 7.3 %collective-permute-start.10 = (bf16[32,2176]{1,0:T(8,128)(2,1)S(1)}, bf16[32,2176]{1,0:T(8,128)(2,1)S(1)}, u32[]{:S(2)}, u32[]{:S(2)}) collective-permute-start(bf16[32,2176]{1,0:T(8,128)(2,1)S(1)} %collective-permute-done.6.refs_2_), channel_id=1, source_target_pairs={{0,2},{2,0},{1,3},{3,1},{4,6},{6,4},{5,7},{7,5},{8,10},{10,8},{9,1... | collective-permute-start | bytes 417800 | tf_op jit(solution)/shard_map/ppermute | solution.py:170
  35.4 7.5 %collective-permute-start.7 = (bf16[32,2176]{1,0:T(8,128)(2,1)S(1)}, bf16[32,2176]{1,0:T(8,128)(2,1)S(1)}, u32[]{:S(2)}, u32[]{:S(2)}) collective-permute-start(bf16[32,2176]{1,0:T(8,128)(2,1)S(1)} %collective-permute-done.6.refs_2_), channel_id=1, source_target_pairs={{0,4},{4,0},{8,12},{12,8},{1,5},{5,1},{9,13},{13,9},{2,6},{6,2},{1... | collective-permute-start | bytes 417800 | tf_op jit(solution)/shard_map/ppermute | solution.py:170
  37.4 5.5 %collective-permute-start.12 = (bf16[32,2176]{1,0:T(8,128)(2,1)S(1)}, bf16[32,2176]{1,0:T(8,128)(2,1)S(1)}, u32[]{:S(2)}, u32[]{:S(2)}) collective-permute-start(bf16[32,2176]{1,0:T(8,128)(2,1)S(1)} %pad_maximum_fusion.refs_0_), channel_id=1, source_target_pairs={{0,1},{1,0},{2,3},{3,2},{4,5},{5,4},{6,7},{7,6},{8,9},{9,8},{10,11... | collective-permute-start | bytes 417800 | tf_op jit(solution)/shard_map/ppermute | solution.py:170
  37.4 6.0 %collective-permute-start.13 = (bf16[32,2176]{1,0:T(8,128)(2,1)S(1)}, bf16[32,2176]{1,0:T(8,128)(2,1)S(1)}, u32[]{:S(2)}, u32[]{:S(2)}) collective-permute-start(bf16[32,2176]{1,0:T(8,128)(2,1)S(1)} %collective-permute-done.5.refs_1_), channel_id=1, source_target_pairs={{0,1},{1,0},{2,3},{3,2},{4,5},{5,4},{6,7},{7,6},{8,9},{9,8},{10,11... | collective-permute-start | bytes 417800 | tf_op jit(solution)/shard_map/ppermute | solution.py:170
  41.4 2.1 %collective-permute-start.14 = (bf16[32,2176]{1,0:T(8,128)(2,1)S(1)}, bf16[32,2176]{1,0:T(8,128)(2,1)S(1)}, u32[]{:S(2)}, u32[]{:S(2)}) collective-permute-start(bf16[32,2176]{1,0:T(8,128)(2,1)S(1)} %collective-permute-done.6.refs_2_), channel_id=1, source_target_pairs={{0,1},{1,0},{2,3},{3,2},{4,5},{5,4},{6,7},{7,6},{8,9},{9,8},{10,11... | collective-permute-start | bytes 417800 | tf_op jit(solution)/shard_map/ppermute | solution.py:170
  42.0 2.0 %collective-permute-start.16 = (bf16[32,2176]{1,0:T(8,128)(2,1)S(1)}, bf16[32,2176]{1,0:T(8,128)(2,1)S(1)}, u32[]{:S(2)}, u32[]{:S(2)}) collective-permute-start(bf16[32,2176]{1,0:T(8,128)(2,1)S(1)} %collective-permute-done.8.refs_4_), channel_id=1, source_target_pairs={{0,1},{1,0},{2,3},{3,2},{4,5},{5,4},{6,7},{7,6},{8,9},{9,8},{10,11... | collective-permute-start | bytes 417800 | tf_op jit(solution)/shard_map/ppermute | solution.py:170
  43.0 1.4 %collective-permute-start.17 = (bf16[32,2176]{1,0:T(8,128)(2,1)S(1)}, bf16[32,2176]{1,0:T(8,128)(2,1)S(1)}, u32[]{:S(2)}, u32[]{:S(2)}) collective-permute-start(bf16[32,2176]{1,0:T(8,128)(2,1)S(1)} %collective-permute-done.9.refs_5_), channel_id=1, source_target_pairs={{0,1},{1,0},{2,3},{3,2},{4,5},{5,4},{6,7},{7,6},{8,9},{9,8},{10,11... | collective-permute-start | bytes 417800 | tf_op jit(solution)/shard_map/ppermute | solution.py:170
  43.0 1.6 %collective-permute-start.15 = (bf16[32,2176]{1,0:T(8,128)(2,1)S(1)}, bf16[32,2176]{1,0:T(8,128)(2,1)S(1)}, u32[]{:S(2)}, u32[]{:S(2)}) collective-permute-start(bf16[32,2176]{1,0:T(8,128)(2,1)S(1)} %collective-permute-done.7.refs_3_), channel_id=1, source_target_pairs={{0,1},{1,0},{2,3},{3,2},{4,5},{5,4},{6,7},{7,6},{8,9},{9,8},{10,11... | collective-permute-start | bytes 417800 | tf_op jit(solution)/shard_map/ppermute | solution.py:170
  43.5 1.4 %collective-permute-start.18 = (bf16[32,2176]{1,0:T(8,128)(2,1)S(1)}, bf16[32,2176]{1,0:T(8,128)(2,1)S(1)}, u32[]{:S(2)}, u32[]{:S(2)}) collective-permute-start(bf16[32,2176]{1,0:T(8,128)(2,1)S(1)} %collective-permute-done.10.refs_6_), channel_id=1, source_target_pairs={{0,1},{1,0},{2,3},{3,2},{4,5},{5,4},{6,7},{7,6},{8,9},{9,8},{10,11... | collective-permute-start | bytes 417800 | tf_op jit(solution)/shard_map/ppermute | solution.py:170
  43.6 1.5 %collective-permute-start.19 = (bf16[32,2176]{1,0:T(8,128)(2,1)S(1)}, bf16[32,2176]{1,0:T(8,128)(2,1)S(1)}, u32[]{:S(2)}, u32[]{:S(2)}) collective-permute-start(bf16[32,2176]{1,0:T(8,128)(2,1)S(1)} %collective-permute-done.11.refs_7_), channel_id=1, source_target_pairs={{0,1},{1,0},{2,3},{3,2},{4,5},{5,4},{6,7},{7,6},{8,9},{9,8},{10,11... | collective-permute-start | bytes 417800 | tf_op jit(solution)/shard_map/ppermute | solution.py:170
  59.0 1.6 %collective-permute-start.22 = (bf16[64,2048]{1,0:T(8,128)(2,1)S(1)}, bf16[64,2048]{1,0:T(8,128)(2,1)S(1)}, u32[]{:S(2)}, u32[]{:S(2)}) collective-permute-start(bf16[64,2048]{1,0:T(8,128)(2,1)S(1)} %get-tuple-element.56), channel_id=1, source_target_pairs={{0,1},{1,0},{2,3},{3,2},{4,5},{5,4},{6,7},{7,6},{8,9},{9,8},{10,11... | collective-permute-start | bytes 786440 | tf_op jit(solution)/shard_map/ppermute | solution.py:170
  59.3 3.4 %collective-permute-start.20 = (bf16[64,2048]{1,0:T(8,128)(2,1)S(1)}, bf16[64,2048]{1,0:T(8,128)(2,1)S(1)}, u32[]{:S(2)}, u32[]{:S(2)}) collective-permute-start(bf16[64,2048]{1,0:T(8,128)(2,1)S(1)} %get-tuple-element.50), channel_id=1, source_target_pairs={{0,1},{1,0},{2,3},{3,2},{4,5},{5,4},{6,7},{7,6},{8,9},{9,8},{10,11... | collective-permute-start | bytes 786440 | tf_op jit(solution)/shard_map/ppermute | solution.py:170
  59.5 3.3 %collective-permute-start.21 = (bf16[128,2048]{1,0:T(8,128)(2,1)S(1)}, bf16[128,2048]{1,0:T(8,128)(2,1)S(1)}, u32[]{:S(2)}, u32[]{:S(2)}) collective-permute-start(bf16[128,2048]{1,0:T(8,128)(2,1)S(1)} %get-tuple-element.52), channel_id=1, source_target_pairs={{0,1},{1,0},{2,3},{3,2},{4,5},{5,4},{6,7},{7,6},{8,9},{9,8},{10,11... | collective-permute-start | bytes 1572872 | tf_op jit(solution)/shard_map/ppermute | solution.py:170
  60.7 7.3 %collective-permute-start.23 = (bf16[32,2048]{1,0:T(8,128)(2,1)S(1)}, bf16[32,2048]{1,0:T(8,128)(2,1)S(1)}, u32[]{:S(2)}, u32[]{:S(2)}) collective-permute-start(bf16[32,2048]{1,0:T(8,128)(2,1)S(1)} %get-tuple-element.62), channel_id=1, source_target_pairs={{0,6},{2,4},{4,2},{6,0},{8,14},{10,12},{12,10},{14,8},{1,7},{3,5},... | collective-permute-start | bytes 393224 | tf_op jit(solution)/shard_map/ppermute | solution.py:177
  61.3 9.0 %collective-permute-start.24 = (bf16[32,2048]{1,0:T(8,128)(2,1)S(1)}, bf16[32,2048]{1,0:T(8,128)(2,1)S(1)}, u32[]{:S(2)}, u32[]{:S(2)}) collective-permute-start(bf16[32,2048]{1,0:T(8,128)(2,1)S(1)} %get-tuple-element.63), channel_id=1, source_target_pairs={{0,2},{2,0},{1,3},{3,1},{4,6},{6,4},{5,7},{7,5},{8,10},{10,8},{9,1... | collective-permute-start | bytes 393224 | tf_op jit(solution)/shard_map/ppermute | solution.py:170
  63.0 7.3 %collective-permute-start.25 = (bf16[32,2048]{1,0:T(8,128)(2,1)S(1)}, bf16[32,2048]{1,0:T(8,128)(2,1)S(1)}, u32[]{:S(2)}, u32[]{:S(2)}) collective-permute-start(bf16[32,2048]{1,0:T(8,128)(2,1)S(1)} %slice.36), channel_id=1, source_target_pairs={{0,4},{4,0},{8,12},{12,8},{1,5},{5,1},{9,13},{13,9},{2,6},{6,2},{1... | collective-permute-start | bytes 393224 | tf_op jit(solution)/shard_map/ppermute | solution.py:170
  64.5 9.8 %collective-permute-start.27 = (bf16[32,2048]{1,0:T(8,128)(2,1)S(1)}, bf16[32,2048]{1,0:T(8,128)(2,1)S(1)}, u32[]{:S(2)}, u32[]{:S(2)}) collective-permute-start(bf16[32,2048]{1,0:T(8,128)(2,1)S(1)} %get-tuple-element.59), channel_id=1, source_target_pairs={{0,4},{4,0},{8,12},{12,8},{1,5},{5,1},{9,13},{13,9},{2,6},{6,2},{1... | collective-permute-start | bytes 393224 | tf_op jit(solution)/shard_map/ppermute | solution.py:170
  65.1 9.2 %collective-permute-start.29 = (bf16[32,2048]{1,0:T(8,128)(2,1)S(1)}, bf16[32,2048]{1,0:T(8,128)(2,1)S(1)}, u32[]{:S(2)}, u32[]{:S(2)}) collective-permute-start(bf16[32,2048]{1,0:T(8,128)(2,1)S(1)} %get-tuple-element.60), channel_id=1, source_target_pairs={{0,2},{2,0},{1,3},{3,1},{4,6},{6,4},{5,7},{7,5},{8,10},{10,8},{9,1... | collective-permute-start | bytes 393224 | tf_op jit(solution)/shard_map/ppermute | solution.py:170
  68.0 10.5 %collective-permute-start.28 = (bf16[32,2048]{1,0:T(8,128)(2,1)S(1)}, bf16[32,2048]{1,0:T(8,128)(2,1)S(1)}, u32[]{:S(2)}, u32[]{:S(2)}) collective-permute-start(bf16[32,2048]{1,0:T(8,128)(2,1)S(1)} %get-tuple-element.61), channel_id=1, source_target_pairs={{0,6},{2,4},{4,2},{6,0},{8,14},{10,12},{12,10},{14,8},{1,7},{3,5},... | collective-permute-start | bytes 393224 | tf_op jit(solution)/shard_map/ppermute | solution.py:177
  70.3 8.2 %collective-permute-start.26 = (bf16[32,2048]{1,0:T(8,128)(2,1)S(1)}, bf16[32,2048]{1,0:T(8,128)(2,1)S(1)}, u32[]{:S(2)}, u32[]{:S(2)}) collective-permute-start(bf16[32,2048]{1,0:T(8,128)(2,1)S(1)} %add_convert_fusion.4), channel_id=1, source_target_pairs={{0,8},{4,12},{8,0},{12,4},{1,9},{5,13},{9,1},{13,5},{2,10},{6,14},... | collective-permute-start | bytes 393224 | tf_op jit(solution)/shard_map/ppermute | solution.py:170

commit v12 on v11

--- a/solution.py
+++ b/solution.py
@@ -177,10 +177,6 @@
     return lax.ppermute(x, ("ctx", "exp"), [(i, i ^ mask) for i in range(size)])
 
 
-def from_earlier(x, axis, bits):
-    return lax.ppermute(x, axis, [(i, i ^ bits) for i in range(lax.axis_size(axis)) if i < i ^ bits])
-
-
 def in_hbm(x):
     return pltpu.with_memory_space_constraint(x, pltpu.HBM)
 
@@ -577,7 +573,7 @@
     key_head = lax.dynamic_slice_in_dim(keys, shared * HEAD_DIMENSION, HEAD_DIMENSION, 1)
     value_head = lax.dynamic_slice_in_dim(values, shared * HEAD_DIMENSION, HEAD_DIMENSION, 1)
     kv = jnp.concatenate([key_head, value_head], axis=1)
-    kv_pieces = [from_earlier(kv, "ctx", bits) for bits in KV_ORDER]
+    kv_pieces = [flip(kv, "ctx", bits) for bits in KV_ORDER]
     *own, routing = own_block(
         place, kv, expert_ids, router_probs, queries, out_weight, resid, n_exp, n_tp
     )

time: 79.5 us -> 77.4 us (0.974)
  starting transfers between devices: 29 us -> 25.4 us
  waiting for transfers between devices: 28 us -> 29.6 us
    ppermute x3 -> x0, starting transfers between devices: 10.7 us -> none  [from_earlier(): lax.ppermute(x, axis, [(i, i ^ bits) for i in range(lax.axis_size(axis))...]
    ppermute x23 -> x26, starting transfers between devices: 13.9 us -> 20.5 us  [flip(): lax.ppermute(x, axis, [(i, i ^ bit) for i in range(lax.axis_size(axis))])]
    ppermute x4, waiting for transfers between devices: 9.92 us -> 11.2 us  [flip_both(): return lax.ppermute(x, ('ctx', 'exp'), [(i, i ^ mask) for i in range(size)])]
    ppermute x23 -> x26, waiting for transfers between devices: 18.1 us -> 18.4 us  [flip(): lax.ppermute(x, axis, [(i, i ^ bit) for i in range(lax.axis_size(axis))])]
  transfers between devices with their start and end apart: 30 -> 30, of which waited for: 15 -> 19; matrix products, arithmetic and copies ran while one was open for 1% -> 1% of each run, Pallas kernels for 4% -> 4%
where the time goes in v12:
time: 77.4 us; the launch traced here: 77.2 us
  waiting for transfers between devices  29.6 us (38%)
  starting transfers between devices  25.4 us (33%)
  Pallas kernels  19.7 us (25%)
  other arithmetic  1.51 us (2%)
  local copies, waits for them, and re-layouts  0.84 us (1%)
    ppermute x26, starting transfers between devices, flip(): lax.ppermute(x, axis, [(i, i ^ bit) for i in range(lax.axis_size(axis))])  20.5 us
    ppermute x26, waiting for transfers between devices, flip(): lax.ppermute(x, axis, [(i, i ^ bit) for i in range(lax.axis_size(axis))])  18.4 us
    pallas_call x1, Pallas kernels, cube_experts(): pl.pallas_call(functools.partial(expert_kernel, len(pieces), depth, exper...  13.9 us
    ppermute x4, waiting for transfers between devices, flip_both(): return lax.ppermute(x, ('ctx', 'exp'), [(i, i ^ mask) for i in range(size)])  11.2 us
    ppermute x4, starting transfers between devices, flip_both(): return lax.ppermute(x, ('ctx', 'exp'), [(i, i ^ mask) for i in range(size)])  4.92 us
    pallas_call x1, Pallas kernels, own_block(): pl.pallas_call(functools.partial(own_block_kernel, (n_exp, n_tp, heads, p...  3.09 us
    pallas_call x1, Pallas kernels, attend_project(): pl.pallas_call(functools.partial(attention_kernel, (n_ctx, n_exp, n_tp, h...  2.75 us
  transfers between devices with their start and end apart: 30, of which 19 were waited for; matrix products, arithmetic and copies ran while one was open for 1% of the time, Pallas kernels for 4%

profile of v12, /device:TPU:0, one launch (start us, length us, event | category | flops | bytes accessed | tf_op | source)
XLA Modules:
  0.0 77.2 jit_solution(5958274655547260306)
XLA Ops:
  0.0 0.8 %constant_dynamic-slice_fusion = (bf16[128,128]{1,0:T(8,128)(2,1)S(1)}, bf16[128,128]{1,0:T(8,128)(2,1)S(1)}) fusion(bf16[128,512]{1,0:T(8,128)(2,1)} %param.12, s32[]{:T(128)S(6)} %select_n.13, bf16[128,512]{1,0:T(8,128)(2,1)} %param.11), kind=kLoop, calls=%fused_computation.15 | loop fusion | bytes 131076 | tf_op jit(solution)/shard_map/dynamic_slice | solution.py:574
  0.8 5.1 %collective-permute-start.2 = (bf16[128,256]{1,0:T(8,128)(2,1)S(1)}, bf16[128,256]{1,0:T(8,128)(2,1)S(1)}, u32[]{:S(2)}, u32[]{:S(2)}) collective-permute-start(bf16[128,256]{1,0:T(8,128)(2,1)S(1)} %pad_maximum_fusion.1.kv_ref), channel_id=1, source_target_pairs={{0,12},{4,8},{8,4},{12,0},{1,13},{5,9},{9,5},{13,1},{2,14},{6,10},... | collective-permute-start | bytes 196616 | tf_op jit(solution)/shard_map/ppermute | solution.py:170
  5.9 0.6 collective-permute-start
  6.6 3.1 %own_block.1 = (bf16[1024,128]{1,0:T(8,128)(2,1)S(1)}, bf16[1024,2048]{1,0:T(8,128)(2,1)S(1)}, bf16[32,2048]{1,0:T(8,128)(2,1)S(1)}, f32[1024,128]{1,0:T(8,128)S...) custom-call(s32[3]{0:T(128)S(1)} %pad_add_fusion.place, ...), custom_call_target="tpu_custom_call" | custom-call | flops 100663296 | bytes 4980736 | tf_op jit(solution)/shard_map/own_block/pallas_call | solution.py:267
  9.7 1.8 %collective-permute-done.1.refs_1_ = bf16[128,256]{1,0:T(8,128)(2,1)S(1)} collective-permute-done((bf16[128,256]{1,0:T(8,128)(2,1)S(1)}, bf16[128,256]{1,0:T(8,128)(2,1)S(1)}, u32[]{:S(2)}, u32[]{:S(2)}) %collective-permute-start.1) | collective-permute-done | bytes 65568 | tf_op jit(solution)/shard_map/ppermute | solution.py:170
  11.5 2.7 %attend_project.1 = (f32[32,2048]{1,0:T(8,128)S(1)}, bf16[32,2048]{1,0:T(8,128)(2,1)S(1)}, bf16[64,2048]{1,0:T(8,128)(2,1)S(1)}) custom-call(s32[3]{0:T(128)S(1)} %pad_add_fusion.place, bf16[128,256]{1,0:T(8,128)(2,1)S(1)} %collective-permute-done.refs_0_, bf16[128,256]{1,0:T(8,128)(2,1)S(1)} %collective-permute-done.1.refs_1_, ...), custom_call_target="tpu_custom_call" | custom-call | flops 838860800 | bytes 4980736 | tf_op jit(solution)/shard_map/attend_project/pallas_call | solution.py:351
  14.3 1.5 %collective-permute-done.3 = bf16[64,2048]{1,0:T(8,128)(2,1)S(1)} collective-permute-done((bf16[64,2048]{1,0:T(8,128)(2,1)S(1)}, bf16[64,2048]{1,0:T(8,128)(2,1)S(1)}, u32[]{:S(2)}, u32[]{:S(2)}) %collective-permute-start.3) | collective-permute-done | bytes 262176 | tf_op jit(solution)/shard_map/ppermute | solution.py:170
  16.0 1.6 %collective-permute-start.4 = (bf16[32,2048]{1,0:T(8,128)(2,1)S(1)}, bf16[32,2048]{1,0:T(8,128)(2,1)S(1)}, u32[]{:S(2)}, u32[]{:S(2)}) collective-permute-start(bf16[32,2048]{1,0:T(8,128)(2,1)S(1)} %fusion), channel_id=1, source_target_pairs={{0,2},{2,0},{1,3},{3,1},{4,6},{6,4},{5,7},{7,5},{8,10},{10,8},{9,1... | collective-permute-start | bytes 393224 | tf_op jit(solution)/shard_map/ppermute | solution.py:170
  17.5 4.0 %collective-permute-done.4 = bf16[32,2048]{1,0:T(8,128)(2,1)S(1)} collective-permute-done((bf16[32,2048]{1,0:T(8,128)(2,1)S(1)}, bf16[32,2048]{1,0:T(8,128)(2,1)S(1)}, u32[]{:S(2)}, u32[]{:S(2)}) %collective-permute-start.4) | collective-permute-done | bytes 131104 | tf_op jit(solution)/shard_map/ppermute | solution.py:170
  21.6 0.2 multiply_reduce_fusion
  21.8 1.7 %collective-permute-start.6 = (bf16[32,2176]{1,0:T(8,128)(2,1)S(1)}, bf16[32,2176]{1,0:T(8,128)(2,1)S(1)}, u32[]{:S(2)}, u32[]{:S(2)}) collective-permute-start(bf16[32,2176]{1,0:T(8,128)(2,1)S(1)} %pad_maximum_fusion.refs_0_), channel_id=1, source_target_pairs={{0,8},{4,12},{8,0},{12,4},{1,9},{5,13},{9,1},{13,5},{2,10},{6,14},... | collective-permute-start | bytes 417800 | tf_op jit(solution)/shard_map/ppermute | solution.py:170
  23.5 2.6 %collective-permute-start.9 = (bf16[32,2176]{1,0:T(8,128)(2,1)S(1)}, bf16[32,2176]{1,0:T(8,128)(2,1)S(1)}, u32[]{:S(2)}, u32[]{:S(2)}) collective-permute-start(bf16[32,2176]{1,0:T(8,128)(2,1)S(1)} %pad_maximum_fusion.refs_0_), channel_id=1, source_target_pairs={{0,6},{2,4},{4,2},{6,0},{8,14},{10,12},{12,10},{14,8},{1,7},{3,5},... | collective-permute-start | bytes 417800 | tf_op jit(solution)/shard_map/ppermute | solution.py:177
  26.1 0.5 collective-permute-start.8
  26.7 0.3 collective-permute-start.5
  27.0 3.7 %collective-permute-done.6.refs_2_ = bf16[32,2176]{1,0:T(8,128)(2,1)S(1)} collective-permute-done((bf16[32,2176]{1,0:T(8,128)(2,1)S(1)}, bf16[32,2176]{1,0:T(8,128)(2,1)S(1)}, u32[]{:S(2)}, u32[]{:S(2)}) %collective-permute-start.6) | collective-permute-done | bytes 139296 | tf_op jit(solution)/shard_map/ppermute | solution.py:170
  30.7 0.8 collective-permute-start.11
  31.4 0.8 %collective-permute-start.10 = (bf16[32,2176]{1,0:T(8,128)(2,1)S(1)}, bf16[32,2176]{1,0:T(8,128)(2,1)S(1)}, u32[]{:S(2)}, u32[]{:S(2)}) collective-permute-start(bf16[32,2176]{1,0:T(8,128)(2,1)S(1)} %collective-permute-done.6.refs_2_), channel_id=1, source_target_pairs={{0,2},{2,0},{1,3},{3,1},{4,6},{6,4},{5,7},{7,5},{8,10},{10,8},{9,1... | collective-permute-start | bytes 417800 | tf_op jit(solution)/shard_map/ppermute | solution.py:170
  32.3 0.5 collective-permute-done.9.refs_5_
  32.8 1.4 %collective-permute-start.7 = (bf16[32,2176]{1,0:T(8,128)(2,1)S(1)}, bf16[32,2176]{1,0:T(8,128)(2,1)S(1)}, u32[]{:S(2)}, u32[]{:S(2)}) collective-permute-start(bf16[32,2176]{1,0:T(8,128)(2,1)S(1)} %collective-permute-done.6.refs_2_), channel_id=1, source_target_pairs={{0,4},{4,0},{8,12},{12,8},{1,5},{5,1},{9,13},{13,9},{2,6},{6,2},{1... | collective-permute-start | bytes 417800 | tf_op jit(solution)/shard_map/ppermute | solution.py:170
  34.2 0.9 %collective-permute-done.5.refs_1_ = bf16[32,2176]{1,0:T(8,128)(2,1)S(1)} collective-permute-done((bf16[32,2176]{1,0:T(8,128)(2,1)S(1)}, bf16[32,2176]{1,0:T(8,128)(2,1)S(1)}, u32[]{:S(2)}, u32[]{:S(2)}) %collective-permute-start.5) | collective-permute-done | bytes 139296 | tf_op jit(solution)/shard_map/ppermute | solution.py:170
  35.0 0.5 collective-permute-start.13
  35.6 3.1 %collective-permute-done.11.refs_7_ = bf16[32,2176]{1,0:T(8,128)(2,1)S(1)} collective-permute-done((bf16[32,2176]{1,0:T(8,128)(2,1)S(1)}, bf16[32,2176]{1,0:T(8,128)(2,1)S(1)}, u32[]{:S(2)}, u32[]{:S(2)}) %collective-permute-start.11) | collective-permute-done | bytes 139296 | tf_op jit(solution)/shard_map/ppermute | solution.py:177
  38.6 0.7 collective-permute-done.10.refs_6_
  39.4 1.0 %collective-permute-done.7.refs_3_ = bf16[32,2176]{1,0:T(8,128)(2,1)S(1)} collective-permute-done((bf16[32,2176]{1,0:T(8,128)(2,1)S(1)}, bf16[32,2176]{1,0:T(8,128)(2,1)S(1)}, u32[]{:S(2)}, u32[]{:S(2)}) %collective-permute-start.7) | collective-permute-done | bytes 139296 | tf_op jit(solution)/shard_map/ppermute | solution.py:170
  40.4 0.5 collective-permute-start.15
  41.0 0.4 collective-permute-start.19
  41.4 0.3 collective-permute-done.17.refs_13_
  41.8 0.2 collective-permute-done.15.refs_11_
  42.0 0.3 collective-permute-done.18.refs_14_
  42.3 0.2 collective-permute-done.19.refs_15_
  42.5 13.9 %experts.1 = (bf16[64,2048]{1,0:T(8,128)(2,1)S(1)}, bf16[64,2048]{1,0:T(8,128)(2,1)S(1)}, bf16[128,2048]{1,0:T(8,128)(2,1)S(1)}, bf16[64,2048]{1,0:T(8,128)(2,1)...) custom-call(s32[1]{0:T(128)} %bitcast.5.first_ref, bf16[32,2176]{1,0:T(8,128)(2,1)S(1)} %pad_maximum_fusion.refs_0_, ...), custom_call_target="tpu_custom_call" | custom-call | flops 3489660928 | bytes 39845888 | tf_op jit(solution)/shard_map/experts/pallas_call | solution.py:497
  56.4 0.4 collective-permute-start.22
  56.8 0.2 collective-permute-start.20
  57.0 0.3 collective-permute-start.21
  57.3 0.7 collective-permute-done.22
  58.1 1.0 %collective-permute-start.23 = (bf16[32,2048]{1,0:T(8,128)(2,1)S(1)}, bf16[32,2048]{1,0:T(8,128)(2,1)S(1)}, u32[]{:S(2)}, u32[]{:S(2)}) collective-permute-start(bf16[32,2048]{1,0:T(8,128)(2,1)S(1)} %get-tuple-element.62), channel_id=1, source_target_pairs={{0,6},{2,4},{4,2},{6,0},{8,14},{10,12},{12,10},{14,8},{1,7},{3,5},... | collective-permute-start | bytes 393224 | tf_op jit(solution)/shard_map/ppermute | solution.py:177
  59.0 1.2 %collective-permute-start.24 = (bf16[32,2048]{1,0:T(8,128)(2,1)S(1)}, bf16[32,2048]{1,0:T(8,128)(2,1)S(1)}, u32[]{:S(2)}, u32[]{:S(2)}) collective-permute-start(bf16[32,2048]{1,0:T(8,128)(2,1)S(1)} %get-tuple-element.63), channel_id=1, source_target_pairs={{0,2},{2,0},{1,3},{3,1},{4,6},{6,4},{5,7},{7,5},{8,10},{10,8},{9,1... | collective-permute-start | bytes 393224 | tf_op jit(solution)/shard_map/ppermute | solution.py:170
  60.4 1.5 %collective-permute-start.25 = (bf16[32,2048]{1,0:T(8,128)(2,1)S(1)}, bf16[32,2048]{1,0:T(8,128)(2,1)S(1)}, u32[]{:S(2)}, u32[]{:S(2)}) collective-permute-start(bf16[32,2048]{1,0:T(8,128)(2,1)S(1)} %slice.36), channel_id=1, source_target_pairs={{0,4},{4,0},{8,12},{12,8},{1,5},{5,1},{9,13},{13,9},{2,6},{6,2},{1... | collective-permute-start | bytes 393224 | tf_op jit(solution)/shard_map/ppermute | solution.py:170
  62.0 0.7 collective-permute-start.27
  62.6 0.9 %collective-permute-start.29 = (bf16[32,2048]{1,0:T(8,128)(2,1)S(1)}, bf16[32,2048]{1,0:T(8,128)(2,1)S(1)}, u32[]{:S(2)}, u32[]{:S(2)}) collective-permute-start(bf16[32,2048]{1,0:T(8,128)(2,1)S(1)} %get-tuple-element.60), channel_id=1, source_target_pairs={{0,2},{2,0},{1,3},{3,1},{4,6},{6,4},{5,7},{7,5},{8,10},{10,8},{9,1... | collective-permute-start | bytes 393224 | tf_op jit(solution)/shard_map/ppermute | solution.py:170
  63.5 1.9 %collective-permute-done.23 = bf16[32,2048]{1,0:T(8,128)(2,1)S(1)} collective-permute-done((bf16[32,2048]{1,0:T(8,128)(2,1)S(1)}, bf16[32,2048]{1,0:T(8,128)(2,1)S(1)}, u32[]{:S(2)}, u32[]{:S(2)}) %collective-permute-start.23) | collective-permute-done | bytes 131104 | tf_op jit(solution)/shard_map/ppermute | solution.py:177
  65.4 0.6 collective-permute-start.28
  66.0 1.7 %collective-permute-done.24 = bf16[32,2048]{1,0:T(8,128)(2,1)S(1)} collective-permute-done((bf16[32,2048]{1,0:T(8,128)(2,1)S(1)}, bf16[32,2048]{1,0:T(8,128)(2,1)S(1)}, u32[]{:S(2)}, u32[]{:S(2)}) %collective-permute-start.24) | collective-permute-done | bytes 131104 | tf_op jit(solution)/shard_map/ppermute | solution.py:170
  67.7 1.7 %collective-permute-start.26 = (bf16[32,2048]{1,0:T(8,128)(2,1)S(1)}, bf16[32,2048]{1,0:T(8,128)(2,1)S(1)}, u32[]{:S(2)}, u32[]{:S(2)}) collective-permute-start(bf16[32,2048]{1,0:T(8,128)(2,1)S(1)} %add_convert_fusion.4), channel_id=1, source_target_pairs={{0,8},{4,12},{8,0},{12,4},{1,9},{5,13},{9,1},{13,5},{2,10},{6,14},... | collective-permute-start | bytes 393224 | tf_op jit(solution)/shard_map/ppermute | solution.py:170
  69.5 0.9 %collective-permute-done.27 = bf16[32,2048]{1,0:T(8,128)(2,1)S(1)} collective-permute-done((bf16[32,2048]{1,0:T(8,128)(2,1)S(1)}, bf16[32,2048]{1,0:T(8,128)(2,1)S(1)}, u32[]{:S(2)}, u32[]{:S(2)}) %collective-permute-start.27) | collective-permute-done | bytes 131104 | tf_op jit(solution)/shard_map/ppermute | solution.py:170
  70.4 5.6 %collective-permute-done.28 = bf16[32,2048]{1,0:T(8,128)(2,1)S(1)} collective-permute-done((bf16[32,2048]{1,0:T(8,128)(2,1)S(1)}, bf16[32,2048]{1,0:T(8,128)(2,1)S(1)}, u32[]{:S(2)}, u32[]{:S(2)}) %collective-permute-start.28) | collective-permute-done | bytes 131104 | tf_op jit(solution)/shard_map/ppermute | solution.py:177
  76.0 0.4 collective-permute-done.26
  76.4 0.8 add_convert_fusion.3
  (32 shorter events, 0.8 us)
Async XLA Ops:
  0.8 8.9 %collective-permute-start.2 = (bf16[128,256]{1,0:T(8,128)(2,1)S(1)}, bf16[128,256]{1,0:T(8,128)(2,1)S(1)}, u32[]{:S(2)}, u32[]{:S(2)}) collective-permute-start(bf16[128,256]{1,0:T(8,128)(2,1)S(1)} %pad_maximum_fusion.1.kv_ref), channel_id=1, source_target_pairs={{0,12},{4,8},{8,4},{12,0},{1,13},{5,9},{9,5},{13,1},{2,14},{6,10},... | collective-permute-start | bytes 196616 | tf_op jit(solution)/shard_map/ppermute | solution.py:170
  5.9 5.6 %collective-permute-start.1 = (bf16[128,256]{1,0:T(8,128)(2,1)S(1)}, bf16[128,256]{1,0:T(8,128)(2,1)S(1)}, u32[]{:S(2)}, u32[]{:S(2)}) collective-permute-start(bf16[128,256]{1,0:T(8,128)(2,1)S(1)} %pad_maximum_fusion.1.kv_ref), channel_id=1, source_target_pairs={{0,8},{4,12},{8,0},{12,4},{1,9},{5,13},{9,1},{13,5},{2,10},{6,14},... | collective-permute-start | bytes 196616 | tf_op jit(solution)/shard_map/ppermute | solution.py:170
  5.9 5.6 %collective-permute-start = (bf16[128,256]{1,0:T(8,128)(2,1)S(1)}, bf16[128,256]{1,0:T(8,128)(2,1)S(1)}, u32[]{:S(2)}, u32[]{:S(2)}) collective-permute-start(bf16[128,256]{1,0:T(8,128)(2,1)S(1)} %pad_maximum_fusion.1.kv_ref), channel_id=1, source_target_pairs={{0,4},{4,0},{8,12},{12,8},{1,5},{5,1},{9,13},{13,9},{2,6},{6,2},{1... | collective-permute-start | bytes 196616 | tf_op jit(solution)/shard_map/ppermute | solution.py:170
  14.3 1.6 %collective-permute-start.3 = (bf16[64,2048]{1,0:T(8,128)(2,1)S(1)}, bf16[64,2048]{1,0:T(8,128)(2,1)S(1)}, u32[]{:S(2)}, u32[]{:S(2)}) collective-permute-start(bf16[64,2048]{1,0:T(8,128)(2,1)S(1)} %get-tuple-element.38), channel_id=1, source_target_pairs={{0,1},{1,0},{2,3},{3,2},{4,5},{5,4},{6,7},{7,6},{8,9},{9,8},{10,11... | collective-permute-start | bytes 786440 | tf_op jit(solution)/shard_map/ppermute | solution.py:170
  16.0 5.6 %collective-permute-start.4 = (bf16[32,2048]{1,0:T(8,128)(2,1)S(1)}, bf16[32,2048]{1,0:T(8,128)(2,1)S(1)}, u32[]{:S(2)}, u32[]{:S(2)}) collective-permute-start(bf16[32,2048]{1,0:T(8,128)(2,1)S(1)} %fusion), channel_id=1, source_target_pairs={{0,2},{2,0},{1,3},{3,1},{4,6},{6,4},{5,7},{7,5},{8,10},{10,8},{9,1... | collective-permute-start | bytes 393224 | tf_op jit(solution)/shard_map/ppermute | solution.py:170
  21.8 8.8 %collective-permute-start.6 = (bf16[32,2176]{1,0:T(8,128)(2,1)S(1)}, bf16[32,2176]{1,0:T(8,128)(2,1)S(1)}, u32[]{:S(2)}, u32[]{:S(2)}) collective-permute-start(bf16[32,2176]{1,0:T(8,128)(2,1)S(1)} %pad_maximum_fusion.refs_0_), channel_id=1, source_target_pairs={{0,8},{4,12},{8,0},{12,4},{1,9},{5,13},{9,1},{13,5},{2,10},{6,14},... | collective-permute-start | bytes 417800 | tf_op jit(solution)/shard_map/ppermute | solution.py:170
  23.5 9.3 %collective-permute-start.9 = (bf16[32,2176]{1,0:T(8,128)(2,1)S(1)}, bf16[32,2176]{1,0:T(8,128)(2,1)S(1)}, u32[]{:S(2)}, u32[]{:S(2)}) collective-permute-start(bf16[32,2176]{1,0:T(8,128)(2,1)S(1)} %pad_maximum_fusion.refs_0_), channel_id=1, source_target_pairs={{0,6},{2,4},{4,2},{6,0},{8,14},{10,12},{12,10},{14,8},{1,7},{3,5},... | collective-permute-start | bytes 417800 | tf_op jit(solution)/shard_map/ppermute | solution.py:177
  26.1 8.1 %collective-permute-start.8 = (bf16[32,2176]{1,0:T(8,128)(2,1)S(1)}, bf16[32,2176]{1,0:T(8,128)(2,1)S(1)}, u32[]{:S(2)}, u32[]{:S(2)}) collective-permute-start(bf16[32,2176]{1,0:T(8,128)(2,1)S(1)} %pad_maximum_fusion.refs_0_), channel_id=1, source_target_pairs={{0,2},{2,0},{1,3},{3,1},{4,6},{6,4},{5,7},{7,5},{8,10},{10,8},{9,1... | collective-permute-start | bytes 417800 | tf_op jit(solution)/shard_map/ppermute | solution.py:170
  26.7 8.4 %collective-permute-start.5 = (bf16[32,2176]{1,0:T(8,128)(2,1)S(1)}, bf16[32,2176]{1,0:T(8,128)(2,1)S(1)}, u32[]{:S(2)}, u32[]{:S(2)}) collective-permute-start(bf16[32,2176]{1,0:T(8,128)(2,1)S(1)} %pad_maximum_fusion.refs_0_), channel_id=1, source_target_pairs={{0,4},{4,0},{8,12},{12,8},{1,5},{5,1},{9,13},{13,9},{2,6},{6,2},{1... | collective-permute-start | bytes 417800 | tf_op jit(solution)/shard_map/ppermute | solution.py:170
  30.7 8.0 %collective-permute-start.11 = (bf16[32,2176]{1,0:T(8,128)(2,1)S(1)}, bf16[32,2176]{1,0:T(8,128)(2,1)S(1)}, u32[]{:S(2)}, u32[]{:S(2)}) collective-permute-start(bf16[32,2176]{1,0:T(8,128)(2,1)S(1)} %collective-permute-done.6.refs_2_), channel_id=1, source_target_pairs={{0,6},{2,4},{4,2},{6,0},{8,14},{10,12},{12,10},{14,8},{1,7},{3,5},... | collective-permute-start | bytes 417800 | tf_op jit(solution)/shard_map/ppermute | solution.py:177
  31.4 7.9 %collective-permute-start.10 = (bf16[32,2176]{1,0:T(8,128)(2,1)S(1)}, bf16[32,2176]{1,0:T(8,128)(2,1)S(1)}, u32[]{:S(2)}, u32[]{:S(2)}) collective-permute-start(bf16[32,2176]{1,0:T(8,128)(2,1)S(1)} %collective-permute-done.6.refs_2_), channel_id=1, source_target_pairs={{0,2},{2,0},{1,3},{3,1},{4,6},{6,4},{5,7},{7,5},{8,10},{10,8},{9,1... | collective-permute-start | bytes 417800 | tf_op jit(solution)/shard_map/ppermute | solution.py:170
  32.8 7.6 %collective-permute-start.7 = (bf16[32,2176]{1,0:T(8,128)(2,1)S(1)}, bf16[32,2176]{1,0:T(8,128)(2,1)S(1)}, u32[]{:S(2)}, u32[]{:S(2)}) collective-permute-start(bf16[32,2176]{1,0:T(8,128)(2,1)S(1)} %collective-permute-done.6.refs_2_), channel_id=1, source_target_pairs={{0,4},{4,0},{8,12},{12,8},{1,5},{5,1},{9,13},{13,9},{2,6},{6,2},{1... | collective-permute-start | bytes 417800 | tf_op jit(solution)/shard_map/ppermute | solution.py:170
  35.0 5.4 %collective-permute-start.12 = (bf16[32,2176]{1,0:T(8,128)(2,1)S(1)}, bf16[32,2176]{1,0:T(8,128)(2,1)S(1)}, u32[]{:S(2)}, u32[]{:S(2)}) collective-permute-start(bf16[32,2176]{1,0:T(8,128)(2,1)S(1)} %pad_maximum_fusion.refs_0_), channel_id=1, source_target_pairs={{0,1},{1,0},{2,3},{3,2},{4,5},{5,4},{6,7},{7,6},{8,9},{9,8},{10,11... | collective-permute-start | bytes 417800 | tf_op jit(solution)/shard_map/ppermute | solution.py:170
  35.0 5.9 %collective-permute-start.13 = (bf16[32,2176]{1,0:T(8,128)(2,1)S(1)}, bf16[32,2176]{1,0:T(8,128)(2,1)S(1)}, u32[]{:S(2)}, u32[]{:S(2)}) collective-permute-start(bf16[32,2176]{1,0:T(8,128)(2,1)S(1)} %collective-permute-done.5.refs_1_), channel_id=1, source_target_pairs={{0,1},{1,0},{2,3},{3,2},{4,5},{5,4},{6,7},{7,6},{8,9},{9,8},{10,11... | collective-permute-start | bytes 417800 | tf_op jit(solution)/shard_map/ppermute | solution.py:170
  38.6 2.4 %collective-permute-start.14 = (bf16[32,2176]{1,0:T(8,128)(2,1)S(1)}, bf16[32,2176]{1,0:T(8,128)(2,1)S(1)}, u32[]{:S(2)}, u32[]{:S(2)}) collective-permute-start(bf16[32,2176]{1,0:T(8,128)(2,1)S(1)} %collective-permute-done.6.refs_2_), channel_id=1, source_target_pairs={{0,1},{1,0},{2,3},{3,2},{4,5},{5,4},{6,7},{7,6},{8,9},{9,8},{10,11... | collective-permute-start | bytes 417800 | tf_op jit(solution)/shard_map/ppermute | solution.py:170
  39.4 2.1 %collective-permute-start.16 = (bf16[32,2176]{1,0:T(8,128)(2,1)S(1)}, bf16[32,2176]{1,0:T(8,128)(2,1)S(1)}, u32[]{:S(2)}, u32[]{:S(2)}) collective-permute-start(bf16[32,2176]{1,0:T(8,128)(2,1)S(1)} %collective-permute-done.8.refs_4_), channel_id=1, source_target_pairs={{0,1},{1,0},{2,3},{3,2},{4,5},{5,4},{6,7},{7,6},{8,9},{9,8},{10,11... | collective-permute-start | bytes 417800 | tf_op jit(solution)/shard_map/ppermute | solution.py:170
  40.4 1.4 %collective-permute-start.17 = (bf16[32,2176]{1,0:T(8,128)(2,1)S(1)}, bf16[32,2176]{1,0:T(8,128)(2,1)S(1)}, u32[]{:S(2)}, u32[]{:S(2)}) collective-permute-start(bf16[32,2176]{1,0:T(8,128)(2,1)S(1)} %collective-permute-done.9.refs_5_), channel_id=1, source_target_pairs={{0,1},{1,0},{2,3},{3,2},{4,5},{5,4},{6,7},{7,6},{8,9},{9,8},{10,11... | collective-permute-start | bytes 417800 | tf_op jit(solution)/shard_map/ppermute | solution.py:170
  40.4 1.6 %collective-permute-start.15 = (bf16[32,2176]{1,0:T(8,128)(2,1)S(1)}, bf16[32,2176]{1,0:T(8,128)(2,1)S(1)}, u32[]{:S(2)}, u32[]{:S(2)}) collective-permute-start(bf16[32,2176]{1,0:T(8,128)(2,1)S(1)} %collective-permute-done.7.refs_3_), channel_id=1, source_target_pairs={{0,1},{1,0},{2,3},{3,2},{4,5},{5,4},{6,7},{7,6},{8,9},{9,8},{10,11... | collective-permute-start | bytes 417800 | tf_op jit(solution)/shard_map/ppermute | solution.py:170
  40.9 1.4 %collective-permute-start.18 = (bf16[32,2176]{1,0:T(8,128)(2,1)S(1)}, bf16[32,2176]{1,0:T(8,128)(2,1)S(1)}, u32[]{:S(2)}, u32[]{:S(2)}) collective-permute-start(bf16[32,2176]{1,0:T(8,128)(2,1)S(1)} %collective-permute-done.10.refs_6_), channel_id=1, source_target_pairs={{0,1},{1,0},{2,3},{3,2},{4,5},{5,4},{6,7},{7,6},{8,9},{9,8},{10,11... | collective-permute-start | bytes 417800 | tf_op jit(solution)/shard_map/ppermute | solution.py:170
  41.0 1.5 %collective-permute-start.19 = (bf16[32,2176]{1,0:T(8,128)(2,1)S(1)}, bf16[32,2176]{1,0:T(8,128)(2,1)S(1)}, u32[]{:S(2)}, u32[]{:S(2)}) collective-permute-start(bf16[32,2176]{1,0:T(8,128)(2,1)S(1)} %collective-permute-done.11.refs_7_), channel_id=1, source_target_pairs={{0,1},{1,0},{2,3},{3,2},{4,5},{5,4},{6,7},{7,6},{8,9},{9,8},{10,11... | collective-permute-start | bytes 417800 | tf_op jit(solution)/shard_map/ppermute | solution.py:170
  56.4 1.6 %collective-permute-start.22 = (bf16[64,2048]{1,0:T(8,128)(2,1)S(1)}, bf16[64,2048]{1,0:T(8,128)(2,1)S(1)}, u32[]{:S(2)}, u32[]{:S(2)}) collective-permute-start(bf16[64,2048]{1,0:T(8,128)(2,1)S(1)} %get-tuple-element.56), channel_id=1, source_target_pairs={{0,1},{1,0},{2,3},{3,2},{4,5},{5,4},{6,7},{7,6},{8,9},{9,8},{10,11... | collective-permute-start | bytes 786440 | tf_op jit(solution)/shard_map/ppermute | solution.py:170
  56.8 3.4 %collective-permute-start.20 = (bf16[64,2048]{1,0:T(8,128)(2,1)S(1)}, bf16[64,2048]{1,0:T(8,128)(2,1)S(1)}, u32[]{:S(2)}, u32[]{:S(2)}) collective-permute-start(bf16[64,2048]{1,0:T(8,128)(2,1)S(1)} %get-tuple-element.50), channel_id=1, source_target_pairs={{0,1},{1,0},{2,3},{3,2},{4,5},{5,4},{6,7},{7,6},{8,9},{9,8},{10,11... | collective-permute-start | bytes 786440 | tf_op jit(solution)/shard_map/ppermute | solution.py:170
  57.0 3.3 %collective-permute-start.21 = (bf16[128,2048]{1,0:T(8,128)(2,1)S(1)}, bf16[128,2048]{1,0:T(8,128)(2,1)S(1)}, u32[]{:S(2)}, u32[]{:S(2)}) collective-permute-start(bf16[128,2048]{1,0:T(8,128)(2,1)S(1)} %get-tuple-element.52), channel_id=1, source_target_pairs={{0,1},{1,0},{2,3},{3,2},{4,5},{5,4},{6,7},{7,6},{8,9},{9,8},{10,11... | collective-permute-start | bytes 1572872 | tf_op jit(solution)/shard_map/ppermute | solution.py:170
  58.1 7.3 %collective-permute-start.23 = (bf16[32,2048]{1,0:T(8,128)(2,1)S(1)}, bf16[32,2048]{1,0:T(8,128)(2,1)S(1)}, u32[]{:S(2)}, u32[]{:S(2)}) collective-permute-start(bf16[32,2048]{1,0:T(8,128)(2,1)S(1)} %get-tuple-element.62), channel_id=1, source_target_pairs={{0,6},{2,4},{4,2},{6,0},{8,14},{10,12},{12,10},{14,8},{1,7},{3,5},... | collective-permute-start | bytes 393224 | tf_op jit(solution)/shard_map/ppermute | solution.py:177
  59.0 8.6 %collective-permute-start.24 = (bf16[32,2048]{1,0:T(8,128)(2,1)S(1)}, bf16[32,2048]{1,0:T(8,128)(2,1)S(1)}, u32[]{:S(2)}, u32[]{:S(2)}) collective-permute-start(bf16[32,2048]{1,0:T(8,128)(2,1)S(1)} %get-tuple-element.63), channel_id=1, source_target_pairs={{0,2},{2,0},{1,3},{3,1},{4,6},{6,4},{5,7},{7,5},{8,10},{10,8},{9,1... | collective-permute-start | bytes 393224 | tf_op jit(solution)/shard_map/ppermute | solution.py:170
  60.4 7.2 %collective-permute-start.25 = (bf16[32,2048]{1,0:T(8,128)(2,1)S(1)}, bf16[32,2048]{1,0:T(8,128)(2,1)S(1)}, u32[]{:S(2)}, u32[]{:S(2)}) collective-permute-start(bf16[32,2048]{1,0:T(8,128)(2,1)S(1)} %slice.36), channel_id=1, source_target_pairs={{0,4},{4,0},{8,12},{12,8},{1,5},{5,1},{9,13},{13,9},{2,6},{6,2},{1... | collective-permute-start | bytes 393224 | tf_op jit(solution)/shard_map/ppermute | solution.py:170
  62.0 8.4 %collective-permute-start.27 = (bf16[32,2048]{1,0:T(8,128)(2,1)S(1)}, bf16[32,2048]{1,0:T(8,128)(2,1)S(1)}, u32[]{:S(2)}, u32[]{:S(2)}) collective-permute-start(bf16[32,2048]{1,0:T(8,128)(2,1)S(1)} %get-tuple-element.59), channel_id=1, source_target_pairs={{0,4},{4,0},{8,12},{12,8},{1,5},{5,1},{9,13},{13,9},{2,6},{6,2},{1... | collective-permute-start | bytes 393224 | tf_op jit(solution)/shard_map/ppermute | solution.py:170
  62.6 7.8 %collective-permute-start.29 = (bf16[32,2048]{1,0:T(8,128)(2,1)S(1)}, bf16[32,2048]{1,0:T(8,128)(2,1)S(1)}, u32[]{:S(2)}, u32[]{:S(2)}) collective-permute-start(bf16[32,2048]{1,0:T(8,128)(2,1)S(1)} %get-tuple-element.60), channel_id=1, source_target_pairs={{0,2},{2,0},{1,3},{3,1},{4,6},{6,4},{5,7},{7,5},{8,10},{10,8},{9,1... | collective-permute-start | bytes 393224 | tf_op jit(solution)/shard_map/ppermute | solution.py:170
  65.4 10.6 %collective-permute-start.28 = (bf16[32,2048]{1,0:T(8,128)(2,1)S(1)}, bf16[32,2048]{1,0:T(8,128)(2,1)S(1)}, u32[]{:S(2)}, u32[]{:S(2)}) collective-permute-start(bf16[32,2048]{1,0:T(8,128)(2,1)S(1)} %get-tuple-element.61), channel_id=1, source_target_pairs={{0,6},{2,4},{4,2},{6,0},{8,14},{10,12},{12,10},{14,8},{1,7},{3,5},... | collective-permute-start | bytes 393224 | tf_op jit(solution)/shard_map/ppermute | solution.py:177
  67.7 8.7 %collective-permute-start.26 = (bf16[32,2048]{1,0:T(8,128)(2,1)S(1)}, bf16[32,2048]{1,0:T(8,128)(2,1)S(1)}, u32[]{:S(2)}, u32[]{:S(2)}) collective-permute-start(bf16[32,2048]{1,0:T(8,128)(2,1)S(1)} %add_convert_fusion.4), channel_id=1, source_target_pairs={{0,8},{4,12},{8,0},{12,4},{1,9},{5,13},{9,1},{13,5},{2,10},{6,14},... | collective-permute-start | bytes 393224 | tf_op jit(solution)/shard_map/ppermute | solution.py:170

commit v13 on v12

--- a/solution.py
+++ b/solution.py
@@ -304,8 +304,8 @@
     rows = n_exp * n_tp * part
     kv_refs, refs = refs[: n_ctx - 1], refs[n_ctx - 1 :]
     q_ref, w_ref, resid_ref, out_ref, sum_ref, max_ref = refs[:6]
-    base_ref, across_ref, other_ref = refs[6:9]
-    k_all, v_all, att, att_rel = refs[9:]
+    base_ref, across_ref, other_ref, other_across_ref = refs[6:10]
+    k_all, v_all, att, att_rel = refs[10:]
     ctx, exp, tp = place[0], place[1], place[2]
     for i, kv_ref in enumerate(kv_refs):
         at = slice(i * rows, (i + 1) * rows)
@@ -338,7 +338,8 @@
     projected = jnp.dot(att_rel[...], w_ref[...], preferred_element_type=F32)
     base_ref[...] = resid_ref[...].astype(F32) + projected[:part]
     across_ref[...] = projected[part : 2 * part].astype(BF)
-    other_ref[...] = projected[2 * part :].astype(BF)
+    other_ref[...] = projected[2 * part : 3 * part].astype(BF)
+    other_across_ref[...] = projected[3 * part :].astype(BF)
 
 
 def attend_project(place, pieces, own, n_exp, n_tp):
@@ -353,10 +354,11 @@
         out_shape=(
             jax.ShapeDtypeStruct((part, model), F32),
             jax.ShapeDtypeStruct((part, model), BF),
-            jax.ShapeDtypeStruct((2 * part, model), BF),
+            jax.ShapeDtypeStruct((part, model), BF),
+            jax.ShapeDtypeStruct((part, model), BF),
         ),
         in_specs=[pl.BlockSpec(memory_space=pltpu.SMEM)] + [vmem] * (n_ctx - 1 + len(own)),
-        out_specs=(vmem,) * 3,
+        out_specs=(vmem,) * 4,
         scratch_shapes=[
             pltpu.VMEM(((n_ctx - 1) * rows, HEAD_DIMENSION), BF),
             pltpu.VMEM(((n_ctx - 1) * rows, 2 * HEAD_DIMENSION), BF),
@@ -488,7 +490,7 @@
     halves, sides = 2, 2
     experts = rows // halves
     tokens = len(pieces) * pieces[0].shape[0] // sides
-    depth = 4
+    depth = 5
     vmem = pl.BlockSpec(memory_space=pltpu.VMEM)
     hbm = pl.BlockSpec(memory_space=pltpu.HBM)
 
@@ -577,11 +579,13 @@
     *own, routing = own_block(
         place, kv, expert_ids, router_probs, queries, out_weight, resid, n_exp, n_tp
     )
-    base, across, other = attend_project(place, kv_pieces, own, n_exp, n_tp)
-
-    other = flip(other, "tp", 1).astype(F32)
-    across = flip((across.astype(F32) + other[part:]).astype(BF), "exp", 1)
-    hidden = base + other[:part] + across.astype(F32)
+    base, across, other, other_across = attend_project(place, kv_pieces, own, n_exp, n_tp)
+
+    other_across = flip(other_across, "tp", 1).astype(F32)
+    across = (across.astype(F32) + other_across).astype(BF)
+    across = flip(across, "exp", 1)
+    other = flip(other, "tp", 1)
+    hidden = base + other.astype(F32) + across.astype(F32)
     mean_square = jnp.mean(hidden * hidden, axis=1, keepdims=True)
     normed = (hidden * lax.rsqrt(mean_square + 1e-06)).astype(BF)
     normed = jnp.concatenate([normed, routing], axis=1)
@@ -593,7 +597,7 @@
     far_across = flip(far, "exp", 1)
     last_across = flip_both(far)
     last = flip(far, "ctx", 1)
-    early = lax.optimization_barrier((normed, near, far, across, near_across))
+    early = (normed,) + lax.optimization_barrier((near, far, across, near_across))
     late = lax.optimization_barrier((far_across, last_across, last))
     pieces = [normed, near, far, last, across, near_across, far_across, last_across]
     pieces += [flip(piece, "tp", 1) for piece in early[:3] + late[2:] + early[3:] + late[:2]]

time: 77.4 us -> 77.2 us (level)
    ppermute x26 -> x27, waiting for transfers between devices: 18.4 us -> 17.8 us  [flip(): lax.ppermute(x, axis, [(i, i ^ bit) for i in range(lax.axis_size(axis))])]
    ppermute x26 -> x27, starting transfers between devices: 20.5 us -> 20.4 us  [flip(): lax.ppermute(x, axis, [(i, i ^ bit) for i in range(lax.axis_size(axis))])]
  transfers between devices with their start and end apart: 30 -> 31, of which waited for: 19 -> 19; matrix products, arithmetic and copies ran while one was open for 1% -> 1% of each run, Pallas kernels for 4% -> 4%
where the time goes in v13:
time: 77.2 us; the launch traced here: 77 us
  waiting for transfers between devices  29.5 us (38%)
  starting transfers between devices  25.3 us (33%)
  Pallas kernels  19.8 us (26%)
  other arithmetic  1.51 us (2%)
  local copies, waits for them, and re-layouts  0.84 us (1%)
    ppermute x27, starting transfers between devices, flip(): lax.ppermute(x, axis, [(i, i ^ bit) for i in range(lax.axis_size(axis))])  20.4 us
    ppermute x27, waiting for transfers between devices, flip(): lax.ppermute(x, axis, [(i, i ^ bit) for i in range(lax.axis_size(axis))])  17.8 us
    pallas_call x1, Pallas kernels, cube_experts(): pl.pallas_call(functools.partial(expert_kernel, len(pieces), depth, exper...  13.9 us
    ppermute x4, waiting for transfers between devices, flip_both(): return lax.ppermute(x, ('ctx', 'exp'), [(i, i ^ mask) for i in range(size)])  11.7 us
    ppermute x4, starting transfers between devices, flip_both(): return lax.ppermute(x, ('ctx', 'exp'), [(i, i ^ mask) for i in range(size)])  4.88 us
    pallas_call x1, Pallas kernels, own_block(): pl.pallas_call(functools.partial(own_block_kernel, (n_exp, n_tp, heads, p...  3.09 us
    pallas_call x1, Pallas kernels, attend_project(): pl.pallas_call(functools.partial(attention_kernel, (n_ctx, n_exp, n_tp, h...  2.75 us
  transfers between devices with their start and end apart: 31, of which 19 were waited for; matrix products, arithmetic and copies ran while one was open for 1% of the time, Pallas kernels for 4%

profile of v13, /device:TPU:0, one launch (start us, length us, event | category | flops | bytes accessed | tf_op | source)
XLA Modules:
  0.0 77.0 jit_solution(14392585161947826263)
XLA Ops:
  0.0 0.8 %constant_dynamic-slice_fusion = (bf16[128,128]{1,0:T(8,128)(2,1)S(1)}, bf16[128,128]{1,0:T(8,128)(2,1)S(1)}) fusion(bf16[128,512]{1,0:T(8,128)(2,1)} %param.12, s32[]{:T(128)S(6)} %select_n.13, bf16[128,512]{1,0:T(8,128)(2,1)} %param.11), kind=kLoop, calls=%fused_computation.13 | loop fusion | bytes 131076 | tf_op jit(solution)/shard_map/dynamic_slice | solution.py:576
  0.8 5.1 %collective-permute-start.2 = (bf16[128,256]{1,0:T(8,128)(2,1)S(1)}, bf16[128,256]{1,0:T(8,128)(2,1)S(1)}, u32[]{:S(2)}, u32[]{:S(2)}) collective-permute-start(bf16[128,256]{1,0:T(8,128)(2,1)S(1)} %pad_maximum_fusion.1.kv_ref), channel_id=1, source_target_pairs={{0,12},{4,8},{8,4},{12,0},{1,13},{5,9},{9,5},{13,1},{2,14},{6,10},... | collective-permute-start | bytes 196616 | tf_op jit(solution)/shard_map/ppermute | solution.py:170
  5.9 0.6 collective-permute-start
  6.6 3.1 %own_block.1 = (bf16[1024,128]{1,0:T(8,128)(2,1)S(1)}, bf16[1024,2048]{1,0:T(8,128)(2,1)S(1)}, bf16[32,2048]{1,0:T(8,128)(2,1)S(1)}, f32[1024,128]{1,0:T(8,128)S...) custom-call(s32[3]{0:T(128)S(1)} %pad_add_fusion.place, ...), custom_call_target="tpu_custom_call" | custom-call | flops 100663296 | bytes 4980736 | tf_op jit(solution)/shard_map/own_block/pallas_call | solution.py:267
  9.7 1.8 %collective-permute-done.1.refs_1_ = bf16[128,256]{1,0:T(8,128)(2,1)S(1)} collective-permute-done((bf16[128,256]{1,0:T(8,128)(2,1)S(1)}, bf16[128,256]{1,0:T(8,128)(2,1)S(1)}, u32[]{:S(2)}, u32[]{:S(2)}) %collective-permute-start.1) | collective-permute-done | bytes 65568 | tf_op jit(solution)/shard_map/ppermute | solution.py:170
  11.5 2.7 %attend_project.1 = (f32[32,2048]{1,0:T(8,128)S(1)}, bf16[32,2048]{1,0:T(8,128)(2,1)S(1)}, bf16[32,2048]{1,0:T(8,128)(2,1)S(1)}, bf16[32,2048]{1,0:T(8,128)(2,1)S(1)}) custom-call(s32[3]{0:T(128)S(1)} %pad_add_fusion.place, bf16[128,256]{1,0:T(8,128)(2,1)S(1)} %collective-permute-done.refs_0_, bf16[128,256]{1,0:T(8,128)(2,1)S(1)} %collective-permute-done.1.refs_1_, ...), custom_call_target="tpu_custom_call" | custom-call | flops 838860800 | bytes 4980736 | tf_op jit(solution)/shard_map/attend_project/pallas_call | solution.py:352
  14.3 0.5 collective-permute-start.3
  14.8 0.8 %collective-permute-done.4 = bf16[32,2048]{1,0:T(8,128)(2,1)S(1)} collective-permute-done((bf16[32,2048]{1,0:T(8,128)(2,1)S(1)}, bf16[32,2048]{1,0:T(8,128)(2,1)S(1)}, u32[]{:S(2)}, u32[]{:S(2)}) %collective-permute-start.4) | collective-permute-done | bytes 131104 | tf_op jit(solution)/shard_map/ppermute | solution.py:170
  15.7 1.6 %collective-permute-start.5 = (bf16[32,2048]{1,0:T(8,128)(2,1)S(1)}, bf16[32,2048]{1,0:T(8,128)(2,1)S(1)}, u32[]{:S(2)}, u32[]{:S(2)}) collective-permute-start(bf16[32,2048]{1,0:T(8,128)(2,1)S(1)} %add_convert_fusion.5), channel_id=1, source_target_pairs={{0,2},{2,0},{1,3},{3,1},{4,6},{6,4},{5,7},{7,5},{8,10},{10,8},{9,1... | collective-permute-start | bytes 393224 | tf_op jit(solution)/shard_map/ppermute | solution.py:170
  17.3 4.0 %collective-permute-done.5 = bf16[32,2048]{1,0:T(8,128)(2,1)S(1)} collective-permute-done((bf16[32,2048]{1,0:T(8,128)(2,1)S(1)}, bf16[32,2048]{1,0:T(8,128)(2,1)S(1)}, u32[]{:S(2)}, u32[]{:S(2)}) %collective-permute-start.5) | collective-permute-done | bytes 131104 | tf_op jit(solution)/shard_map/ppermute | solution.py:170
  21.3 0.2 multiply_reduce_fusion
  21.6 1.7 %collective-permute-start.7 = (bf16[32,2176]{1,0:T(8,128)(2,1)S(1)}, bf16[32,2176]{1,0:T(8,128)(2,1)S(1)}, u32[]{:S(2)}, u32[]{:S(2)}) collective-permute-start(bf16[32,2176]{1,0:T(8,128)(2,1)S(1)} %pad_maximum_fusion.refs_0_), channel_id=1, source_target_pairs={{0,8},{4,12},{8,0},{12,4},{1,9},{5,13},{9,1},{13,5},{2,10},{6,14},... | collective-permute-start | bytes 417800 | tf_op jit(solution)/shard_map/ppermute | solution.py:170
  23.3 2.6 %collective-permute-start.10 = (bf16[32,2176]{1,0:T(8,128)(2,1)S(1)}, bf16[32,2176]{1,0:T(8,128)(2,1)S(1)}, u32[]{:S(2)}, u32[]{:S(2)}) collective-permute-start(bf16[32,2176]{1,0:T(8,128)(2,1)S(1)} %pad_maximum_fusion.refs_0_), channel_id=1, source_target_pairs={{0,6},{2,4},{4,2},{6,0},{8,14},{10,12},{12,10},{14,8},{1,7},{3,5},... | collective-permute-start | bytes 417800 | tf_op jit(solution)/shard_map/ppermute | solution.py:177
  25.9 0.5 collective-permute-start.9
  26.4 0.3 collective-permute-start.6
  26.8 3.7 %collective-permute-done.7.refs_2_ = bf16[32,2176]{1,0:T(8,128)(2,1)S(1)} collective-permute-done((bf16[32,2176]{1,0:T(8,128)(2,1)S(1)}, bf16[32,2176]{1,0:T(8,128)(2,1)S(1)}, u32[]{:S(2)}, u32[]{:S(2)}) %collective-permute-start.7) | collective-permute-done | bytes 139296 | tf_op jit(solution)/shard_map/ppermute | solution.py:170
  30.5 0.7 collective-permute-start.12
  31.2 0.9 %collective-permute-start.11 = (bf16[32,2176]{1,0:T(8,128)(2,1)S(1)}, bf16[32,2176]{1,0:T(8,128)(2,1)S(1)}, u32[]{:S(2)}, u32[]{:S(2)}) collective-permute-start(bf16[32,2176]{1,0:T(8,128)(2,1)S(1)} %collective-permute-done.7.refs_2_), channel_id=1, source_target_pairs={{0,2},{2,0},{1,3},{3,1},{4,6},{6,4},{5,7},{7,5},{8,10},{10,8},{9,1... | collective-permute-start | bytes 417800 | tf_op jit(solution)/shard_map/ppermute | solution.py:170
  32.1 0.6 collective-permute-done.10.refs_5_
  32.6 1.3 %collective-permute-start.8 = (bf16[32,2176]{1,0:T(8,128)(2,1)S(1)}, bf16[32,2176]{1,0:T(8,128)(2,1)S(1)}, u32[]{:S(2)}, u32[]{:S(2)}) collective-permute-start(bf16[32,2176]{1,0:T(8,128)(2,1)S(1)} %collective-permute-done.7.refs_2_), channel_id=1, source_target_pairs={{0,4},{4,0},{8,12},{12,8},{1,5},{5,1},{9,13},{13,9},{2,6},{6,2},{1... | collective-permute-start | bytes 417800 | tf_op jit(solution)/shard_map/ppermute | solution.py:170
  34.0 0.9 %collective-permute-done.6.refs_1_ = bf16[32,2176]{1,0:T(8,128)(2,1)S(1)} collective-permute-done((bf16[32,2176]{1,0:T(8,128)(2,1)S(1)}, bf16[32,2176]{1,0:T(8,128)(2,1)S(1)}, u32[]{:S(2)}, u32[]{:S(2)}) %collective-permute-start.6) | collective-permute-done | bytes 139296 | tf_op jit(solution)/shard_map/ppermute | solution.py:170
  34.8 3.6 %collective-permute-done.12.refs_7_ = bf16[32,2176]{1,0:T(8,128)(2,1)S(1)} collective-permute-done((bf16[32,2176]{1,0:T(8,128)(2,1)S(1)}, bf16[32,2176]{1,0:T(8,128)(2,1)S(1)}, u32[]{:S(2)}, u32[]{:S(2)}) %collective-permute-start.12) | collective-permute-done | bytes 139296 | tf_op jit(solution)/shard_map/ppermute | solution.py:177
  38.4 0.7 collective-permute-done.11.refs_6_
  39.2 1.0 %collective-permute-done.8.refs_3_ = bf16[32,2176]{1,0:T(8,128)(2,1)S(1)} collective-permute-done((bf16[32,2176]{1,0:T(8,128)(2,1)S(1)}, bf16[32,2176]{1,0:T(8,128)(2,1)S(1)}, u32[]{:S(2)}, u32[]{:S(2)}) %collective-permute-start.8) | collective-permute-done | bytes 139296 | tf_op jit(solution)/shard_map/ppermute | solution.py:170
  40.2 0.5 collective-permute-start.16
  40.8 0.4 collective-permute-start.20
  41.2 0.3 collective-permute-done.18.refs_13_
  41.6 0.2 collective-permute-done.16.refs_11_
  41.8 0.3 collective-permute-done.19.refs_14_
  42.1 0.2 collective-permute-done.20.refs_15_
  42.3 13.9 %experts.1 = (bf16[64,2048]{1,0:T(8,128)(2,1)S(1)}, bf16[64,2048]{1,0:T(8,128)(2,1)S(1)}, bf16[128,2048]{1,0:T(8,128)(2,1)S(1)}, bf16[64,2048]{1,0:T(8,128)(2,1)...) custom-call(s32[1]{0:T(128)} %bitcast.5.first_ref, bf16[32,2176]{1,0:T(8,128)(2,1)S(1)} %pad_maximum_fusion.refs_0_, ...), custom_call_target="tpu_custom_call" | custom-call | flops 3489660928 | bytes 39845888 | tf_op jit(solution)/shard_map/experts/pallas_call | solution.py:499
  56.2 0.4 collective-permute-start.23
  56.6 0.2 collective-permute-start.21
  56.8 0.3 collective-permute-start.22
  57.1 0.7 collective-permute-done.23
  57.9 0.9 %collective-permute-start.24 = (bf16[32,2048]{1,0:T(8,128)(2,1)S(1)}, bf16[32,2048]{1,0:T(8,128)(2,1)S(1)}, u32[]{:S(2)}, u32[]{:S(2)}) collective-permute-start(bf16[32,2048]{1,0:T(8,128)(2,1)S(1)} %get-tuple-element.60), channel_id=1, source_target_pairs={{0,6},{2,4},{4,2},{6,0},{8,14},{10,12},{12,10},{14,8},{1,7},{3,5},... | collective-permute-start | bytes 393224 | tf_op jit(solution)/shard_map/ppermute | solution.py:177
  58.8 1.2 %collective-permute-start.25 = (bf16[32,2048]{1,0:T(8,128)(2,1)S(1)}, bf16[32,2048]{1,0:T(8,128)(2,1)S(1)}, u32[]{:S(2)}, u32[]{:S(2)}) collective-permute-start(bf16[32,2048]{1,0:T(8,128)(2,1)S(1)} %get-tuple-element.61), channel_id=1, source_target_pairs={{0,2},{2,0},{1,3},{3,1},{4,6},{6,4},{5,7},{7,5},{8,10},{10,8},{9,1... | collective-permute-start | bytes 393224 | tf_op jit(solution)/shard_map/ppermute | solution.py:170
  60.3 1.5 %collective-permute-start.26 = (bf16[32,2048]{1,0:T(8,128)(2,1)S(1)}, bf16[32,2048]{1,0:T(8,128)(2,1)S(1)}, u32[]{:S(2)}, u32[]{:S(2)}) collective-permute-start(bf16[32,2048]{1,0:T(8,128)(2,1)S(1)} %slice.28), channel_id=1, source_target_pairs={{0,4},{4,0},{8,12},{12,8},{1,5},{5,1},{9,13},{13,9},{2,6},{6,2},{1... | collective-permute-start | bytes 393224 | tf_op jit(solution)/shard_map/ppermute | solution.py:170
  61.8 0.7 collective-permute-start.28
  62.4 0.8 %collective-permute-start.30 = (bf16[32,2048]{1,0:T(8,128)(2,1)S(1)}, bf16[32,2048]{1,0:T(8,128)(2,1)S(1)}, u32[]{:S(2)}, u32[]{:S(2)}) collective-permute-start(bf16[32,2048]{1,0:T(8,128)(2,1)S(1)} %get-tuple-element.58), channel_id=1, source_target_pairs={{0,2},{2,0},{1,3},{3,1},{4,6},{6,4},{5,7},{7,5},{8,10},{10,8},{9,1... | collective-permute-start | bytes 393224 | tf_op jit(solution)/shard_map/ppermute | solution.py:170
  63.3 1.9 %collective-permute-done.24 = bf16[32,2048]{1,0:T(8,128)(2,1)S(1)} collective-permute-done((bf16[32,2048]{1,0:T(8,128)(2,1)S(1)}, bf16[32,2048]{1,0:T(8,128)(2,1)S(1)}, u32[]{:S(2)}, u32[]{:S(2)}) %collective-permute-start.24) | collective-permute-done | bytes 131104 | tf_op jit(solution)/shard_map/ppermute | solution.py:177
  65.2 0.6 collective-permute-start.29
  65.8 1.7 %collective-permute-done.25 = bf16[32,2048]{1,0:T(8,128)(2,1)S(1)} collective-permute-done((bf16[32,2048]{1,0:T(8,128)(2,1)S(1)}, bf16[32,2048]{1,0:T(8,128)(2,1)S(1)}, u32[]{:S(2)}, u32[]{:S(2)}) %collective-permute-start.25) | collective-permute-done | bytes 131104 | tf_op jit(solution)/shard_map/ppermute | solution.py:170
  67.6 1.7 %collective-permute-start.27 = (bf16[32,2048]{1,0:T(8,128)(2,1)S(1)}, bf16[32,2048]{1,0:T(8,128)(2,1)S(1)}, u32[]{:S(2)}, u32[]{:S(2)}) collective-permute-start(bf16[32,2048]{1,0:T(8,128)(2,1)S(1)} %add_convert_fusion.4), channel_id=1, source_target_pairs={{0,8},{4,12},{8,0},{12,4},{1,9},{5,13},{9,1},{13,5},{2,10},{6,14},... | collective-permute-start | bytes 393224 | tf_op jit(solution)/shard_map/ppermute | solution.py:170
  69.3 0.9 %collective-permute-done.28 = bf16[32,2048]{1,0:T(8,128)(2,1)S(1)} collective-permute-done((bf16[32,2048]{1,0:T(8,128)(2,1)S(1)}, bf16[32,2048]{1,0:T(8,128)(2,1)S(1)}, u32[]{:S(2)}, u32[]{:S(2)}) %collective-permute-start.28) | collective-permute-done | bytes 131104 | tf_op jit(solution)/shard_map/ppermute | solution.py:170
  70.2 5.6 %collective-permute-done.29 = bf16[32,2048]{1,0:T(8,128)(2,1)S(1)} collective-permute-done((bf16[32,2048]{1,0:T(8,128)(2,1)S(1)}, bf16[32,2048]{1,0:T(8,128)(2,1)S(1)}, u32[]{:S(2)}, u32[]{:S(2)}) %collective-permute-start.29) | collective-permute-done | bytes 131104 | tf_op jit(solution)/shard_map/ppermute | solution.py:177
  75.9 0.4 collective-permute-done.27
  76.2 0.8 %add_convert_fusion.3 = bf16[32,2048]{1,0:T(8,128)(2,1)} fusion(bf16[32,2048]{1,0:T(8,128)(2,1)S(1)} %collective-permute-done.30, bf16[32,2048]{1,0:T(8,128)(2,1)S(1)} %collective-permute-done.29, bf16[32,2048]{1,0:T(8,128)(2,1)S(1)} %collective-permute-done.28, bf16[32,2048]{1,0:T(8,128)(2,1)S(1)} %collective-permute-done.27, ...), kind=kLoop, calls=%fused_computation.3 | loop fusion | flops 983040 | bytes 1310720 | tf_op jit(solution)/shard_map/convert_element_type | solution.py:607
  (33 shorter events, 0.8 us)
Async XLA Ops:
  0.8 8.9 %collective-permute-start.2 = (bf16[128,256]{1,0:T(8,128)(2,1)S(1)}, bf16[128,256]{1,0:T(8,128)(2,1)S(1)}, u32[]{:S(2)}, u32[]{:S(2)}) collective-permute-start(bf16[128,256]{1,0:T(8,128)(2,1)S(1)} %pad_maximum_fusion.1.kv_ref), channel_id=1, source_target_pairs={{0,12},{4,8},{8,4},{12,0},{1,13},{5,9},{9,5},{13,1},{2,14},{6,10},... | collective-permute-start | bytes 196616 | tf_op jit(solution)/shard_map/ppermute | solution.py:170
  5.9 5.6 %collective-permute-start.1 = (bf16[128,256]{1,0:T(8,128)(2,1)S(1)}, bf16[128,256]{1,0:T(8,128)(2,1)S(1)}, u32[]{:S(2)}, u32[]{:S(2)}) collective-permute-start(bf16[128,256]{1,0:T(8,128)(2,1)S(1)} %pad_maximum_fusion.1.kv_ref), channel_id=1, source_target_pairs={{0,8},{4,12},{8,0},{12,4},{1,9},{5,13},{9,1},{13,5},{2,10},{6,14},... | collective-permute-start | bytes 196616 | tf_op jit(solution)/shard_map/ppermute | solution.py:170
  5.9 5.6 %collective-permute-start = (bf16[128,256]{1,0:T(8,128)(2,1)S(1)}, bf16[128,256]{1,0:T(8,128)(2,1)S(1)}, u32[]{:S(2)}, u32[]{:S(2)}) collective-permute-start(bf16[128,256]{1,0:T(8,128)(2,1)S(1)} %pad_maximum_fusion.1.kv_ref), channel_id=1, source_target_pairs={{0,4},{4,0},{8,12},{12,8},{1,5},{5,1},{9,13},{13,9},{2,6},{6,2},{1... | collective-permute-start | bytes 196616 | tf_op jit(solution)/shard_map/ppermute | solution.py:170
  14.3 1.4 %collective-permute-start.4 = (bf16[32,2048]{1,0:T(8,128)(2,1)S(1)}, bf16[32,2048]{1,0:T(8,128)(2,1)S(1)}, u32[]{:S(2)}, u32[]{:S(2)}) collective-permute-start(bf16[32,2048]{1,0:T(8,128)(2,1)S(1)} %get-tuple-element.40), channel_id=1, source_target_pairs={{0,1},{1,0},{2,3},{3,2},{4,5},{5,4},{6,7},{7,6},{8,9},{9,8},{10,11... | collective-permute-start | bytes 393224 | tf_op jit(solution)/shard_map/ppermute | solution.py:170
  14.3 2.9 %collective-permute-start.3 = (bf16[32,2048]{1,0:T(8,128)(2,1)S(1)}, bf16[32,2048]{1,0:T(8,128)(2,1)S(1)}, u32[]{:S(2)}, u32[]{:S(2)}) collective-permute-start(bf16[32,2048]{1,0:T(8,128)(2,1)S(1)} %get-tuple-element.38), channel_id=1, source_target_pairs={{0,1},{1,0},{2,3},{3,2},{4,5},{5,4},{6,7},{7,6},{8,9},{9,8},{10,11... | collective-permute-start | bytes 393224 | tf_op jit(solution)/shard_map/ppermute | solution.py:170
  15.7 5.6 %collective-permute-start.5 = (bf16[32,2048]{1,0:T(8,128)(2,1)S(1)}, bf16[32,2048]{1,0:T(8,128)(2,1)S(1)}, u32[]{:S(2)}, u32[]{:S(2)}) collective-permute-start(bf16[32,2048]{1,0:T(8,128)(2,1)S(1)} %add_convert_fusion.5), channel_id=1, source_target_pairs={{0,2},{2,0},{1,3},{3,1},{4,6},{6,4},{5,7},{7,5},{8,10},{10,8},{9,1... | collective-permute-start | bytes 393224 | tf_op jit(solution)/shard_map/ppermute | solution.py:170
  21.6 8.8 %collective-permute-start.7 = (bf16[32,2176]{1,0:T(8,128)(2,1)S(1)}, bf16[32,2176]{1,0:T(8,128)(2,1)S(1)}, u32[]{:S(2)}, u32[]{:S(2)}) collective-permute-start(bf16[32,2176]{1,0:T(8,128)(2,1)S(1)} %pad_maximum_fusion.refs_0_), channel_id=1, source_target_pairs={{0,8},{4,12},{8,0},{12,4},{1,9},{5,13},{9,1},{13,5},{2,10},{6,14},... | collective-permute-start | bytes 417800 | tf_op jit(solution)/shard_map/ppermute | solution.py:170
  23.3 9.4 %collective-permute-start.10 = (bf16[32,2176]{1,0:T(8,128)(2,1)S(1)}, bf16[32,2176]{1,0:T(8,128)(2,1)S(1)}, u32[]{:S(2)}, u32[]{:S(2)}) collective-permute-start(bf16[32,2176]{1,0:T(8,128)(2,1)S(1)} %pad_maximum_fusion.refs_0_), channel_id=1, source_target_pairs={{0,6},{2,4},{4,2},{6,0},{8,14},{10,12},{12,10},{14,8},{1,7},{3,5},... | collective-permute-start | bytes 417800 | tf_op jit(solution)/shard_map/ppermute | solution.py:177
  25.9 8.1 %collective-permute-start.9 = (bf16[32,2176]{1,0:T(8,128)(2,1)S(1)}, bf16[32,2176]{1,0:T(8,128)(2,1)S(1)}, u32[]{:S(2)}, u32[]{:S(2)}) collective-permute-start(bf16[32,2176]{1,0:T(8,128)(2,1)S(1)} %pad_maximum_fusion.refs_0_), channel_id=1, source_target_pairs={{0,2},{2,0},{1,3},{3,1},{4,6},{6,4},{5,7},{7,5},{8,10},{10,8},{9,1... | collective-permute-start | bytes 417800 | tf_op jit(solution)/shard_map/ppermute | solution.py:170
  26.4 8.4 %collective-permute-start.6 = (bf16[32,2176]{1,0:T(8,128)(2,1)S(1)}, bf16[32,2176]{1,0:T(8,128)(2,1)S(1)}, u32[]{:S(2)}, u32[]{:S(2)}) collective-permute-start(bf16[32,2176]{1,0:T(8,128)(2,1)S(1)} %pad_maximum_fusion.refs_0_), channel_id=1, source_target_pairs={{0,4},{4,0},{8,12},{12,8},{1,5},{5,1},{9,13},{13,9},{2,6},{6,2},{1... | collective-permute-start | bytes 417800 | tf_op jit(solution)/shard_map/ppermute | solution.py:170
  30.5 8.0 %collective-permute-start.12 = (bf16[32,2176]{1,0:T(8,128)(2,1)S(1)}, bf16[32,2176]{1,0:T(8,128)(2,1)S(1)}, u32[]{:S(2)}, u32[]{:S(2)}) collective-permute-start(bf16[32,2176]{1,0:T(8,128)(2,1)S(1)} %collective-permute-done.7.refs_2_), channel_id=1, source_target_pairs={{0,6},{2,4},{4,2},{6,0},{8,14},{10,12},{12,10},{14,8},{1,7},{3,5},... | collective-permute-start | bytes 417800 | tf_op jit(solution)/shard_map/ppermute | solution.py:177
  31.2 7.9 %collective-permute-start.11 = (bf16[32,2176]{1,0:T(8,128)(2,1)S(1)}, bf16[32,2176]{1,0:T(8,128)(2,1)S(1)}, u32[]{:S(2)}, u32[]{:S(2)}) collective-permute-start(bf16[32,2176]{1,0:T(8,128)(2,1)S(1)} %collective-permute-done.7.refs_2_), channel_id=1, source_target_pairs={{0,2},{2,0},{1,3},{3,1},{4,6},{6,4},{5,7},{7,5},{8,10},{10,8},{9,1... | collective-permute-start | bytes 417800 | tf_op jit(solution)/shard_map/ppermute | solution.py:170
  32.6 7.6 %collective-permute-start.8 = (bf16[32,2176]{1,0:T(8,128)(2,1)S(1)}, bf16[32,2176]{1,0:T(8,128)(2,1)S(1)}, u32[]{:S(2)}, u32[]{:S(2)}) collective-permute-start(bf16[32,2176]{1,0:T(8,128)(2,1)S(1)} %collective-permute-done.7.refs_2_), channel_id=1, source_target_pairs={{0,4},{4,0},{8,12},{12,8},{1,5},{5,1},{9,13},{13,9},{2,6},{6,2},{1... | collective-permute-start | bytes 417800 | tf_op jit(solution)/shard_map/ppermute | solution.py:170
  34.0 6.2 %collective-permute-start.13 = (bf16[32,2176]{1,0:T(8,128)(2,1)S(1)}, bf16[32,2176]{1,0:T(8,128)(2,1)S(1)}, u32[]{:S(2)}, u32[]{:S(2)}) collective-permute-start(bf16[32,2176]{1,0:T(8,128)(2,1)S(1)} %pad_maximum_fusion.refs_0_), channel_id=1, source_target_pairs={{0,1},{1,0},{2,3},{3,2},{4,5},{5,4},{6,7},{7,6},{8,9},{9,8},{10,11... | collective-permute-start | bytes 417800 | tf_op jit(solution)/shard_map/ppermute | solution.py:170
  34.8 5.9 %collective-permute-start.14 = (bf16[32,2176]{1,0:T(8,128)(2,1)S(1)}, bf16[32,2176]{1,0:T(8,128)(2,1)S(1)}, u32[]{:S(2)}, u32[]{:S(2)}) collective-permute-start(bf16[32,2176]{1,0:T(8,128)(2,1)S(1)} %collective-permute-done.6.refs_1_), channel_id=1, source_target_pairs={{0,1},{1,0},{2,3},{3,2},{4,5},{5,4},{6,7},{7,6},{8,9},{9,8},{10,11... | collective-permute-start | bytes 417800 | tf_op jit(solution)/shard_map/ppermute | solution.py:170
  38.4 2.4 %collective-permute-start.15 = (bf16[32,2176]{1,0:T(8,128)(2,1)S(1)}, bf16[32,2176]{1,0:T(8,128)(2,1)S(1)}, u32[]{:S(2)}, u32[]{:S(2)}) collective-permute-start(bf16[32,2176]{1,0:T(8,128)(2,1)S(1)} %collective-permute-done.7.refs_2_), channel_id=1, source_target_pairs={{0,1},{1,0},{2,3},{3,2},{4,5},{5,4},{6,7},{7,6},{8,9},{9,8},{10,11... | collective-permute-start | bytes 417800 | tf_op jit(solution)/shard_map/ppermute | solution.py:170
  39.2 2.1 %collective-permute-start.17 = (bf16[32,2176]{1,0:T(8,128)(2,1)S(1)}, bf16[32,2176]{1,0:T(8,128)(2,1)S(1)}, u32[]{:S(2)}, u32[]{:S(2)}) collective-permute-start(bf16[32,2176]{1,0:T(8,128)(2,1)S(1)} %collective-permute-done.9.refs_4_), channel_id=1, source_target_pairs={{0,1},{1,0},{2,3},{3,2},{4,5},{5,4},{6,7},{7,6},{8,9},{9,8},{10,11... | collective-permute-start | bytes 417800 | tf_op jit(solution)/shard_map/ppermute | solution.py:170
  40.2 1.4 %collective-permute-start.18 = (bf16[32,2176]{1,0:T(8,128)(2,1)S(1)}, bf16[32,2176]{1,0:T(8,128)(2,1)S(1)}, u32[]{:S(2)}, u32[]{:S(2)}) collective-permute-start(bf16[32,2176]{1,0:T(8,128)(2,1)S(1)} %collective-permute-done.10.refs_5_), channel_id=1, source_target_pairs={{0,1},{1,0},{2,3},{3,2},{4,5},{5,4},{6,7},{7,6},{8,9},{9,8},{10,11... | collective-permute-start | bytes 417800 | tf_op jit(solution)/shard_map/ppermute | solution.py:170
  40.2 1.6 %collective-permute-start.16 = (bf16[32,2176]{1,0:T(8,128)(2,1)S(1)}, bf16[32,2176]{1,0:T(8,128)(2,1)S(1)}, u32[]{:S(2)}, u32[]{:S(2)}) collective-permute-start(bf16[32,2176]{1,0:T(8,128)(2,1)S(1)} %collective-permute-done.8.refs_3_), channel_id=1, source_target_pairs={{0,1},{1,0},{2,3},{3,2},{4,5},{5,4},{6,7},{7,6},{8,9},{9,8},{10,11... | collective-permute-start | bytes 417800 | tf_op jit(solution)/shard_map/ppermute | solution.py:170
  40.7 1.4 %collective-permute-start.19 = (bf16[32,2176]{1,0:T(8,128)(2,1)S(1)}, bf16[32,2176]{1,0:T(8,128)(2,1)S(1)}, u32[]{:S(2)}, u32[]{:S(2)}) collective-permute-start(bf16[32,2176]{1,0:T(8,128)(2,1)S(1)} %collective-permute-done.11.refs_6_), channel_id=1, source_target_pairs={{0,1},{1,0},{2,3},{3,2},{4,5},{5,4},{6,7},{7,6},{8,9},{9,8},{10,11... | collective-permute-start | bytes 417800 | tf_op jit(solution)/shard_map/ppermute | solution.py:170
  40.8 1.5 %collective-permute-start.20 = (bf16[32,2176]{1,0:T(8,128)(2,1)S(1)}, bf16[32,2176]{1,0:T(8,128)(2,1)S(1)}, u32[]{:S(2)}, u32[]{:S(2)}) collective-permute-start(bf16[32,2176]{1,0:T(8,128)(2,1)S(1)} %collective-permute-done.12.refs_7_), channel_id=1, source_target_pairs={{0,1},{1,0},{2,3},{3,2},{4,5},{5,4},{6,7},{7,6},{8,9},{9,8},{10,11... | collective-permute-start | bytes 417800 | tf_op jit(solution)/shard_map/ppermute | solution.py:170
  56.2 1.6 %collective-permute-start.23 = (bf16[64,2048]{1,0:T(8,128)(2,1)S(1)}, bf16[64,2048]{1,0:T(8,128)(2,1)S(1)}, u32[]{:S(2)}, u32[]{:S(2)}) collective-permute-start(bf16[64,2048]{1,0:T(8,128)(2,1)S(1)} %get-tuple-element.56), channel_id=1, source_target_pairs={{0,1},{1,0},{2,3},{3,2},{4,5},{5,4},{6,7},{7,6},{8,9},{9,8},{10,11... | collective-permute-start | bytes 786440 | tf_op jit(solution)/shard_map/ppermute | solution.py:170
  56.6 3.4 %collective-permute-start.21 = (bf16[64,2048]{1,0:T(8,128)(2,1)S(1)}, bf16[64,2048]{1,0:T(8,128)(2,1)S(1)}, u32[]{:S(2)}, u32[]{:S(2)}) collective-permute-start(bf16[64,2048]{1,0:T(8,128)(2,1)S(1)} %get-tuple-element.50), channel_id=1, source_target_pairs={{0,1},{1,0},{2,3},{3,2},{4,5},{5,4},{6,7},{7,6},{8,9},{9,8},{10,11... | collective-permute-start | bytes 786440 | tf_op jit(solution)/shard_map/ppermute | solution.py:170
  56.8 3.3 %collective-permute-start.22 = (bf16[128,2048]{1,0:T(8,128)(2,1)S(1)}, bf16[128,2048]{1,0:T(8,128)(2,1)S(1)}, u32[]{:S(2)}, u32[]{:S(2)}) collective-permute-start(bf16[128,2048]{1,0:T(8,128)(2,1)S(1)} %get-tuple-element.52), channel_id=1, source_target_pairs={{0,1},{1,0},{2,3},{3,2},{4,5},{5,4},{6,7},{7,6},{8,9},{9,8},{10,11... | collective-permute-start | bytes 1572872 | tf_op jit(solution)/shard_map/ppermute | solution.py:170
  57.9 7.3 %collective-permute-start.24 = (bf16[32,2048]{1,0:T(8,128)(2,1)S(1)}, bf16[32,2048]{1,0:T(8,128)(2,1)S(1)}, u32[]{:S(2)}, u32[]{:S(2)}) collective-permute-start(bf16[32,2048]{1,0:T(8,128)(2,1)S(1)} %get-tuple-element.60), channel_id=1, source_target_pairs={{0,6},{2,4},{4,2},{6,0},{8,14},{10,12},{12,10},{14,8},{1,7},{3,5},... | collective-permute-start | bytes 393224 | tf_op jit(solution)/shard_map/ppermute | solution.py:177
  58.8 8.6 %collective-permute-start.25 = (bf16[32,2048]{1,0:T(8,128)(2,1)S(1)}, bf16[32,2048]{1,0:T(8,128)(2,1)S(1)}, u32[]{:S(2)}, u32[]{:S(2)}) collective-permute-start(bf16[32,2048]{1,0:T(8,128)(2,1)S(1)} %get-tuple-element.61), channel_id=1, source_target_pairs={{0,2},{2,0},{1,3},{3,1},{4,6},{6,4},{5,7},{7,5},{8,10},{10,8},{9,1... | collective-permute-start | bytes 393224 | tf_op jit(solution)/shard_map/ppermute | solution.py:170
  60.3 7.2 %collective-permute-start.26 = (bf16[32,2048]{1,0:T(8,128)(2,1)S(1)}, bf16[32,2048]{1,0:T(8,128)(2,1)S(1)}, u32[]{:S(2)}, u32[]{:S(2)}) collective-permute-start(bf16[32,2048]{1,0:T(8,128)(2,1)S(1)} %slice.28), channel_id=1, source_target_pairs={{0,4},{4,0},{8,12},{12,8},{1,5},{5,1},{9,13},{13,9},{2,6},{6,2},{1... | collective-permute-start | bytes 393224 | tf_op jit(solution)/shard_map/ppermute | solution.py:170
  61.8 8.4 %collective-permute-start.28 = (bf16[32,2048]{1,0:T(8,128)(2,1)S(1)}, bf16[32,2048]{1,0:T(8,128)(2,1)S(1)}, u32[]{:S(2)}, u32[]{:S(2)}) collective-permute-start(bf16[32,2048]{1,0:T(8,128)(2,1)S(1)} %get-tuple-element.57), channel_id=1, source_target_pairs={{0,4},{4,0},{8,12},{12,8},{1,5},{5,1},{9,13},{13,9},{2,6},{6,2},{1... | collective-permute-start | bytes 393224 | tf_op jit(solution)/shard_map/ppermute | solution.py:170
  62.4 7.8 %collective-permute-start.30 = (bf16[32,2048]{1,0:T(8,128)(2,1)S(1)}, bf16[32,2048]{1,0:T(8,128)(2,1)S(1)}, u32[]{:S(2)}, u32[]{:S(2)}) collective-permute-start(bf16[32,2048]{1,0:T(8,128)(2,1)S(1)} %get-tuple-element.58), channel_id=1, source_target_pairs={{0,2},{2,0},{1,3},{3,1},{4,6},{6,4},{5,7},{7,5},{8,10},{10,8},{9,1... | collective-permute-start | bytes 393224 | tf_op jit(solution)/shard_map/ppermute | solution.py:170
  65.2 10.6 %collective-permute-start.29 = (bf16[32,2048]{1,0:T(8,128)(2,1)S(1)}, bf16[32,2048]{1,0:T(8,128)(2,1)S(1)}, u32[]{:S(2)}, u32[]{:S(2)}) collective-permute-start(bf16[32,2048]{1,0:T(8,128)(2,1)S(1)} %get-tuple-element.59), channel_id=1, source_target_pairs={{0,6},{2,4},{4,2},{6,0},{8,14},{10,12},{12,10},{14,8},{1,7},{3,5},... | collective-permute-start | bytes 393224 | tf_op jit(solution)/shard_map/ppermute | solution.py:177
  67.6 8.7 %collective-permute-start.27 = (bf16[32,2048]{1,0:T(8,128)(2,1)S(1)}, bf16[32,2048]{1,0:T(8,128)(2,1)S(1)}, u32[]{:S(2)}, u32[]{:S(2)}) collective-permute-start(bf16[32,2048]{1,0:T(8,128)(2,1)S(1)} %add_convert_fusion.4), channel_id=1, source_target_pairs={{0,8},{4,12},{8,0},{12,4},{1,9},{5,13},{9,1},{13,5},{2,10},{6,14},... | collective-permute-start | bytes 393224 | tf_op jit(solution)/shard_map/ppermute | solution.py:170

commit v14 on v12

--- a/solution.py
+++ b/solution.py
@@ -185,7 +185,7 @@
     return lax.dot_general(a, b, (((1,), (1,)), ((), ())), preferred_element_type=F32)
 
 
-KV_ORDER = (1, 2, 3)
+KV_ORDER = ((1, 3), (2,))
 
 
 def own_block_kernel(sizes, place, kv_ref, ids_hbm, probs_hbm, q_hbm, w_hbm, resid_hbm, *refs):
@@ -299,33 +299,68 @@
     return lax.dot_general(a, b, (((0,), (0,)), ((), ())), preferred_element_type=F32)
 
 
-def attention_kernel(sizes, place, *refs):
-    n_ctx, n_exp, n_tp, heads, part = sizes
-    rows = n_exp * n_tp * part
-    kv_refs, refs = refs[: n_ctx - 1], refs[n_ctx - 1 :]
-    q_ref, w_ref, resid_ref, out_ref, sum_ref, max_ref = refs[:6]
-    base_ref, across_ref, other_ref = refs[6:9]
-    k_all, v_all, att, att_rel = refs[9:]
-    ctx, exp, tp = place[0], place[1], place[2]
+def fold_blocks(bits_of, ctx, kv_refs, q_ref, state, k_all, v_all):
+    out_ref, sum_ref, max_ref = state
+    rows = kv_refs[0].shape[0]
     for i, kv_ref in enumerate(kv_refs):
         at = slice(i * rows, (i + 1) * rows)
         k_all[at, :] = kv_ref[:, :HEAD_DIMENSION]
         v_all[at, :HEAD_DIMENSION] = kv_ref[:, HEAD_DIMENSION:]
-    v_all[:, HEAD_DIMENSION:] = jnp.ones(((n_ctx - 1) * rows, HEAD_DIMENSION), BF)
-    piece = lax.broadcasted_iota(jnp.int32, (1, (n_ctx - 1) * rows), 1) // rows
+    v_all[:, HEAD_DIMENSION:] = jnp.ones((len(kv_refs) * rows, HEAD_DIMENSION), BF)
+    piece = lax.broadcasted_iota(jnp.int32, (1, len(kv_refs) * rows), 1) // rows
     earlier = jnp.zeros_like(piece)
-    for i, bits in enumerate(KV_ORDER):
+    for i, bits in enumerate(bits_of):
         there = jnp.where(lax.bitwise_xor(ctx, bits) < ctx, 1, 0)
         earlier = earlier + jnp.where(piece == i, there, 0)
-    allowed = earlier == 1
     scale = 1.0 / math.sqrt(HEAD_DIMENSION)
-    s = jnp.where(allowed, dot_rows(q_ref[...], k_all[...]) * scale, -1e30)
-    own_top = max_ref[...]
-    top = jnp.maximum(own_top, jnp.max(s, axis=1, keepdims=True))
-    keep = jnp.exp(own_top - top)
+    s = jnp.where(earlier == 1, dot_rows(q_ref[...], k_all[...]) * scale, -1e30)
+    old_top = max_ref[...]
+    top = jnp.maximum(old_top, jnp.max(s, axis=1, keepdims=True))
+    keep = jnp.exp(old_top - top)
     out = jnp.dot(jnp.exp(s - top[:, :1]).astype(BF), v_all[...], preferred_element_type=F32)
     total = sum_ref[...] * keep + out[:, HEAD_DIMENSION:]
-    out = out_ref[...] * keep + out[:, :HEAD_DIMENSION]
+    return out_ref[...] * keep + out[:, :HEAD_DIMENSION], total, top
+
+
+def fold_kernel(bits_of, place, *refs):
+    count = len(bits_of)
+    kv_refs, (q_ref, *state), (k_all, v_all) = refs[:count], refs[count : count + 4], refs[-2:]
+    folded = fold_blocks(bits_of, place[0], kv_refs, q_ref, state, k_all, v_all)
+    for ref, value in zip(refs[count + 4 :], folded):
+        ref[...] = value
+
+
+def fold_earlier(bits_of, place, pieces, queries, state):
+    rows, count = pieces[0].shape[0], len(pieces)
+    vmem = pl.BlockSpec(memory_space=pltpu.VMEM)
+    return pl.pallas_call(
+        functools.partial(fold_kernel, bits_of),
+        out_shape=tuple(jax.ShapeDtypeStruct(x.shape, x.dtype) for x in state),
+        in_specs=[pl.BlockSpec(memory_space=pltpu.SMEM)] + [vmem] * (count + 4),
+        out_specs=(vmem,) * 3,
+        scratch_shapes=[
+            pltpu.VMEM((count * rows, HEAD_DIMENSION), BF),
+            pltpu.VMEM((count * rows, 2 * HEAD_DIMENSION), BF),
+        ],
+        compiler_params=pltpu.CompilerParams(vmem_limit_bytes=20 * MIB),
+        cost_estimate=pl.CostEstimate(
+            flops=6 * queries.size * count * rows,
+            bytes_accessed=16 * queries.size,
+            transcendentals=queries.shape[0] * count * rows,
+        ),
+        name="fold_earlier",
+    )(place, *pieces, queries, *state)
+
+
+def attention_kernel(sizes, place, *refs):
+    bits_of, n_exp, n_tp, heads, part = sizes
+    rows = n_exp * n_tp * part
+    kv_refs, refs = refs[: len(bits_of)], refs[len(bits_of) :]
+    q_ref, w_ref, resid_ref, *state = refs[:6]
+    base_ref, across_ref, other_ref = refs[6:9]
+    k_all, v_all, att, att_rel = refs[9:]
+    ctx, exp, tp = place[0], place[1], place[2]
+    out, total, _ = fold_blocks(bits_of, ctx, kv_refs, q_ref, state, k_all, v_all)
     att[...] = (out / total).astype(BF)
     for t in range(n_tp):
         for x in range(n_exp):
@@ -341,33 +376,33 @@
     other_ref[...] = projected[2 * part :].astype(BF)
 
 
-def attend_project(place, pieces, own, n_exp, n_tp):
+def attend_project(bits_of, place, pieces, own, n_exp, n_tp):
     queries, out_weight, resid = own[:3]
     width, model = out_weight.shape
-    n_ctx, heads = len(pieces) + 1, width // HEAD_DIMENSION
+    count, heads = len(pieces), width // HEAD_DIMENSION
     rows = queries.shape[0] // heads
     part = resid.shape[0]
     vmem = pl.BlockSpec(memory_space=pltpu.VMEM)
     return pl.pallas_call(
-        functools.partial(attention_kernel, (n_ctx, n_exp, n_tp, heads, part)),
+        functools.partial(attention_kernel, (bits_of, n_exp, n_tp, heads, part)),
         out_shape=(
             jax.ShapeDtypeStruct((part, model), F32),
             jax.ShapeDtypeStruct((part, model), BF),
             jax.ShapeDtypeStruct((2 * part, model), BF),
         ),
-        in_specs=[pl.BlockSpec(memory_space=pltpu.SMEM)] + [vmem] * (n_ctx - 1 + len(own)),
+        in_specs=[pl.BlockSpec(memory_space=pltpu.SMEM)] + [vmem] * (count + len(own)),
         out_specs=(vmem,) * 3,
         scratch_shapes=[
-            pltpu.VMEM(((n_ctx - 1) * rows, HEAD_DIMENSION), BF),
-            pltpu.VMEM(((n_ctx - 1) * rows, 2 * HEAD_DIMENSION), BF),
+            pltpu.VMEM((count * rows, HEAD_DIMENSION), BF),
+            pltpu.VMEM((count * rows, 2 * HEAD_DIMENSION), BF),
             pltpu.VMEM((heads * rows, HEAD_DIMENSION), BF),
             pltpu.VMEM((rows, width), BF),
         ],
         compiler_params=pltpu.CompilerParams(vmem_limit_bytes=20 * MIB),
         cost_estimate=pl.CostEstimate(
-            flops=2 * rows * width * (3 * (n_ctx - 1) * rows + model),
+            flops=2 * rows * width * (3 * count * rows + model),
             bytes_accessed=2 * (rows * width + width * model + rows * model),
-            transcendentals=rows * n_ctx * rows * heads,
+            transcendentals=rows * count * rows * heads,
         ),
         name="attend_project",
     )(place, *pieces, *own)
@@ -573,11 +608,14 @@
     key_head = lax.dynamic_slice_in_dim(keys, shared * HEAD_DIMENSION, HEAD_DIMENSION, 1)
     value_head = lax.dynamic_slice_in_dim(values, shared * HEAD_DIMENSION, HEAD_DIMENSION, 1)
     kv = jnp.concatenate([key_head, value_head], axis=1)
-    kv_pieces = [flip(kv, "ctx", bits) for bits in KV_ORDER]
+    early, late = KV_ORDER
+    early_pieces = [flip(kv, "ctx", bits) for bits in early]
+    late_pieces = [flip(kv, "ctx", bits) for bits in late]
     *own, routing = own_block(
         place, kv, expert_ids, router_probs, queries, out_weight, resid, n_exp, n_tp
     )
-    base, across, other = attend_project(place, kv_pieces, own, n_exp, n_tp)
+    own[3:] = fold_earlier(early, place, early_pieces, own[0], own[3:])
+    base, across, other = attend_project(late, place, late_pieces, own, n_exp, n_tp)
 
     other = flip(other, "tp", 1).astype(F32)
     across = flip((across.astype(F32) + other[part:]).astype(BF), "exp", 1)

time: 77.4 us -> 77.5 us (level)
  waiting for transfers between devices: 29.6 us -> 27.3 us
  starting transfers between devices: 25.4 us -> 26.8 us
  Pallas kernels: 19.7 us -> 20.6 us
    ppermute x26, waiting for transfers between devices: 18.4 us -> 16.2 us  [flip(): lax.ppermute(x, axis, [(i, i ^ bit) for i in range(lax.axis_size(axis))])]
    ppermute x4, starting transfers between devices: 4.92 us -> 6.4 us  [flip_both(): return lax.ppermute(x, ('ctx', 'exp'), [(i, i ^ mask) for i in range(size)])]
    pallas_call x1 -> x2, Pallas kernels: 2.75 us -> 3.65 us  [the longest x1 2.04 us: attend_project(): pl.pallas_call(functools.partial(attention_kernel, (bits_of, n_exp, n_tp,...]
  transfers between devices with their start and end apart: 30 -> 30, of which waited for: 19 -> 21; matrix products, arithmetic and copies ran while one was open for 1% -> 1% of each run, Pallas kernels for 4% -> 6%
where the time goes in v14:
time: 77.5 us; the launch traced here: 77.3 us
  waiting for transfers between devices  27.3 us (35%)
  starting transfers between devices  26.8 us (35%)
  Pallas kernels  20.6 us (27%)
  other arithmetic  1.51 us (2%)
  local copies, waits for them, and re-layouts  0.84 us (1%)
    ppermute x26, starting transfers between devices, flip(): lax.ppermute(x, axis, [(i, i ^ bit) for i in range(lax.axis_size(axis))])  20.4 us
    ppermute x26, waiting for transfers between devices, flip(): lax.ppermute(x, axis, [(i, i ^ bit) for i in range(lax.axis_size(axis))])  16.2 us
    pallas_call x1, Pallas kernels, cube_experts(): pl.pallas_call(functools.partial(expert_kernel, len(pieces), depth, exper...  13.9 us
    ppermute x4, waiting for transfers between devices, flip_both(): return lax.ppermute(x, ('ctx', 'exp'), [(i, i ^ mask) for i in range(size)])  11.1 us
    ppermute x4, starting transfers between devices, flip_both(): return lax.ppermute(x, ('ctx', 'exp'), [(i, i ^ mask) for i in range(size)])  6.4 us
    pallas_call x1, Pallas kernels, own_block(): pl.pallas_call(functools.partial(own_block_kernel, (n_exp, n_tp, heads, p...  3.09 us
    pallas_call x1, Pallas kernels, attend_project(): pl.pallas_call(functools.partial(attention_kernel, (bits_of, n_exp, n_tp,...  2.04 us
    pallas_call x1, Pallas kernels, fold_earlier(): pl.pallas_call(functools.partial(fold_kernel, bits_of), out_shape=tuple((...  1.62 us
  transfers between devices with their start and end apart: 30, of which 21 were waited for; matrix products, arithmetic and copies ran while one was open for 1% of the time, Pallas kernels for 6%

profile of v14, /device:TPU:0, one launch (start us, length us, event | category | flops | bytes accessed | tf_op | source)
XLA Modules:
  0.0 77.3 jit_solution(9754147460804197667)
XLA Ops:
  0.0 0.8 %constant_dynamic-slice_fusion = (bf16[128,128]{1,0:T(8,128)(2,1)S(1)}, bf16[128,128]{1,0:T(8,128)(2,1)S(1)}) fusion(bf16[128,512]{1,0:T(8,128)(2,1)} %param.12, s32[]{:T(128)S(6)} %select_n.13, bf16[128,512]{1,0:T(8,128)(2,1)} %param.11), kind=kLoop, calls=%fused_computation.15 | loop fusion | bytes 131076 | tf_op jit(solution)/shard_map/dynamic_slice | solution.py:609
  0.8 5.1 %collective-permute-start.2 = (bf16[128,256]{1,0:T(8,128)(2,1)S(1)}, bf16[128,256]{1,0:T(8,128)(2,1)S(1)}, u32[]{:S(2)}, u32[]{:S(2)}) collective-permute-start(bf16[128,256]{1,0:T(8,128)(2,1)S(1)} %pad_maximum_fusion.1.kv_ref), channel_id=1, source_target_pairs={{0,12},{4,8},{8,4},{12,0},{1,13},{5,9},{9,5},{13,1},{2,14},{6,10},... | collective-permute-start | bytes 196616 | tf_op jit(solution)/shard_map/ppermute | solution.py:170
  5.9 0.6 collective-permute-start
  6.6 3.1 %own_block.1 = (bf16[1024,128]{1,0:T(8,128)(2,1)S(1)}, bf16[1024,2048]{1,0:T(8,128)(2,1)S(1)}, bf16[32,2048]{1,0:T(8,128)(2,1)S(1)}, f32[1024,128]{1,0:T(8,128)S...) custom-call(s32[3]{0:T(128)S(1)} %pad_add_fusion.place, ...), custom_call_target="tpu_custom_call" | custom-call | flops 100663296 | bytes 4980736 | tf_op jit(solution)/shard_map/own_block/pallas_call | solution.py:267
  9.7 0.8 %collective-permute-done.1.refs_0_ = bf16[128,256]{1,0:T(8,128)(2,1)S(1)} collective-permute-done((bf16[128,256]{1,0:T(8,128)(2,1)S(1)}, bf16[128,256]{1,0:T(8,128)(2,1)S(1)}, u32[]{:S(2)}, u32[]{:S(2)}) %collective-permute-start.1) | collective-permute-done | bytes 65568 | tf_op jit(solution)/shard_map/ppermute | solution.py:170
  10.6 1.6 %fold_earlier.1 = (f32[1024,128]{1,0:T(8,128)S(1)}, f32[1024,128]{1,0:T(8,128)S(1)}, f32[1024,128]{1,0:T(8,128)S(1)}) custom-call(s32[3]{0:T(128)S(1)} %pad_add_fusion.place, bf16[128,256]{1,0:T(8,128)(2,1)S(1)} %collective-permute-done.1.refs_0_, bf16[128,256]{1,0:T(8,128)(2,1)S(1)} %collective-permute-done.2.refs_1_, ...), custom_call_target="tpu_custom_call" | custom-call | flops 201326592 | bytes 2097152 | tf_op jit(solution)/shard_map/fold_earlier/pallas_call | solution.py:336
  12.2 2.0 %attend_project.1 = (f32[32,2048]{1,0:T(8,128)S(1)}, bf16[32,2048]{1,0:T(8,128)(2,1)S(1)}, bf16[64,2048]{1,0:T(8,128)(2,1)S(1)}) custom-call(s32[3]{0:T(128)S(1)} %pad_add_fusion.place, bf16[128,256]{1,0:T(8,128)(2,1)S(1)} %collective-permute-done.refs_0_, bf16[1024,128]{1,0:T(8,128)(2,1)S(1)} %get-tuple-element.34.refs_2_.refs_1_, ...), custom_call_target="tpu_custom_call" | custom-call | flops 637534208 | bytes 4980736 | tf_op jit(solution)/shard_map/attend_project/pallas_call | solution.py:386
  14.3 1.5 %collective-permute-done.3 = bf16[64,2048]{1,0:T(8,128)(2,1)S(1)} collective-permute-done((bf16[64,2048]{1,0:T(8,128)(2,1)S(1)}, bf16[64,2048]{1,0:T(8,128)(2,1)S(1)}, u32[]{:S(2)}, u32[]{:S(2)}) %collective-permute-start.3) | collective-permute-done | bytes 262176 | tf_op jit(solution)/shard_map/ppermute | solution.py:170
  15.9 1.7 %collective-permute-start.4 = (bf16[32,2048]{1,0:T(8,128)(2,1)S(1)}, bf16[32,2048]{1,0:T(8,128)(2,1)S(1)}, u32[]{:S(2)}, u32[]{:S(2)}) collective-permute-start(bf16[32,2048]{1,0:T(8,128)(2,1)S(1)} %fusion), channel_id=1, source_target_pairs={{0,2},{2,0},{1,3},{3,1},{4,6},{6,4},{5,7},{7,5},{8,10},{10,8},{9,1... | collective-permute-start | bytes 393224 | tf_op jit(solution)/shard_map/ppermute | solution.py:170
  17.6 3.9 %collective-permute-done.4 = bf16[32,2048]{1,0:T(8,128)(2,1)S(1)} collective-permute-done((bf16[32,2048]{1,0:T(8,128)(2,1)S(1)}, bf16[32,2048]{1,0:T(8,128)(2,1)S(1)}, u32[]{:S(2)}, u32[]{:S(2)}) %collective-permute-start.4) | collective-permute-done | bytes 131104 | tf_op jit(solution)/shard_map/ppermute | solution.py:170
  21.8 1.5 %collective-permute-start.6 = (bf16[32,2176]{1,0:T(8,128)(2,1)S(1)}, bf16[32,2176]{1,0:T(8,128)(2,1)S(1)}, u32[]{:S(2)}, u32[]{:S(2)}) collective-permute-start(bf16[32,2176]{1,0:T(8,128)(2,1)S(1)} %pad_maximum_fusion.refs_0_), channel_id=1, source_target_pairs={{0,8},{4,12},{8,0},{12,4},{1,9},{5,13},{9,1},{13,5},{2,10},{6,14},... | collective-permute-start | bytes 417800 | tf_op jit(solution)/shard_map/ppermute | solution.py:170
  23.3 3.0 %collective-permute-start.9 = (bf16[32,2176]{1,0:T(8,128)(2,1)S(1)}, bf16[32,2176]{1,0:T(8,128)(2,1)S(1)}, u32[]{:S(2)}, u32[]{:S(2)}) collective-permute-start(bf16[32,2176]{1,0:T(8,128)(2,1)S(1)} %pad_maximum_fusion.refs_0_), channel_id=1, source_target_pairs={{0,6},{2,4},{4,2},{6,0},{8,14},{10,12},{12,10},{14,8},{1,7},{3,5},... | collective-permute-start | bytes 417800 | tf_op jit(solution)/shard_map/ppermute | solution.py:177
  26.3 0.5 collective-permute-start.8
  26.9 3.8 %collective-permute-done.6.refs_2_ = bf16[32,2176]{1,0:T(8,128)(2,1)S(1)} collective-permute-done((bf16[32,2176]{1,0:T(8,128)(2,1)S(1)}, bf16[32,2176]{1,0:T(8,128)(2,1)S(1)}, u32[]{:S(2)}, u32[]{:S(2)}) %collective-permute-start.6) | collective-permute-done | bytes 139296 | tf_op jit(solution)/shard_map/ppermute | solution.py:170
  30.6 0.9 %collective-permute-start.11 = (bf16[32,2176]{1,0:T(8,128)(2,1)S(1)}, bf16[32,2176]{1,0:T(8,128)(2,1)S(1)}, u32[]{:S(2)}, u32[]{:S(2)}) collective-permute-start(bf16[32,2176]{1,0:T(8,128)(2,1)S(1)} %collective-permute-done.6.refs_2_), channel_id=1, source_target_pairs={{0,6},{2,4},{4,2},{6,0},{8,14},{10,12},{12,10},{14,8},{1,7},{3,5},... | collective-permute-start | bytes 417800 | tf_op jit(solution)/shard_map/ppermute | solution.py:177
  31.6 0.7 collective-permute-start.10
  32.3 0.5 collective-permute-done.9.refs_5_
  32.8 1.3 %collective-permute-start.7 = (bf16[32,2176]{1,0:T(8,128)(2,1)S(1)}, bf16[32,2176]{1,0:T(8,128)(2,1)S(1)}, u32[]{:S(2)}, u32[]{:S(2)}) collective-permute-start(bf16[32,2176]{1,0:T(8,128)(2,1)S(1)} %collective-permute-done.6.refs_2_), channel_id=1, source_target_pairs={{0,4},{4,0},{8,12},{12,8},{1,5},{5,1},{9,13},{13,9},{2,6},{6,2},{1... | collective-permute-start | bytes 417800 | tf_op jit(solution)/shard_map/ppermute | solution.py:170
  34.1 0.2 collective-permute-done.5.refs_1_
  34.4 0.5 collective-permute-start.13
  34.9 3.9 %collective-permute-done.11.refs_7_ = bf16[32,2176]{1,0:T(8,128)(2,1)S(1)} collective-permute-done((bf16[32,2176]{1,0:T(8,128)(2,1)S(1)}, bf16[32,2176]{1,0:T(8,128)(2,1)S(1)}, u32[]{:S(2)}, u32[]{:S(2)}) %collective-permute-start.11) | collective-permute-done | bytes 139296 | tf_op jit(solution)/shard_map/ppermute | solution.py:177
  38.8 0.2 collective-permute-done.10.refs_6_
  39.0 0.3 collective-permute-start.16
  39.3 0.7 collective-permute-done.7.refs_3_
  40.0 0.5 collective-permute-start.15
  40.6 0.4 collective-permute-start.19
  41.1 0.3 collective-permute-done.17.refs_13_
  41.4 0.2 collective-permute-done.15.refs_11_
  41.6 0.3 collective-permute-done.18.refs_14_
  42.1 13.9 %experts.1 = (bf16[64,2048]{1,0:T(8,128)(2,1)S(1)}, bf16[64,2048]{1,0:T(8,128)(2,1)S(1)}, bf16[128,2048]{1,0:T(8,128)(2,1)S(1)}, bf16[64,2048]{1,0:T(8,128)(2,1)...) custom-call(s32[1]{0:T(128)} %bitcast.5.first_ref, bf16[32,2176]{1,0:T(8,128)(2,1)S(1)} %pad_maximum_fusion.refs_0_, ...), custom_call_target="tpu_custom_call" | custom-call | flops 3489660928 | bytes 39845888 | tf_op jit(solution)/shard_map/experts/pallas_call | solution.py:532
  56.0 0.4 collective-permute-start.22
  56.4 0.2 collective-permute-start.20
  56.6 0.3 collective-permute-start.21
  56.9 0.7 collective-permute-done.22
  57.7 1.3 %collective-permute-start.23 = (bf16[32,2048]{1,0:T(8,128)(2,1)S(1)}, bf16[32,2048]{1,0:T(8,128)(2,1)S(1)}, u32[]{:S(2)}, u32[]{:S(2)}) collective-permute-start(bf16[32,2048]{1,0:T(8,128)(2,1)S(1)} %get-tuple-element.68), channel_id=1, source_target_pairs={{0,6},{2,4},{4,2},{6,0},{8,14},{10,12},{12,10},{14,8},{1,7},{3,5},... | collective-permute-start | bytes 393224 | tf_op jit(solution)/shard_map/ppermute | solution.py:177
  59.0 1.1 %collective-permute-start.24 = (bf16[32,2048]{1,0:T(8,128)(2,1)S(1)}, bf16[32,2048]{1,0:T(8,128)(2,1)S(1)}, u32[]{:S(2)}, u32[]{:S(2)}) collective-permute-start(bf16[32,2048]{1,0:T(8,128)(2,1)S(1)} %get-tuple-element.69), channel_id=1, source_target_pairs={{0,2},{2,0},{1,3},{3,1},{4,6},{6,4},{5,7},{7,5},{8,10},{10,8},{9,1... | collective-permute-start | bytes 393224 | tf_op jit(solution)/shard_map/ppermute | solution.py:170
  60.4 1.2 %collective-permute-start.25 = (bf16[32,2048]{1,0:T(8,128)(2,1)S(1)}, bf16[32,2048]{1,0:T(8,128)(2,1)S(1)}, u32[]{:S(2)}, u32[]{:S(2)}) collective-permute-start(bf16[32,2048]{1,0:T(8,128)(2,1)S(1)} %slice.36), channel_id=1, source_target_pairs={{0,4},{4,0},{8,12},{12,8},{1,5},{5,1},{9,13},{13,9},{2,6},{6,2},{1... | collective-permute-start | bytes 393224 | tf_op jit(solution)/shard_map/ppermute | solution.py:170
  61.6 1.0 %collective-permute-start.27 = (bf16[32,2048]{1,0:T(8,128)(2,1)S(1)}, bf16[32,2048]{1,0:T(8,128)(2,1)S(1)}, u32[]{:S(2)}, u32[]{:S(2)}) collective-permute-start(bf16[32,2048]{1,0:T(8,128)(2,1)S(1)} %get-tuple-element.65), channel_id=1, source_target_pairs={{0,4},{4,0},{8,12},{12,8},{1,5},{5,1},{9,13},{13,9},{2,6},{6,2},{1... | collective-permute-start | bytes 393224 | tf_op jit(solution)/shard_map/ppermute | solution.py:170
  62.6 0.9 %collective-permute-start.29 = (bf16[32,2048]{1,0:T(8,128)(2,1)S(1)}, bf16[32,2048]{1,0:T(8,128)(2,1)S(1)}, u32[]{:S(2)}, u32[]{:S(2)}) collective-permute-start(bf16[32,2048]{1,0:T(8,128)(2,1)S(1)} %get-tuple-element.66), channel_id=1, source_target_pairs={{0,2},{2,0},{1,3},{3,1},{4,6},{6,4},{5,7},{7,5},{8,10},{10,8},{9,1... | collective-permute-start | bytes 393224 | tf_op jit(solution)/shard_map/ppermute | solution.py:170
  63.5 1.6 %collective-permute-done.23 = bf16[32,2048]{1,0:T(8,128)(2,1)S(1)} collective-permute-done((bf16[32,2048]{1,0:T(8,128)(2,1)S(1)}, bf16[32,2048]{1,0:T(8,128)(2,1)S(1)}, u32[]{:S(2)}, u32[]{:S(2)}) %collective-permute-start.23) | collective-permute-done | bytes 131104 | tf_op jit(solution)/shard_map/ppermute | solution.py:177
  65.0 1.2 %collective-permute-start.28 = (bf16[32,2048]{1,0:T(8,128)(2,1)S(1)}, bf16[32,2048]{1,0:T(8,128)(2,1)S(1)}, u32[]{:S(2)}, u32[]{:S(2)}) collective-permute-start(bf16[32,2048]{1,0:T(8,128)(2,1)S(1)} %get-tuple-element.67), channel_id=1, source_target_pairs={{0,6},{2,4},{4,2},{6,0},{8,14},{10,12},{12,10},{14,8},{1,7},{3,5},... | collective-permute-start | bytes 393224 | tf_op jit(solution)/shard_map/ppermute | solution.py:177
  66.3 1.0 %collective-permute-done.24 = bf16[32,2048]{1,0:T(8,128)(2,1)S(1)} collective-permute-done((bf16[32,2048]{1,0:T(8,128)(2,1)S(1)}, bf16[32,2048]{1,0:T(8,128)(2,1)S(1)}, u32[]{:S(2)}, u32[]{:S(2)}) %collective-permute-start.24) | collective-permute-done | bytes 131104 | tf_op jit(solution)/shard_map/ppermute | solution.py:170
  67.3 0.3 collective-permute-done.25
  67.7 1.9 %collective-permute-start.26 = (bf16[32,2048]{1,0:T(8,128)(2,1)S(1)}, bf16[32,2048]{1,0:T(8,128)(2,1)S(1)}, u32[]{:S(2)}, u32[]{:S(2)}) collective-permute-start(bf16[32,2048]{1,0:T(8,128)(2,1)S(1)} %add_convert_fusion.4), channel_id=1, source_target_pairs={{0,8},{4,12},{8,0},{12,4},{1,9},{5,13},{9,1},{13,5},{2,10},{6,14},... | collective-permute-start | bytes 393224 | tf_op jit(solution)/shard_map/ppermute | solution.py:170
  69.6 0.8 %collective-permute-done.27 = bf16[32,2048]{1,0:T(8,128)(2,1)S(1)} collective-permute-done((bf16[32,2048]{1,0:T(8,128)(2,1)S(1)}, bf16[32,2048]{1,0:T(8,128)(2,1)S(1)}, u32[]{:S(2)}, u32[]{:S(2)}) %collective-permute-start.27) | collective-permute-done | bytes 131104 | tf_op jit(solution)/shard_map/ppermute | solution.py:170
  70.6 5.1 %collective-permute-done.28 = bf16[32,2048]{1,0:T(8,128)(2,1)S(1)} collective-permute-done((bf16[32,2048]{1,0:T(8,128)(2,1)S(1)}, bf16[32,2048]{1,0:T(8,128)(2,1)S(1)}, u32[]{:S(2)}, u32[]{:S(2)}) %collective-permute-start.28) | collective-permute-done | bytes 131104 | tf_op jit(solution)/shard_map/ppermute | solution.py:177
  75.7 0.8 %collective-permute-done.26 = bf16[32,2048]{1,0:T(8,128)(2,1)S(1)} collective-permute-done((bf16[32,2048]{1,0:T(8,128)(2,1)S(1)}, bf16[32,2048]{1,0:T(8,128)(2,1)S(1)}, u32[]{:S(2)}, u32[]{:S(2)}) %collective-permute-start.26) | collective-permute-done | bytes 131104 | tf_op jit(solution)/shard_map/ppermute | solution.py:170
  76.5 0.8 add_convert_fusion.3
  (33 shorter events, 1.4 us)
Async XLA Ops:
  0.8 8.9 %collective-permute-start.2 = (bf16[128,256]{1,0:T(8,128)(2,1)S(1)}, bf16[128,256]{1,0:T(8,128)(2,1)S(1)}, u32[]{:S(2)}, u32[]{:S(2)}) collective-permute-start(bf16[128,256]{1,0:T(8,128)(2,1)S(1)} %pad_maximum_fusion.1.kv_ref), channel_id=1, source_target_pairs={{0,12},{4,8},{8,4},{12,0},{1,13},{5,9},{9,5},{13,1},{2,14},{6,10},... | collective-permute-start | bytes 196616 | tf_op jit(solution)/shard_map/ppermute | solution.py:170
  5.9 4.7 %collective-permute-start.1 = (bf16[128,256]{1,0:T(8,128)(2,1)S(1)}, bf16[128,256]{1,0:T(8,128)(2,1)S(1)}, u32[]{:S(2)}, u32[]{:S(2)}) collective-permute-start(bf16[128,256]{1,0:T(8,128)(2,1)S(1)} %pad_maximum_fusion.1.kv_ref), channel_id=1, source_target_pairs={{0,4},{4,0},{8,12},{12,8},{1,5},{5,1},{9,13},{13,9},{2,6},{6,2},{1... | collective-permute-start | bytes 196616 | tf_op jit(solution)/shard_map/ppermute | solution.py:170
  5.9 6.3 %collective-permute-start = (bf16[128,256]{1,0:T(8,128)(2,1)S(1)}, bf16[128,256]{1,0:T(8,128)(2,1)S(1)}, u32[]{:S(2)}, u32[]{:S(2)}) collective-permute-start(bf16[128,256]{1,0:T(8,128)(2,1)S(1)} %pad_maximum_fusion.1.kv_ref), channel_id=1, source_target_pairs={{0,8},{4,12},{8,0},{12,4},{1,9},{5,13},{9,1},{13,5},{2,10},{6,14},... | collective-permute-start | bytes 196616 | tf_op jit(solution)/shard_map/ppermute | solution.py:170
  14.2 1.6 %collective-permute-start.3 = (bf16[64,2048]{1,0:T(8,128)(2,1)S(1)}, bf16[64,2048]{1,0:T(8,128)(2,1)S(1)}, u32[]{:S(2)}, u32[]{:S(2)}) collective-permute-start(bf16[64,2048]{1,0:T(8,128)(2,1)S(1)} %get-tuple-element.44), channel_id=1, source_target_pairs={{0,1},{1,0},{2,3},{3,2},{4,5},{5,4},{6,7},{7,6},{8,9},{9,8},{10,11... | collective-permute-start | bytes 786440 | tf_op jit(solution)/shard_map/ppermute | solution.py:170
  15.9 5.6 %collective-permute-start.4 = (bf16[32,2048]{1,0:T(8,128)(2,1)S(1)}, bf16[32,2048]{1,0:T(8,128)(2,1)S(1)}, u32[]{:S(2)}, u32[]{:S(2)}) collective-permute-start(bf16[32,2048]{1,0:T(8,128)(2,1)S(1)} %fusion), channel_id=1, source_target_pairs={{0,2},{2,0},{1,3},{3,1},{4,6},{6,4},{5,7},{7,5},{8,10},{10,8},{9,1... | collective-permute-start | bytes 393224 | tf_op jit(solution)/shard_map/ppermute | solution.py:170
  21.8 8.8 %collective-permute-start.6 = (bf16[32,2176]{1,0:T(8,128)(2,1)S(1)}, bf16[32,2176]{1,0:T(8,128)(2,1)S(1)}, u32[]{:S(2)}, u32[]{:S(2)}) collective-permute-start(bf16[32,2176]{1,0:T(8,128)(2,1)S(1)} %pad_maximum_fusion.refs_0_), channel_id=1, source_target_pairs={{0,8},{4,12},{8,0},{12,4},{1,9},{5,13},{9,1},{13,5},{2,10},{6,14},... | collective-permute-start | bytes 417800 | tf_op jit(solution)/shard_map/ppermute | solution.py:170
  23.3 9.5 %collective-permute-start.9 = (bf16[32,2176]{1,0:T(8,128)(2,1)S(1)}, bf16[32,2176]{1,0:T(8,128)(2,1)S(1)}, u32[]{:S(2)}, u32[]{:S(2)}) collective-permute-start(bf16[32,2176]{1,0:T(8,128)(2,1)S(1)} %pad_maximum_fusion.refs_0_), channel_id=1, source_target_pairs={{0,6},{2,4},{4,2},{6,0},{8,14},{10,12},{12,10},{14,8},{1,7},{3,5},... | collective-permute-start | bytes 417800 | tf_op jit(solution)/shard_map/ppermute | solution.py:177
  26.3 7.9 %collective-permute-start.8 = (bf16[32,2176]{1,0:T(8,128)(2,1)S(1)}, bf16[32,2176]{1,0:T(8,128)(2,1)S(1)}, u32[]{:S(2)}, u32[]{:S(2)}) collective-permute-start(bf16[32,2176]{1,0:T(8,128)(2,1)S(1)} %pad_maximum_fusion.refs_0_), channel_id=1, source_target_pairs={{0,2},{2,0},{1,3},{3,1},{4,6},{6,4},{5,7},{7,5},{8,10},{10,8},{9,1... | collective-permute-start | bytes 417800 | tf_op jit(solution)/shard_map/ppermute | solution.py:170
  26.8 7.6 %collective-permute-start.5 = (bf16[32,2176]{1,0:T(8,128)(2,1)S(1)}, bf16[32,2176]{1,0:T(8,128)(2,1)S(1)}, u32[]{:S(2)}, u32[]{:S(2)}) collective-permute-start(bf16[32,2176]{1,0:T(8,128)(2,1)S(1)} %pad_maximum_fusion.refs_0_), channel_id=1, source_target_pairs={{0,4},{4,0},{8,12},{12,8},{1,5},{5,1},{9,13},{13,9},{2,6},{6,2},{1... | collective-permute-start | bytes 417800 | tf_op jit(solution)/shard_map/ppermute | solution.py:170
  30.6 8.1 %collective-permute-start.11 = (bf16[32,2176]{1,0:T(8,128)(2,1)S(1)}, bf16[32,2176]{1,0:T(8,128)(2,1)S(1)}, u32[]{:S(2)}, u32[]{:S(2)}) collective-permute-start(bf16[32,2176]{1,0:T(8,128)(2,1)S(1)} %collective-permute-done.6.refs_2_), channel_id=1, source_target_pairs={{0,6},{2,4},{4,2},{6,0},{8,14},{10,12},{12,10},{14,8},{1,7},{3,5},... | collective-permute-start | bytes 417800 | tf_op jit(solution)/shard_map/ppermute | solution.py:177
  31.6 7.4 %collective-permute-start.10 = (bf16[32,2176]{1,0:T(8,128)(2,1)S(1)}, bf16[32,2176]{1,0:T(8,128)(2,1)S(1)}, u32[]{:S(2)}, u32[]{:S(2)}) collective-permute-start(bf16[32,2176]{1,0:T(8,128)(2,1)S(1)} %collective-permute-done.6.refs_2_), channel_id=1, source_target_pairs={{0,2},{2,0},{1,3},{3,1},{4,6},{6,4},{5,7},{7,5},{8,10},{10,8},{9,1... | collective-permute-start | bytes 417800 | tf_op jit(solution)/shard_map/ppermute | solution.py:170
  32.8 7.2 %collective-permute-start.7 = (bf16[32,2176]{1,0:T(8,128)(2,1)S(1)}, bf16[32,2176]{1,0:T(8,128)(2,1)S(1)}, u32[]{:S(2)}, u32[]{:S(2)}) collective-permute-start(bf16[32,2176]{1,0:T(8,128)(2,1)S(1)} %collective-permute-done.6.refs_2_), channel_id=1, source_target_pairs={{0,4},{4,0},{8,12},{12,8},{1,5},{5,1},{9,13},{13,9},{2,6},{6,2},{1... | collective-permute-start | bytes 417800 | tf_op jit(solution)/shard_map/ppermute | solution.py:170
  34.4 5.7 %collective-permute-start.12 = (bf16[32,2176]{1,0:T(8,128)(2,1)S(1)}, bf16[32,2176]{1,0:T(8,128)(2,1)S(1)}, u32[]{:S(2)}, u32[]{:S(2)}) collective-permute-start(bf16[32,2176]{1,0:T(8,128)(2,1)S(1)} %pad_maximum_fusion.refs_0_), channel_id=1, source_target_pairs={{0,1},{1,0},{2,3},{3,2},{4,5},{5,4},{6,7},{7,6},{8,9},{9,8},{10,11... | collective-permute-start | bytes 417800 | tf_op jit(solution)/shard_map/ppermute | solution.py:170
  34.4 6.2 %collective-permute-start.13 = (bf16[32,2176]{1,0:T(8,128)(2,1)S(1)}, bf16[32,2176]{1,0:T(8,128)(2,1)S(1)}, u32[]{:S(2)}, u32[]{:S(2)}) collective-permute-start(bf16[32,2176]{1,0:T(8,128)(2,1)S(1)} %collective-permute-done.5.refs_1_), channel_id=1, source_target_pairs={{0,1},{1,0},{2,3},{3,2},{4,5},{5,4},{6,7},{7,6},{8,9},{9,8},{10,11... | collective-permute-start | bytes 417800 | tf_op jit(solution)/shard_map/ppermute | solution.py:170
  38.8 1.8 %collective-permute-start.14 = (bf16[32,2176]{1,0:T(8,128)(2,1)S(1)}, bf16[32,2176]{1,0:T(8,128)(2,1)S(1)}, u32[]{:S(2)}, u32[]{:S(2)}) collective-permute-start(bf16[32,2176]{1,0:T(8,128)(2,1)S(1)} %collective-permute-done.6.refs_2_), channel_id=1, source_target_pairs={{0,1},{1,0},{2,3},{3,2},{4,5},{5,4},{6,7},{7,6},{8,9},{9,8},{10,11... | collective-permute-start | bytes 417800 | tf_op jit(solution)/shard_map/ppermute | solution.py:170
  39.0 2.0 %collective-permute-start.16 = (bf16[32,2176]{1,0:T(8,128)(2,1)S(1)}, bf16[32,2176]{1,0:T(8,128)(2,1)S(1)}, u32[]{:S(2)}, u32[]{:S(2)}) collective-permute-start(bf16[32,2176]{1,0:T(8,128)(2,1)S(1)} %collective-permute-done.8.refs_4_), channel_id=1, source_target_pairs={{0,1},{1,0},{2,3},{3,2},{4,5},{5,4},{6,7},{7,6},{8,9},{9,8},{10,11... | collective-permute-start | bytes 417800 | tf_op jit(solution)/shard_map/ppermute | solution.py:170
  40.0 1.4 %collective-permute-start.17 = (bf16[32,2176]{1,0:T(8,128)(2,1)S(1)}, bf16[32,2176]{1,0:T(8,128)(2,1)S(1)}, u32[]{:S(2)}, u32[]{:S(2)}) collective-permute-start(bf16[32,2176]{1,0:T(8,128)(2,1)S(1)} %collective-permute-done.9.refs_5_), channel_id=1, source_target_pairs={{0,1},{1,0},{2,3},{3,2},{4,5},{5,4},{6,7},{7,6},{8,9},{9,8},{10,11... | collective-permute-start | bytes 417800 | tf_op jit(solution)/shard_map/ppermute | solution.py:170
  40.0 1.6 %collective-permute-start.15 = (bf16[32,2176]{1,0:T(8,128)(2,1)S(1)}, bf16[32,2176]{1,0:T(8,128)(2,1)S(1)}, u32[]{:S(2)}, u32[]{:S(2)}) collective-permute-start(bf16[32,2176]{1,0:T(8,128)(2,1)S(1)} %collective-permute-done.7.refs_3_), channel_id=1, source_target_pairs={{0,1},{1,0},{2,3},{3,2},{4,5},{5,4},{6,7},{7,6},{8,9},{9,8},{10,11... | collective-permute-start | bytes 417800 | tf_op jit(solution)/shard_map/ppermute | solution.py:170
  40.6 1.4 %collective-permute-start.18 = (bf16[32,2176]{1,0:T(8,128)(2,1)S(1)}, bf16[32,2176]{1,0:T(8,128)(2,1)S(1)}, u32[]{:S(2)}, u32[]{:S(2)}) collective-permute-start(bf16[32,2176]{1,0:T(8,128)(2,1)S(1)} %collective-permute-done.10.refs_6_), channel_id=1, source_target_pairs={{0,1},{1,0},{2,3},{3,2},{4,5},{5,4},{6,7},{7,6},{8,9},{9,8},{10,11... | collective-permute-start | bytes 417800 | tf_op jit(solution)/shard_map/ppermute | solution.py:170
  40.6 1.5 %collective-permute-start.19 = (bf16[32,2176]{1,0:T(8,128)(2,1)S(1)}, bf16[32,2176]{1,0:T(8,128)(2,1)S(1)}, u32[]{:S(2)}, u32[]{:S(2)}) collective-permute-start(bf16[32,2176]{1,0:T(8,128)(2,1)S(1)} %collective-permute-done.11.refs_7_), channel_id=1, source_target_pairs={{0,1},{1,0},{2,3},{3,2},{4,5},{5,4},{6,7},{7,6},{8,9},{9,8},{10,11... | collective-permute-start | bytes 417800 | tf_op jit(solution)/shard_map/ppermute | solution.py:170
  56.0 1.6 %collective-permute-start.22 = (bf16[64,2048]{1,0:T(8,128)(2,1)S(1)}, bf16[64,2048]{1,0:T(8,128)(2,1)S(1)}, u32[]{:S(2)}, u32[]{:S(2)}) collective-permute-start(bf16[64,2048]{1,0:T(8,128)(2,1)S(1)} %get-tuple-element.62), channel_id=1, source_target_pairs={{0,1},{1,0},{2,3},{3,2},{4,5},{5,4},{6,7},{7,6},{8,9},{9,8},{10,11... | collective-permute-start | bytes 786440 | tf_op jit(solution)/shard_map/ppermute | solution.py:170
  56.4 3.7 %collective-permute-start.20 = (bf16[64,2048]{1,0:T(8,128)(2,1)S(1)}, bf16[64,2048]{1,0:T(8,128)(2,1)S(1)}, u32[]{:S(2)}, u32[]{:S(2)}) collective-permute-start(bf16[64,2048]{1,0:T(8,128)(2,1)S(1)} %get-tuple-element.56), channel_id=1, source_target_pairs={{0,1},{1,0},{2,3},{3,2},{4,5},{5,4},{6,7},{7,6},{8,9},{9,8},{10,11... | collective-permute-start | bytes 786440 | tf_op jit(solution)/shard_map/ppermute | solution.py:170
  56.6 3.6 %collective-permute-start.21 = (bf16[128,2048]{1,0:T(8,128)(2,1)S(1)}, bf16[128,2048]{1,0:T(8,128)(2,1)S(1)}, u32[]{:S(2)}, u32[]{:S(2)}) collective-permute-start(bf16[128,2048]{1,0:T(8,128)(2,1)S(1)} %get-tuple-element.58), channel_id=1, source_target_pairs={{0,1},{1,0},{2,3},{3,2},{4,5},{5,4},{6,7},{7,6},{8,9},{9,8},{10,11... | collective-permute-start | bytes 1572872 | tf_op jit(solution)/shard_map/ppermute | solution.py:170
  57.7 7.3 %collective-permute-start.23 = (bf16[32,2048]{1,0:T(8,128)(2,1)S(1)}, bf16[32,2048]{1,0:T(8,128)(2,1)S(1)}, u32[]{:S(2)}, u32[]{:S(2)}) collective-permute-start(bf16[32,2048]{1,0:T(8,128)(2,1)S(1)} %get-tuple-element.68), channel_id=1, source_target_pairs={{0,6},{2,4},{4,2},{6,0},{8,14},{10,12},{12,10},{14,8},{1,7},{3,5},... | collective-permute-start | bytes 393224 | tf_op jit(solution)/shard_map/ppermute | solution.py:177
  59.0 8.3 %collective-permute-start.24 = (bf16[32,2048]{1,0:T(8,128)(2,1)S(1)}, bf16[32,2048]{1,0:T(8,128)(2,1)S(1)}, u32[]{:S(2)}, u32[]{:S(2)}) collective-permute-start(bf16[32,2048]{1,0:T(8,128)(2,1)S(1)} %get-tuple-element.69), channel_id=1, source_target_pairs={{0,2},{2,0},{1,3},{3,1},{4,6},{6,4},{5,7},{7,5},{8,10},{10,8},{9,1... | collective-permute-start | bytes 393224 | tf_op jit(solution)/shard_map/ppermute | solution.py:170
  60.4 7.2 %collective-permute-start.25 = (bf16[32,2048]{1,0:T(8,128)(2,1)S(1)}, bf16[32,2048]{1,0:T(8,128)(2,1)S(1)}, u32[]{:S(2)}, u32[]{:S(2)}) collective-permute-start(bf16[32,2048]{1,0:T(8,128)(2,1)S(1)} %slice.36), channel_id=1, source_target_pairs={{0,4},{4,0},{8,12},{12,8},{1,5},{5,1},{9,13},{13,9},{2,6},{6,2},{1... | collective-permute-start | bytes 393224 | tf_op jit(solution)/shard_map/ppermute | solution.py:170
  61.6 8.8 %collective-permute-start.27 = (bf16[32,2048]{1,0:T(8,128)(2,1)S(1)}, bf16[32,2048]{1,0:T(8,128)(2,1)S(1)}, u32[]{:S(2)}, u32[]{:S(2)}) collective-permute-start(bf16[32,2048]{1,0:T(8,128)(2,1)S(1)} %get-tuple-element.65), channel_id=1, source_target_pairs={{0,4},{4,0},{8,12},{12,8},{1,5},{5,1},{9,13},{13,9},{2,6},{6,2},{1... | collective-permute-start | bytes 393224 | tf_op jit(solution)/shard_map/ppermute | solution.py:170
  62.6 8.0 %collective-permute-start.29 = (bf16[32,2048]{1,0:T(8,128)(2,1)S(1)}, bf16[32,2048]{1,0:T(8,128)(2,1)S(1)}, u32[]{:S(2)}, u32[]{:S(2)}) collective-permute-start(bf16[32,2048]{1,0:T(8,128)(2,1)S(1)} %get-tuple-element.66), channel_id=1, source_target_pairs={{0,2},{2,0},{1,3},{3,1},{4,6},{6,4},{5,7},{7,5},{8,10},{10,8},{9,1... | collective-permute-start | bytes 393224 | tf_op jit(solution)/shard_map/ppermute | solution.py:170
  65.0 10.6 %collective-permute-start.28 = (bf16[32,2048]{1,0:T(8,128)(2,1)S(1)}, bf16[32,2048]{1,0:T(8,128)(2,1)S(1)}, u32[]{:S(2)}, u32[]{:S(2)}) collective-permute-start(bf16[32,2048]{1,0:T(8,128)(2,1)S(1)} %get-tuple-element.67), channel_id=1, source_target_pairs={{0,6},{2,4},{4,2},{6,0},{8,14},{10,12},{12,10},{14,8},{1,7},{3,5},... | collective-permute-start | bytes 393224 | tf_op jit(solution)/shard_map/ppermute | solution.py:177
  67.7 8.9 %collective-permute-start.26 = (bf16[32,2048]{1,0:T(8,128)(2,1)S(1)}, bf16[32,2048]{1,0:T(8,128)(2,1)S(1)}, u32[]{:S(2)}, u32[]{:S(2)}) collective-permute-start(bf16[32,2048]{1,0:T(8,128)(2,1)S(1)} %add_convert_fusion.4), channel_id=1, source_target_pairs={{0,8},{4,12},{8,0},{12,4},{1,9},{5,13},{9,1},{13,5},{2,10},{6,14},... | collective-permute-start | bytes 393224 | tf_op jit(solution)/shard_map/ppermute | solution.py:170
